TPU v7x, 32 devices: a whole 2x2x4 slice. The times are simulated.
32 devices in a mesh: section: 2 (over x), dp: 16 (over z, y, core).
Axes of the slice: x: 2, y: 2, z: 4, core: 2. Of those that a mesh axis runs over, the one named last changes fastest.
Arguments:
- tokens: bfloat16 [32, 1024, 768], P('dp'), may hold values from -6 to 6
- mask_pos: int32 [32, 160], P('dp'), may hold values from 0 to 1023, as said below
- mask_count: int32 [32], P('dp'), may hold values from 80 to 160, as said below
- mask_vec: bfloat16 [768], replicated, may hold values from -5 to 5
- proj_weight: bfloat16 [2, 768, 1536], P('section'), may hold values from -0.21875 to 0.21875
- proj_bias: bfloat16 [2, 1152], P('section'), may hold values from -3 to 3
- depth_kernel: bfloat16 [2, 9, 768], P('section'), may hold values from -2 to 2
- point_weight: bfloat16 [2, 768, 384], P('section'), may hold values from -0.21875 to 0.21875
- point_bias: bfloat16 [2, 384], P('section'), may hold values from -3 to 3
- kernel_weight: bfloat16 [2, 384, 54], P('section'), may hold values from -0.3125 to 0.3125
- kernel_bias: bfloat16 [2, 54], P('section'), may hold values from -3 to 3
- out_weight: bfloat16 [2, 768, 768], P('section'), may hold values from -0.75 to 0.75
- out_bias: bfloat16 [2, 768], P('section'), may hold values from -2 to 2
- norm_gain: bfloat16 [2, 768], P('section'), may hold values from 0.099609375 to 1.8984375
- norm_shift: bfloat16 [2, 768], P('section'), may hold values from -2 to 2
- inner_weight: bfloat16 [2, 2, 384, 1536], P('section'), may hold values from -0.3125 to 0.3125
- inner_bias: bfloat16 [2, 3072], P('section'), may hold values from -2 to 2
- second_feed_weight: bfloat16 [2, 2, 1536, 384], P('section'), may hold values from -0.15625 to 0.15625
- second_feed_bias: bfloat16 [2, 768], P('section'), may hold values from -2 to 2
- final_gain: bfloat16 [2, 768], P('section'), may hold values from 0.099609375 to 1.8984375
- final_shift: bfloat16 [2, 768], P('section'), may hold values from -2 to 2
- cotangent: bfloat16 [32, 1024, 768], P('dp'), may hold values from -6 to 6
Outputs:
- states: bfloat16 [2, 32, 1024, 768], P('section', 'dp')
- in_grads: bfloat16 [2, 32, 1024, 768], P('section', 'dp')
- mask_grad: float32 [768], replicated
- proj_weight_grad: float32 [2, 768, 1536], P('section')
- proj_bias_grad: float32 [2, 1152], P('section')
- depth_kernel_grad: float32 [2, 9, 768], P('section')
- point_weight_grad: float32 [2, 768, 384], P('section')
- point_bias_grad: float32 [2, 384], P('section')
- kernel_weight_grad: float32 [2, 384, 54], P('section')
- kernel_bias_grad: float32 [2, 54], P('section')
- out_weight_grad: float32 [2, 768, 768], P('section')
- out_bias_grad: float32 [2, 768], P('section')
- norm_gain_grad: float32 [2, 768], P('section')
- norm_shift_grad: float32 [2, 768], P('section')
- inner_weight_grad: float32 [2, 2, 384, 1536], P('section')
- inner_bias_grad: float32 [2, 3072], P('section')
- outer_weight_grad: float32 [2, 2, 1536, 384], P('section')
- outer_bias_grad: float32 [2, 768], P('section')
- final_gain_grad: float32 [2, 768], P('section')
- final_shift_grad: float32 [2, 768], P('section')
Inputs may be any that keep to these rules, and one draw needn't show every extreme that they name: `mask_pos`: in sequence r the first mask_count[r] entries are distinct positions; the entries after them are padding and mark nothing. `mask_count`: some sequence has 160 masked positions and some has 80.
All inputs are finite; a program needn't handle non-finite values.
Results may differ from a plain program's by a relative error of at most 0.035.
Values may be sent and summed in bfloat16 or wider, within the bound.
No kernel may reach another device: no remote copies, remote signals or barrier semaphores. Data moves between devices by JAX's collectives and lax.ppermute only.
A program may use at most 384 MiB of HBM per device.

v0:
```python
from functools import partial

import jax
import jax.numpy as jnp
from jax import lax
from jax.sharding import PartitionSpec as P

MICRO = 2


def shifted(block, axis, distance):
    devices = range(lax.axis_size(axis))
    route = [(i - distance, i) for i in devices if i - distance in devices]
    return lax.ppermute(block, axis, route)


def contract_rows(left, right):
    return lax.dot_general(
        left, right, (((0,), (0,)), ((), ())), preferred_element_type=jnp.float32
    )


def times_transposed(left, right):
    return lax.dot_general(
        left, right, (((1,), (1,)), ((), ())), preferred_element_type=jnp.float32
    )


def norm_forward(values, gain, shift):
    mean = jnp.mean(values, axis=-1, keepdims=True)
    centered = values - mean
    inverse = lax.rsqrt(jnp.mean(centered * centered, axis=-1, keepdims=True) + 1e-06)
    unit = centered * inverse
    return (unit * gain.astype(jnp.float32) + shift.astype(jnp.float32), unit, inverse)


def norm_backward(grad, unit, inverse, gain):
    gain_grad = jnp.sum(grad * unit, axis=0)
    shift_grad = jnp.sum(grad, axis=0)
    scaled = grad * gain.astype(jnp.float32)
    back = inverse * (
        scaled
        - jnp.mean(scaled, axis=-1, keepdims=True)
        - unit * jnp.mean(scaled * unit, axis=-1, keepdims=True)
    )
    return (back, gain_grad, shift_grad)


def attention_forward(q_low, k_low, v_low):
    batch_rows, sequence_length, heads, head_size = q_low.shape
    block = min(512, sequence_length)
    pieces = sequence_length // block
    scale = head_size ** (-0.5)

    def sequence(args):
        q_seq, k_seq, v_seq = args

        def piece(q_blk):
            scores = (
                jnp.einsum("qhe,khe->hqk", q_blk, k_seq, preferred_element_type=jnp.float32) * scale
            )
            probs = jax.nn.softmax(scores, axis=-1)
            return jnp.einsum(
                "hqk,khe->qhe",
                probs.astype(jnp.bfloat16),
                v_seq,
                preferred_element_type=jnp.float32,
            )

        return lax.map(piece, q_seq.reshape(pieces, block, heads, head_size)).reshape(
            sequence_length, heads, head_size
        )

    return lax.map(sequence, (q_low, k_low, v_low))


def attention_backward(q_low, k_low, v_low, grad_low):
    batch_rows, sequence_length, heads, head_size = q_low.shape
    block = min(512, sequence_length)
    pieces = sequence_length // block
    scale = head_size ** (-0.5)

    def sequence(args):
        q_seq, k_seq, v_seq, g_seq = args

        def piece(carry, blocks):
            key_grad, value_grad = carry
            q_blk, g_blk = blocks
            scores = (
                jnp.einsum("qhe,khe->hqk", q_blk, k_seq, preferred_element_type=jnp.float32) * scale
            )
            probs = jax.nn.softmax(scores, axis=-1)
            upstream = jnp.einsum("qhe,khe->hqk", g_blk, v_seq, preferred_element_type=jnp.float32)
            soft = probs * (upstream - jnp.sum(upstream * probs, axis=-1, keepdims=True))
            soft_low = (soft * scale).astype(jnp.bfloat16)
            query_grad = jnp.einsum(
                "hqk,khe->qhe", soft_low, k_seq, preferred_element_type=jnp.float32
            )
            key_grad = key_grad + jnp.einsum(
                "hqk,qhe->khe", soft_low, q_blk, preferred_element_type=jnp.float32
            )
            value_grad = value_grad + jnp.einsum(
                "hqk,qhe->khe",
                probs.astype(jnp.bfloat16),
                g_blk,
                preferred_element_type=jnp.float32,
            )
            return ((key_grad, value_grad), query_grad)

        zeros = jnp.zeros((sequence_length, heads, head_size), jnp.float32)
        shaped = (
            q_seq.reshape(pieces, block, heads, head_size),
            g_seq.reshape(pieces, block, heads, head_size),
        )
        (key_grad, value_grad), query_grads = lax.scan(piece, (zeros, zeros), shaped)
        return (query_grads.reshape(sequence_length, heads, head_size), key_grad, value_grad)

    return lax.map(sequence, (q_low, k_low, v_low, grad_low))


def layer_forward(params, hidden):
    (
        proj_weight,
        proj_bias,
        depth_kernel,
        point_weight,
        point_bias,
        kernel_weight,
        kernel_bias,
        out_weight,
        out_bias,
        norm_gain,
        norm_shift,
        inner_weight,
        inner_bias,
        second_feed_weight,
        second_feed_bias,
        final_gain,
        final_shift,
    ) = params
    batch_rows, sequence_length, width = hidden.shape
    span = kernel_weight.shape[0]
    taps = depth_kernel.shape[0]
    heads = kernel_bias.shape[0] // taps
    head_size = span // heads
    groups = inner_weight.shape[0]
    half = taps // 2
    count = batch_rows * sequence_length
    flat = hidden.reshape(count, width)
    proj = jnp.dot(flat, proj_weight, preferred_element_type=jnp.float32)
    bias = proj_bias.astype(jnp.float32)
    query = proj[:, :span] + bias[:span]
    keys = proj[:, span : 2 * span]
    values = proj[:, 2 * span : 3 * span] + bias[span : 2 * span]
    spanned = proj[:, 3 * span :] + bias[2 * span :]
    padded = jnp.pad(hidden.astype(jnp.float32), ((0, 0), (half, half), (0, 0)))
    depth_taps = depth_kernel.astype(jnp.float32)
    depth = depth_taps[0] * padded[:, 0:sequence_length]
    for tap in range(1, taps):
        depth = depth + depth_taps[tap] * padded[:, tap : tap + sequence_length]
    depth_low = depth.astype(jnp.bfloat16).reshape(count, width)
    keyconv = jnp.dot(
        depth_low, point_weight, preferred_element_type=jnp.float32
    ) + point_bias.astype(jnp.float32)
    mixed = (keyconv * query).astype(jnp.bfloat16)
    logits = jnp.dot(mixed, kernel_weight, preferred_element_type=jnp.float32) + kernel_bias.astype(
        jnp.float32
    )
    kern = jax.nn.softmax(logits.reshape(batch_rows, sequence_length, heads, taps), axis=-1)
    span_pad = jnp.pad(
        spanned.reshape(batch_rows, sequence_length, heads, head_size),
        ((0, 0), (half, half), (0, 0), (0, 0)),
    )
    dynamic = kern[..., 0:1] * span_pad[:, 0:sequence_length]
    for tap in range(1, taps):
        dynamic = dynamic + kern[..., tap : tap + 1] * span_pad[:, tap : tap + sequence_length]
    q_low = query.astype(jnp.bfloat16).reshape(batch_rows, sequence_length, heads, head_size)
    k_low = keys.astype(jnp.bfloat16).reshape(batch_rows, sequence_length, heads, head_size)
    v_low = values.astype(jnp.bfloat16).reshape(batch_rows, sequence_length, heads, head_size)
    attend = attention_forward(q_low, k_low, v_low)
    context = jnp.concatenate(
        [attend.reshape(count, span), dynamic.reshape(count, span)], axis=1
    ).astype(jnp.bfloat16)
    summed = (
        jnp.dot(context, out_weight, preferred_element_type=jnp.float32)
        + out_bias.astype(jnp.float32)
        + flat.astype(jnp.float32)
    )
    normed, unit_one, inverse_one = norm_forward(summed, norm_gain, norm_shift)
    grouped = normed.astype(jnp.bfloat16).reshape(count, groups, width // groups)
    inner = jnp.einsum("ngc,gcf->ngf", grouped, inner_weight, preferred_element_type=jnp.float32)
    inner = inner.reshape(count, -1) + inner_bias.astype(jnp.float32)
    activation_values = jax.nn.gelu(inner, approximate=False).astype(jnp.bfloat16)
    second_projection = jnp.einsum(
        "soz,ozl->sol",
        activation_values.reshape(count, groups, -1),
        second_feed_weight,
        preferred_element_type=jnp.float32,
    ).reshape(count, width) + second_feed_bias.astype(jnp.float32)
    final, unit_two, inverse_two = norm_forward(second_projection + normed, final_gain, final_shift)
    kept = (
        query,
        keyconv,
        mixed,
        kern,
        span_pad,
        depth_low,
        q_low,
        k_low,
        v_low,
        context,
        normed,
        unit_one,
        inverse_one,
        inner,
        activation_values,
        unit_two,
        inverse_two,
    )
    return (final.reshape(batch_rows, sequence_length, width), kept)


def layer_backward(params, hidden, kept, grad_out):
    (
        proj_weight,
        proj_bias,
        depth_kernel,
        point_weight,
        point_bias,
        kernel_weight,
        kernel_bias,
        out_weight,
        out_bias,
        norm_gain,
        norm_shift,
        inner_weight,
        inner_bias,
        second_feed_weight,
        second_feed_bias,
        final_gain,
        final_shift,
    ) = params
    (
        query,
        keyconv,
        mixed,
        kern,
        span_pad,
        depth_low,
        q_low,
        k_low,
        v_low,
        context,
        normed,
        unit_one,
        inverse_one,
        inner,
        activation_values,
        unit_two,
        inverse_two,
    ) = kept
    batch_rows, sequence_length, width = hidden.shape
    span = kernel_weight.shape[0]
    taps = depth_kernel.shape[0]
    heads = kernel_bias.shape[0] // taps
    head_size = span // heads
    groups = inner_weight.shape[0]
    half = taps // 2
    count = batch_rows * sequence_length
    flat = hidden.reshape(count, width)
    dsum, final_gain_grad, final_shift_grad = norm_backward(
        grad_out.reshape(count, width), unit_two, inverse_two, final_gain
    )
    outer_bias_grad = jnp.sum(dsum, axis=0)
    reduced_sum_gradient = dsum.astype(jnp.bfloat16).reshape(count, groups, width // groups)
    grouped_activations = activation_values.reshape(count, groups, -1)
    outer_weight_grad = jnp.einsum(
        "lzi,lzm->zim",
        grouped_activations,
        reduced_sum_gradient,
        preferred_element_type=jnp.float32,
    )
    dactive = jnp.einsum(
        "mjv,jtv->mjt", reduced_sum_gradient, second_feed_weight, preferred_element_type=jnp.float32
    ).reshape(count, -1)
    gelu_back = jax.vjp(partial(jax.nn.gelu, approximate=False), inner)[1]
    dinner = gelu_back(dactive)[0]
    inner_bias_grad = jnp.sum(dinner, axis=0)
    dinner_low = dinner.astype(jnp.bfloat16).reshape(count, groups, -1)
    grouped = normed.astype(jnp.bfloat16).reshape(count, groups, width // groups)
    inner_weight_grad = jnp.einsum(
        "ngc,ngf->gcf", grouped, dinner_low, preferred_element_type=jnp.float32
    )
    dnormed = (
        jnp.einsum(
            "ngf,gcf->ngc", dinner_low, inner_weight, preferred_element_type=jnp.float32
        ).reshape(count, width)
        + dsum
    )
    dsummed, norm_gain_grad, norm_shift_grad = norm_backward(
        dnormed, unit_one, inverse_one, norm_gain
    )
    out_bias_grad = jnp.sum(dsummed, axis=0)
    dsummed_low = dsummed.astype(jnp.bfloat16)
    out_weight_grad = contract_rows(context, dsummed_low)
    dcontext = times_transposed(dsummed_low, out_weight).astype(jnp.bfloat16)
    dattend = dcontext[:, :span].reshape(batch_rows, sequence_length, heads, head_size)
    ddynamic = (
        dcontext[:, span:]
        .astype(jnp.float32)
        .reshape(batch_rows, sequence_length, heads, head_size)
    )
    dkern = jnp.stack(
        [
            jnp.sum(ddynamic * span_pad[:, tap : tap + sequence_length], axis=-1)
            for tap in range(taps)
        ],
        axis=-1,
    )
    spread_pad = jnp.pad(ddynamic, ((0, 0), (half, half), (0, 0), (0, 0)))
    kern_pad = jnp.pad(kern, ((0, 0), (half, half), (0, 0), (0, 0)))
    dspans = (
        kern_pad[:, 2 * half : 2 * half + sequence_length, :, 0:1]
        * spread_pad[:, 2 * half : 2 * half + sequence_length]
    )
    for tap in range(1, taps):
        begin = 2 * half - tap
        dspans = (
            dspans
            + kern_pad[:, begin : begin + sequence_length, :, tap : tap + 1]
            * spread_pad[:, begin : begin + sequence_length]
        )
    dlogits = kern * (dkern - jnp.sum(dkern * kern, axis=-1, keepdims=True))
    dlogits = dlogits.reshape(count, heads * taps)
    kernel_bias_grad = jnp.sum(dlogits, axis=0)
    dlogits_low = dlogits.astype(jnp.bfloat16)
    kernel_weight_grad = contract_rows(mixed, dlogits_low)
    dmixed = times_transposed(dlogits_low, kernel_weight)
    dkeyconv = dmixed * query
    point_bias_grad = jnp.sum(dkeyconv, axis=0)
    dkeyconv_low = dkeyconv.astype(jnp.bfloat16)
    point_weight_grad = contract_rows(depth_low, dkeyconv_low)
    ddepth = times_transposed(dkeyconv_low, point_weight).reshape(
        batch_rows, sequence_length, width
    )
    hidden_pad = jnp.pad(hidden.astype(jnp.float32), ((0, 0), (half, half), (0, 0)))
    depth_kernel_grad = jnp.stack(
        [
            jnp.sum(ddepth * hidden_pad[:, tap : tap + sequence_length], axis=(0, 1))
            for tap in range(taps)
        ],
        axis=0,
    )
    ddepth_pad = jnp.pad(ddepth, ((0, 0), (half, half), (0, 0)))
    depth_taps = depth_kernel.astype(jnp.float32)
    dconv = depth_taps[0] * ddepth_pad[:, 2 * half : 2 * half + sequence_length]
    for tap in range(1, taps):
        begin = 2 * half - tap
        dconv = dconv + depth_taps[tap] * ddepth_pad[:, begin : begin + sequence_length]
    dquery_att, dkeys, dvalues = attention_backward(q_low, k_low, v_low, dattend)
    dquery = dquery_att.reshape(count, span) + dmixed * keyconv
    dvalues = dvalues.reshape(count, span)
    dspans = dspans.reshape(count, span)
    proj_bias_grad = jnp.concatenate(
        [jnp.sum(dquery, axis=0), jnp.sum(dvalues, axis=0), jnp.sum(dspans, axis=0)]
    )
    dproj_low = jnp.concatenate(
        [dquery, dkeys.reshape(count, span), dvalues, dspans], axis=1
    ).astype(jnp.bfloat16)
    proj_weight_grad = contract_rows(flat, dproj_low)
    dhidden = times_transposed(dproj_low, proj_weight) + dsummed + dconv.reshape(count, width)
    grads = (
        proj_weight_grad,
        proj_bias_grad,
        depth_kernel_grad,
        point_weight_grad,
        point_bias_grad,
        kernel_weight_grad,
        kernel_bias_grad,
        out_weight_grad,
        out_bias_grad,
        norm_gain_grad,
        norm_shift_grad,
        inner_weight_grad,
        inner_bias_grad,
        outer_weight_grad,
        outer_bias_grad,
        final_gain_grad,
        final_shift_grad,
    )
    return (dhidden.reshape(batch_rows, sequence_length, width), grads)


def local(
    tokens,
    mask_pos,
    mask_count,
    mask_vec,
    proj_weight,
    proj_bias,
    depth_kernel,
    point_weight,
    point_bias,
    kernel_weight,
    kernel_bias,
    out_weight,
    out_bias,
    norm_gain,
    norm_shift,
    inner_weight,
    inner_bias,
    second_feed_weight,
    second_feed_bias,
    final_gain,
    final_shift,
    cotangent,
):
    params = tuple(
        (
            array[0]
            for array in (
                proj_weight,
                proj_bias,
                depth_kernel,
                point_weight,
                point_bias,
                kernel_weight,
                kernel_bias,
                out_weight,
                out_bias,
                norm_gain,
                norm_shift,
                inner_weight,
                inner_bias,
                second_feed_weight,
                second_feed_bias,
                final_gain,
                final_shift,
            )
        )
    )
    section = lax.axis_index("section")
    sections = lax.axis_size("section")
    rows, sequence_length, width = tokens.shape
    per = rows // MICRO
    slots = jnp.arange(mask_pos.shape[1], dtype=jnp.int32)[None, :] < mask_count[:, None]
    hits = (
        mask_pos[:, :, None] == jnp.arange(sequence_length, dtype=jnp.int32)[None, None, :]
    ) & slots[:, :, None]
    masked = jnp.any(hits, axis=1)
    filled = jnp.where(masked[:, :, None], mask_vec[None, None, :], tokens)
    first_section = section == 0
    last_section = section == sections - 1
    ticks = MICRO + sections - 1

    def active_forward(value):
        produced, kept = layer_forward(params, value)
        kept_part = ()
        return (produced, kept_part)

    def resting_forward(value):
        produced = jnp.zeros(value.shape, jnp.float32)
        kept_part = ()
        return (produced, kept_part)

    incoming = jnp.zeros((per, sequence_length, width), jnp.bfloat16)
    entries = []
    results = []
    for tick in range(ticks):
        micro = tick - section
        valid = (micro >= 0) & (micro < MICRO)
        start = min(tick, MICRO - 1) * per
        layer_in = jnp.where(first_section, filled[start : start + per], incoming)
        produced, kept = lax.cond(valid, active_forward, resting_forward, layer_in)
        produced_low = produced.astype(jnp.bfloat16)
        entries.append(layer_in)
        results.append(produced_low)
        if tick + 1 < ticks:
            incoming = shifted(produced_low, "section", 1)
    entry_stack = jnp.stack(entries)
    result_stack = jnp.stack(results)
    states = jnp.concatenate(
        [
            lax.dynamic_index_in_dim(result_stack, micro + section, 0, keepdims=False)
            for micro in range(MICRO)
        ],
        axis=0,
    )

    def active_backward(args):
        value, grad, stored = args
        memo = layer_forward(params, value)[1]
        return layer_backward(params, value, memo, grad)

    def resting_backward(args):
        value, grad, stored = args
        return (
            jnp.zeros(value.shape, jnp.float32),
            tuple((jnp.zeros(item.shape, jnp.float32) for item in params)),
        )

    totals = tuple((jnp.zeros(item.shape, jnp.float32) for item in params))
    back_in = jnp.zeros((per, sequence_length, width), jnp.bfloat16)
    back_results = []
    for tick in range(ticks):
        micro = tick - (sections - 1 - section)
        valid = (micro >= 0) & (micro < MICRO)
        index = jnp.clip(micro, 0, MICRO - 1)
        own_grad = lax.dynamic_slice_in_dim(cotangent, index * per, per, 0)
        grad_in = jnp.where(last_section, own_grad, back_in).astype(jnp.float32)
        layer_in = lax.dynamic_index_in_dim(entry_stack, index + section, 0, keepdims=False)
        stored = None
        dhidden, grads = lax.cond(
            valid, active_backward, resting_backward, (layer_in, grad_in, stored)
        )
        totals = tuple((total + grad for total, grad in zip(totals, grads)))
        back_results.append(dhidden)
        if tick + 1 < ticks:
            back_in = shifted(dhidden.astype(jnp.bfloat16), "section", -1)
    totals = lax.psum(
        (
            totals[0],
            totals[1],
            totals[2],
            totals[3],
            totals[4],
            totals[5],
            totals[6],
            totals[7],
            totals[8],
            totals[9],
            totals[10],
            totals[11],
            totals[12],
            totals[13],
            totals[14],
            totals[15],
            totals[16],
        ),
        "dp",
    )
    back_stack = jnp.stack(back_results)
    in_grad = jnp.concatenate(
        [
            lax.dynamic_index_in_dim(back_stack, micro + sections - 1 - section, 0, keepdims=False)
            for micro in range(MICRO)
        ],
        axis=0,
    )
    replaced = masked[:, :, None] & first_section
    chosen = jnp.where(replaced, 0.0, in_grad).astype(jnp.bfloat16)
    mask_part = jnp.sum(jnp.where(replaced, in_grad, 0.0), axis=(0, 1))
    mask_grad = lax.psum(mask_part, ("section", "dp"))
    return (states[None], chosen[None], mask_grad) + tuple((total[None] for total in totals))


def solution(mesh):
    return jax.shard_map(
        local,
        mesh=mesh,
        in_specs=(
            P("dp", None, None),
            P("dp", None),
            P("dp"),
            P(),
            P("section", None, None),
            P("section", None),
            P("section", None, None),
            P("section", None, None),
            P("section", None),
            P("section", None, None),
            P("section", None),
            P("section", None, None),
            P("section", None),
            P("section", None),
            P("section", None),
            P("section", None, None, None),
            P("section", None),
            P("section", None, None, None),
            P("section", None),
            P("section", None),
            P("section", None),
            P("dp", None, None),
        ),
        out_specs=(
            P("section", "dp", None, None),
            P("section", "dp", None, None),
            P(),
            P("section", None, None),
            P("section", None),
            P("section", None, None),
            P("section", None, None),
            P("section", None),
            P("section", None, None),
            P("section", None),
            P("section", None, None),
            P("section", None),
            P("section", None),
            P("section", None),
            P("section", None, None, None),
            P("section", None),
            P("section", None, None, None),
            P("section", None),
            P("section", None),
            P("section", None),
        ),
        check_vma=False,
    )
```

profile of v0, /device:TPU:0, one launch (start us, length us, event | category | flops | bytes accessed | tf_op | source)
XLA Modules:
  0.0 2041.2 jit_solution(17758433644979008051)
XLA Ops:
  18.6 127.7 %conditional.6 = (bf16[1,1024,768]{1,2,0:T(8,128)(2,1)}, bf16[1,1,1024,768]{2,3,1,0:T(8,128)(2,1)}) conditional(s32[]{:T(128)} %convert_element_type.749, () %tuple.131, (bf16[1,1024,768]{1,2,0:T(8,128)(2,1)S(1)}, bf16[768,1536]{1,0:T(8,128)(2,1)S(1)}, bf16[1152]{0:T(1024)(128)(2,1)S(1)}, bf16[9,768]{1,0:T(8,128)(2,1)S(1)}, ...), branch_computations={%region_1.2_spmd, %region_2.13_spmd} | conditional | flops 10185022464 | bytes 146578128 | solution.py:474
  25.5 19.3 fusion.394
  57.3 26.5 %while.226 = (s32[]{:T(128)}, bf16[2,512,6,64]{1,3,2,0:T(8,128)(2,1)S(1)}, bf16[2,512,6,64]{1,3,2,0:T(8,128)(2,1)S(1)}, bf16[1024,6,64]{0,2,1:T(8,128)(2,1)S(1)}, bf16[1024,6,64]{0,2,1:T(8,128)(2,1)S(1)}, /*index=5*/s32[]{:T(128)}) while((s32[]{:T(128)}, bf16[2,512,6,64]{1,3,2,0:T(8,128)(2,1)S(1)}, bf16[2,512,6,64]{1,3,2,0:T(8,128)(2,1)S(1)}, ...), condition=%wide.region_6.6_spmd, body=%wide.region_3.5_spmd.sunk | while | flops 821036032 | bytes 27947084 | solution.py:70
  90.7 48.5 %fusion.361 = f32[2,1024,384]{1,2,0:T(8,128)} fusion(bf16[2,1536,384]{2,1,0:T(8,128)(2,1)} %get-tuple-element.1616, bf16[1024,2,384]{0,2,1:T(8,128)(2,1)} %bitcast.1616, bf16[2,384,1536]{2,1,0:T(8,128)(2,1)} %get-tuple-element.942, f32[2,1536]{1,0:T(2,128)S(1)} %reshape.2798), kind=kOutput, calls=%fused_computation.285 | convolution fusion | flops 5039456256 | bytes 9449472 | tf_op jit(solution)/shard_map/cond/branch_1_fun/soz,ozl->sol/dot_general | solution.py:194
  147.9 34.7 %collective-permute-done = bf16[1,1024,768]{1,2,0:T(8,128)(2,1)S(1)} collective-permute-done((bf16[1,1024,768]{1,2,0:T(8,128)(2,1)}, bf16[1,1024,768]{1,2,0:T(8,128)(2,1)S(1)}, u32[]{:S(2)}, u32[]{:S(2)}) %collective-permute-start) | collective-permute-done | bytes 1572896 | tf_op jit(solution)/shard_map/ppermute | solution.py:14
  185.4 117.5 %conditional.7 = (bf16[1,1024,768]{1,2,0:T(8,128)(2,1)}, bf16[1,1,1024,768]{2,3,1,0:T(8,128)(2,1)}) conditional(s32[]{:T(128)} %convert_element_type.750, () %tuple.133, (bf16[1,1024,768]{1,2,0:T(8,128)(2,1)}, bf16[768,1536]{1,0:T(8,128)(2,1)S(1)}, bf16[1152]{0:T(1024)(128)(2,1)S(1)}, bf16[9,768]{1,0:T(8,128)(2,1)S(1)}, ...), branch_computations={%region_13.14_spmd, %region_14.25_spmd} | conditional | flops 10185022464 | bytes 138713776 | solution.py:474
  226.8 26.5 %while.227 = (s32[]{:T(128)}, bf16[2,512,6,64]{1,3,2,0:T(8,128)(2,1)S(1)}, bf16[2,512,6,64]{1,3,2,0:T(8,128)(2,1)S(1)}, bf16[1024,6,64]{0,2,1:T(8,128)(2,1)S(1)}, bf16[1024,6,64]{0,2,1:T(8,128)(2,1)S(1)}, /*index=5*/s32[]{:T(128)}) while((s32[]{:T(128)}, bf16[2,512,6,64]{1,3,2,0:T(8,128)(2,1)S(1)}, bf16[2,512,6,64]{1,3,2,0:T(8,128)(2,1)S(1)}, ...), condition=%wide.region_18.18_spmd, body=%wide.region_15.17_spmd.sunk | while | flops 821036032 | bytes 27947084 | solution.py:70
  260.2 35.9 %fusion.471 = f32[2,1024,384]{1,2,0:T(8,128)} fusion(bf16[2,1536,384]{2,1,0:T(8,128)(2,1)} %get-tuple-element.1634, bf16[1024,2,384]{0,2,1:T(8,128)(2,1)} %bitcast.1617, bf16[2,384,1536]{2,1,0:T(8,128)(2,1)} %get-tuple-element.967, f32[2,1536]{1,0:T(2,128)S(1)} %reshape.2799), kind=kOutput, calls=%fused_computation.443 | convolution fusion | flops 5039456256 | bytes 9449472 | tf_op jit(solution)/shard_map/cond/branch_1_fun/soz,ozl->sol/dot_general | solution.py:194
  319.0 22.2 %collective-permute-done.1 = bf16[1,1024,768]{1,2,0:T(8,128)(2,1)} collective-permute-done((bf16[1,1024,768]{1,2,0:T(8,128)(2,1)}, bf16[1,1024,768]{1,2,0:T(8,128)(2,1)}, u32[]{:S(2)}, u32[]{:S(2)}) %collective-permute-start.1) | collective-permute-done | bytes 1572896 | tf_op jit(solution)/shard_map/ppermute | solution.py:14
  345.6 23.7 %conditional.9 = (f32[1,1024,768]{1,2,0:T(8,128)}, f32[768,1536]{1,0:T(8,128)}, f32[1152]{0:T(1024)S(1)}, f32[9,768]{1,0:T(8,128)}, f32[768,384]{1,0:T(8,128)}, ...) conditional(s32[]{:T(128)} %convert_element_type.752, ...), branch_computations={%region_37.38_spmd, %region_38.89_spmd} | conditional | flops 30615441408 | bytes 746869760 | solution.py:513
  375.0 419.3 %collective-permute-done.2 = bf16[1,1024,768]{1,2,0:T(8,128)(2,1)} collective-permute-done((bf16[1,1024,768]{1,2,0:T(8,128)(2,1)}, bf16[1,1024,768]{1,2,0:T(8,128)(2,1)}, u32[]{:S(2)}, u32[]{:S(2)}) %collective-permute-start.2) | collective-permute-done | bytes 1572896 | tf_op jit(solution)/shard_map/ppermute | solution.py:14
  797.7 405.1 %conditional.10 = (f32[1,1024,768]{1,2,0:T(8,128)}, f32[768,1536]{1,0:T(8,128)}, f32[1152]{0:T(1024)S(1)}, f32[9,768]{1,0:T(8,128)}, f32[768,384]{1,0:T(8,128)},...) conditional(s32[]{:T(128)} %convert_element_type.754, ...), branch_computations={%region_89.90_spmd, %region_90.141_spmd} | conditional | flops 30615441408 | bytes 746863552 | solution.py:513
  828.3 26.9 %while.222 = (s32[]{:T(128)}, bf16[2,512,6,64]{1,3,2,0:T(8,128)(2,1)S(1)}, bf16[2,512,6,64]{1,3,2,0:T(8,128)(2,1)S(1)}, bf16[1024,6,64]{0,2,1:T(8,128)(2,1)S(1)}, bf16[1024,6,64]{0,2,1:T(8,128)(2,1)S(1)}, /*index=5*/s32[]{:T(128)}) while((s32[]{:T(128)}, bf16[2,512,6,64]{1,3,2,0:T(8,128)(2,1)S(1)}, bf16[2,512,6,64]{1,3,2,0:T(8,128)(2,1)S(1)}, ...), condition=%wide.region_94.94_spmd, body=%wide.region_91.93_spmd.sunk | while | flops 821036032 | bytes 27947084 | solution.py:70
  864.6 33.6 %fusion.772 = (bf16[1024,2,1536]{2,0,1:T(8,128)(2,1)S(1)}, f32[1024,2,1536]{2,0,1:T(8,128)}, f32[2,1024,1536]{2,1,0:T(8,128)}) fusion(f32[2,1536]{1,0:T(2,128)S(1)} %reshape.2806, bf16[1024,2,384]{0,2,1:T(8,128)(2,1)} %bitcast.1608, bf16[2,384,1536]{2,1,0:T(8,128)(2,1)} %get-tuple-element.1067), kind=kOutput, calls=%fused_computation.961 | convolution fusion | flops 2623537152 | bytes 35401728 | tf_op jit(solution)/shard_map/cond/branch_1_fun/ngc,gcf->ngf/dot_general | solution.py:191
  952.0 187.9 %while.223 = (s32[]{:T(128)}, f32[1024,6,64]{0,2,1:T(8,128)}, f32[1024,6,64]{0,2,1:T(8,128)}, f32[2,512,6,64]{1,0,3,2:T(2,128)}, bf16[2,512,6,64]{1,3,2,0:T(8,12...) while((s32[]{:T(128)}, f32[1024,6,64]{0,2,1:T(8,128)}, ...), condition=%wide.region_109.109_spmd.clone, body=%wide.region_105.108_spmd.clone.sunk | while | flops 2074616832 | bytes 133768376 | solution.py:115
  967.8 21.3 %fusion.1329 = f32[1,512,6,64]{1,3,2,0:T(8,128)S(1)} fusion(bf16[1024,6,64]{0,2,1:T(8,128)(2,1)S(1)} %copy-done.132, f32[6,512,1024]{2,1,0:T(8,128)} %fusion.1327, f32[6,512,1024]{2,1,0:T(8,128)} %get-tuple-element.2577, f32[6,512]{1,0:T(8,128)S(1)} %get-tuple-element.2578), kind=kOutput, calls=%fused_computation.165.clone.1 | convolution fusion | flops 424677376 | bytes 26750976 | tf_op jit(solution)/shard_map/cond/branch_1_fun/while/body/eval_jaxpr/while/body/eval_jaxpr/hqk,khe->qhe/dot_general | solution.py:96
  1011.6 33.9 %bitcast_add_fusion.26 = f32[1024,6,64]{0,2,1:T(8,128)} fusion(f32[1024,6,64]{0,2,1:T(8,128)} %get-tuple-element.2748, f32[6,512,1024]{2,1,0:T(8,128)} %fusion.1327, pred[]{:T(512)S(6)} %compare.31, bf16[2,512,6,64]{1,3,2,0:T(8,128)(2,1)S(1)} %copy-done.128, s32[]{:T(128)} %get-tuple-element.2747, f32[6,512,1024]{2,1,0:T(8,128)} %get-tuple-element.2577, ...), kind=kOutput, calls=%fused_computation.163.clone.1 | convolution fusion | flops 425463808 | bytes 53903872 | tf_op jit(solution)/shard_map/cond/branch_1_fun/while/body/eval_jaxpr/while/body/eval_jaxpr/hqk,qhe->khe/dot_general | solution.py:99
  1061.2 21.3 %fusion.1329 = f32[1,512,6,64]{1,3,2,0:T(8,128)S(1)} fusion(bf16[1024,6,64]{0,2,1:T(8,128)(2,1)S(1)} %copy-done.132, f32[6,512,1024]{2,1,0:T(8,128)} %fusion.1327, f32[6,512,1024]{2,1,0:T(8,128)} %get-tuple-element.2577, f32[6,512]{1,0:T(8,128)S(1)} %get-tuple-element.2578), kind=kOutput, calls=%fused_computation.165.clone.1 | convolution fusion | flops 424677376 | bytes 26750976 | tf_op jit(solution)/shard_map/cond/branch_1_fun/while/body/eval_jaxpr/while/body/eval_jaxpr/hqk,khe->qhe/dot_general | solution.py:96
  1105.5 34.2 %bitcast_add_fusion.26 = f32[1024,6,64]{0,2,1:T(8,128)} fusion(f32[1024,6,64]{0,2,1:T(8,128)} %get-tuple-element.2748, f32[6,512,1024]{2,1,0:T(8,128)} %fusion.1327, pred[]{:T(512)S(6)} %compare.31, bf16[2,512,6,64]{1,3,2,0:T(8,128)(2,1)S(1)} %copy-done.128, s32[]{:T(128)} %get-tuple-element.2747, f32[6,512,1024]{2,1,0:T(8,128)} %get-tuple-element.2577, ...), kind=kOutput, calls=%fused_computation.163.clone.1 | convolution fusion | flops 425463808 | bytes 53903872 | tf_op jit(solution)/shard_map/cond/branch_1_fun/while/body/eval_jaxpr/while/body/eval_jaxpr/hqk,qhe->khe/dot_general | solution.py:99
  1208.5 34.6 %collective-permute-done.3 = bf16[1,1024,768]{1,2,0:T(8,128)(2,1)} collective-permute-done((bf16[1,1024,768]{1,2,0:T(8,128)(2,1)}, bf16[1,1024,768]{1,2,0:T(8,128)(2,1)}, u32[]{:S(2)}, u32[]{:S(2)}) %collective-permute-start.3) | collective-permute-done | bytes 1572896 | tf_op jit(solution)/shard_map/ppermute | solution.py:14
  1246.5 418.7 %conditional.11 = (f32[768,1536]{1,0:T(8,128)}, f32[1152]{0:T(1024)S(1)}, f32[9,768]{1,0:T(8,128)}, f32[768,384]{1,0:T(8,128)}, f32[384]{0:T(512)}, /*index=5*/f...) conditional(s32[]{:T(128)} %convert_element_type.757, ...), branch_computations={%region_141.142_spmd, %region_142.193_spmd} | conditional | flops 30615441408 | bytes 797164672 | solution.py:513
  1277.4 26.7 %while.224 = (s32[]{:T(128)}, bf16[2,512,6,64]{1,3,2,0:T(8,128)(2,1)S(1)}, bf16[2,512,6,64]{1,3,2,0:T(8,128)(2,1)S(1)}, bf16[1024,6,64]{0,2,1:T(8,128)(2,1)S(1)}, bf16[1024,6,64]{0,2,1:T(8,128)(2,1)S(1)}, /*index=5*/s32[]{:T(128)}) while((s32[]{:T(128)}, bf16[2,512,6,64]{1,3,2,0:T(8,128)(2,1)S(1)}, ...), condition=%wide.region_146.146_spmd, body=%wide.region_143.145_spmd.sunk | while | flops 821036032 | bytes 27947084 | solution.py:70
  1313.5 33.9 %fusion.881 = (bf16[1024,2,1536]{2,0,1:T(8,128)(2,1)S(1)}, f32[1024,2,1536]{2,0,1:T(8,128)}, f32[2,1024,1536]{2,1,0:T(8,128)}) fusion(f32[2,1536]{1,0:T(2,128)S(1)} %reshape.2810, bf16[1024,2,384]{0,2,1:T(8,128)(2,1)} %bitcast.1604, bf16[2,384,1536]{2,1,0:T(8,128)(2,1)} %get-tuple-element.1106), kind=kOutput, calls=%fused_computation.1203 | convolution fusion | flops 2623537152 | bytes 35401728 | tf_op jit(solution)/shard_map/cond/branch_1_fun/ngc,gcf->ngf/dot_general | solution.py:191
  1393.3 188.2 %while.225 = (s32[]{:T(128)}, f32[1024,6,64]{0,2,1:T(8,128)}, f32[1024,6,64]{0,2,1:T(8,128)}, f32[2,512,6,64]{1,0,3,2:T(2,128)}, bf16[2,512,6,64]{1,3,2,0:T(8,12...) while((s32[]{:T(128)}, f32[1024,6,64]{0,2,1:T(8,128)}, ...), condition=%wide.region_161.161_spmd.clone, body=%wide.region_157.160_spmd.clone.sunk | while | flops 2074616832 | bytes 133768376 | solution.py:115
  1409.2 21.3 %fusion.1311 = f32[1,512,6,64]{1,3,2,0:T(8,128)S(1)} fusion(bf16[1024,6,64]{0,2,1:T(8,128)(2,1)S(1)} %copy-done.136, f32[6,512,1024]{2,1,0:T(8,128)} %fusion.1309, f32[6,512,1024]{2,1,0:T(8,128)} %get-tuple-element.2560, f32[6,512]{1,0:T(8,128)S(1)} %get-tuple-element.2561), kind=kOutput, calls=%fused_computation.205.clone.1 | convolution fusion | flops 424677376 | bytes 26750976 | tf_op jit(solution)/shard_map/cond/branch_1_fun/while/body/eval_jaxpr/while/body/eval_jaxpr/hqk,khe->qhe/dot_general | solution.py:96
  1453.0 33.9 %bitcast_add_fusion.24 = f32[1024,6,64]{0,2,1:T(8,128)} fusion(f32[1024,6,64]{0,2,1:T(8,128)} %get-tuple-element.2796, f32[6,512,1024]{2,1,0:T(8,128)} %fusion.1309, pred[]{:T(512)S(6)} %compare.30, bf16[2,512,6,64]{1,3,2,0:T(8,128)(2,1)S(1)} %copy-done.134, s32[]{:T(128)} %get-tuple-element.2795, f32[6,512,1024]{2,1,0:T(8,128)} %get-tuple-element.2560, ...), kind=kOutput, calls=%fused_computation.203.clone.1 | convolution fusion | flops 425463808 | bytes 53903872 | tf_op jit(solution)/shard_map/cond/branch_1_fun/while/body/eval_jaxpr/while/body/eval_jaxpr/hqk,qhe->khe/dot_general | solution.py:99
  1502.6 21.3 %fusion.1311 = f32[1,512,6,64]{1,3,2,0:T(8,128)S(1)} fusion(bf16[1024,6,64]{0,2,1:T(8,128)(2,1)S(1)} %copy-done.136, f32[6,512,1024]{2,1,0:T(8,128)} %fusion.1309, f32[6,512,1024]{2,1,0:T(8,128)} %get-tuple-element.2560, f32[6,512]{1,0:T(8,128)S(1)} %get-tuple-element.2561), kind=kOutput, calls=%fused_computation.205.clone.1 | convolution fusion | flops 424677376 | bytes 26750976 | tf_op jit(solution)/shard_map/cond/branch_1_fun/while/body/eval_jaxpr/while/body/eval_jaxpr/hqk,khe->qhe/dot_general | solution.py:96
  1546.9 34.2 %bitcast_add_fusion.24 = f32[1024,6,64]{0,2,1:T(8,128)} fusion(f32[1024,6,64]{0,2,1:T(8,128)} %get-tuple-element.2796, f32[6,512,1024]{2,1,0:T(8,128)} %fusion.1309, pred[]{:T(512)S(6)} %compare.30, bf16[2,512,6,64]{1,3,2,0:T(8,128)(2,1)S(1)} %copy-done.134, s32[]{:T(128)} %get-tuple-element.2795, f32[6,512,1024]{2,1,0:T(8,128)} %get-tuple-element.2560, ...), kind=kOutput, calls=%fused_computation.203.clone.1 | convolution fusion | flops 425463808 | bytes 53903872 | tf_op jit(solution)/shard_map/cond/branch_1_fun/while/body/eval_jaxpr/while/body/eval_jaxpr/hqk,qhe->khe/dot_general | solution.py:99
  1605.2 22.0 %fusion.905 = f32[1,1,1024,768]{2,3,1,0:T(8,128)S(1)} fusion(f32[1,1024,768]{1,2,0:T(8,128)} %bitcast.1591, f32[1024,768]{0,1:T(8,128)} %get-tuple-element.2198, f32[1024,768]{0,1:T(8,128)} %copy-done.84, bf16[768,1536]{1,0:T(8,128)(2,1)} %get-tuple-element.1094, f32[768]{0:T(1024)} %copy-done.354, f32[768]{0:T(1024)} %copy-done.350, ...), kind=kOutput, calls=%fused_computation.1256 | convolution fusion | flops 2443444224 | bytes 18115584 | tf_op jit(solution)/shard_map/cond/branch_1_fun/dot_general | solution.py:24
  1731.1 39.9 %psum.126 = f32[768]{0:T(1024)} all-reduce(f32[768]{0:T(1024)S(1)} %fusion.983), channel_id=1, replica_groups=mesh['section'=2,'dp'=16] {'section','dp'}, use_global_device_ids=true, to_apply=%region_194.195 | all-reduce | flops 768 | bytes 6144 | tf_op jit(solution)/shard_map/psum | solution.py:553
  1771.7 64.7 %all-reduce.21 = (f32[1,1152]{1,0:T(1,128)}, f32[1,9,768]{2,0,1:T(1,128)}, f32[1,384]{1,0:T(1,128)}, f32[1,54]{1,0:T(1,128)}, f32[1,768]{1,0:T(1,128)}, /*index=...) all-reduce(f32[1,1152]{1,0:T(1,128)S(1)} %broadcast_in_dim.225, ...), channel_id=1, replica_groups=mesh['section'=2,'dp'=16] {'dp'}, use_global_device_ids=true, to_apply=%region_196.197 | all-reduce | flops 16182 | bytes 129456 | tf_op jit(solution)/shard_map/psum | solution.py:520
  1839.6 179.9 %all-reduce.25.cloned.1.call-done = (f32[1,768,1536]{2,1,0:T(8,128)}, f32[1,768,384]{2,1,0:T(8,128)}, f32[1,384,54]{1,0,2:T(1,128)}, f32[1,768,768]{2,1,0:T(8,12...) async-done(((f32[1,768,1536]{2,1,0:T(8,128)}, f32[1,768,384]{2,1,0:T(8,128)}, f32[1,384,54]{1,0,2:T(1,128)}, f32[1,768,768]{2,1,0:T(8,128)}, ...) | async-done | bytes 17777680 | tf_op jit(solution)/shard_map/psum | solution.py:520
  (1113 shorter events, 800.3 us)
Async XLA Ops:
  7.2 2012.3 %all-reduce.25.cloned.1.call-start = ((), (), s32[]{:S(2)}) async-start(), calls=%async_computation | async-start | bytes 35555328 | tf_op jit(solution)/shard_map/psum | solution.py:520
  11.6 334.1 %copy-start.172 = (bf16[3072]{0:T(1024)(128)(2,1)}, bf16[3072]{0:T(1024)(128)(2,1)S(1)}, u32[]{:S(2)}) copy-start(bf16[3072]{0:T(1024)(128)(2,1)S(1)} %reduce.212) | copy-start | bytes 18436
  11.6 334.0 %copy-start.168 = (bf16[1152]{0:T(1024)(128)(2,1)}, bf16[1152]{0:T(1024)(128)(2,1)S(1)}, u32[]{:S(2)}) copy-start(bf16[1152]{0:T(1024)(128)(2,1)S(1)} %reduce.207) | copy-start | bytes 6916
  90.7 48.5 %copy-start.192 = (bf16[768]{0:T(1024)(128)(2,1)S(1)}, bf16[768]{0:T(1024)(128)(2,1)}, u32[]{:S(2)}) copy-start(bf16[768]{0:T(1024)(128)(2,1)} %get-tuple-element.945) | copy-start | bytes 4612 | tf_op jit(solution)/shard_map/cond
  146.3 39.0 %copy-start.60 = (bf16[1,768,384]{2,1,0:T(8,128)(2,1)S(1)}, bf16[1,768,384]{2,1,0:T(8,128)(2,1)}, u32[]{:S(2)}) copy-start(bf16[1,768,384]{2,1,0:T(8,128)(2,1)} %param.59) | copy-start | bytes 1769476
  146.3 39.0 %copy-start.112 = (bf16[1,9,768]{2,1,0:T(8,128)(2,1)S(1)}, bf16[1,9,768]{2,1,0:T(8,128)(2,1)}, u32[]{:S(2)}) copy-start(bf16[1,9,768]{2,1,0:T(8,128)(2,1)} %param.58) | copy-start | bytes 41476
  146.3 39.0 %copy-start.230 = (bf16[384]{0:T(512)(128)(2,1)S(1)}, bf16[384]{0:T(512)(128)(2,1)}, u32[]{:S(2)}) copy-start(bf16[384]{0:T(512)(128)(2,1)} %copy-done.229) | copy-start | bytes 2308
  146.4 39.0 %copy-start.400 = (bf16[1,54]{1,0:T(2,128)(2,1)S(1)}, bf16[1,54]{1,0:T(2,128)(2,1)}, u32[]{:S(2)}) copy-start(bf16[1,54]{1,0:T(2,128)(2,1)} %param.62) | copy-start | bytes 328
  146.4 36.3 %collective-permute-start = (bf16[1,1024,768]{1,2,0:T(8,128)(2,1)}, bf16[1,1024,768]{1,2,0:T(8,128)(2,1)S(1)}, u32[]{:S(2)}, u32[]{:S(2)}) collective-permute-start(bf16[1,1024,768]{1,2,0:T(8,128)(2,1)} %get-tuple-element.1194), channel_id=1, source_target_pairs={{0,16},{1,17},{2,18},{3,19},{4,20},{5,21},{6,22},{7,23},{8,24},{9,... | collective-permute-start | bytes 4718600 | tf_op jit(solution)/shard_map/ppermute | solution.py:14
  147.9 37.5 %copy-start.384 = (bf16[1,768,1536]{2,1,0:T(8,128)(2,1)S(1)}, bf16[1,768,1536]{2,1,0:T(8,128)(2,1)}, u32[]{:S(2)}) copy-start(bf16[1,768,1536]{2,1,0:T(8,128)(2,1)} %param.56) | copy-start | bytes 7077892
  260.2 35.9 %copy-start.193 = (bf16[768]{0:T(1024)(128)(2,1)S(1)}, bf16[768]{0:T(1024)(128)(2,1)}, u32[]{:S(2)}) copy-start(bf16[768]{0:T(1024)(128)(2,1)} %get-tuple-element.970) | copy-start | bytes 4612 | tf_op jit(solution)/shard_map/cond
  302.9 38.3 %collective-permute-start.1 = (bf16[1,1024,768]{1,2,0:T(8,128)(2,1)}, bf16[1,1024,768]{1,2,0:T(8,128)(2,1)}, u32[]{:S(2)}, u32[]{:S(2)}) collective-permute-start(bf16[1,1024,768]{1,2,0:T(8,128)(2,1)} %get-tuple-element.1196), channel_id=1, source_target_pairs={{0,16},{1,17},{2,18},{3,19},{4,20},{5,21},{6,22},{7,23},{8,24},{9,... | collective-permute-start | bytes 4718600 | tf_op jit(solution)/shard_map/ppermute | solution.py:14
  372.8 421.6 %collective-permute-start.2 = (bf16[1,1024,768]{1,2,0:T(8,128)(2,1)}, bf16[1,1024,768]{1,2,0:T(8,128)(2,1)}, u32[]{:S(2)}, u32[]{:S(2)}) collective-permute-start(bf16[1,1024,768]{1,2,0:T(8,128)(2,1)} %convert_element_type.755), channel_id=1, source_target_pairs={{16,0},{17,1},{18,2},{19,3},{20,4},{21,5},{22,6},{23,7},{24,8},{25... | collective-permute-start | bytes 4718600 | tf_op jit(solution)/shard_map/ppermute | solution.py:14
  375.0 422.7 %copy-start.62 = (bf16[1,768,384]{2,1,0:T(8,128)(2,1)S(1)}, bf16[1,768,384]{2,1,0:T(8,128)(2,1)}, u32[]{:S(2)}) copy-start(bf16[1,768,384]{2,1,0:T(8,128)(2,1)} %param.59) | copy-start | bytes 1769476
  375.0 422.7 %copy-start.114 = (bf16[1,9,768]{2,1,0:T(8,128)(2,1)S(1)}, bf16[1,9,768]{2,1,0:T(8,128)(2,1)}, u32[]{:S(2)}) copy-start(bf16[1,9,768]{2,1,0:T(8,128)(2,1)} %param.58) | copy-start | bytes 41476
  375.0 422.7 %copy-start.169 = (bf16[1152]{0:T(1024)(128)(2,1)S(1)}, bf16[1152]{0:T(1024)(128)(2,1)}, u32[]{:S(2)}) copy-start(bf16[1152]{0:T(1024)(128)(2,1)} %copy-done.168) | copy-start | bytes 6916
  375.0 422.7 %copy-start.173 = (bf16[3072]{0:T(1024)(128)(2,1)S(1)}, bf16[3072]{0:T(1024)(128)(2,1)}, u32[]{:S(2)}) copy-start(bf16[3072]{0:T(1024)(128)(2,1)} %copy-done.172) | copy-start | bytes 18436
  375.0 422.7 %copy-start.182 = (bf16[768]{0:T(1024)(128)(2,1)S(1)}, bf16[768]{0:T(1024)(128)(2,1)}, u32[]{:S(2)}) copy-start(bf16[768]{0:T(1024)(128)(2,1)} %reduce.210) | copy-start | bytes 4612
  375.0 422.7 %copy-start.232 = (bf16[384]{0:T(512)(128)(2,1)S(1)}, bf16[384]{0:T(512)(128)(2,1)}, u32[]{:S(2)}) copy-start(bf16[384]{0:T(512)(128)(2,1)} %copy-done.229) | copy-start | bytes 2308
  375.0 422.7 %copy-start.402 = (bf16[1,54]{1,0:T(2,128)(2,1)S(1)}, bf16[1,54]{1,0:T(2,128)(2,1)}, u32[]{:S(2)}) copy-start(bf16[1,54]{1,0:T(2,128)(2,1)} %param.62) | copy-start | bytes 328
  864.6 33.6 %copy-start.390 = (bf16[2,1536,384]{2,1,0:T(8,128)(2,1)S(1)}, bf16[2,1536,384]{2,1,0:T(8,128)(2,1)}, u32[]{:S(2)}) copy-start(bf16[2,1536,384]{2,1,0:T(8,128)(2,1)} %get-tuple-element.1069) | copy-start | bytes 7077892 | tf_op jit(solution)/shard_map/cond
  1206.3 36.8 %collective-permute-start.3 = (bf16[1,1024,768]{1,2,0:T(8,128)(2,1)}, bf16[1,1024,768]{1,2,0:T(8,128)(2,1)}, u32[]{:S(2)}, u32[]{:S(2)}) collective-permute-start(bf16[1,1024,768]{1,2,0:T(8,128)(2,1)} %convert_element_type.758), channel_id=1, source_target_pairs={{16,0},{17,1},{18,2},{19,3},{20,4},{21,5},{22,6},{23,7},{24,8},{25... | collective-permute-start | bytes 4718600 | tf_op jit(solution)/shard_map/ppermute | solution.py:14
  1208.5 38.0 %copy-start.63 = (bf16[1,768,384]{2,1,0:T(8,128)(2,1)S(1)}, bf16[1,768,384]{2,1,0:T(8,128)(2,1)}, u32[]{:S(2)}) copy-start(bf16[1,768,384]{2,1,0:T(8,128)(2,1)} %param.59) | copy-start | bytes 1769476
  1208.5 38.0 %copy-start.115 = (bf16[1,9,768]{2,1,0:T(8,128)(2,1)S(1)}, bf16[1,9,768]{2,1,0:T(8,128)(2,1)}, u32[]{:S(2)}) copy-start(bf16[1,9,768]{2,1,0:T(8,128)(2,1)} %param.58) | copy-start | bytes 41476
  1208.5 38.0 %copy-start.170 = (bf16[1152]{0:T(1024)(128)(2,1)S(1)}, bf16[1152]{0:T(1024)(128)(2,1)}, u32[]{:S(2)}) copy-start(bf16[1152]{0:T(1024)(128)(2,1)} %copy-done.168) | copy-start | bytes 6916
  1208.5 37.9 %copy-start.174 = (bf16[3072]{0:T(1024)(128)(2,1)S(1)}, bf16[3072]{0:T(1024)(128)(2,1)}, u32[]{:S(2)}) copy-start(bf16[3072]{0:T(1024)(128)(2,1)} %copy-done.172) | copy-start | bytes 18436
  1208.5 37.9 %copy-start.233 = (bf16[384]{0:T(512)(128)(2,1)S(1)}, bf16[384]{0:T(512)(128)(2,1)}, u32[]{:S(2)}) copy-start(bf16[384]{0:T(512)(128)(2,1)} %copy-done.229) | copy-start | bytes 2308
  1208.5 37.9 %copy-start.403 = (bf16[1,54]{1,0:T(2,128)(2,1)S(1)}, bf16[1,54]{1,0:T(2,128)(2,1)}, u32[]{:S(2)}) copy-start(bf16[1,54]{1,0:T(2,128)(2,1)} %param.62) | copy-start | bytes 328
  1313.5 33.9 %copy-start.391 = (bf16[2,1536,384]{2,1,0:T(8,128)(2,1)S(1)}, bf16[2,1536,384]{2,1,0:T(8,128)(2,1)}, u32[]{:S(2)}) copy-start(bf16[2,1536,384]{2,1,0:T(8,128)(2,1)} %get-tuple-element.1108) | copy-start | bytes 7077892 | tf_op jit(solution)/shard_map/cond
  1730.4 41.3 %copy-start.236 = (f32[3072]{0:T(1024)S(1)}, f32[3072]{0:T(1024)}, u32[]{:S(2)}) copy-start(f32[3072]{0:T(1024)} %copy-done.235) | copy-start | bytes 36868
  1730.4 41.3 %copy-start.238 = (f32[3072]{0:T(1024)S(1)}, f32[3072]{0:T(1024)}, u32[]{:S(2)}) copy-start(f32[3072]{0:T(1024)} %copy-done.237) | copy-start | bytes 36868
  1730.4 41.3 %copy-start.240 = (f32[3072]{0:T(1024)S(1)}, f32[3072]{0:T(1024)}, u32[]{:S(2)}) copy-start(f32[3072]{0:T(1024)} %copy-done.239) | copy-start | bytes 36868
  (290 other events, 1382.2 us)
Sparse Core Ops, SparseCore 0:
  1701.0 318.4 all-reduce.24
where the time goes:
time: 2060 us; the launch traced here: 2040 us
  matrix products  819 us (40%)
  waiting for transfers between devices  691 us (34%)
  other arithmetic  192 us (9%)
  local copies, waits for them, and re-layouts  190 us (9%)
  blocking collectives  105 us (5%)
    ppermute x4, waiting for transfers between devices, shifted(): return lax.ppermute(block, axis, route)  511 us
    psum x1, waiting for transfers between devices, local(): lax.psum((totals[0], totals[1], totals[2], totals[3], totals[4], totals[5...  180 us
    dot_general x4, matrix products, piece(): jnp.einsum('hqk,qhe->khe', soft_low, q_blk, preferred_element_type=jnp.fl...  136 us
    dot_general x4, matrix products, layer_forward(): jnp.einsum('soz,ozl->sol', activation_values.reshape(count, groups, -1),...  89.7 us
    sub x12, matrix products, piece(): probs = jax.nn.softmax(scores, axis=-1)  89.5 us
    dot_general x4, matrix products, piece(): jnp.einsum('hqk,khe->qhe', soft_low, k_seq, preferred_element_type=jnp.fl...  85.1 us
    dot_general x2, matrix products, layer_forward(): jnp.einsum('ngc,gcf->ngf', grouped, inner_weight, preferred_element_type=...  67.6 us
    psum x1, blocking collectives, local(): lax.psum((totals[0], totals[1], totals[2], totals[3], totals[4], totals[5...  64.7 us
  transfers between devices with their start and end apart: 5, of which 5 were waited for; matrix products, arithmetic and copies ran while one was open for 2% of the time, Pallas kernels for 0%

commit v1 on v0

v1 whole, which is shorter than its diff:
```python
from functools import partial

import jax
import jax.numpy as jnp
from jax import lax
from jax.experimental import pallas as pl
from jax.experimental.pallas import tpu as pltpu
from jax.sharding import PartitionSpec as P

BF = jnp.bfloat16
F32 = jnp.float32
RB = 256
PAD = 8
SUB = 8
LOG2E = 1.4426950408889634
INV_SQRT2 = 0.7071067811865476
INV_SQRT2PI = 0.3989422804014327
EPS = 1e-06
VMEM = 56 * 1024 * 1024


def dot(a, b):
    return jnp.dot(a, b, preferred_element_type=F32)


def dot_nt(a, b):
    return lax.dot_general(a, b, (((1,), (1,)), ((), ())), preferred_element_type=F32)


def params(limit=VMEM):
    return pltpu.CompilerParams(vmem_limit_bytes=limit)


def whole(shape):
    zeros = (0,) * len(shape)
    return pl.BlockSpec(shape, lambda *_: zeros)


def rows_of(width):
    return pl.BlockSpec((RB, width), lambda i: (i, 0))


def cols_of(height):
    return pl.BlockSpec((height, RB), lambda i: (0, i))


def sds(shape, dtype):
    return jax.ShapeDtypeStruct(shape, dtype)


def norm_rows(z):
    mean = jnp.mean(z, axis=-1, keepdims=True)
    c = z - mean
    r = lax.rsqrt(jnp.mean(c * c, axis=-1, keepdims=True) + EPS)
    return c * r, r


def tap_softmax(logits_t, taps):
    parts = [logits_t[j * SUB : (j + 1) * SUB] for j in range(taps)]
    top = parts[0]
    for part in parts[1:]:
        top = jnp.maximum(top, part)
    exps = [jnp.exp(part - top) for part in parts]
    total = exps[0]
    for part in exps[1:]:
        total = total + part
    inv = 1.0 / total
    return jnp.concatenate([part * inv for part in exps], axis=0)


def fill_padded(dst, src, rows):
    width = dst.shape[1]
    dst[0:PAD, :] = jnp.zeros((PAD, width), F32)
    dst[rows + PAD : rows + 2 * PAD, :] = jnp.zeros((PAD, width), F32)
    for b in range(rows // RB):
        dst[PAD + b * RB : PAD + (b + 1) * RB, :] = src[b * RB : (b + 1) * RB, :].astype(F32)


def proj_kernel(
    h_ref, wp_ref, bq_ref, bv_ref, bs_ref, dk_ref, pw_ref, pb_ref, kwt_ref, kbt_ref,
    q2_ref, k_ref, v_ref, sp_ref, q2t_ref, kt_ref, vt_ref, dep_ref, kc_ref, mx_ref, kern_ref,
    hp_ref,
):
    i = pl.program_id(0)
    rows, width = h_ref.shape
    att = bq_ref.shape[1]
    taps = dk_ref.shape[0]
    half = taps // 2

    @pl.when(i == 0)
    def _():
        fill_padded(hp_ref, h_ref, rows)

    base = pl.multiple_of(i * RB, RB)
    hb = h_ref[pl.ds(base, RB), :]
    query = dot(hb, wp_ref[:, 0:att]) + bq_ref[...]
    q2 = query * (0.125 * LOG2E)
    q2_ref[...] = q2.astype(BF)
    q2t_ref[...] = q2.T.astype(BF)
    keys = dot(hb, wp_ref[:, att : 2 * att])
    k_ref[...] = keys.astype(BF)
    kt_ref[...] = keys.T.astype(BF)
    values = dot(hb, wp_ref[:, 2 * att : 3 * att]) + bv_ref[...]
    v_ref[...] = values.astype(BF)
    vt_ref[...] = values.T.astype(BF)
    sp_ref[...] = (dot(hb, wp_ref[:, 3 * att : 4 * att]) + bs_ref[...]).astype(BF)
    for c in range(width // 128):
        cols = slice(c * 128, (c + 1) * 128)
        win = hp_ref[pl.ds(base, RB + 2 * PAD), cols]
        acc = dk_ref[0:1, cols] * win[PAD - half : PAD - half + RB]
        for j in range(1, taps):
            acc = acc + dk_ref[j : j + 1, cols] * win[PAD - half + j : PAD - half + j + RB]
        dep_ref[:, cols] = acc.astype(BF)
    keyconv = dot(dep_ref[...], pw_ref[...]) + pb_ref[...]
    kc_ref[...] = keyconv.astype(BF)
    mixed = (keyconv * query).astype(BF)
    mx_ref[...] = mixed
    logits_t = dot_nt(kwt_ref[...], mixed) + kbt_ref[...]
    kern_ref[...] = tap_softmax(logits_t, taps)


def run_proj(h, p):
    rows, width = h.shape
    att = p["pw"].shape[1]
    taps = p["dk"].shape[0]
    t8 = taps * SUB
    return pl.pallas_call(
        proj_kernel,
        grid=(rows // RB,),
        in_specs=[
            whole((rows, width)), whole(p["wp"].shape), whole((1, att)), whole((1, att)), whole((1, att)),
            whole(p["dk"].shape), whole(p["pw"].shape), whole((1, att)), whole((t8, att)), whole((t8, 1)),
        ],
        out_specs=[rows_of(att)] * 4 + [cols_of(att)] * 3
        + [rows_of(width), rows_of(att), rows_of(att), cols_of(t8)],
        out_shape=[sds((rows, att), BF)] * 4 + [sds((att, rows), BF)] * 3
        + [sds((rows, width), BF), sds((rows, att), BF), sds((rows, att), BF), sds((t8, rows), F32)],
        scratch_shapes=[pltpu.VMEM((rows + 2 * PAD, width), F32)],
        compiler_params=params(),
        name="proj_fwd",
    )(h, p["wp"], p["bq"], p["bv"], p["bs"], p["dk"], p["pw"], p["pb"], p["kwt"], p["kbt"])


def attn_kernel(k_ref, qt_ref, vt_ref, at_ref, lse_ref, *, head, qb):
    rows = k_ref.shape[0]
    k = k_ref[...]
    ones = jnp.ones((16, rows), BF)
    zeros = jnp.zeros((head, qb), BF)
    for b in range(rows // qb):
        cols = slice(b * qb, (b + 1) * qb)
        for s in range(2):
            lo = s * head
            qt = qt_ref[lo : lo + head, cols]
            qz = jnp.concatenate([qt, zeros] if s == 0 else [zeros, qt], axis=0)
            st = dot(k, qz)
            top = jnp.max(st, axis=0, keepdims=True)
            pr = jnp.exp2(st - top).astype(BF)
            vx = jnp.concatenate([vt_ref[lo : lo + head, :], ones], axis=0)
            ot = dot(vx, pr)
            total = ot[head : head + 1]
            at_ref[lo : lo + head, cols] = ot[0:head] * (1.0 / total)
            lse_ref[0, s : s + 1, cols] = top + jnp.log2(total)


def run_attn(k, q2t, vt, head):
    att, rows = q2t.shape
    pairs = att // (2 * head)
    blk = pl.BlockSpec((2 * head, rows), lambda g: (g, 0))
    return pl.pallas_call(
        partial(attn_kernel, head=head, qb=256),
        grid=(pairs,),
        in_specs=[pl.BlockSpec((rows, 2 * head), lambda g: (0, g)), blk, blk],
        out_specs=[blk, pl.BlockSpec((1, SUB, rows), lambda g: (g, 0, 0))],
        out_shape=[sds((att, rows), F32), sds((pairs, SUB, rows), F32)],
        compiler_params=params(),
        name="attn_fwd",
    )(k, q2t, vt)


def ffn_kernel(
    at_ref, sp_ref, kern_ref, h_ref, ex_ref, wo_ref, bo_ref, g1_ref, s1_ref, w1_ref, b1_ref, w2_ref, b2_ref,
    g2_ref, s2_ref,
    ctx_ref, u1_ref, r1_ref, nl_ref, act_ref, gp_ref, u2_ref, r2_ref, out_ref,
    spp_ref,
):
    i = pl.program_id(0)
    rows, att = sp_ref.shape
    taps = kern_ref.shape[0] // SUB
    half = taps // 2
    groups, gin, gout = w1_ref.shape

    @pl.when(i == 0)
    def _():
        fill_padded(spp_ref, sp_ref, rows)

    base = pl.multiple_of(i * RB, RB)
    ctx_ref[:, 0:att] = at_ref[...].T.astype(BF)
    kn = kern_ref[...].T.astype(BF)
    for c in range(att // 128):
        cols = slice(c * 128, (c + 1) * 128)
        win = spp_ref[pl.ds(base, RB + 2 * PAD), cols]
        acc = jnp.zeros((RB, 128), F32)
        for j in range(taps):
            kexp = dot(kn, ex_ref[j, :, cols])
            acc = acc + kexp * win[PAD - half + j : PAD - half + j + RB]
        ctx_ref[:, att + c * 128 : att + (c + 1) * 128] = acc.astype(BF)
    z = dot(ctx_ref[...], wo_ref[...]) + bo_ref[...] + h_ref[...].astype(F32)
    u1, r1 = norm_rows(z)
    u1_ref[...] = u1.astype(BF)
    r1_ref[...] = r1
    normed = u1 * g1_ref[...] + s1_ref[...]
    nl = normed.astype(BF)
    nl_ref[...] = nl
    fb = 512
    outs = []
    for g in range(groups):
        x = nl[:, g * gin : (g + 1) * gin]
        acc = None
        for f in range(gout // fb):
            fs = slice(f * fb, (f + 1) * fb)
            full = slice(g * gout + f * fb, g * gout + (f + 1) * fb)
            inner = dot(x, w1_ref[g, :, fs]) + b1_ref[:, full]
            cdf = 0.5 + 0.5 * lax.erf(inner * INV_SQRT2)
            pdf = jnp.exp(inner * inner * -0.5) * INV_SQRT2PI
            a = (inner * cdf).astype(BF)
            act_ref[:, full] = a
            gp_ref[:, full] = (cdf + inner * pdf).astype(BF)
            part = dot(a, w2_ref[g, fs, :])
            acc = part if acc is None else acc + part
        outs.append(acc)
    z2 = jnp.concatenate(outs, axis=1) + b2_ref[...] + normed
    u2, r2 = norm_rows(z2)
    u2_ref[...] = u2.astype(BF)
    r2_ref[...] = r2
    out_ref[...] = (u2 * g2_ref[...] + s2_ref[...]).astype(BF)


def run_ffn(at, sp, kern, h, ex, p):
    rows, width = h.shape
    att = sp.shape[1]
    t8 = kern.shape[0]
    groups, gin, gout = p["w1"].shape
    ff = groups * gout
    return pl.pallas_call(
        ffn_kernel,
        grid=(rows // RB,),
        in_specs=[
            cols_of(att), whole((rows, att)), cols_of(t8), rows_of(width), whole(ex.shape),
            whole((width, width)), whole((1, width)), whole((1, width)), whole((1, width)),
            whole(p["w1"].shape), whole((1, ff)), whole(p["w2"].shape), whole((1, width)),
            whole((1, width)), whole((1, width)),
        ],
        out_specs=[rows_of(width), rows_of(width), rows_of(1), rows_of(width), rows_of(ff), rows_of(ff),
                   rows_of(width), rows_of(1), rows_of(width)],
        out_shape=[sds((rows, width), BF), sds((rows, width), BF), sds((rows, 1), F32), sds((rows, width), BF),
                   sds((rows, ff), BF), sds((rows, ff), BF), sds((rows, width), BF), sds((rows, 1), F32),
                   sds((rows, width), BF)],
        scratch_shapes=[pltpu.VMEM((rows + 2 * PAD, att), F32)],
        compiler_params=params(),
        name="ffn_fwd",
    )(at, sp, kern, h, ex, p["wo"], p["bo"], p["g1"], p["s1"], p["w1"], p["b1"], p["w2"], p["b2"],
      p["g2"], p["s2"])


def add_sum(ref, value, first):
    total = jnp.sum(value, axis=0, keepdims=True)

    @pl.when(first)
    def _():
        ref[...] = total

    @pl.when(jnp.logical_not(first))
    def _():
        ref[...] += total


def norm_back(dy, u, r, gain):
    g = dy * gain
    return r * (g - jnp.mean(g, axis=-1, keepdims=True) - u * jnp.mean(g * u, axis=-1, keepdims=True))


def ffn_back_kernel(
    dy_ref, u2_ref, r2_ref, g2_ref, w2_ref, gp_ref, w1_ref, u1_ref, r1_ref, g1_ref, wo_ref,
    ds_ref, di_ref, dz_ref, dat_ref, dan_ref, ddn_ref, vec_ref, db1_ref,
):
    i = pl.program_id(0)
    first = i == 0
    groups, gin, gout = w1_ref.shape
    att = dan_ref.shape[1]

    @pl.when(first)
    def _():
        vec_ref[...] = jnp.zeros(vec_ref.shape, F32)
        db1_ref[...] = jnp.zeros(db1_ref.shape, F32)

    dy = dy_ref[...].astype(F32)
    u2 = u2_ref[...].astype(F32)
    vec_ref[0:1, :] += jnp.sum(dy * u2, axis=0, keepdims=True)
    vec_ref[1:2, :] += jnp.sum(dy, axis=0, keepdims=True)
    dsum = norm_back(dy, u2, r2_ref[...], g2_ref[...])
    vec_ref[2:3, :] += jnp.sum(dsum, axis=0, keepdims=True)
    dlow = dsum.astype(BF)
    ds_ref[...] = dlow
    fb = 512
    outs = []
    for g in range(groups):
        x = dlow[:, g * gin : (g + 1) * gin]
        acc = None
        for f in range(gout // fb):
            fs = slice(f * fb, (f + 1) * fb)
            full = slice(g * gout + f * fb, g * gout + (f + 1) * fb)
            dinner = dot_nt(x, w2_ref[g, fs, :]) * gp_ref[:, full].astype(F32)
            db1_ref[:, full] += jnp.sum(dinner, axis=0, keepdims=True)
            dil = dinner.astype(BF)
            di_ref[:, full] = dil
            part = dot_nt(dil, w1_ref[g, :, fs])
            acc = part if acc is None else acc + part
        outs.append(acc)
    dn = jnp.concatenate(outs, axis=1) + dsum
    u1 = u1_ref[...].astype(F32)
    vec_ref[3:4, :] += jnp.sum(dn * u1, axis=0, keepdims=True)
    vec_ref[4:5, :] += jnp.sum(dn, axis=0, keepdims=True)
    dz = norm_back(dn, u1, r1_ref[...], g1_ref[...])
    vec_ref[5:6, :] += jnp.sum(dz, axis=0, keepdims=True)
    dzl = dz.astype(BF)
    dz_ref[...] = dzl
    dctx = dot_nt(dzl, wo_ref[...])
    dan_ref[...] = dctx[:, 0:att].astype(BF)
    dat_ref[...] = dctx[:, 0:att].T.astype(BF)
    ddn_ref[...] = dctx[:, att:].astype(BF)


def run_ffn_back(dy, keep, p):
    rows, width = dy.shape
    groups, gin, gout = p["w1"].shape
    ff = groups * gout
    att = p["pw"].shape[1]
    return pl.pallas_call(
        ffn_back_kernel,
        grid=(rows // RB,),
        in_specs=[
            rows_of(width), rows_of(width), rows_of(1), whole((1, width)), whole(p["w2"].shape), rows_of(ff),
            whole(p["w1"].shape), rows_of(width), rows_of(1), whole((1, width)), whole((width, width)),
        ],
        out_specs=[rows_of(width), rows_of(ff), rows_of(width), cols_of(att), rows_of(att),
                   rows_of(width - att), whole((SUB, width)), whole((1, ff))],
        out_shape=[sds((rows, width), BF), sds((rows, ff), BF), sds((rows, width), BF), sds((att, rows), BF),
                   sds((rows, att), BF), sds((rows, width - att), BF), sds((SUB, width), F32), sds((1, ff), F32)],
        compiler_params=params(),
        name="ffn_bwd",
    )(dy, keep["u2"], keep["r2"], p["g2"], p["w2"], keep["gp"], p["w1"], keep["u1"], keep["r1"], p["g1"], p["wo"])


def conv_back_kernel(
    ddn_ref, sp_ref, kern_ref, kc_ref, q2_ref, h_ref, dz_ref, ex_ref, ext_ref, kwt_ref, pw_ref, dk_ref,
    dl_ref, dqm_ref, dsp_ref, dkc_ref, res_ref, dkg_ref, dpb_ref, dkb_ref,
    ddp_ref, spp_ref, hp_ref, dep_ref, knp_ref,
):
    phase = pl.program_id(0)
    i = pl.program_id(1)
    rows, att = sp_ref.shape
    width = h_ref.shape[1]
    taps = dk_ref.shape[0]
    half = taps // 2

    @pl.when((phase == 0) & (i == 0))
    def _():
        fill_padded(ddp_ref, ddn_ref, rows)
        fill_padded(spp_ref, sp_ref, rows)
        fill_padded(hp_ref, h_ref, rows)
        dep_ref[0:PAD, :] = jnp.zeros((PAD, width), F32)
        dep_ref[rows + PAD : rows + 2 * PAD, :] = jnp.zeros((PAD, width), F32)
        knp_ref[0:PAD, :] = jnp.zeros((PAD, knp_ref.shape[1]), F32)
        knp_ref[rows + PAD : rows + 2 * PAD, :] = jnp.zeros((PAD, knp_ref.shape[1]), F32)
        dkg_ref[...] = jnp.zeros(dkg_ref.shape, F32)
        dpb_ref[...] = jnp.zeros(dpb_ref.shape, F32)
        dkb_ref[...] = jnp.zeros(dkb_ref.shape, F32)

    base = pl.multiple_of(i * RB, RB)

    @pl.when(phase == 0)
    def _():
        dd = ddn_ref[pl.ds(base, RB), :].astype(F32)
        dkern = None
        for j in range(taps):
            prods = []
            for c in range(att // 128):
                cols = slice(c * 128, (c + 1) * 128)
                win = spp_ref[pl.ds(base, RB + 2 * PAD), cols]
                prods.append((dd[:, cols] * win[PAD - half + j : PAD - half + j + RB]).astype(BF))
            part = dot(jnp.concatenate(prods, axis=1), ext_ref[j])
            dkern = part if dkern is None else dkern + part
        dkt = dkern.T
        kt = kern_ref[...]
        knp_ref[pl.ds(base + PAD, RB), :] = kt.T
        tot = kt[0:SUB] * dkt[0:SUB]
        for j in range(1, taps):
            tot = tot + kt[j * SUB : (j + 1) * SUB] * dkt[j * SUB : (j + 1) * SUB]
        dlt = jnp.concatenate(
            [kt[j * SUB : (j + 1) * SUB] * (dkt[j * SUB : (j + 1) * SUB] - tot) for j in range(taps)], axis=0
        )
        dkb_ref[...] += jnp.sum(dlt, axis=1, keepdims=True)
        dl = dlt.T.astype(BF)
        dl_ref[...] = dl
        dmixed = dot(dl, kwt_ref[...])
        query = q2_ref[...].astype(F32) * (8.0 / LOG2E)
        dqm_ref[...] = (dmixed * kc_ref[...].astype(F32)).astype(BF)
        dkc = dmixed * query
        dpb_ref[...] += jnp.sum(dkc, axis=0, keepdims=True)
        dkcl = dkc.astype(BF)
        dkc_ref[...] = dkcl
        dep_ref[pl.ds(base + PAD, RB), :] = dot_nt(dkcl, pw_ref[...])

    @pl.when(phase == 1)
    def _():
        for c in range(width // 128):
            cols = slice(c * 128, (c + 1) * 128)
            win = dep_ref[pl.ds(base, RB + 2 * PAD), cols]
            mid = win[PAD : PAD + RB]
            hw = hp_ref[pl.ds(base, RB + 2 * PAD), cols]
            acc = dz_ref[:, cols].astype(F32)
            for j in range(taps):
                acc = acc + dk_ref[j : j + 1, cols] * win[PAD + half - j : PAD + half - j + RB]
                dkg_ref[j : j + 1, cols] += jnp.sum(
                    mid * hw[PAD - half + j : PAD - half + j + RB], axis=0, keepdims=True
                )
            res_ref[:, cols] = acc.astype(BF)
        kn = knp_ref[pl.ds(base, RB + 2 * PAD), :].astype(BF)
        for c in range(att // 128):
            cols = slice(c * 128, (c + 1) * 128)
            win = ddp_ref[pl.ds(base, RB + 2 * PAD), cols]
            acc = jnp.zeros((RB, 128), F32)
            for j in range(taps):
                prod = dot(kn, ex_ref[j, :, cols]) * win
                acc = acc + prod[PAD + half - j : PAD + half - j + RB]
            dsp_ref[:, cols] = acc.astype(BF)


def run_conv_back(ddn, dz, h, keep, ex, ext, p):
    rows, att = ddn.shape
    width = h.shape[1]
    taps = p["dk"].shape[0]
    t8 = taps * SUB
    last = rows // RB - 1

    def early(width):
        return pl.BlockSpec((RB, width), lambda ph, i: (jnp.where(ph == 0, i, last), 0))

    def late(width):
        return pl.BlockSpec((RB, width), lambda ph, i: (jnp.where(ph == 1, i, 0), 0))

    return pl.pallas_call(
        conv_back_kernel,
        grid=(2, rows // RB),
        in_specs=[
            whole((rows, att)), whole((rows, att)),
            pl.BlockSpec((t8, RB), lambda ph, i: (0, jnp.where(ph == 0, i, last))),
            early(att), early(att), whole((rows, width)), late(width), whole(ex.shape), whole(ext.shape),
            whole((t8, att)), whole(p["pw"].shape), whole(p["dk"].shape),
        ],
        out_specs=[early(t8), early(att), late(att), early(att), late(width), whole(p["dk"].shape),
                   whole((1, att)), whole((t8, 1))],
        out_shape=[sds((rows, t8), BF), sds((rows, att), BF), sds((rows, att), BF), sds((rows, att), BF),
                   sds((rows, width), BF), sds(p["dk"].shape, F32), sds((1, att), F32), sds((t8, 1), F32)],
        scratch_shapes=[
            pltpu.VMEM((rows + 2 * PAD, att), F32), pltpu.VMEM((rows + 2 * PAD, att), F32),
            pltpu.VMEM((rows + 2 * PAD, width), F32), pltpu.VMEM((rows + 2 * PAD, width), F32),
            pltpu.VMEM((rows + 2 * PAD, t8), F32),
        ],
        compiler_params=params(),
        name="conv_bwd",
    )(ddn, keep["sp"], keep["kern"], keep["kc"], keep["q2"], h, dz, ex, ext, p["kwt"], p["pw"], p["dk"])


def attn_back_kernel(
    k_ref, v_ref, q2_ref, do_ref, qt_ref, kt_ref, dot_ref, at_ref, lse_ref,
    dq_ref, dk_ref, dv_ref, ak_ref, av_ref, *, head, qb,
):
    rows = k_ref.shape[0]
    k = k_ref[...]
    v = v_ref[...]
    zeros = jnp.zeros((head, qb), BF)
    lane = lax.broadcasted_iota(jnp.int32, (1, 2 * head), 1)
    for b in range(rows // qb):
        cols = slice(b * qb, (b + 1) * qb)
        dqs = []
        for s in range(2):
            lo = s * head
            side = (lane >= lo) & (lane < lo + head)
            qt = qt_ref[lo : lo + head, cols]
            qz = jnp.concatenate([qt, zeros] if s == 0 else [zeros, qt], axis=0)
            dt = dot_ref[lo : lo + head, cols]
            dz = jnp.concatenate([dt, zeros] if s == 0 else [zeros, dt], axis=0)
            dd = jnp.sum(dt.astype(F32) * at_ref[lo : lo + head, cols], axis=0, keepdims=True)
            pr = jnp.exp2(dot(k, qz) - lse_ref[0, s : s + 1, cols])
            ds = (pr * (dot(v, dz) - dd)).astype(BF)
            dqs.append(dot(kt_ref[lo : lo + head, :], ds))
            qn = jnp.where(side, q2_ref[cols, :], jnp.zeros((), BF))
            dn = jnp.where(side, do_ref[cols, :], jnp.zeros((), BF))
            gv = dot(pr.astype(BF), dn)
            gk = dot(ds, qn)
            if b == 0 and s == 0:
                av_ref[...] = gv
                ak_ref[...] = gk
            else:
                av_ref[...] += gv
                ak_ref[...] += gk
        dq_ref[cols, :] = (jnp.concatenate(dqs, axis=0).T * 0.125).astype(BF)
    dk_ref[...] = (ak_ref[...] * (1.0 / LOG2E)).astype(BF)
    dv_ref[...] = av_ref[...].astype(BF)


def run_attn_back(do, dot_t, keep, head):
    rows, att = do.shape
    pairs = att // (2 * head)
    nat = pl.BlockSpec((rows, 2 * head), lambda g: (0, g))
    tra = pl.BlockSpec((2 * head, rows), lambda g: (g, 0))
    return pl.pallas_call(
        partial(attn_back_kernel, head=head, qb=256),
        grid=(pairs,),
        in_specs=[nat, nat, nat, nat, tra, tra, tra, tra, pl.BlockSpec((1, SUB, rows), lambda g: (g, 0, 0))],
        out_specs=[nat] * 3,
        out_shape=[sds((rows, att), BF)] * 3,
        scratch_shapes=[pltpu.VMEM((rows, 2 * head), F32)] * 2,
        compiler_params=params(),
        name="attn_bwd",
    )(keep["k"], keep["v"], keep["q2"], do, keep["q2t"], keep["kt"], dot_t, keep["at"], keep["lse"])


def in_back_kernel(
    dq_ref, dqm_ref, dk_ref, dv_ref, dsp_ref, wp_ref, res_ref, m_ref,
    dp_ref, dh_ref, db_ref, mg_ref,
):
    i = pl.program_id(0)
    att = dq_ref.shape[1]

    @pl.when(i == 0)
    def _():
        db_ref[...] = jnp.zeros(db_ref.shape, F32)
        mg_ref[...] = jnp.zeros(mg_ref.shape, F32)

    dq = dq_ref[...].astype(F32) + dqm_ref[...].astype(F32)
    parts = (dq.astype(BF), dk_ref[...], dv_ref[...], dsp_ref[...])
    db_ref[0:1, :] += jnp.sum(dq, axis=0, keepdims=True)
    db_ref[1:2, :] += jnp.sum(parts[2].astype(F32), axis=0, keepdims=True)
    db_ref[2:3, :] += jnp.sum(parts[3].astype(F32), axis=0, keepdims=True)
    for n, part in enumerate(parts):
        dp_ref[:, n * att : (n + 1) * att] = part
    dh = dot_nt(dp_ref[...], wp_ref[...]) + res_ref[...].astype(F32)
    m = m_ref[...]
    mg_ref[...] += jnp.sum(dh * m, axis=0, keepdims=True)
    dh_ref[...] = (dh * (1.0 - m)).astype(BF)


def run_in_back(dq, dqm, dk, dv, dsp, res, mask, p):
    rows, width = res.shape
    att = dq.shape[1]
    return pl.pallas_call(
        in_back_kernel,
        grid=(rows // RB,),
        in_specs=[rows_of(att)] * 5 + [whole(p["wp"].shape), rows_of(width), rows_of(1)],
        out_specs=[rows_of(4 * att), rows_of(width), whole((SUB, att)), whole((1, width))],
        out_shape=[sds((rows, 4 * att), BF), sds((rows, width), BF), sds((SUB, att), F32), sds((1, width), F32)],
        compiler_params=params(),
        name="in_bwd",
    )(dq, dqm, dk, dv, dsp, p["wp"], res, mask)


def prepare(weights):
    (wp, bp, dk, pw, pb, kw, kb, wo, bo, g1, s1, w1, b1, w2, b2, g2, s2) = weights
    att = pw.shape[1]
    taps = dk.shape[0]
    heads = kb.shape[0] // taps

    def row(v):
        return v.astype(F32).reshape(1, -1)

    kwt = jnp.pad(kw.reshape(att, heads, taps).transpose(2, 1, 0), ((0, 0), (0, SUB - heads), (0, 0)))
    kbt = jnp.pad(kb.astype(F32).reshape(heads, taps).T, ((0, 0), (0, SUB - heads)))
    return {
        "wp": wp, "bq": row(bp[:att]), "bv": row(bp[att : 2 * att]), "bs": row(bp[2 * att :]),
        "dk": dk.astype(F32), "pw": pw, "pb": row(pb),
        "kwt": kwt.reshape(taps * SUB, att), "kbt": kbt.reshape(taps * SUB, 1),
        "wo": wo, "bo": row(bo), "g1": row(g1), "s1": row(s1), "w1": w1, "b1": row(b1), "w2": w2, "b2": row(b2),
        "g2": row(g2), "s2": row(s2),
    }


def spread_matrices(taps, heads, head):
    src = jnp.arange(taps * SUB)[None, :, None]
    tap = jnp.arange(taps)[:, None, None]
    feature = jnp.arange(heads * head)[None, None, :]
    ex = (src == tap * SUB + feature // head).astype(BF)
    return ex, ex.transpose(0, 2, 1)


def layer_forward(h, p, ex, head):
    q2, k, v, sp, q2t, kt, vt, dep, kc, mx, kern = run_proj(h, p)
    at, lse = run_attn(k, q2t, vt, head)
    ctx, u1, r1, nl, act, gp, u2, r2, out = run_ffn(at, sp, kern, h, ex, p)
    keep = dict(h=h, q2=q2, k=k, v=v, sp=sp, q2t=q2t, kt=kt, dep=dep, kc=kc, mx=mx, kern=kern, at=at, lse=lse,
                ctx=ctx, u1=u1, r1=r1, nl=nl, act=act, gp=gp, u2=u2, r2=r2)
    return out, keep


def rows_product(left, right):
    return lax.dot_general(left, right, (((0,), (0,)), ((), ())), preferred_element_type=F32)


def grouped_product(left, right, groups):
    a = left.shape[1] // groups
    b = right.shape[1] // groups
    return jnp.stack([
        rows_product(left[:, g * a : (g + 1) * a], right[:, g * b : (g + 1) * b]) for g in range(groups)
    ])


def layer_backward(dy, keep, mask, p, ex, ext, head):
    groups = p["w1"].shape[0]
    att = p["pw"].shape[1]
    taps = p["dk"].shape[0]
    heads = att // head
    ds, di, dz, dat, dan, ddn, vec, db1 = run_ffn_back(dy, keep, p)
    dw2 = grouped_product(keep["act"], ds, groups)
    dw1 = grouped_product(keep["nl"], di, groups)
    dwo = rows_product(keep["ctx"], dz)
    dl, dqm, dsp, dkc, res, dkg, dpb, dkb = run_conv_back(ddn, dz, keep["h"], keep, ex, ext, p)
    dkw = rows_product(keep["mx"], dl)
    dpw = rows_product(keep["dep"], dkc)
    dq, dkk, dvv = run_attn_back(dan, dat, keep, head)
    dp, dh, dbp, mg = run_in_back(dq, dqm, dkk, dvv, dsp, res, mask, p)
    dwp = rows_product(keep["h"], dp)
    small = {
        "bp": dbp[0:3].reshape(-1), "dk": dkg, "pb": dpb[0],
        "kw": dkw.reshape(att, taps, SUB)[:, :, :heads].transpose(0, 2, 1).reshape(att, heads * taps),
        "kb": dkb.reshape(taps, SUB)[:, :heads].T.reshape(-1),
        "bo": vec[5], "g1": vec[3], "s1": vec[4], "b1": db1[0], "b2": vec[2], "g2": vec[0], "s2": vec[1],
    }
    return dh, mg[0], {"wp": dwp, "pw": dpw, "wo": dwo, "w1": dw1, "w2": dw2}, small


def swap(x):
    return lax.ppermute(x, "section", [(0, 1), (1, 0)])


def to_other_core(x):
    return lax.ppermute(x, "dp", [(i, i ^ 1) for i in range(lax.axis_size("dp"))])


BIG = ("wp", "w1", "w2", "wo", "pw")
VECTORS = ("bp", "dk", "pb", "kw", "kb", "bo", "g1", "s1", "b1", "b2", "g2", "s2")


def pack_small(small, mask_grad, width, rows):
    lines = []
    for name in VECTORS:
        flat = small[name].reshape(-1)
        lines.append(jnp.pad(flat, (0, -flat.size % width)).reshape(-1, width))
    body = jnp.concatenate(lines)
    body = jnp.pad(body, ((0, rows - body.shape[0] - mask_grad.size // width), (0, 0)))
    return jnp.concatenate([body, mask_grad.reshape(-1, width)]).astype(BF)


def unpack_small(packed, shapes, width):
    out = {}
    at = 0
    for name in VECTORS:
        shape = shapes[name]
        size = 1
        for n in shape:
            size *= n
        lines = -(-size // width)
        out[name] = packed[at : at + lines].reshape(-1)[:size].reshape(shape)
        at += lines
    return out


def local(
    tokens, mask_pos, mask_count, mask_vec,
    proj_weight, proj_bias, depth_kernel, point_weight, point_bias, kernel_weight, kernel_bias, out_weight, out_bias,
    norm_gain, norm_shift, inner_weight, inner_bias, second_feed_weight, second_feed_bias, final_gain, final_shift,
    cotangent,
):
    section = lax.axis_index("section")
    first = section == 0
    core = lax.axis_index("dp") % 2
    devices = lax.axis_size("dp")
    own = [
        a[0]
        for a in (
            proj_weight, proj_bias, depth_kernel, point_weight, point_bias, kernel_weight, kernel_bias, out_weight,
            out_bias, norm_gain, norm_shift, inner_weight, inner_bias, second_feed_weight, second_feed_bias,
            final_gain, final_shift,
        )
    ]
    large = (0, 3, 7, 11, 13)

    def fetch(a):
        flat = a.reshape(-1, a.shape[-1])
        n = flat.shape[0] // 2
        got = swap(lax.dynamic_slice_in_dim(flat, core * n, n, 0))
        more = to_other_core(got)
        lower = core == 0
        return jnp.concatenate([jnp.where(lower, got, more), jnp.where(lower, more, got)]).reshape(a.shape)

    rest = [i for i in range(len(own)) if i not in large]
    flat = swap(jnp.concatenate([own[i].reshape(-1) for i in rest]))
    other = [None] * len(own)
    at = 0
    for i in rest:
        other[i] = flat[at : at + own[i].size].reshape(own[i].shape)
        at += own[i].size
    for i in large:
        other[i] = fetch(own[i])
    layers = [
        [jnp.where(first, a, b) for a, b in zip(own, other)],
        [jnp.where(first, b, a) for a, b in zip(own, other)],
    ]
    seq, width = tokens.shape[1:]
    taps = depth_kernel.shape[1]
    att = point_weight.shape[2]
    heads = kernel_bias.shape[1] // taps
    head = att // heads
    ex, ext = spread_matrices(taps, heads, head)
    shapes = dict(zip(
        ("wp", "bp", "dk", "pw", "pb", "kw", "kb", "wo", "bo", "g1", "s1", "w1", "b1", "w2", "b2", "g2", "s2"),
        [a.shape for a in own],
    ))

    def mine(a):
        return lax.dynamic_index_in_dim(a, section, 0, keepdims=False)

    pos, count = mine(mask_pos), mine(mask_count)
    hits = (pos[:, None] == jnp.arange(seq, dtype=jnp.int32)[None, :]) & (
        jnp.arange(pos.shape[0], dtype=jnp.int32) < count
    )[:, None]
    masked = jnp.any(hits, axis=0)[:, None]
    hidden = jnp.where(masked, mask_vec[None, :], mine(tokens))
    mask = masked.astype(F32)
    p = [prepare(w) for w in layers]
    keeps = []
    outs = []
    for q in p:
        hidden, keep = layer_forward(hidden, q, ex, head)
        keeps.append(keep)
        outs.append(hidden)

    def place(a, b):
        kept = jnp.where(first, a, b)
        got = swap(jnp.where(first, b, a))
        return jnp.stack([jnp.where(first, kept, got), jnp.where(first, got, kept)])

    states = place(*outs)
    lines = 256 * max(1, devices // 256)
    small_width = att

    def scatter(big, small, mg):
        flats = [big[n].astype(BF).reshape(-1, big[n].shape[-1]) for n in BIG]
        flats.append(pack_small(small, mg, small_width, lines))
        return lax.psum_scatter(tuple(flats), "dp", scatter_dimension=0, tiled=True)

    d1, _, big1, small1 = layer_backward(mine(cotangent), keeps[1], jnp.zeros_like(mask), p[1], ex, ext, head)
    sums1 = scatter(big1, small1, jnp.zeros((width,), F32))
    d0, mg, big0, small0 = layer_backward(d1, keeps[0], mask, p[0], ex, ext, head)
    sums0 = scatter(big0, small0, mg)
    in_grads = place(d0, d1)
    own_sums = [jnp.where(first, a, b) + swap(jnp.where(first, b, a)) for a, b in zip(sums0[:-1], sums1[:-1])]
    s0 = sums0[-1] + swap(sums0[-1])
    s1 = sums1[-1] + swap(sums1[-1])
    chunk = lines // devices
    line = lax.axis_index("dp") * chunk + jnp.arange(chunk)
    own_sums.append(jnp.where((line >= lines - width // small_width)[:, None] | first, s0, s1))
    full = lax.all_gather(tuple(own_sums), "dp", axis=0, tiled=True)
    grads = {n: a.astype(F32).reshape(shapes[n]) for n, a in zip(BIG, full)}
    packed = full[-1].astype(F32)
    grads.update(unpack_small(packed, shapes, small_width))
    mask_grad = packed[lines - width // small_width :].reshape(-1)
    order = ("wp", "bp", "dk", "pw", "pb", "kw", "kb", "wo", "bo", "g1", "s1", "w1", "b1", "w2", "b2", "g2", "s2")
    return (states[None], in_grads[None], mask_grad) + tuple(grads[n][None] for n in order)


def solution(mesh):
    def part(dims, *lead):
        return P(*(lead + (None,) * (dims - len(lead))))

    weights = (3, 2, 3, 3, 2, 3, 2, 3, 2, 2, 2, 4, 2, 4, 2, 2, 2)
    return jax.shard_map(
        local,
        mesh=mesh,
        in_specs=(part(3, "dp"), part(2, "dp"), part(1, "dp"), P())
        + tuple(part(n, "section") for n in weights)
        + (part(3, "dp"),),
        out_specs=(part(4, "section", "dp"), part(4, "section", "dp"), P())
        + tuple(part(n, "section") for n in weights),
        check_vma=False,
    )
```

time: 2060 us -> 1280 us (0.62)
  matrix products: 819 us -> 55.8 us
  Pallas kernels: 0 us -> 255 us
  local copies, waits for them, and re-layouts: 190 us -> 80 us
  other arithmetic: 192 us -> 87.3 us
  blocking collectives: 105 us -> 41.7 us
    dot_general x68 -> x16, matrix products: 730 us -> 55.8 us  [rows_product(): lax.dot_general(left, right, (((0,), (0,)), ((), ())), preferred_element_...]
    reduce_scatter x0 -> x12, waiting for transfers between devices: none -> 551 us  [scatter(): return lax.psum_scatter(tuple(flats), 'dp', scatter_dimension=0, tiled=True)]
    ppermute x4 -> x20, waiting for transfers between devices: 511 us -> 45 us  [the longest x15 45 us: swap(): return lax.ppermute(x, 'section', [(0, 1), (1, 0)])]
    pallas_call x0 -> x14, Pallas kernels: none -> 255 us  [the longest x2 53.6 us: run_conv_back(): pl.pallas_call(conv_back_kernel, grid=(2, rows // RB), in_specs=[whole((r...]
    psum x1 -> x0, waiting for transfers between devices: 180 us -> none  [local(): lax.psum((totals[0], totals[1], totals[2], totals[3], totals[4], totals[5...]
    all_gather x0 -> x4, waiting for transfers between devices: none -> 113 us  [local(): full = lax.all_gather(tuple(own_sums), 'dp', axis=0, tiled=True)]
    psum x2 -> x0, blocking collectives: 105 us -> none  [the longest x1 64.7 us: local(): lax.psum((totals[0], totals[1], totals[2], totals[3], totals[4], totals[5...]
    sub x12 -> x0, matrix products: 89.5 us -> none  [piece(): probs = jax.nn.softmax(scores, axis=-1)]
  transfers between devices with their start and end apart: 5 -> 36, of which waited for: 5 -> 19; matrix products, arithmetic and copies ran while one was open for 2% -> 15% of each run, Pallas kernels for 0% -> 4%
where the time goes in v1:
time: 1280 us; the launch traced here: 1270 us
  waiting for transfers between devices  709 us (55%)
  Pallas kernels  255 us (20%)
  other arithmetic  87.3 us (7%)
  local copies, waits for them, and re-layouts  80 us (6%)
  matrix products  55.8 us (4%)
  blocking collectives  41.7 us (3%)
  starting transfers between devices  24.6 us (2%)
  between operations  15.4 us (1%)
    reduce_scatter x12, waiting for transfers between devices, scatter(): return lax.psum_scatter(tuple(flats), 'dp', scatter_dimension=0, tiled=True)  551 us
    all_gather x4, waiting for transfers between devices, local(): full = lax.all_gather(tuple(own_sums), 'dp', axis=0, tiled=True)  113 us
    dot_general x16, matrix products, rows_product(): lax.dot_general(left, right, (((0,), (0,)), ((), ())), preferred_element_...  55.8 us
    pallas_call x2, Pallas kernels, run_conv_back(): pl.pallas_call(conv_back_kernel, grid=(2, rows // RB), in_specs=[whole((r...  53.6 us
    pallas_call x2, Pallas kernels, run_ffn(): pl.pallas_call(ffn_kernel, grid=(rows // RB,), in_specs=[cols_of(att), wh...  45.2 us
    ppermute x15, waiting for transfers between devices, swap(): return lax.ppermute(x, 'section', [(0, 1), (1, 0)])  45 us
    all_gather x2, blocking collectives, local(): full = lax.all_gather(tuple(own_sums), 'dp', axis=0, tiled=True)  41.7 us
    pallas_call x2, Pallas kernels, run_attn_back(): pl.pallas_call(partial(attn_back_kernel, head=head, qb=256), grid=(pairs,...  40.1 us
  transfers between devices with their start and end apart: 36, of which 19 were waited for; matrix products, arithmetic and copies ran while one was open for 15% of the time, Pallas kernels for 4%

profile of v1, /device:TPU:0, one launch (start us, length us, event | category | flops | bytes accessed | tf_op | source)
XLA Modules:
  0.0 1269.1 jit_solution(794084808293716821)
XLA Ops:
  19.2 6.9 concatenate.34
  80.9 29.3 %collective-permute-done.5 = bf16[384,768]{1,0:T(8,128)(2,1)} collective-permute-done((bf16[384,768]{1,0:T(8,128)(2,1)S(1)}, bf16[384,768]{1,0:T(8,128)(2,1)}, u32[]{:S(2)}, u32[]{:S(2)}) %collective-permute-start.5) | collective-permute-done | bytes 589856 | tf_op jit(solution)/shard_map/ppermute | solution.py:643
  133.8 12.7 %proj_fwd.2 = (bf16[1024,384]{1,0:T(8,128)(2,1)}, bf16[1024,384]{1,0:T(8,128)(2,1)}, bf16[1024,384]{1,0:T(8,128)(2,1)}, bf16[1024,384]{1,0:T(8,128)(2,1)}, bf16[...) custom-call(bf16[1024,768]{1,0:T(8,128)(2,1)} %bitcast_select_fusion, ...), custom_call_target="tpu_custom_call" | custom-call | tf_op jit(solution)/shard_map/proj_fwd/pallas_call | solution.py:127
  146.5 19.4 %attn_fwd.2 = (f32[384,1024]{1,0:T(8,128)}, f32[3,8,1024]{2,1,0:T(8,128)}) custom-call(bf16[1024,384]{1,0:T(8,128)(2,1)} %get-tuple-element.109.k_ref, bf16[384,1024]{1,0:T(8,128)(2,1)} %get-tuple-element.110.qt_ref, bf16[384,1024]{1,0:T(8,128)(2,1)} %get-tuple-element.111.vt_ref), custom_call_target="tpu_custom_call" | custom-call | tf_op jit(solution)/shard_map/attn_fwd/pallas_call | solution.py:169
  165.9 22.6 %ffn_fwd.2 = (bf16[1024,768]{1,0:T(8,128)(2,1)}, bf16[1024,768]{1,0:T(8,128)(2,1)}, f32[1024,1]{1,0:T(8,128)}, bf16[1024,768]{1,0:T(8,128)(2,1)}, bf16[1024,3072...) custom-call(f32[384,1024]{1,0:T(8,128)} %get-tuple-element.112.at_re, ...), custom_call_target="tpu_custom_call" | custom-call | tf_op jit(solution)/shard_map/ffn_fwd/pallas_call | solution.py:244
  188.5 12.7 %proj_fwd.3 = (bf16[1024,384]{1,0:T(8,128)(2,1)}, bf16[1024,384]{1,0:T(8,128)(2,1)}, bf16[1024,384]{1,0:T(8,128)(2,1)}, bf16[1024,384]{1,0:T(8,128)(2,1)}, bf16[...) custom-call(bf16[1024,768]{1,0:T(8,128)(2,1)} %get-tuple-element.115, ...), custom_call_target="tpu_custom_call" | custom-call | tf_op jit(solution)/shard_map/proj_fwd/pallas_call | solution.py:127
  201.2 19.1 %attn_fwd.3 = (f32[384,1024]{1,0:T(8,128)}, f32[3,8,1024]{2,1,0:T(8,128)}) custom-call(bf16[1024,384]{1,0:T(8,128)(2,1)} %get-tuple-element.116.k_ref, bf16[384,1024]{1,0:T(8,128)(2,1)} %get-tuple-element.117.qt_ref, bf16[384,1024]{1,0:T(8,128)(2,1)} %get-tuple-element.118.vt_ref), custom_call_target="tpu_custom_call" | custom-call | tf_op jit(solution)/shard_map/attn_fwd/pallas_call | solution.py:169
  220.3 22.6 %ffn_fwd.3 = (bf16[1024,768]{1,0:T(8,128)(2,1)}, bf16[1024,768]{1,0:T(8,128)(2,1)}, f32[1024,1]{1,0:T(8,128)}, bf16[1024,768]{1,0:T(8,128)(2,1)}, bf16[1024,3072...) custom-call(f32[384,1024]{1,0:T(8,128)} %get-tuple-element.119.at_re, ...), custom_call_target="tpu_custom_call" | custom-call | tf_op jit(solution)/shard_map/ffn_fwd/pallas_call | solution.py:244
  242.9 18.1 %ffn_bwd.2 = (bf16[1024,768]{1,0:T(8,128)(2,1)}, bf16[1024,3072]{1,0:T(8,128)(2,1)}, bf16[1024,768]{1,0:T(8,128)(2,1)}, bf16[384,1024]{1,0:T(8,128)(2,1)}, bf16[...) custom-call(bf16[1024,768]{1,0:T(8,128)(2,1)} %dynamic-slice_bitcast_fusion.dy_ref, ...), custom_call_target="tpu_custom_call" | custom-call | tf_op jit(solution)/shard_map/ffn_bwd/pallas_call | solution.py:338
  261.0 26.9 %conv_bwd.2 = (bf16[1024,72]{1,0:T(8,128)(2,1)}, bf16[1024,384]{1,0:T(8,128)(2,1)}, bf16[1024,384]{1,0:T(8,128)(2,1)}, bf16[1024,384]{1,0:T(8,128)(2,1)}, bf16[1...) custom-call(bf16[1024,384]{1,0:T(8,128)(2,1)} %get-tuple-element.137.ddn_ref, ...), custom_call_target="tpu_custom_call" | custom-call | tf_op jit(solution)/shard_map/conv_bwd/pallas_call | solution.py:452
  287.9 20.0 %attn_bwd.2 = (bf16[1024,384]{1,0:T(8,128)(2,1)}, bf16[1024,384]{1,0:T(8,128)(2,1)}, bf16[1024,384]{1,0:T(8,128)(2,1)}) custom-call(bf16[1024,384]{1,0:T(8,128)(2,1)} %get-tuple-element.116.k_ref, bf16[1024,384]{1,0:T(8,128)(2,1)} %get-tuple-element.125.v_ref, bf16[1024,384]{1,0:T(8,128)(2,1)} %get-tuple-element.126.q2_ref, ...), custom_call_target="tpu_custom_call" | custom-call | tf_op jit(solution)/shard_map/attn_bwd/pallas_call | solution.py:518
  308.8 7.7 in_bwd.2
  316.5 18.6 %ffn_bwd.3 = (bf16[1024,768]{1,0:T(8,128)(2,1)}, bf16[1024,3072]{1,0:T(8,128)(2,1)}, bf16[1024,768]{1,0:T(8,128)(2,1)}, bf16[384,1024]{1,0:T(8,128)(2,1)}, bf16[...) custom-call(bf16[1024,768]{1,0:T(8,128)(2,1)} %get-tuple-element.145.dy_ref, ...), custom_call_target="tpu_custom_call" | custom-call | tf_op jit(solution)/shard_map/ffn_bwd/pallas_call | solution.py:338
  391.8 26.7 %conv_bwd.3 = (bf16[1024,72]{1,0:T(8,128)(2,1)}, bf16[1024,384]{1,0:T(8,128)(2,1)}, bf16[1024,384]{1,0:T(8,128)(2,1)}, bf16[1024,384]{1,0:T(8,128)(2,1)}, bf16[1...) custom-call(bf16[1024,384]{1,0:T(8,128)(2,1)} %get-tuple-element.156.ddn_ref, ...), custom_call_target="tpu_custom_call" | custom-call | tf_op jit(solution)/shard_map/conv_bwd/pallas_call | solution.py:452
  418.5 20.1 %attn_bwd.3 = (bf16[1024,384]{1,0:T(8,128)(2,1)}, bf16[1024,384]{1,0:T(8,128)(2,1)}, bf16[1024,384]{1,0:T(8,128)(2,1)}) custom-call(bf16[1024,384]{1,0:T(8,128)(2,1)} %get-tuple-element.109.k_ref, bf16[1024,384]{1,0:T(8,128)(2,1)} %get-tuple-element.123.v_ref, bf16[1024,384]{1,0:T(8,128)(2,1)} %get-tuple-element.124.q2_ref, ...), custom_call_target="tpu_custom_call" | custom-call | tf_op jit(solution)/shard_map/attn_bwd/pallas_call | solution.py:518
  438.6 7.9 in_bwd.3
  446.5 6.1 convolution_convert_fusion.1
  480.6 45.3 %reduce-scatter.33.cloned.1.call-done = bf16[192,384]{1,0:T(8,128)(2,1)} async-done(((bf16[3072,384]{1,0:T(8,128)(2,1)}), bf16[192,384]{1,0:T(8,128)(2,1)}) %reduce-scatter.33.cloned.1.call-update) | async-done | bytes 147472 | tf_op jit(solution)/shard_map/reduce_scatter | solution.py:760
  525.9 66.6 %reduce-scatter.35.cloned.1.call-done = bf16[192,384]{1,0:T(8,128)(2,1)} async-done(((bf16[3072,384]{1,0:T(8,128)(2,1)}), bf16[192,384]{1,0:T(8,128)(2,1)}) %reduce-scatter.35.cloned.1.call-update) | async-done | bytes 147472 | tf_op jit(solution)/shard_map/reduce_scatter | solution.py:760
  600.4 58.3 %reduce-scatter.29.cloned.1.call-done = bf16[48,1536]{1,0:T(8,128)(2,1)} async-done(((bf16[768,1536]{1,0:T(8,128)(2,1)}), bf16[48,1536]{1,0:T(8,128)(2,1)}) %reduce-scatter.29.cloned.1.call-update) | async-done | bytes 147472 | tf_op jit(solution)/shard_map/reduce_scatter | solution.py:760
  658.7 66.6 %reduce-scatter.31.cloned.1.call-done = bf16[48,1536]{1,0:T(8,128)(2,1)} async-done(((bf16[768,1536]{1,0:T(8,128)(2,1)}), bf16[48,1536]{1,0:T(8,128)(2,1)}) %reduce-scatter.31.cloned.1.call-update) | async-done | bytes 147472 | tf_op jit(solution)/shard_map/reduce_scatter | solution.py:760
  733.1 58.5 %reduce-scatter.19.cloned.1.call-done = bf16[48,1536]{1,0:T(8,128)(2,1)} async-done(((bf16[768,1536]{1,0:T(8,128)(2,1)}), bf16[48,1536]{1,0:T(8,128)(2,1)}) %reduce-scatter.19.cloned.1.call-update) | async-done | bytes 147472 | tf_op jit(solution)/shard_map/reduce_scatter | solution.py:760
  791.7 66.7 %reduce-scatter.17.cloned.1.call-done = bf16[48,1536]{1,0:T(8,128)(2,1)} async-done(((bf16[768,1536]{1,0:T(8,128)(2,1)}), bf16[48,1536]{1,0:T(8,128)(2,1)}) %reduce-scatter.17.cloned.1.call-update) | async-done | bytes 147472 | tf_op jit(solution)/shard_map/reduce_scatter | solution.py:760
  870.4 44.2 %reduce-scatter.13.cloned.1.call-done = bf16[16,384]{1,0:T(8,128)(2,1)} async-done(((bf16[256,384]{1,0:T(8,128)(2,1)}), bf16[16,384]{1,0:T(8,128)(2,1)}) %reduce-scatter.13.cloned.1.call-update) | async-done | bytes 12304 | tf_op jit(solution)/shard_map/reduce_scatter | solution.py:760
  916.0 54.6 %reduce-scatter.15.cloned.1.call-done = bf16[16,384]{1,0:T(8,128)(2,1)} async-done(((bf16[256,384]{1,0:T(8,128)(2,1)}), bf16[16,384]{1,0:T(8,128)(2,1)}) %reduce-scatter.15.cloned.1.call-update) | async-done | bytes 12304 | tf_op jit(solution)/shard_map/reduce_scatter | solution.py:760
  974.9 19.9 %all_gather.18 = bf16[256,384]{1,0:T(8,128)(2,1)S(1)} all-gather(bf16[16,384]{1,0:T(8,128)(2,1)S(1)} %add_select_fusion), channel_id=1, replica_groups=mesh['section'=2,'dp'=16] {'dp'}, dimensions={0}, use_global_device_ids=true | all-gather | bytes 208896 | tf_op jit(solution)/shard_map/all_gather | solution.py:773
  996.2 31.9 %reduce-scatter.23.cloned.1.call-done = bf16[48,384]{1,0:T(8,128)(2,1)} async-done(((bf16[768,384]{1,0:T(8,128)(2,1)}), bf16[48,384]{1,0:T(8,128)(2,1)}) %reduce-scatter.23.cloned.1.call-update) | async-done | bytes 36880 | tf_op jit(solution)/shard_map/reduce_scatter | solution.py:760
  1028.1 57.7 %reduce-scatter.21.cloned.1.call-done = bf16[48,384]{1,0:T(8,128)(2,1)} async-done(((bf16[768,384]{1,0:T(8,128)(2,1)}), bf16[48,384]{1,0:T(8,128)(2,1)}) %reduce-scatter.21.cloned.1.call-update) | async-done | bytes 36880 | tf_op jit(solution)/shard_map/reduce_scatter | solution.py:760
  1102.3 21.8 %all_gather.20 = bf16[768,384]{1,0:T(8,128)(2,1)S(1)} all-gather(bf16[48,384]{1,0:T(8,128)(2,1)S(1)} %select_add_fusion.4), channel_id=1, replica_groups=mesh['section'=2,'dp'=16] {'dp'}, dimensions={0}, use_global_device_ids=true | all-gather | bytes 626688 | tf_op jit(solution)/shard_map/all_gather | solution.py:773
  1135.4 34.6 %all-gather.11.cloned.1.call-done = bf16[3072,384]{1,0:T(8,128)(2,1)} async-done(((bf16[192,384]{1,0:T(8,128)(2,1)}), bf16[3072,384]{1,0:T(8,128)(2,1)}) %all-gather.11.cloned.1.call-update) | async-done | bytes 2359312 | tf_op jit(solution)/shard_map/all_gather | solution.py:773
  1174.1 39.6 %all-gather.9.cloned.1.call-done = bf16[768,1536]{1,0:T(8,128)(2,1)} async-done(((bf16[48,1536]{1,0:T(8,128)(2,1)}), bf16[768,1536]{1,0:T(8,128)(2,1)}) %all-gather.9.cloned.1.call-update) | async-done | bytes 2359312 | tf_op jit(solution)/shard_map/all_gather | solution.py:773
  1218.2 39.2 %all-gather.5.cloned.1.call-done = bf16[768,1536]{1,0:T(8,128)(2,1)} async-done(((bf16[48,1536]{1,0:T(8,128)(2,1)}), bf16[768,1536]{1,0:T(8,128)(2,1)}) %all-gather.5.cloned.1.call-update) | async-done | bytes 2359312 | tf_op jit(solution)/shard_map/all_gather | solution.py:773
  (388 shorter events, 250.7 us)
Async XLA Ops:
  7.3 466.3 %reduce-scatter.25.cloned.1.call-start = ((), (), s32[]{:S(2)}) async-start(), calls=%async_computation.19 | async-start | bytes 1253376 | tf_op jit(solution)/shard_map/reduce_scatter | solution.py:760
  9.9 103.8 %collective-permute-start = (bf16[384,1536]{1,0:T(8,128)(2,1)}, bf16[384,1536]{1,0:T(8,128)(2,1)}, u32[]{:S(2)}, u32[]{:S(2)}) collective-permute-start(bf16[384,1536]{1,0:T(8,128)(2,1)} %dynamic-slice_bitcast_fusion.1), channel_id=1, source_target_pairs={{0,16},{16,0},{1,17},{17,1},{2,18},{18,2},{3,19},{19,3},{4,20},{20... | collective-permute-start | bytes 3538952 | tf_op jit(solution)/shard_map/ppermute | solution.py:643
  12.9 66.7 %collective-permute-start.3 = (bf16[384,384]{1,0:T(8,128)(2,1)S(1)}, bf16[384,384]{1,0:T(8,128)(2,1)}, u32[]{:S(2)}, u32[]{:S(2)}) collective-permute-start(bf16[384,384]{1,0:T(8,128)(2,1)S(1)} %dynamic-slice_bitcast_fusion.3), channel_id=1, source_target_pairs={{0,16},{16,0},{1,17},{17,1},{2,18},{18,2},{3,19},{19,3},{4,20},{20... | collective-permute-start | bytes 884744 | tf_op jit(solution)/shard_map/ppermute | solution.py:643
  26.0 21.9 %collective-permute-start.2 = (bf16[36918]{0:T(1024)(128)(2,1)}, bf16[36918]{0:T(1024)(128)(2,1)}, u32[]{:S(2)}, u32[]{:S(2)}) collective-permute-start(bf16[36918]{0:T(1024)(128)(2,1)} %concatenate.34), channel_id=1, source_target_pairs={{0,16},{16,0},{1,17},{17,1},{2,18},{18,2},{3,19},{19,3},{4,20},{20... | collective-permute-start | bytes 221516 | tf_op jit(solution)/shard_map/ppermute | solution.py:643
  30.6 79.7 %collective-permute-start.9 = (bf16[1536,384]{1,0:T(8,128)(2,1)}, bf16[1536,384]{1,0:T(8,128)(2,1)}, u32[]{:S(2)}, u32[]{:S(2)}) collective-permute-start(bf16[1536,384]{1,0:T(8,128)(2,1)} %constant_dynamic-slice_fusion), channel_id=1, source_target_pairs={{0,16},{16,0},{1,17},{17,1},{2,18},{18,2},{3,19},{19,3},{4,20},{20... | collective-permute-start | bytes 3538952 | tf_op jit(solution)/shard_map/ppermute | solution.py:643
  31.7 82.0 %collective-permute-start.7 = (bf16[384,1536]{1,0:T(8,128)(2,1)}, bf16[384,1536]{1,0:T(8,128)(2,1)}, u32[]{:S(2)}, u32[]{:S(2)}) collective-permute-start(bf16[384,1536]{1,0:T(8,128)(2,1)} %constant_dynamic-slice_fusion.1), channel_id=1, source_target_pairs={{0,16},{16,0},{1,17},{17,1},{2,18},{18,2},{3,19},{19,3},{4,20},{20... | collective-permute-start | bytes 3538952 | tf_op jit(solution)/shard_map/ppermute | solution.py:643
  47.9 62.4 %collective-permute-start.5 = (bf16[384,768]{1,0:T(8,128)(2,1)S(1)}, bf16[384,768]{1,0:T(8,128)(2,1)}, u32[]{:S(2)}, u32[]{:S(2)}) collective-permute-start(bf16[384,768]{1,0:T(8,128)(2,1)S(1)} %dynamic-slice_bitcast_fusion.2), channel_id=1, source_target_pairs={{0,16},{16,0},{1,17},{17,1},{2,18},{18,2},{3,19},{19,3},{4,20},{20... | collective-permute-start | bytes 1769480 | tf_op jit(solution)/shard_map/ppermute | solution.py:643
  79.6 31.8 %collective-permute-start.4 = (bf16[384,384]{1,0:T(8,128)(2,1)}, bf16[384,384]{1,0:T(8,128)(2,1)S(1)}, u32[]{:S(2)}, u32[]{:S(2)}) collective-permute-start(bf16[384,384]{1,0:T(8,128)(2,1)} %collective-permute-done.3), channel_id=1, source_target_pairs={{0,1},{1,0},{2,3},{3,2},{4,5},{5,4},{6,7},{7,6},{8,9},{9,8},{10,11... | collective-permute-start | bytes 884744 | tf_op jit(solution)/shard_map/ppermute | solution.py:647
  110.3 6.9 collective-permute-start.10
  113.7 15.0 %collective-permute-start.1 = (bf16[384,1536]{1,0:T(8,128)(2,1)}, bf16[384,1536]{1,0:T(8,128)(2,1)S(1)}, u32[]{:S(2)}, u32[]{:S(2)}) collective-permute-start(bf16[384,1536]{1,0:T(8,128)(2,1)} %collective-permute-done), channel_id=1, source_target_pairs={{0,1},{1,0},{2,3},{3,2},{4,5},{5,4},{6,7},{7,6},{8,9},{9,8},{10,11... | collective-permute-start | bytes 3538952 | tf_op jit(solution)/shard_map/ppermute | solution.py:647
  113.7 9.4 collective-permute-start.8
  339.1 134.6 %reduce-scatter.27.cloned.1.call-start = ((), (), s32[]{:S(2)}) async-start(), calls=%async_computation.20 | async-start | bytes 1253376 | tf_op jit(solution)/shard_map/reduce_scatter | solution.py:760
  343.2 182.7 %reduce-scatter.33.cloned.1.call-start = ((), (), s32[]{:S(2)}) async-start(), calls=%async_computation.25 | async-start | bytes 2506752 | tf_op jit(solution)/shard_map/reduce_scatter | solution.py:760
  352.6 239.9 %reduce-scatter.35.cloned.1.call-start = ((), (), s32[]{:S(2)}) async-start(), calls=%async_computation.26 | async-start | bytes 2506752 | tf_op jit(solution)/shard_map/reduce_scatter | solution.py:760
  363.4 295.3 %reduce-scatter.29.cloned.1.call-start = ((), (), s32[]{:S(2)}) async-start(), calls=%async_computation.22 | async-start | bytes 2506752 | tf_op jit(solution)/shard_map/reduce_scatter | solution.py:760
  373.1 352.2 %reduce-scatter.31.cloned.1.call-start = ((), (), s32[]{:S(2)}) async-start(), calls=%async_computation.23 | async-start | bytes 2506752 | tf_op jit(solution)/shard_map/reduce_scatter | solution.py:760
  382.9 408.7 %reduce-scatter.19.cloned.1.call-start = ((), (), s32[]{:S(2)}) async-start(), calls=%async_computation.15 | async-start | bytes 2506752 | tf_op jit(solution)/shard_map/reduce_scatter | solution.py:760
  390.1 468.3 %reduce-scatter.17.cloned.1.call-start = ((), (), s32[]{:S(2)}) async-start(), calls=%async_computation.14 | async-start | bytes 2506752 | tf_op jit(solution)/shard_map/reduce_scatter | solution.py:760
  452.6 461.9 %reduce-scatter.13.cloned.1.call-start = ((), (), s32[]{:S(2)}) async-start(), calls=%async_computation.12 | async-start | bytes 208896 | tf_op jit(solution)/shard_map/reduce_scatter | solution.py:760
  461.6 509.0 %reduce-scatter.15.cloned.1.call-start = ((), (), s32[]{:S(2)}) async-start(), calls=%async_computation.13 | async-start | bytes 208896 | tf_op jit(solution)/shard_map/reduce_scatter | solution.py:760
  466.7 561.4 %reduce-scatter.23.cloned.1.call-start = ((), (), s32[]{:S(2)}) async-start(), calls=%async_computation.18 | async-start | bytes 626688 | tf_op jit(solution)/shard_map/reduce_scatter | solution.py:760
  470.5 615.3 %reduce-scatter.21.cloned.1.call-start = ((), (), s32[]{:S(2)}) async-start(), calls=%async_computation.17 | async-start | bytes 626688 | tf_op jit(solution)/shard_map/reduce_scatter | solution.py:760
  473.6 659.0 %all-gather.7.cloned.1.call-start = ((), (), s32[]{:S(2)}) async-start(), calls=%async_computation.21 | async-start | bytes 1253376 | tf_op jit(solution)/shard_map/all_gather | solution.py:773
  480.5 689.5 %all-gather.11.cloned.1.call-start = ((), (), s32[]{:S(2)}) async-start(), calls=%async_computation.27 | async-start | bytes 2506752 | tf_op jit(solution)/shard_map/all_gather | solution.py:773
  593.5 5.2 collective-permute-start.19
  600.3 613.4 %all-gather.9.cloned.1.call-start = ((), (), s32[]{:S(2)}) async-start(), calls=%async_computation.24 | async-start | bytes 2506752 | tf_op jit(solution)/shard_map/all_gather | solution.py:773
  726.3 5.2 collective-permute-start.18
  733.1 524.4 %all-gather.5.cloned.1.call-start = ((), (), s32[]{:S(2)}) async-start(), calls=%async_computation.16 | async-start | bytes 2506752 | tf_op jit(solution)/shard_map/all_gather | solution.py:773
  867.5 257.7 %collective-permute-start.12 = (bf16[1024,768]{1,0:T(8,128)(2,1)}, bf16[1024,768]{1,0:T(8,128)(2,1)}, u32[]{:S(2)}, u32[]{:S(2)}) collective-permute-start(bf16[1024,768]{1,0:T(8,128)(2,1)} %broadcast_select_fusion), channel_id=1, source_target_pairs={{0,16},{16,0},{1,17},{17,1},{2,18},{18,2},{3,19},{19,3},{4,20},{20... | collective-permute-start | bytes 4718600 | tf_op jit(solution)/shard_map/ppermute | solution.py:643
  914.6 60.3 %collective-permute-start.13 = (bf16[16,384]{1,0:T(8,128)(2,1)}, bf16[16,384]{1,0:T(8,128)(2,1)S(1)}, u32[]{:S(2)}, u32[]{:S(2)}) collective-permute-start(bf16[16,384]{1,0:T(8,128)(2,1)} %reduce-scatter.13.cloned.1.call-done), channel_id=1, source_target_pairs={{0,16},{16,0},{1,17},{17,1},{2,18},{18,2},{3,19},{19,3},{4,20},{20... | collective-permute-start | bytes 36872 | tf_op jit(solution)/shard_map/ppermute | solution.py:643
  974.8 154.1 %collective-permute-start.11 = (bf16[1024,768]{1,0:T(8,128)(2,1)}, bf16[1024,768]{1,0:T(8,128)(2,1)}, u32[]{:S(2)}, u32[]{:S(2)}) collective-permute-start(bf16[1024,768]{1,0:T(8,128)(2,1)} %broadcast_select_fusion.2), channel_id=1, source_target_pairs={{0,16},{16,0},{1,17},{17,1},{2,18},{18,2},{3,19},{19,3},{4,20},{20... | collective-permute-start | bytes 4718600 | tf_op jit(solution)/shard_map/ppermute | solution.py:643
  1086.6 14.8 %collective-permute-start.16 = (bf16[48,384]{1,0:T(8,128)(2,1)S(1)}, bf16[48,384]{1,0:T(8,128)(2,1)S(1)}, u32[]{:S(2)}, u32[]{:S(2)}) collective-permute-start(bf16[48,384]{1,0:T(8,128)(2,1)S(1)} %broadcast_select_fusion.18), channel_id=1, source_target_pairs={{0,16},{16,0},{1,17},{17,1},{2,18},{18,2},{3,19},{19,3},{4,20},{20... | collective-permute-start | bytes 110600 | tf_op jit(solution)/shard_map/ppermute | solution.py:643
  (58 other events, 655.0 us)
Sparse Core Ops, SparseCore 0:
  339.2 59.5 reduce-scatter.24
  403.0 57.0 reduce-scatter.26
  463.8 62.0 reduce-scatter.32
  530.6 61.9 reduce-scatter.34
  596.7 61.9 reduce-scatter.28
  663.4 61.9 reduce-scatter.30
  729.7 61.9 reduce-scatter.18
  796.5 61.8 reduce-scatter.16
  861.9 52.6 reduce-scatter.12
  917.9 52.6 reduce-scatter.14
  974.1 53.9 reduce-scatter.22
  1031.9 53.8 reduce-scatter.20
  1088.1 38.4 all-gather.6
  1128.7 41.2 all-gather.10
  1172.7 40.9 all-gather.8
  1216.4 40.9 all-gather.4

commit v2 on v1

v2 whole, which is shorter than its diff:
```python
from functools import partial

import jax
import jax.numpy as jnp
from jax import lax
from jax.experimental import pallas as pl
from jax.experimental.pallas import tpu as pltpu
from jax.sharding import PartitionSpec as P

BF = jnp.bfloat16
F32 = jnp.float32
RB = 256
PAD = 8
SUB = 8
LOG2E = 1.4426950408889634
INV_SQRT2 = 0.7071067811865476
INV_SQRT2PI = 0.3989422804014327
EPS = 1e-06
VMEM = 56 * 1024 * 1024


def dot(a, b):
    return jnp.dot(a, b, preferred_element_type=F32)


def dot_nt(a, b):
    return lax.dot_general(a, b, (((1,), (1,)), ((), ())), preferred_element_type=F32)


def params(limit=VMEM):
    return pltpu.CompilerParams(vmem_limit_bytes=limit)


def whole(shape):
    zeros = (0,) * len(shape)
    return pl.BlockSpec(shape, lambda *_: zeros)


def rows_of(width):
    return pl.BlockSpec((RB, width), lambda i: (i, 0))


def cols_of(height):
    return pl.BlockSpec((height, RB), lambda i: (0, i))


def cost(us):
    return pl.CostEstimate(flops=int(us * 1.1e9), bytes_accessed=0, transcendentals=0)


def sds(shape, dtype):
    return jax.ShapeDtypeStruct(shape, dtype)


HBM = pl.BlockSpec(memory_space=pl.ANY)
SMEM = pl.BlockSpec(memory_space=pltpu.SMEM)


def copies(pairs, sems):
    all_copies = [pltpu.make_async_copy(src, dst, sems.at[n]) for n, (src, dst) in enumerate(pairs)]
    for c in all_copies:
        c.start()
    for c in all_copies:
        c.wait()


def tile_pairs(buffer, at, array, start, shape):
    rows, cols = shape
    beside = buffer.shape[1] // cols
    lines = rows // 4 // beside
    out = []
    for k in range(beside):
        span = pl.ds(pl.multiple_of(start + k * lines, 16), lines)
        out.append((buffer.at[pl.ds(at, lines), pl.ds(k * cols, cols)], array.at[span, :]))
    return out, lines


GROUPS = {"A": ("wp", "pw"), "B": ("w1", "wo"), "C": ("w2",)}


def fetch(place_ref, layer, name, shapes, own, pieces, into, sems):
    mine = place_ref[1] == layer

    @pl.when(mine)
    def _():
        copies([(own[n], into[n]) for n in into], sems)

    @pl.when(jnp.logical_not(mine))
    def _():
        a, b, c = pieces
        pairs = []
        for j, (got, at) in enumerate(((a, 0), (b, 0), (c, 0), (c, a.shape[0]))):
            for n in GROUPS[name]:
                rows, cols = shapes[n]
                lines = rows // 4 * cols // got.shape[1]
                if n in into:
                    pairs += tile_pairs(got, at, into[n], (place_ref[0] ^ j) * (rows // 4), shapes[n])[0]
                at += lines
        copies(pairs, sems)


def call(kernel, p, wants, inputs, *, grid, in_specs, out_specs, out_shape, scratch_shapes=(), name, us):
    used = [g for g in GROUPS if any(n in wants for n in GROUPS[g])]
    operands = []
    layout = []
    for g in used:
        names = [n for n in GROUPS[g] if n in wants]
        layout.append((g, names))
        operands += [p["own"][n] for n in names] + p["pieces"][g]
    shapes = {n: p["own"][n].shape for n in p["own"]}
    outs = out_shape if isinstance(out_shape, list) else [out_shape]
    tiles = max(
        max(4 * sum(p["pieces"][g][0].shape[1] // shapes[n][1] for n in names), len(names)) for g, names in layout
    )

    def body(place_ref, *refs):
        refs = list(refs)
        sources = refs[: len(operands)]
        rest = refs[len(operands) : len(refs) - len(wants) - 1]
        into = dict(zip(wants, refs[len(refs) - len(wants) - 1 : -1]))
        first = pl.program_id(0) == 0
        for axis in range(1, len(grid)):
            first = first & (pl.program_id(axis) == 0)

        @pl.when(first)
        def _():
            at = 0
            for g, names in layout:
                own = dict(zip(names, sources[at : at + len(names)]))
                pieces = sources[at + len(names) : at + len(names) + 3]
                at += len(names) + 3
                fetch(place_ref, p["l"], g, shapes, own, pieces, {n: into[n] for n in names}, refs[-1])

        kernel(*[into[n] for n in wants], *rest)

    return pl.pallas_call(
        body,
        grid=grid,
        in_specs=[SMEM] + [HBM] * len(operands) + list(in_specs),
        out_specs=out_specs,
        out_shape=out_shape,
        scratch_shapes=list(scratch_shapes)
        + [pltpu.VMEM(shapes[n], BF) for n in wants]
        + [pltpu.SemaphoreType.DMA((tiles,))],
        compiler_params=params(),
        cost_estimate=cost(us),
        name=name,
    )(p["place"], *operands, *inputs)


def vector_parts(vec_ref, att, width):
    at = 4 * att
    views = [vec_ref.at[:, at + n * width : at + (n + 1) * width] for n in range(6)]
    return views + [vec_ref.at[:, at + 6 * width :]]


def norm_rows(z):
    mean = jnp.mean(z, axis=-1, keepdims=True)
    c = z - mean
    r = lax.rsqrt(jnp.mean(c * c, axis=-1, keepdims=True) + EPS)
    return c * r, r


def tap_softmax(logits_t, taps):
    parts = [logits_t[j * SUB : (j + 1) * SUB] for j in range(taps)]
    top = parts[0]
    for part in parts[1:]:
        top = jnp.maximum(top, part)
    exps = [jnp.exp(part - top) for part in parts]
    total = exps[0]
    for part in exps[1:]:
        total = total + part
    inv = 1.0 / total
    return jnp.concatenate([part * inv for part in exps], axis=0)


def fill_padded(dst, src, rows):
    width = dst.shape[1]
    dst[0:PAD, :] = jnp.zeros((PAD, width), F32)
    dst[rows + PAD : rows + 2 * PAD, :] = jnp.zeros((PAD, width), F32)
    for b in range(rows // RB):
        dst[PAD + b * RB : PAD + (b + 1) * RB, :] = src[b * RB : (b + 1) * RB, :].astype(F32)


def proj_kernel(
    wp_ref, pw_ref, h_ref, vec_ref, dk_ref, kwt_ref, kbt_ref,
    q2_ref, k_ref, v_ref, sp_ref, q2t_ref, kt_ref, vt_ref, dep_ref, kc_ref, mx_ref, kern_ref,
    hp_ref,
):
    i = pl.program_id(0)
    rows, width = h_ref.shape
    att = pw_ref.shape[1]
    taps = dk_ref.shape[0]
    half = taps // 2

    @pl.when(i == 0)
    def _():
        fill_padded(hp_ref, h_ref, rows)

    base = pl.multiple_of(i * RB, RB)
    hb = h_ref[pl.ds(base, RB), :]
    query = dot(hb, wp_ref[:, 0:att]) + vec_ref[:, 0:att]
    q2 = query * (0.125 * LOG2E)
    q2_ref[...] = q2.astype(BF)
    q2t_ref[...] = q2.T.astype(BF)
    keys = dot(hb, wp_ref[:, att : 2 * att])
    k_ref[...] = keys.astype(BF)
    kt_ref[...] = keys.T.astype(BF)
    values = dot(hb, wp_ref[:, 2 * att : 3 * att]) + vec_ref[:, att : 2 * att]
    v_ref[...] = values.astype(BF)
    vt_ref[...] = values.T.astype(BF)
    sp_ref[...] = (dot(hb, wp_ref[:, 3 * att : 4 * att]) + vec_ref[:, 2 * att : 3 * att]).astype(BF)
    for c in range(width // 128):
        cols = slice(c * 128, (c + 1) * 128)
        win = hp_ref[pl.ds(base, RB + 2 * PAD), cols]
        acc = dk_ref[0:1, cols] * win[PAD - half : PAD - half + RB]
        for j in range(1, taps):
            acc = acc + dk_ref[j : j + 1, cols] * win[PAD - half + j : PAD - half + j + RB]
        dep_ref[:, cols] = acc.astype(BF)
    keyconv = dot(dep_ref[...], pw_ref[...]) + vec_ref[:, 3 * att : 4 * att]
    kc_ref[...] = keyconv.astype(BF)
    mixed = (keyconv * query).astype(BF)
    mx_ref[...] = mixed
    logits_t = dot_nt(kwt_ref[...], mixed) + kbt_ref[...]
    kern_ref[...] = tap_softmax(logits_t, taps)


def run_proj(h, p):
    rows, width = h.shape
    att = p["own"]["pw"].shape[1]
    taps = p["dk"].shape[0]
    t8 = taps * SUB
    return call(
        proj_kernel, p, ("wp", "pw"), (h, p["vec"], p["dk"], p["kwt"], p["kbt"]),
        grid=(rows // RB,),
        in_specs=[whole((rows, width)), whole(p["vec"].shape), whole(p["dk"].shape), whole((t8, att)), whole((t8, 1))],
        out_specs=[rows_of(att)] * 4 + [cols_of(att)] * 3
        + [rows_of(width), rows_of(att), rows_of(att), cols_of(t8)],
        out_shape=[sds((rows, att), BF)] * 4 + [sds((att, rows), BF)] * 3
        + [sds((rows, width), BF), sds((rows, att), BF), sds((rows, att), BF), sds((t8, rows), F32)],
        scratch_shapes=[pltpu.VMEM((rows + 2 * PAD, width), F32)],
        name="proj_fwd", us=13,
    )


def attn_kernel(k_ref, qt_ref, vt_ref, at_ref, lse_ref, *, head, qb):
    rows = k_ref.shape[0]
    k = k_ref[...]
    ones = jnp.ones((16, rows), BF)
    zeros = jnp.zeros((head, qb), BF)
    for b in range(rows // qb):
        cols = slice(b * qb, (b + 1) * qb)
        for s in range(2):
            lo = s * head
            qt = qt_ref[lo : lo + head, cols]
            qz = jnp.concatenate([qt, zeros] if s == 0 else [zeros, qt], axis=0)
            st = dot(k, qz)
            top = jnp.max(st, axis=0, keepdims=True)
            pr = jnp.exp2(st - top).astype(BF)
            vx = jnp.concatenate([vt_ref[lo : lo + head, :], ones], axis=0)
            ot = dot(vx, pr)
            total = ot[head : head + 1]
            at_ref[lo : lo + head, cols] = ot[0:head] * (1.0 / total)
            lse_ref[0, s : s + 1, cols] = top + jnp.log2(total)


def run_attn(k, q2t, vt, head):
    att, rows = q2t.shape
    pairs = att // (2 * head)
    blk = pl.BlockSpec((2 * head, rows), lambda g: (g, 0))
    return pl.pallas_call(
        partial(attn_kernel, head=head, qb=256),
        grid=(pairs,),
        in_specs=[pl.BlockSpec((rows, 2 * head), lambda g: (0, g)), blk, blk],
        out_specs=[blk, pl.BlockSpec((1, SUB, rows), lambda g: (g, 0, 0))],
        out_shape=[sds((att, rows), F32), sds((pairs, SUB, rows), F32)],
        compiler_params=params(),
        cost_estimate=cost(19),
        name="attn_fwd",
    )(k, q2t, vt)


def ffn_kernel(
    w1_ref, wo_ref, w2_ref, at_ref, sp_ref, kern_ref, h_ref, ex_ref, vec_ref,
    ctx_ref, u1_ref, r1_ref, nl_ref, act_ref, gp_ref, u2_ref, r2_ref, out_ref,
    spp_ref,
):
    i = pl.program_id(0)
    rows, att = sp_ref.shape
    taps = kern_ref.shape[0] // SUB
    half = taps // 2
    width = h_ref.shape[1]
    gout, gin = w1_ref.shape[1], w2_ref.shape[1]
    groups = width // gin
    bo, g1, s1, b2, g2, s2, b1 = vector_parts(vec_ref, att, width)

    @pl.when(i == 0)
    def _():
        fill_padded(spp_ref, sp_ref, rows)

    base = pl.multiple_of(i * RB, RB)
    ctx_ref[:, 0:att] = at_ref[...].T.astype(BF)
    kn = kern_ref[...].T.astype(BF)
    for c in range(att // 128):
        cols = slice(c * 128, (c + 1) * 128)
        win = spp_ref[pl.ds(base, RB + 2 * PAD), cols]
        acc = jnp.zeros((RB, 128), F32)
        for j in range(taps):
            kexp = dot(kn, ex_ref[j, :, cols])
            acc = acc + kexp * win[PAD - half + j : PAD - half + j + RB]
        ctx_ref[:, att + c * 128 : att + (c + 1) * 128] = acc.astype(BF)
    z = dot(ctx_ref[...], wo_ref[...]) + bo[...] + h_ref[...].astype(F32)
    u1, r1 = norm_rows(z)
    u1_ref[...] = u1.astype(BF)
    r1_ref[...] = r1
    normed = u1 * g1[...] + s1[...]
    nl = normed.astype(BF)
    nl_ref[...] = nl
    fb = 512
    outs = []
    for g in range(groups):
        x = nl[:, g * gin : (g + 1) * gin]
        acc = None
        for f in range(gout // fb):
            fs = slice(f * fb, (f + 1) * fb)
            full = slice(g * gout + f * fb, g * gout + (f + 1) * fb)
            inner = dot(x, w1_ref[g * gin : (g + 1) * gin, fs]) + b1[:, full]
            cdf = 0.5 + 0.5 * lax.erf(inner * INV_SQRT2)
            pdf = jnp.exp(inner * inner * -0.5) * INV_SQRT2PI
            a = (inner * cdf).astype(BF)
            act_ref[:, full] = a
            gp_ref[:, full] = (cdf + inner * pdf).astype(BF)
            part = dot(a, w2_ref[full, :])
            acc = part if acc is None else acc + part
        outs.append(acc)
    z2 = jnp.concatenate(outs, axis=1) + b2[...] + normed
    u2, r2 = norm_rows(z2)
    u2_ref[...] = u2.astype(BF)
    r2_ref[...] = r2
    out_ref[...] = (u2 * g2[...] + s2[...]).astype(BF)


def run_ffn(at, sp, kern, h, ex, p):
    rows, width = h.shape
    att = sp.shape[1]
    t8 = kern.shape[0]
    ff = p["own"]["w2"].shape[0]
    return call(
        ffn_kernel, p, ("w1", "wo", "w2"), (at, sp, kern, h, ex, p["vec"]),
        grid=(rows // RB,),
        in_specs=[cols_of(att), whole((rows, att)), cols_of(t8), rows_of(width), whole(ex.shape),
                  whole(p["vec"].shape)],
        out_specs=[rows_of(width), rows_of(width), rows_of(1), rows_of(width), rows_of(ff), rows_of(ff),
                   rows_of(width), rows_of(1), rows_of(width)],
        out_shape=[sds((rows, width), BF), sds((rows, width), BF), sds((rows, 1), F32), sds((rows, width), BF),
                   sds((rows, ff), BF), sds((rows, ff), BF), sds((rows, width), BF), sds((rows, 1), F32),
                   sds((rows, width), BF)],
        scratch_shapes=[pltpu.VMEM((rows + 2 * PAD, att), F32)],
        name="ffn_fwd", us=22,
    )


def add_sum(ref, value, first):
    total = jnp.sum(value, axis=0, keepdims=True)

    @pl.when(first)
    def _():
        ref[...] = total

    @pl.when(jnp.logical_not(first))
    def _():
        ref[...] += total


def norm_back(dy, u, r, gain):
    g = dy * gain
    return r * (g - jnp.mean(g, axis=-1, keepdims=True) - u * jnp.mean(g * u, axis=-1, keepdims=True))


def ffn_back_kernel(
    w1_ref, wo_ref, w2_ref, dy_ref, u2_ref, r2_ref, gp_ref, u1_ref, r1_ref, prm_ref,
    ds_ref, di_ref, dz_ref, dat_ref, dan_ref, ddn_ref, vec_ref, db1_ref,
):
    i = pl.program_id(0)
    first = i == 0
    gout, gin = w1_ref.shape[1], w2_ref.shape[1]
    groups = dy_ref.shape[1] // gin
    att = dan_ref.shape[1]
    _, g1, _, _, g2, _, _ = vector_parts(prm_ref, att, dy_ref.shape[1])

    @pl.when(first)
    def _():
        vec_ref[...] = jnp.zeros(vec_ref.shape, F32)
        db1_ref[...] = jnp.zeros(db1_ref.shape, F32)

    dy = dy_ref[...].astype(F32)
    u2 = u2_ref[...].astype(F32)
    vec_ref[0:1, :] += jnp.sum(dy * u2, axis=0, keepdims=True)
    vec_ref[1:2, :] += jnp.sum(dy, axis=0, keepdims=True)
    dsum = norm_back(dy, u2, r2_ref[...], g2[...])
    vec_ref[2:3, :] += jnp.sum(dsum, axis=0, keepdims=True)
    dlow = dsum.astype(BF)
    ds_ref[...] = dlow
    fb = 512
    outs = []
    for g in range(groups):
        x = dlow[:, g * gin : (g + 1) * gin]
        acc = None
        for f in range(gout // fb):
            fs = slice(f * fb, (f + 1) * fb)
            full = slice(g * gout + f * fb, g * gout + (f + 1) * fb)
            dinner = dot_nt(x, w2_ref[full, :]) * gp_ref[:, full].astype(F32)
            db1_ref[:, full] += jnp.sum(dinner, axis=0, keepdims=True)
            dil = dinner.astype(BF)
            di_ref[:, full] = dil
            part = dot_nt(dil, w1_ref[g * gin : (g + 1) * gin, fs])
            acc = part if acc is None else acc + part
        outs.append(acc)
    dn = jnp.concatenate(outs, axis=1) + dsum
    u1 = u1_ref[...].astype(F32)
    vec_ref[3:4, :] += jnp.sum(dn * u1, axis=0, keepdims=True)
    vec_ref[4:5, :] += jnp.sum(dn, axis=0, keepdims=True)
    dz = norm_back(dn, u1, r1_ref[...], g1[...])
    vec_ref[5:6, :] += jnp.sum(dz, axis=0, keepdims=True)
    dzl = dz.astype(BF)
    dz_ref[...] = dzl
    dctx = dot_nt(dzl, wo_ref[...])
    dan_ref[...] = dctx[:, 0:att].astype(BF)
    dat_ref[...] = dctx[:, 0:att].T.astype(BF)
    ddn_ref[...] = dctx[:, att:].astype(BF)


def run_ffn_back(dy, keep, p):
    rows, width = dy.shape
    ff = p["own"]["w2"].shape[0]
    att = p["own"]["pw"].shape[1]
    return call(
        ffn_back_kernel, p, ("w1", "wo", "w2"),
        (dy, keep["u2"], keep["r2"], keep["gp"], keep["u1"], keep["r1"], p["vec"]),
        grid=(rows // RB,),
        in_specs=[rows_of(width), rows_of(width), rows_of(1), rows_of(ff), rows_of(width), rows_of(1),
                  whole(p["vec"].shape)],
        out_specs=[rows_of(width), rows_of(ff), rows_of(width), cols_of(att), rows_of(att),
                   rows_of(width - att), whole((SUB, width)), whole((1, ff))],
        out_shape=[sds((rows, width), BF), sds((rows, ff), BF), sds((rows, width), BF), sds((att, rows), BF),
                   sds((rows, att), BF), sds((rows, width - att), BF), sds((SUB, width), F32), sds((1, ff), F32)],
        name="ffn_bwd", us=18,
    )


def conv_back_kernel(
    pw_ref, ddn_ref, sp_ref, kern_ref, kc_ref, q2_ref, h_ref, dz_ref, ex_ref, ext_ref, kwt_ref, dk_ref, dqa_ref,
    dl_ref, dq_ref, dsp_ref, dkc_ref, res_ref, dkg_ref, dpb_ref, dkb_ref, dbp_ref,
    ddp_ref, spp_ref, hp_ref, dep_ref, knp_ref,
):
    phase = pl.program_id(0)
    i = pl.program_id(1)
    rows, att = sp_ref.shape
    width = h_ref.shape[1]
    taps = dk_ref.shape[0]
    half = taps // 2

    @pl.when((phase == 0) & (i == 0))
    def _():
        fill_padded(ddp_ref, ddn_ref, rows)
        fill_padded(spp_ref, sp_ref, rows)
        fill_padded(hp_ref, h_ref, rows)
        dep_ref[0:PAD, :] = jnp.zeros((PAD, width), F32)
        dep_ref[rows + PAD : rows + 2 * PAD, :] = jnp.zeros((PAD, width), F32)
        knp_ref[0:PAD, :] = jnp.zeros((PAD, knp_ref.shape[1]), F32)
        knp_ref[rows + PAD : rows + 2 * PAD, :] = jnp.zeros((PAD, knp_ref.shape[1]), F32)
        dkg_ref[...] = jnp.zeros(dkg_ref.shape, F32)
        dpb_ref[...] = jnp.zeros(dpb_ref.shape, F32)
        dkb_ref[...] = jnp.zeros(dkb_ref.shape, F32)
        dbp_ref[...] = jnp.zeros(dbp_ref.shape, F32)

    base = pl.multiple_of(i * RB, RB)

    @pl.when(phase == 0)
    def _():
        dd = ddn_ref[pl.ds(base, RB), :].astype(F32)
        dkern = None
        for j in range(taps):
            prods = []
            for c in range(att // 128):
                cols = slice(c * 128, (c + 1) * 128)
                win = spp_ref[pl.ds(base, RB + 2 * PAD), cols]
                prods.append((dd[:, cols] * win[PAD - half + j : PAD - half + j + RB]).astype(BF))
            part = dot(jnp.concatenate(prods, axis=1), ext_ref[j])
            dkern = part if dkern is None else dkern + part
        dkt = dkern.T
        kt = kern_ref[...]
        knp_ref[pl.ds(base + PAD, RB), :] = kt.T
        tot = kt[0:SUB] * dkt[0:SUB]
        for j in range(1, taps):
            tot = tot + kt[j * SUB : (j + 1) * SUB] * dkt[j * SUB : (j + 1) * SUB]
        dlt = jnp.concatenate(
            [kt[j * SUB : (j + 1) * SUB] * (dkt[j * SUB : (j + 1) * SUB] - tot) for j in range(taps)], axis=0
        )
        dkb_ref[...] += jnp.sum(dlt, axis=1, keepdims=True)
        dl = dlt.T.astype(BF)
        dl_ref[...] = dl
        dmixed = dot(dl, kwt_ref[...])
        query = q2_ref[...].astype(F32) * (8.0 / LOG2E)
        dq = dqa_ref[...].astype(F32) + dmixed * kc_ref[...].astype(F32)
        dbp_ref[0:1, :] += jnp.sum(dq, axis=0, keepdims=True)
        dq_ref[...] = dq.astype(BF)
        dkc = dmixed * query
        dpb_ref[...] += jnp.sum(dkc, axis=0, keepdims=True)
        dkcl = dkc.astype(BF)
        dkc_ref[...] = dkcl
        dep_ref[pl.ds(base + PAD, RB), :] = dot_nt(dkcl, pw_ref[...])

    @pl.when(phase == 1)
    def _():
        for c in range(width // 128):
            cols = slice(c * 128, (c + 1) * 128)
            win = dep_ref[pl.ds(base, RB + 2 * PAD), cols]
            mid = win[PAD : PAD + RB]
            hw = hp_ref[pl.ds(base, RB + 2 * PAD), cols]
            acc = dz_ref[:, cols].astype(F32)
            for j in range(taps):
                acc = acc + dk_ref[j : j + 1, cols] * win[PAD + half - j : PAD + half - j + RB]
                dkg_ref[j : j + 1, cols] += jnp.sum(
                    mid * hw[PAD - half + j : PAD - half + j + RB], axis=0, keepdims=True
                )
            res_ref[:, cols] = acc.astype(BF)
        kn = knp_ref[pl.ds(base, RB + 2 * PAD), :].astype(BF)
        for c in range(att // 128):
            cols = slice(c * 128, (c + 1) * 128)
            win = ddp_ref[pl.ds(base, RB + 2 * PAD), cols]
            acc = jnp.zeros((RB, 128), F32)
            for j in range(taps):
                prod = dot(kn, ex_ref[j, :, cols]) * win
                acc = acc + prod[PAD + half - j : PAD + half - j + RB]
            dbp_ref[1:2, cols] += jnp.sum(acc, axis=0, keepdims=True)
            dsp_ref[:, cols] = acc.astype(BF)


def run_conv_back(ddn, dz, dqa, h, keep, ex, ext, p):
    rows, att = ddn.shape
    width = h.shape[1]
    taps = p["dk"].shape[0]
    t8 = taps * SUB
    last = rows // RB - 1

    def early(width):
        return pl.BlockSpec((RB, width), lambda ph, i: (jnp.where(ph == 0, i, last), 0))

    def late(width):
        return pl.BlockSpec((RB, width), lambda ph, i: (jnp.where(ph == 1, i, 0), 0))

    return call(
        conv_back_kernel, p, ("pw",),
        (ddn, keep["sp"], keep["kern"], keep["kc"], keep["q2"], h, dz, ex, ext, p["kwt"], p["dk"], dqa),
        grid=(2, rows // RB),
        in_specs=[
            whole((rows, att)), whole((rows, att)),
            pl.BlockSpec((t8, RB), lambda ph, i: (0, jnp.where(ph == 0, i, last))),
            early(att), early(att), whole((rows, width)), late(width), whole(ex.shape), whole(ext.shape),
            whole((t8, att)), whole(p["dk"].shape), early(att),
        ],
        out_specs=[early(t8), early(att), late(att), early(att), late(width), whole(p["dk"].shape),
                   whole((1, att)), whole((t8, 1)), whole((SUB, att))],
        out_shape=[sds((rows, t8), BF), sds((rows, att), BF), sds((rows, att), BF), sds((rows, att), BF),
                   sds((rows, width), BF), sds(p["dk"].shape, F32), sds((1, att), F32), sds((t8, 1), F32),
                   sds((SUB, att), F32)],
        scratch_shapes=[
            pltpu.VMEM((rows + 2 * PAD, att), F32), pltpu.VMEM((rows + 2 * PAD, att), F32),
            pltpu.VMEM((rows + 2 * PAD, width), F32), pltpu.VMEM((rows + 2 * PAD, width), F32),
            pltpu.VMEM((rows + 2 * PAD, t8), F32),
        ],
        name="conv_bwd", us=27,
    )


def attn_back_kernel(
    k_ref, v_ref, q2_ref, do_ref, qt_ref, kt_ref, dot_ref, at_ref, lse_ref,
    dq_ref, dk_ref, dv_ref, dbv_ref, ak_ref, av_ref, *, head, qb,
):
    rows = k_ref.shape[0]
    k = k_ref[...]
    v = v_ref[...]
    zeros = jnp.zeros((head, qb), BF)
    lane = lax.broadcasted_iota(jnp.int32, (1, 2 * head), 1)
    for b in range(rows // qb):
        cols = slice(b * qb, (b + 1) * qb)
        dqs = []
        for s in range(2):
            lo = s * head
            side = (lane >= lo) & (lane < lo + head)
            qt = qt_ref[lo : lo + head, cols]
            qz = jnp.concatenate([qt, zeros] if s == 0 else [zeros, qt], axis=0)
            dt = dot_ref[lo : lo + head, cols]
            dz = jnp.concatenate([dt, zeros] if s == 0 else [zeros, dt], axis=0)
            dd = jnp.sum(dt.astype(F32) * at_ref[lo : lo + head, cols], axis=0, keepdims=True)
            pr = jnp.exp2(dot(k, qz) - lse_ref[0, s : s + 1, cols])
            ds = (pr * (dot(v, dz) - dd)).astype(BF)
            dqs.append(dot(kt_ref[lo : lo + head, :], ds))
            qn = jnp.where(side, q2_ref[cols, :], jnp.zeros((), BF))
            dn = jnp.where(side, do_ref[cols, :], jnp.zeros((), BF))
            gv = dot(pr.astype(BF), dn)
            gk = dot(ds, qn)
            if b == 0 and s == 0:
                av_ref[...] = gv
                ak_ref[...] = gk
            else:
                av_ref[...] += gv
                ak_ref[...] += gk
        dq_ref[cols, :] = (jnp.concatenate(dqs, axis=0).T * 0.125).astype(BF)
    dk_ref[...] = (ak_ref[...] * (1.0 / LOG2E)).astype(BF)
    dv_ref[...] = av_ref[...].astype(BF)
    dbv_ref[...] = jnp.sum(av_ref[...], axis=0, keepdims=True)


def run_attn_back(do, dot_t, keep, head):
    rows, att = do.shape
    pairs = att // (2 * head)
    nat = pl.BlockSpec((rows, 2 * head), lambda g: (0, g))
    tra = pl.BlockSpec((2 * head, rows), lambda g: (g, 0))
    return pl.pallas_call(
        partial(attn_back_kernel, head=head, qb=256),
        grid=(pairs,),
        in_specs=[nat, nat, nat, nat, tra, tra, tra, tra, pl.BlockSpec((1, SUB, rows), lambda g: (g, 0, 0))],
        out_specs=[nat] * 3 + [pl.BlockSpec((1, 2 * head), lambda g: (0, g))],
        out_shape=[sds((rows, att), BF)] * 3 + [sds((1, att), F32)],
        scratch_shapes=[pltpu.VMEM((rows, 2 * head), F32)] * 2,
        compiler_params=params(),
        cost_estimate=cost(20),
        name="attn_bwd",
    )(keep["k"], keep["v"], keep["q2"], do, keep["q2t"], keep["kt"], dot_t, keep["at"], keep["lse"])


def in_back_kernel(wp_ref, dq_ref, dk_ref, dv_ref, dsp_ref, res_ref, m_ref, dh_ref):
    att = dq_ref.shape[1]
    dh = res_ref[...].astype(F32)
    for n, ref in enumerate((dq_ref, dk_ref, dv_ref, dsp_ref)):
        dh = dh + dot_nt(ref[...], wp_ref[:, n * att : (n + 1) * att])
    dh_ref[...] = (dh * (1.0 - m_ref[...])).astype(BF)


def run_in_back(dq, dk, dv, dsp, res, mask, p):
    rows, width = res.shape
    att = dq.shape[1]
    return call(
        in_back_kernel, p, ("wp",), (dq, dk, dv, dsp, res, mask),
        grid=(rows // RB,),
        in_specs=[rows_of(att)] * 4 + [rows_of(width), rows_of(1)],
        out_specs=rows_of(width),
        out_shape=sds((rows, width), BF),
        name="in_bwd", us=8,
    )


def wide_grad_kernel(nl_ref, di_ref, ds_ref, act_ref, out_ref, nt_ref, dt_ref):
    @pl.when(pl.program_id(1) == 0)
    def _():
        nt_ref[...] = nl_ref[...].T
        dt_ref[...] = ds_ref[...].T

    out_ref[0] = dot(nt_ref[...], di_ref[...]).astype(BF)
    out_ref[1] = dot(dt_ref[...], act_ref[...]).astype(BF)


def run_wide_grads(nl, di, ds, act, groups):
    rows, width = nl.shape
    gin = width // groups
    steps = di.shape[1] // groups // width
    narrow = pl.BlockSpec((rows, gin), lambda g, q: (0, g))
    wide = pl.BlockSpec((rows, width), lambda g, q: (0, g * steps + q))
    return pl.pallas_call(
        wide_grad_kernel,
        grid=(groups, steps),
        in_specs=[narrow, wide, narrow, wide],
        out_specs=pl.BlockSpec((2, gin, width), lambda g, q: (0, q * groups + g, 0)),
        out_shape=sds((2, steps * width, width), BF),
        scratch_shapes=[pltpu.VMEM((gin, rows), BF)] * 2,
        compiler_params=params(),
        cost_estimate=cost(6),
        name="ffn_wgrad",
    )(nl, di, ds, act).reshape(2 * steps * width, width)


def mid_grad_kernel(ctx_ref, dz_ref, h_ref, dk_ref, dv_ref, out_ref):
    width = ctx_ref.shape[1]
    att = dk_ref.shape[1]
    out_ref[0:width, :] = dot(ctx_ref[...].T, dz_ref[...]).astype(BF)
    ht = h_ref[...].T
    out_ref[width:, 0:att] = dot(ht, dk_ref[...]).astype(BF)
    out_ref[width:, att:] = dot(ht, dv_ref[...]).astype(BF)


def run_mid_grads(ctx, dz, h, dk, dv):
    width = h.shape[1]
    return pl.pallas_call(
        mid_grad_kernel,
        out_shape=sds((2 * width, width), BF),
        compiler_params=params(),
        cost_estimate=cost(5),
        name="mid_wgrad",
    )(ctx, dz, h, dk, dv)


def last_grad_kernel(
    wp_ref, h_ref, dq_ref, dk_ref, dv_ref, dsp_ref, dep_ref, dkc_ref, mx_ref, dl_ref, m_ref, res_ref,
    out_ref, kw_ref, mg_ref,
):
    width = h_ref.shape[1]
    att = dq_ref.shape[1]
    ht = h_ref[...].T
    out_ref[0:width, 0:att] = dot(ht, dq_ref[...]).astype(BF)
    out_ref[0:width, att:] = dot(ht, dsp_ref[...]).astype(BF)
    out_ref[width : width + att, :] = dot(dkc_ref[...].T, dep_ref[...]).astype(BF)
    kw_ref[...] = dot(dl_ref[...].T, mx_ref[...])
    m = m_ref[...]
    total = dot(m, res_ref[...])
    for n, ref in enumerate((dq_ref, dk_ref, dv_ref, dsp_ref)):
        part = dot(m, ref[...])
        high = part.astype(BF)
        low = (part - high.astype(F32)).astype(BF)
        w = wp_ref[:, n * att : (n + 1) * att]
        total = total + dot_nt(high, w) + dot_nt(low, w)
    mg_ref[...] = total


def run_last_grads(h, dq, dk, dv, dsp, dep, dkc, mx, dl, res, mask_rows, p):
    rows, width = h.shape
    att = dq.shape[1]
    inputs = (h, dq, dk, dv, dsp, dep, dkc, mx, dl, mask_rows, res)
    return call(
        last_grad_kernel, p, ("wp",), inputs,
        grid=(1,),
        in_specs=[whole(a.shape) for a in inputs],
        out_specs=[whole((width + att, width)), whole((dl.shape[1], att)), whole((SUB, width))],
        out_shape=[sds((width + att, width), BF), sds((dl.shape[1], att), F32), sds((SUB, width), F32)],
        name="last_wgrad", us=9,
    )


def vector_pack(bp, pb, bo, g1, s1, b2, g2, s2, b1):
    return jnp.concatenate([bp, pb, bo, g1, s1, b2, g2, s2, b1], axis=1)


def prepare(vec, dk, kwt, kb):
    taps = dk.shape[0]
    heads = kb.shape[0] // taps
    att = kwt.shape[1]
    kwt = jnp.pad(kwt.reshape(heads, taps, att).transpose(1, 0, 2), ((0, 0), (0, SUB - heads), (0, 0)))
    kbt = jnp.pad(kb.astype(F32).reshape(heads, taps).T, ((0, 0), (0, SUB - heads)))
    return dict(vec=vec.astype(F32), dk=dk.astype(F32), kwt=kwt.reshape(taps * SUB, att),
                kbt=kbt.reshape(taps * SUB, 1))


def spread_matrices(taps, heads, head):
    src = jnp.arange(taps * SUB)[None, :, None]
    tap = jnp.arange(taps)[:, None, None]
    feature = jnp.arange(heads * head)[None, None, :]
    ex = (src == tap * SUB + feature // head).astype(BF)
    feature, src = feature.transpose(0, 2, 1), src.transpose(0, 2, 1)
    ext = (src == tap * SUB + feature // head).astype(BF)
    return ex, ext


def layer_forward(h, p, ex, head, slot):
    q2, k, v, sp, q2t, kt, vt, dep, kc, mx, kern = run_proj(h, p)
    k, q2t, vt = slot("attn", (k, q2t, vt))
    at, lse = run_attn(k, q2t, vt, head)
    at = slot("ffn", at)
    ctx, u1, r1, nl, act, gp, u2, r2, out = run_ffn(at, sp, kern, h, ex, p)
    keep = dict(h=h, q2=q2, k=k, v=v, sp=sp, q2t=q2t, kt=kt, dep=dep, kc=kc, mx=mx, kern=kern, at=at, lse=lse,
                ctx=ctx, u1=u1, r1=r1, nl=nl, act=act, gp=gp, u2=u2, r2=r2)
    return out, keep


def small_rows(vec, db1, dkg, dbp, dbv, dpb, dkb, dkw, mg, lines):
    width = vec.shape[1]
    att = dpb.shape[1]

    def wide(a, n):
        return jnp.pad(a, ((0, n - a.shape[0]), (0, width - a.shape[1])))

    rows = [
        wide(dkw, dkw.shape[0]), vec, wide(db1.reshape(-1, width), SUB), wide(dkg, 2 * SUB),
        wide(jnp.concatenate([dbp[0:2], dbv, dpb]), SUB), wide(dkb.reshape(1, -1), SUB - 1), mg,
    ]
    rows = jnp.concatenate(rows)
    return jnp.pad(rows, ((0, lines - rows.shape[0]), (0, 0))).astype(BF)


def small_parts(rows, att, taps, heads, ff):
    t8 = taps * SUB
    width = rows.shape[1]
    at = t8
    vec = rows[at : at + SUB]
    b1 = rows[at + SUB : at + SUB + ff // width].reshape(-1)
    dk = rows[at + 2 * SUB : at + 2 * SUB + taps]
    four = rows[at + 4 * SUB : at + 4 * SUB + 4, :att]
    kb = rows[at + 5 * SUB, :t8].reshape(taps, SUB)[:, :heads].T.reshape(-1)
    kw = rows[:t8, :att].reshape(taps, SUB, att)[:, :heads].transpose(1, 0, 2).reshape(heads * taps, att).T
    return {
        "bp": jnp.concatenate([four[0], four[2], four[1]]), "dk": dk, "pb": four[3], "kw": kw, "kb": kb,
        "bo": vec[5], "g1": vec[3], "s1": vec[4], "b1": b1, "b2": vec[2], "g2": vec[0], "s2": vec[1],
    }, rows[at + 6 * SUB - 1]


def mask_row(taps):
    return taps * SUB + 6 * SUB - 1


def h_groups(p):
    return p["own"]["w1"].shape[0] // p["own"]["w2"].shape[1]


def layer_backward(dy, keep, mask, mask_rows, p, ex, ext, head, lines, slot, send, later):
    groups = h_groups(p)
    h = keep["h"]
    dy = slot("ffn", dy)
    ds, di, dz, dat, dan, ddn, vec, db1 = run_ffn_back(dy, keep, p)
    di, dan = slot("wide", (di, dan))
    wide = run_wide_grads(keep["nl"], di, ds, keep["act"], groups)
    send(0, wide)

    def mid_chunk(dk, dv):
        send(1, run_mid_grads(keep["ctx"], dz, h, dk, dv))

    def last_chunk(dq, dk, dv, dsp, dkc, dl, res, sums):
        last, dkw, mg = run_last_grads(h, dq, dk, dv, dsp, keep["dep"], dkc, keep["mx"], dl, res, mask_rows, p)
        dkg, dpb, dkb, dbp, dbv = sums
        small = small_rows(vec, db1, dkg, dbp, dbv, dpb, dkb, dkw, mg[0:1], lines)
        send(2, jnp.concatenate([last, small]))

    dan, dat = slot("attn", (dan, dat))
    dqa, dk, dv, dbv = run_attn_back(dan, dat, keep, head)
    if not later:
        dqa, dk, dv = slot("mid", (dqa, dk, dv))
        mid_chunk(dk, dv)
    ddn, dqa = slot("conv", (ddn, dqa))
    dl, dq, dsp, dkc, res, dkg, dpb, dkb, dbp = run_conv_back(ddn, dz, dqa, h, keep, ex, ext, p)
    sums = (dkg, dpb, dkb, dbp, dbv)
    if not later:
        dq, dl, res = slot("last", (dq, dl, res))
        last_chunk(dq, dk, dv, dsp, dkc, dl, res, sums)
    dq, res = slot("in", (dq, res))
    dh = run_in_back(dq, dk, dv, dsp, res, mask, p)

    def rest(name, x):
        if name == "attn":
            x, dk_now = lax.optimization_barrier((x, dk))
            mid_chunk(dk_now, dv)
            x, dl_now = slot("last", (x, dl))
            last_chunk(dq, dk, dv, dsp, dkc, dl_now, res, sums)
        return x

    return slot("end", dh), rest


def pack_kernel(place_ref, *refs, names):
    flat = [n for g in names for n in g]
    arrays = dict(zip(flat, refs[: len(flat)]))
    pairs = []
    for buffer, group in zip(refs[len(flat) : -1], names):
        at = 0
        for n in group:
            shape = arrays[n].shape
            tiles, lines = tile_pairs(buffer, at, arrays[n], place_ref[0] * (shape[0] // 4), shape)
            pairs += [(src, dst) for dst, src in tiles]
            at += lines
    copies(pairs, refs[-1])


def pack_quarters(own, place, width):
    names = tuple(GROUPS.values())
    flat = [n for g in names for n in g]
    heights = [sum(own[n].size // 4 // width for n in g) for g in names]
    return pl.pallas_call(
        partial(pack_kernel, names=names),
        in_specs=[SMEM] + [HBM] * len(flat),
        out_specs=[pl.BlockSpec(memory_space=pltpu.VMEM)] * len(names),
        out_shape=[sds((n, width), BF) for n in heights],
        scratch_shapes=[pltpu.SemaphoreType.DMA((sum(width // own[n].shape[1] for n in flat),))],
        compiler_params=params(),
        cost_estimate=cost(3),
        name="pack_weights",
    )(place, *[own[n] for n in flat])


def swap(x):
    return lax.ppermute(x, "section", [(0, 1), (1, 0)])


def across(x, bit):
    return lax.ppermute(x, "dp", [(i, i ^ (1 << bit)) for i in range(lax.axis_size("dp"))])


def move(x, step):
    if step == "scatter":
        return lax.psum_scatter(x, "dp", scatter_dimension=0, tiled=True)
    if step == "gather":
        return lax.all_gather(x, "dp", axis=0, tiled=True)
    return swap(x) if step == "section" else across(x, step)


def my_bit(bit):
    return (lax.axis_index("dp") >> bit) & 1


def row_bits():
    return list(range(lax.axis_size("dp").bit_length() - 1))


NEEDS = {"wide": ("00", "10"), "mid": ("01", "11"), "last": ("02", "12")}


class Flows:
    def __init__(self):
        self.flows = {}
        self.pending = {}
        self.results = {}

    def add(self, name, flow):
        self.flows[name] = flow

    def step(self, names, arrays):
        names = [n for n in names if n in self.flows]
        got = {n: self.pending.pop(n) for n in names if n in self.pending}
        arrays, got = lax.optimization_barrier((arrays, got))
        out = {}
        for n in names:
            if any(other in self.flows for other in NEEDS.get(n, ())):
                continue
            try:
                out[n] = self.flows[n].send(got.get(n))
            except StopIteration as end:
                self.results[n] = end.value
                del self.flows[n]
        steps = {n: v[1] for n, v in out.items()}
        arrays, sent = lax.optimization_barrier((arrays, {n: v[0] for n, v in out.items()}))
        for n, x in sent.items():
            self.pending[n] = move(x, steps[n])
        return arrays

    def finish(self, name):
        while name in self.flows:
            try:
                x, step = self.flows[name].send(self.pending.pop(name, None))
            except StopIteration as end:
                self.results[name] = end.value
                del self.flows[name]
            else:
                self.pending[name] = move(x, step)
        return self.results[name]


def total_of(parts):
    total = parts[0].astype(F32)
    for piece in parts[1:]:
        total = total + piece.astype(F32)
    return total.astype(BF)


def sum_flow(packed, steps):
    parts = [packed]
    for step in steps:
        axis = 1 if step == "section" else 0
        size = parts[0].shape[axis] // 2
        side = lax.axis_index("section") if step == "section" else my_bit(step)

        def half(which, parts=parts, size=size, axis=axis):
            return [lax.dynamic_slice_in_dim(a, which * size, size, axis) for a in parts]

        got = yield total_of(half(1 - side)), step
        parts = half(side) + [got]
    return total_of(parts)


def own_halves_flow(share0, share1, first):
    mine = jnp.where(first, share0, share1)
    got = yield jnp.where(first, share1, share0), "section"
    return jnp.concatenate([jnp.where(first, mine, got), jnp.where(first, got, mine)], axis=1)


def own_total_flow(share0, share1, first):
    got = yield jnp.where(first, share1, share0), "section"
    return total_of([jnp.where(first, share0, share1), got])


def collect_flow(share, steps, ordered):
    for bit in reversed(steps):
        got = yield share, bit
        if bit not in steps[:2] or ordered:
            low = my_bit(bit) == 0
            share = jnp.concatenate([jnp.where(low, share, got), jnp.where(low, got, share)])
        else:
            share = jnp.concatenate([share, got])
    return share


def one_move(x, step):
    return (yield x, step)


def piece_flow(x):
    a = yield x, "section"
    b = yield a, 1
    c = yield jnp.concatenate([a, b]), 0
    return [a, b, c]


def wide_out_kernel(_, a_ref, b_ref, w1_ref, w2_ref):
    w1_ref[...] = a_ref[...].astype(F32)
    w2_ref[...] = b_ref[...].astype(F32).T


def wide_outputs(full, place, groups):
    rows, width = full.shape
    gin = width // groups
    steps = rows // 2 // width
    return pl.pallas_call(
        wide_out_kernel,
        grid_spec=pltpu.PrefetchScalarGridSpec(
            num_scalar_prefetch=1,
            grid=(steps, groups),
            in_specs=[
                pl.BlockSpec((gin, width), lambda q, g, at: ((q ^ at[0]) * groups + g, 0)),
                pl.BlockSpec((gin, width), lambda q, g, at: (((steps + q) ^ at[0]) * groups + g, 0)),
            ],
            out_specs=[
                pl.BlockSpec((gin, width), lambda q, g, at: (g, q)),
                pl.BlockSpec((width, gin), lambda q, g, at: (g * steps + q, 0)),
            ],
        ),
        out_shape=[sds((width, steps * width), F32), sds((groups * steps * width, gin), F32)],
        compiler_params=params(),
        cost_estimate=cost(6),
        name="wide_out",
    )(place, full, full)


def last_out_kernel(at_ref, mid_ref, last_ref, wp_ref, pw_ref, wo_ref):
    place = at_ref[0]
    att = pw_ref.shape[1]
    width = pw_ref.shape[0]
    n = width // 2
    for j in range(2):
        rows = slice(j * n, (j + 1) * n)
        wo_ref[rows, :] = mid_ref[pl.ds(pl.multiple_of((j ^ place) * n, 16), n), :].astype(F32)
        wp_ref[rows, att : 3 * att] = mid_ref[pl.ds(pl.multiple_of(((2 + j) ^ place) * n, 16), n), :].astype(F32)
        wp_ref[rows, 0:att] = last_ref[rows, 0:att].astype(F32)
        wp_ref[rows, 3 * att :] = last_ref[rows, att:].astype(F32)
    pw_ref[...] = last_ref[width : width + att, :].astype(F32).T


def last_outputs(mid, last, place, att):
    width = mid.shape[1]
    vm = pl.BlockSpec(memory_space=pltpu.VMEM)
    return pl.pallas_call(
        last_out_kernel,
        in_specs=[pl.BlockSpec(memory_space=pltpu.SMEM), vm, vm],
        out_specs=[vm] * 3,
        out_shape=[sds((width, 4 * att), F32), sds((width, att), F32), sds((width, width), F32)],
        compiler_params=params(),
        cost_estimate=cost(6),
        name="last_out",
    )(place, mid, last)


FORWARD = {
    "0attn": ("B", "C"),
    "0ffn": ("B", "C"),
}
BACKWARD = {
    "1ffn": ("states",),
    "1attn": ("10",),
    "1in": ("states",),
    "0attn": ("10", "00"),
    "1last": ("11",),
    "0then": ("11", "12"),
    "0mid": ("12",),
    "0conv": ("01", "11", "12"),
    "0last": ("01", "11", "12"),
    "0in": ("02", "11", "12"),
    "0end": ("00", "01", "02", "11", "12"),
}
LAST = (
    ("wide", "01", "02", "11", "12"),
    ("wide", "01", "02"),
    ("01", "02", "mid", "last"),
    ("mid", "last", "rows"),
    ("mid", "last"),
    ("mid", "last"),
    ("mid", "last"),
)


def local(
    tokens, mask_pos, mask_count, mask_vec,
    proj_weight, proj_bias, depth_kernel, point_weight, point_bias, kernel_weight, kernel_bias, out_weight, out_bias,
    norm_gain, norm_shift, inner_weight, inner_bias, second_feed_weight, second_feed_bias, final_gain, final_shift,
    cotangent,
):
    section = lax.axis_index("section")
    first = section == 0
    seq, width = tokens.shape[1:]
    taps = depth_kernel.shape[1]
    att = point_weight.shape[2]
    heads = kernel_bias.shape[1] // taps
    head = att // heads
    groups = inner_weight.shape[1]
    flows = Flows()
    quarter = 2 * my_bit(0) + my_bit(1)
    place = jnp.stack([quarter, section]).astype(jnp.int32)

    own = {
        n: a.reshape(-1, a.shape[-1])
        for n, a in (("wp", proj_weight), ("pw", point_weight), ("w1", inner_weight), ("wo", out_weight),
                     ("w2", second_feed_weight))
    }
    buffers = pack_quarters(own, place, 2 * width)

    def lines_of(a):
        return jnp.pad(a, ((0, 0), (0, width - a.shape[1])))

    vec = vector_pack(proj_bias, point_bias, out_bias, norm_gain, norm_shift, second_feed_bias, final_gain, final_shift,
                      inner_bias)
    span = heads * taps
    little = jnp.concatenate([lines_of(kernel_weight[0].T), depth_kernel[0], lines_of(kernel_bias),
                              vec.reshape(-1, width)])
    flows.add("little", one_move(little, "section"))
    for name, buffer in zip("ABC", buffers):
        flows.add(name, piece_flow(buffer))

    def mine(a):
        return lax.dynamic_index_in_dim(a, section, 0, keepdims=False)

    flows.step(("little", "A"), ())
    pos, count = mine(mask_pos), mine(mask_count)
    hits = (pos[:, None] == jnp.arange(seq, dtype=jnp.int32)[None, :]) & (
        jnp.arange(pos.shape[0], dtype=jnp.int32) < count
    )[:, None]
    masked = jnp.any(hits, axis=0)[:, None]
    hidden = jnp.where(masked, mask_vec[None, :], mine(tokens))
    mask = masked.astype(F32)
    mask_rows = jnp.broadcast_to(masked.reshape(1, seq), (SUB, seq)).astype(BF)
    ex, ext = spread_matrices(taps, heads, head)
    other = flows.finish("little")
    flows.step(("A", "B"), ())
    flows.step(("A", "B", "C"), ())
    pieces = {"A": flows.finish("A")}

    def small(rows):
        return prepare(rows[span + taps + 1 :].reshape(1, -1), rows[span : span + taps], rows[:span, :att],
                       rows[span + taps, :span])

    p = [small(jnp.where(first, little, other)), small(jnp.where(first, other, little))]
    for n in range(2):
        p[n].update(l=n, own=own, pieces=pieces, place=place)

    def forward_slot(layer):
        def slot(name, x):
            x = flows.step(FORWARD.get(str(layer) + name, ()), x)
            if layer == 0 and name == "ffn":
                pieces.update(B=flows.finish("B"), C=flows.finish("C"))
            return x

        return slot

    keeps = []
    outs = []
    for n in range(2):
        hidden, keep = layer_forward(hidden, p[n], ex, head, forward_slot(n))
        keeps.append(keep)
        outs.append(hidden)

    def other_row(a, b):
        return one_move(jnp.where(first, b, a), "section")

    def both_rows(a, b, got):
        kept = jnp.where(first, a, b)
        return jnp.stack([jnp.where(first, kept, got), jnp.where(first, got, kept)])

    flows.add("states", other_row(*outs))
    bits = row_bits()
    turned = bits[:1] + bits[2:] + bits[1:2]
    order = (None, turned[:1] + ["section"] + turned[1:], bits)
    lines = 128

    def backward(layer, dy, mask, mask_rows, before):
        def slot(name, x):
            key = str(layer) + name
            x = flows.step(BACKWARD.get(key, ()), x)
            if before is not None:
                x = before(name, x)
                if name == "attn":
                    x = flows.step(BACKWARD["0then"], x)
            return x

        def send(n, packed):
            flow = one_move(packed, "scatter") if n == 0 else sum_flow(packed, order[n])
            flows.add(str(layer) + str(n), flow)

        return layer_backward(dy, keeps[layer], mask, mask_rows, p[layer], ex, ext, head, lines, slot, send, layer == 1)

    d1, rest = backward(1, mine(cotangent), jnp.zeros_like(mask), jnp.zeros_like(mask_rows), None)
    d0, _ = backward(0, d1, mask, mask_rows, rest)
    states = both_rows(*outs, flows.finish("states"))

    start, n = 0, width + att + lines
    for bit in bits:
        n //= 2
        start = start + my_bit(bit) * n
    line = start + jnp.arange(n)
    marked = (line == width + att + mask_row(taps))[:, None]

    def wide_flow():
        own = yield from own_total_flow(flows.finish("00"), flows.finish("10"), first)
        return (yield own, "gather")

    def mid_flow():
        own = yield from own_halves_flow(flows.finish("01"), flows.finish("11"), first)
        return (yield from collect_flow(own, turned, False))

    def last_flow():
        a, b = flows.finish("02"), flows.finish("12")
        own = yield from own_total_flow(a, jnp.where(marked, a, b), first)
        return (yield from collect_flow(own, bits, True))

    flows.add("wide", wide_flow())
    flows.add("mid", mid_flow())
    flows.add("last", last_flow())
    flows.add("rows", other_row(d0, d1))
    for names in LAST:
        flows.step(names, ())
    in_grads = both_rows(d0, d1, flows.finish("rows"))
    wide, mid, last = [flows.finish(n) for n in ("wide", "mid", "last")]
    w1, w2 = wide_outputs(wide, jnp.zeros((1,), jnp.int32), groups)
    mid_place = (2 * my_bit(0) + my_bit(turned[1])).reshape(1).astype(jnp.int32)
    wp, pw, wo = last_outputs(mid, last, mid_place, att)
    grads, mask_grad = small_parts(last[width + att :].astype(F32), att, taps, heads, inner_bias.shape[1])
    grads.update(wp=wp, pw=pw, wo=wo, w1=w1.reshape(inner_weight.shape[1:]),
                 w2=w2.reshape(second_feed_weight.shape[1:]))
    names = ("wp", "bp", "dk", "pw", "pb", "kw", "kb", "wo", "bo", "g1", "s1", "w1", "b1", "w2", "b2", "g2", "s2")
    return (states[None], in_grads[None], mask_grad) + tuple(grads[n][None] for n in names)


def solution(mesh):
    def part(dims, *lead):
        return P(*(lead + (None,) * (dims - len(lead))))

    weights = (3, 2, 3, 3, 2, 3, 2, 3, 2, 2, 2, 4, 2, 4, 2, 2, 2)
    return jax.shard_map(
        local,
        mesh=mesh,
        in_specs=(part(3, "dp"), part(2, "dp"), part(1, "dp"), P())
        + tuple(part(n, "section") for n in weights)
        + (part(3, "dp"),),
        out_specs=(part(4, "section", "dp"), part(4, "section", "dp"), P())
        + tuple(part(n, "section") for n in weights),
        check_vma=False,
    )
```

time: 1280 us -> 657 us (0.51)
  waiting for transfers between devices: 709 us -> 140 us
  Pallas kernels: 255 us -> 346 us
  matrix products: 55.8 us -> 0 us
  local copies, waits for them, and re-layouts: 80 us -> 33.9 us
  blocking collectives: 41.7 us -> 0 us
  other arithmetic: 87.3 us -> 69.5 us
  starting transfers between devices: 24.6 us -> 41.1 us
    reduce_scatter x12 -> x2, waiting for transfers between devices: 551 us -> 0.01 us  [move(): return lax.psum_scatter(x, 'dp', scatter_dimension=0, tiled=True)]
    all_gather x4 -> x1, waiting for transfers between devices: 113 us -> 0.01 us  [move(): return lax.all_gather(x, 'dp', axis=0, tiled=True)]
    ppermute x5 -> x30, waiting for transfers between devices: 0.01 us -> 98.7 us  [across(): lax.ppermute(x, 'dp', [(i, i ^ 1 << bit) for i in range(lax.axis_size('dp...]
    pallas_call x10 -> x19, Pallas kernels: 176 us -> 268 us  [the longest x12 213 us: call(): pl.pallas_call(body, grid=grid, in_specs=[SMEM] + [HBM] * len(operands) +...]
    dot_general x16 -> x0, matrix products: 55.8 us -> none  [rows_product(): lax.dot_general(left, right, (((0,), (0,)), ((), ())), preferred_element_...]
    all_gather x2 -> x0, blocking collectives: 41.7 us -> none  [local(): full = lax.all_gather(tuple(own_sums), 'dp', axis=0, tiled=True)]
    ppermute x5 -> x30, starting transfers between devices: 1.02 us -> 28.1 us  [across(): lax.ppermute(x, 'dp', [(i, i ^ 1 << bit) for i in range(lax.axis_size('dp...]
    reshape x48 -> x7, local copies, waits for them, and re-layouts: 22.3 us -> 0.15 us  [the longest x2 0.06 us: prepare(): kwt.reshape(heads, taps, att).transpose(1, 0, 2)]
  transfers between devices with their start and end apart: 36 -> 44, of which waited for: 19 -> 20; matrix products, arithmetic and copies ran while one was open for 15% -> 12% of each run, Pallas kernels for 4% -> 33%
where the time goes in v2:
time: 657 us; the launch traced here: 646 us
  Pallas kernels  346 us (53%)
  waiting for transfers between devices  140 us (21%)
  other arithmetic  69.5 us (11%)
  starting transfers between devices  41.1 us (6%)
  local copies, waits for them, and re-layouts  33.9 us (5%)
  between operations  15.1 us (2%)
    pallas_call x12, Pallas kernels, call(): pl.pallas_call(body, grid=grid, in_specs=[SMEM] + [HBM] * len(operands) +...  213 us
    ppermute x30, waiting for transfers between devices, across(): lax.ppermute(x, 'dp', [(i, i ^ 1 << bit) for i in range(lax.axis_size('dp...  98.7 us
    ppermute x11, waiting for transfers between devices, swap(): return lax.ppermute(x, 'section', [(0, 1), (1, 0)])  41.1 us
    pallas_call x2, Pallas kernels, run_attn_back(): pl.pallas_call(partial(attn_back_kernel, head=head, qb=256), grid=(pairs,...  40.6 us
    pallas_call x2, Pallas kernels, run_attn(): pl.pallas_call(partial(attn_kernel, head=head, qb=256), grid=(pairs,), in...  37.7 us
    ppermute x30, starting transfers between devices, across(): lax.ppermute(x, 'dp', [(i, i ^ 1 << bit) for i in range(lax.axis_size('dp...  28.1 us
    pallas_call x2, Pallas kernels, run_wide_grads(): pl.pallas_call(wide_grad_kernel, grid=(groups, steps), in_specs=[narrow,...  23.7 us
    convert_element_type x16, other arithmetic, total_of(): return total.astype(BF)  20.5 us
  transfers between devices with their start and end apart: 44, of which 20 were waited for; matrix products, arithmetic and copies ran while one was open for 12% of the time, Pallas kernels for 33%

profile of v2, /device:TPU:0, one launch (start us, length us, event | category | flops | bytes accessed | tf_op | source)
XLA Modules:
  0.0 645.7 jit_solution(1292587213371171728)
XLA Ops:
  22.2 16.8 %collective-permute-done.refs_2_.refs_1_ = bf16[240,1536]{1,0:T(8,128)(2,1)} collective-permute-done((bf16[240,1536]{1,0:T(8,128)(2,1)}, bf16[240,1536]{1,0:T(8,128)(2,1)}, u32[]{:S(2)}, u32[]{:S(2)}) %collective-permute-start) | collective-permute-done | bytes 737312 | tf_op jit(solution)/shard_map/ppermute | solution.py:888
  47.0 11.1 %collective-permute-done.1.refs_3_.refs_2_ = bf16[240,1536]{1,0:T(8,128)(2,1)} collective-permute-done((bf16[240,1536]{1,0:T(8,128)(2,1)}, bf16[240,1536]{1,0:T(8,128)(2,1)}, u32[]{:S(2)}, u32[]{:S(2)}) %collective-permute-start.1) | collective-permute-done | bytes 737312 | tf_op jit(solution)/shard_map/ppermute | solution.py:892
  71.8 13.8 %proj_fwd.2 = (bf16[1024,384]{1,0:T(8,128)(2,1)}, bf16[1024,384]{1,0:T(8,128)(2,1)}, bf16[1024,384]{1,0:T(8,128)(2,1)}, bf16[1024,384]{1,0:T(8,128)(2,1)}, bf16[...) custom-call(s32[2]{0:T(128)} %pad_add_fusion.place_ref, ...), custom_call_target="tpu_custom_call" | custom-call | flops 14300000256 | tf_op jit(solution)/shard_map/proj_fwd/pallas_call | solution.py:136
  94.3 18.9 %attn_fwd.2 = (f32[384,1024]{1,0:T(8,128)}, f32[3,8,1024]{2,1,0:T(8,128)}) custom-call(bf16[1024,384]{1,0:T(8,128)(2,1)} %get-tuple-element.285.k_ref, bf16[384,1024]{1,0:T(8,128)(2,1)} %get-tuple-element.286.qt_ref, bf16[384,1024]{1,0:T(8,128)(2,1)} %get-tuple-element.287.vt_ref), custom_call_target="tpu_custom_call" | custom-call | flops 20899999744 | tf_op jit(solution)/shard_map/attn_fwd/pallas_call | solution.py:271
  120.8 24.8 %ffn_fwd.2 = (bf16[1024,768]{1,0:T(8,128)(2,1)}, bf16[1024,768]{1,0:T(8,128)(2,1)}, f32[1024,1]{1,0:T(8,128)}, bf16[1024,768]{1,0:T(8,128)(2,1)}, bf16[1024,3072...) custom-call(s32[2]{0:T(128)} %pad_add_fusion.place_ref, ...), custom_call_target="tpu_custom_call" | custom-call | flops 24199999488 | tf_op jit(solution)/shard_map/ffn_fwd/pallas_call | solution.py:136
  145.7 13.8 %proj_fwd.3 = (bf16[1024,384]{1,0:T(8,128)(2,1)}, bf16[1024,384]{1,0:T(8,128)(2,1)}, bf16[1024,384]{1,0:T(8,128)(2,1)}, bf16[1024,384]{1,0:T(8,128)(2,1)}, bf16[...) custom-call(s32[2]{0:T(128)} %pad_add_fusion.place_ref, ...), custom_call_target="tpu_custom_call" | custom-call | flops 14300000256 | tf_op jit(solution)/shard_map/proj_fwd/pallas_call | solution.py:136
  159.4 18.9 %attn_fwd.3 = (f32[384,1024]{1,0:T(8,128)}, f32[3,8,1024]{2,1,0:T(8,128)}) custom-call(bf16[1024,384]{1,0:T(8,128)(2,1)} %get-tuple-element.302.k_ref, bf16[384,1024]{1,0:T(8,128)(2,1)} %get-tuple-element.303.qt_ref, bf16[384,1024]{1,0:T(8,128)(2,1)} %get-tuple-element.304.vt_ref), custom_call_target="tpu_custom_call" | custom-call | flops 20899999744 | tf_op jit(solution)/shard_map/attn_fwd/pallas_call | solution.py:271
  178.3 24.7 %ffn_fwd.3 = (bf16[1024,768]{1,0:T(8,128)(2,1)}, bf16[1024,768]{1,0:T(8,128)(2,1)}, f32[1024,1]{1,0:T(8,128)}, bf16[1024,768]{1,0:T(8,128)(2,1)}, bf16[1024,3072...) custom-call(s32[2]{0:T(128)} %pad_add_fusion.place_ref, ...), custom_call_target="tpu_custom_call" | custom-call | flops 24199999488 | tf_op jit(solution)/shard_map/ffn_fwd/pallas_call | solution.py:136
  204.6 20.3 %ffn_bwd.2 = (bf16[1024,768]{1,0:T(8,128)(2,1)}, bf16[1024,3072]{1,0:T(8,128)(2,1)}, bf16[1024,768]{1,0:T(8,128)(2,1)}, bf16[384,1024]{1,0:T(8,128)(2,1)}, bf16[...) custom-call(s32[2]{0:T(128)} %pad_add_fusion.place_ref, ...), custom_call_target="tpu_custom_call" | custom-call | flops 19800000512 | tf_op jit(solution)/shard_map/ffn_bwd/pallas_call | solution.py:136
  224.9 11.8 %ffn_wgrad.2 = bf16[2,1536,768]{2,1,0:T(8,128)(2,1)} custom-call(bf16[1024,768]{1,0:T(8,128)(2,1)} %get-tuple-element.324.nl_ref, bf16[1024,3072]{1,0:T(8,128)(2,1)} %get-tuple-element.325.di_ref, bf16[1024,768]{1,0:T(8,128)(2,1)} %get-tuple-element.326.ds_ref, bf16[1024,3072]{1,0:T(8,128)(2,1)} %get-tuple-element.327.act_ref), custom_call_target="tpu_custom_call" | custom-call | flops 6600000000 | tf_op jit(solution)/shard_map/ffn_wgrad/pallas_call | solution.py:671
  236.8 20.3 %attn_bwd.2 = (bf16[1024,384]{1,0:T(8,128)(2,1)}, bf16[1024,384]{1,0:T(8,128)(2,1)}, bf16[1024,384]{1,0:T(8,128)(2,1)}, f32[1,384]{1,0:T(1,128)}) custom-call(bf16[1024,384]{1,0:T(8,128)(2,1)} %get-tuple-element.302.k_ref, bf16[1024,384]{1,0:T(8,128)(2,1)} %get-tuple-element.316.v_ref, bf16[1024,384]{1,0:T(8,128)(2,1)} %get-tuple-element.317.q2_ref.refs_8_, ...), custom_call_target="tpu_custom_call" | custom-call | flops 22000001024 | tf_op jit(solution)/shard_map/attn_bwd/pallas_call | solution.py:621
  257.3 28.0 %conv_bwd.2 = (bf16[1024,72]{1,0:T(8,128)(2,1)}, bf16[1024,384]{1,0:T(8,128)(2,1)}, bf16[1024,384]{1,0:T(8,128)(2,1)}, bf16[1024,384]{1,0:T(8,128)(2,1)}, bf16[1...) custom-call(s32[2]{0:T(128)} %pad_add_fusion.place_ref, ...), custom_call_target="tpu_custom_call" | custom-call | flops 29699999744 | tf_op jit(solution)/shard_map/conv_bwd/pallas_call | solution.py:136
  294.6 8.9 %in_bwd.2.refs_9_ = bf16[1024,768]{1,0:T(8,128)(2,1)} custom-call(s32[2]{0:T(128)} %pad_add_fusion.place_ref, bf16[768,1536]{1,0:T(8,128)(2,1)} %bitcast.110, bf16[240,1536]{1,0:T(8,128)(2,1)} %collective-permute-done.refs_2_.refs_1_, bf16[240,1536]{1,0:T(8,128)(2,1)} %collective-permute-done.1.refs_3_.refs_2_, ...), custom_call_target="tpu_custom_call" | custom-call | flops 8800000000 | tf_op jit(solution)/shard_map/in_bwd/pallas_call | solution.py:136
  303.5 20.3 %ffn_bwd.3 = (bf16[1024,768]{1,0:T(8,128)(2,1)}, bf16[1024,3072]{1,0:T(8,128)(2,1)}, bf16[1024,768]{1,0:T(8,128)(2,1)}, bf16[384,1024]{1,0:T(8,128)(2,1)}, bf16[...) custom-call(s32[2]{0:T(128)} %pad_add_fusion.place_ref, ...), custom_call_target="tpu_custom_call" | custom-call | flops 19800000512 | tf_op jit(solution)/shard_map/ffn_bwd/pallas_call | solution.py:136
  325.3 11.8 %ffn_wgrad.3 = bf16[2,1536,768]{2,1,0:T(8,128)(2,1)} custom-call(bf16[1024,768]{1,0:T(8,128)(2,1)} %get-tuple-element.363.nl_ref, bf16[1024,3072]{1,0:T(8,128)(2,1)} %get-tuple-element.364.di_ref, bf16[1024,768]{1,0:T(8,128)(2,1)} %get-tuple-element.365.ds_ref, bf16[1024,3072]{1,0:T(8,128)(2,1)} %get-tuple-element.366.act_ref), custom_call_target="tpu_custom_call" | custom-call | flops 6600000000 | tf_op jit(solution)/shard_map/ffn_wgrad/pallas_call | solution.py:671
  337.2 7.2 %mid_wgrad.2 = bf16[1536,768]{1,0:T(8,128)(2,1)} custom-call(bf16[1024,768]{1,0:T(8,128)(2,1)} %get-tuple-element.375.ctx_ref, bf16[1024,768]{1,0:T(8,128)(2,1)} %get-tuple-element.335.refs_10_.dz_ref, bf16[1024,768]{1,0:T(8,128)(2,1)} %get-tuple-element.298.refs_5_.refs_12_.refs_9_.h_ref.refs_4_, ...), custom_call_target="tpu_custom_call" | custom-call | flops 5500000256 | tf_op jit(solution)/shard_map/mid_wgrad/pallas_call | solution.py:695
  347.3 10.8 %last_wgrad.2 = (bf16[1152,768]{1,0:T(8,128)(2,1)}, f32[72,384]{1,0:T(8,128)}, f32[8,768]{1,0:T(8,128)}) custom-call(s32[2]{0:T(128)} %pad_add_fusion.place_ref, bf16[768,1536]{1,0:T(8,128)(2,1)} %bitcast.111, bf16[240,1536]{1,0:T(8,128)(2,1)} %collective-permute-done.refs_2_.refs_1_, bf16[240,1536]{1,0:T(8,128)(2,1)} %collective-permute-done.1.refs_3_.refs_2_, ...), custom_call_target="tpu_custom_call" | custom-call | flops 9900000256 | tf_op jit(solution)/shard_map/last_wgrad/pallas_call | solution.py:136
  364.1 20.3 %attn_bwd.3 = (bf16[1024,384]{1,0:T(8,128)(2,1)}, bf16[1024,384]{1,0:T(8,128)(2,1)}, bf16[1024,384]{1,0:T(8,128)(2,1)}, f32[1,384]{1,0:T(1,128)}) custom-call(bf16[1024,384]{1,0:T(8,128)(2,1)} %get-tuple-element.285.k_ref, bf16[1024,384]{1,0:T(8,128)(2,1)} %get-tuple-element.354.v_ref, bf16[1024,384]{1,0:T(8,128)(2,1)} %get-tuple-element.355.q2_ref.refs_8_, ...), custom_call_target="tpu_custom_call" | custom-call | flops 22000001024 | tf_op jit(solution)/shard_map/attn_bwd/pallas_call | solution.py:621
  385.8 7.2 %mid_wgrad.3 = bf16[1536,768]{1,0:T(8,128)(2,1)} custom-call(bf16[1024,768]{1,0:T(8,128)(2,1)} %get-tuple-element.414.ctx_ref, bf16[1024,768]{1,0:T(8,128)(2,1)} %get-tuple-element.415.dz_ref.refs_10_, bf16[1024,768]{1,0:T(8,128)(2,1)} %bitcast_select_fusion.refs_5_.refs_12_.h_ref.refs_9_.refs_4_, ...), custom_call_target="tpu_custom_call" | custom-call | flops 5500000256 | tf_op jit(solution)/shard_map/mid_wgrad/pallas_call | solution.py:695
  394.4 11.9 %collective-permute-done.14 = bf16[320,768]{1,0:T(8,128)(2,1)S(1)} collective-permute-done((bf16[320,768]{1,0:T(8,128)(2,1)S(1)}, bf16[320,768]{1,0:T(8,128)(2,1)S(1)}, u32[]{:S(2)}, u32[]{:S(2)}) %collective-permute-start.14) | collective-permute-done | bytes 491552 | tf_op jit(solution)/shard_map/ppermute | solution.py:892
  410.7 28.4 %conv_bwd.3 = (bf16[1024,72]{1,0:T(8,128)(2,1)}, bf16[1024,384]{1,0:T(8,128)(2,1)}, bf16[1024,384]{1,0:T(8,128)(2,1)}, bf16[1024,384]{1,0:T(8,128)(2,1)}, bf16[1...) custom-call(s32[2]{0:T(128)} %pad_add_fusion.place_ref, ...), custom_call_target="tpu_custom_call" | custom-call | flops 29699999744 | tf_op jit(solution)/shard_map/conv_bwd/pallas_call | solution.py:136
  451.8 10.8 %last_wgrad.3 = (bf16[1152,768]{1,0:T(8,128)(2,1)}, f32[72,384]{1,0:T(8,128)}, f32[8,768]{1,0:T(8,128)}) custom-call(s32[2]{0:T(128)} %pad_add_fusion.place_ref, bf16[768,1536]{1,0:T(8,128)(2,1)} %bitcast.112, bf16[240,1536]{1,0:T(8,128)(2,1)} %collective-permute-done.refs_2_.refs_1_, bf16[240,1536]{1,0:T(8,128)(2,1)} %collective-permute-done.1.refs_3_.refs_2_, ...), custom_call_target="tpu_custom_call" | custom-call | flops 9900000256 | tf_op jit(solution)/shard_map/last_wgrad/pallas_call | solution.py:136
  472.5 8.7 %in_bwd.3 = bf16[1024,768]{1,0:T(8,128)(2,1)} custom-call(s32[2]{0:T(128)} %pad_add_fusion.place_ref, bf16[768,1536]{1,0:T(8,128)(2,1)} %bitcast.113, bf16[240,1536]{1,0:T(8,128)(2,1)} %collective-permute-done.refs_2_.refs_1_, bf16[240,1536]{1,0:T(8,128)(2,1)} %collective-permute-done.1.refs_3_.refs_2_, ...), custom_call_target="tpu_custom_call" | custom-call | flops 8800000000 | tf_op jit(solution)/shard_map/in_bwd/pallas_call | solution.py:136
  491.8 6.8 %collective-permute-done.23 = bf16[384,384]{1,0:T(8,128)(2,1)S(1)} collective-permute-done((bf16[384,384]{1,0:T(8,128)(2,1)S(1)}, bf16[384,384]{1,0:T(8,128)(2,1)S(1)}, u32[]{:S(2)}, u32[]{:S(2)}) %collective-permute-start.23) | collective-permute-done | bytes 294944 | tf_op jit(solution)/shard_map/ppermute | solution.py:892
  540.3 10.8 %collective-permute-done.33 = bf16[80,768]{1,0:T(8,128)(2,1)S(1)} collective-permute-done((bf16[80,768]{1,0:T(8,128)(2,1)S(1)}, bf16[80,768]{1,0:T(8,128)(2,1)S(1)}, u32[]{:S(2)}, u32[]{:S(2)}) %collective-permute-start.33) | collective-permute-done | bytes 122912 | tf_op jit(solution)/shard_map/ppermute | solution.py:892
  552.8 14.4 %collective-permute-done.35 = bf16[160,768]{1,0:T(8,128)(2,1)S(1)} collective-permute-done((bf16[160,768]{1,0:T(8,128)(2,1)S(1)}, bf16[160,768]{1,0:T(8,128)(2,1)S(1)}, u32[]{:S(2)}, u32[]{:S(2)}) %collective-permute-start.35) | collective-permute-done | bytes 245792 | tf_op jit(solution)/shard_map/ppermute | solution.py:892
  567.2 5.7 collective-permute-done.36
  576.2 10.4 %collective-permute-done.37 = bf16[320,768]{1,0:T(8,128)(2,1)S(1)} collective-permute-done((bf16[320,768]{1,0:T(8,128)(2,1)S(1)}, bf16[320,768]{1,0:T(8,128)(2,1)S(1)}, u32[]{:S(2)}, u32[]{:S(2)}) %collective-permute-start.37) | collective-permute-done | bytes 491552 | tf_op jit(solution)/shard_map/ppermute | solution.py:892
  586.6 9.1 %collective-permute-done.38 = bf16[384,768]{1,0:T(8,128)(2,1)} collective-permute-done((bf16[384,768]{1,0:T(8,128)(2,1)S(1)}, bf16[384,768]{1,0:T(8,128)(2,1)}, u32[]{:S(2)}, u32[]{:S(2)}) %collective-permute-start.38) | collective-permute-done | bytes 589856 | tf_op jit(solution)/shard_map/ppermute | solution.py:892
  602.4 9.1 %collective-permute-done.32 = bf16[1024,768]{1,0:T(8,128)(2,1)} collective-permute-done((bf16[1024,768]{1,0:T(8,128)(2,1)}, bf16[1024,768]{1,0:T(8,128)(2,1)}, u32[]{:S(2)}, u32[]{:S(2)}) %collective-permute-start.32) | collective-permute-done | bytes 1572896 | tf_op jit(solution)/shard_map/ppermute | solution.py:888
  626.1 5.9 last_out.1
  632.0 6.7 %wide_out.1 = (f32[768,1536]{1,0:T(8,128)}, f32[3072,384]{1,0:T(8,128)}) custom-call(s32[1]{0:T(128)} %constant.674.clone.1._, bf16[3072,768]{1,0:T(8,128)(2,1)} %all-gather.2.cloned.1.call-done.a_ref.b_ref, bf16[3072,768]{1,0:T(8,128)(2,1)} %all-gather.2.cloned.1.call-done.a_ref.b_ref), custom_call_target="tpu_custom_call" | custom-call | flops 6600000000 | tf_op jit(solution)/shard_map/wide_out/pallas_call | solution.py:1018
  (311 shorter events, 182.0 us)
Async XLA Ops:
  7.2 329.9 %reduce-scatter.3.cloned.1.call-start = ((), (), s32[]{:S(2)}) async-start(), calls=%async_computation.2 | async-start | bytes 5013504 | tf_op jit(solution)/shard_map/reduce_scatter | solution.py:897
  19.2 19.8 %collective-permute-start = (bf16[240,1536]{1,0:T(8,128)(2,1)}, bf16[240,1536]{1,0:T(8,128)(2,1)}, u32[]{:S(2)}, u32[]{:S(2)}) collective-permute-start(bf16[240,1536]{1,0:T(8,128)(2,1)} %get-tuple-element.266), channel_id=1, source_target_pairs={{0,16},{16,0},{1,17},{17,1},{2,18},{18,2},{3,19},{19,3},{4,20},{20... | collective-permute-start | bytes 2211848 | tf_op jit(solution)/shard_map/ppermute | solution.py:888
  39.0 22.5 %collective-permute-start.2 = (bf16[288,1536]{1,0:T(8,128)(2,1)}, bf16[288,1536]{1,0:T(8,128)(2,1)}, u32[]{:S(2)}, u32[]{:S(2)}) collective-permute-start(bf16[288,1536]{1,0:T(8,128)(2,1)} %get-tuple-element.269), channel_id=1, source_target_pairs={{0,16},{16,0},{1,17},{17,1},{2,18},{18,2},{3,19},{19,3},{4,20},{20... | collective-permute-start | bytes 2654216 | tf_op jit(solution)/shard_map/ppermute | solution.py:888
  40.7 17.4 %collective-permute-start.1 = (bf16[240,1536]{1,0:T(8,128)(2,1)}, bf16[240,1536]{1,0:T(8,128)(2,1)}, u32[]{:S(2)}, u32[]{:S(2)}) collective-permute-start(bf16[240,1536]{1,0:T(8,128)(2,1)} %collective-permute-done.refs_2_.refs_1_), channel_id=1, source_target_pairs={{0,2},{1,3},{2,0},{3,1},{4,6},{5,7},{6,4},{7,5},{8,10},{9,11},{10,... | collective-permute-start | bytes 2211848 | tf_op jit(solution)/shard_map/ppermute | solution.py:892
  42.2 23.6 %collective-permute-start.4 = (bf16[76,768]{1,0:T(8,128)(2,1)S(1)}, bf16[76,768]{1,0:T(8,128)(2,1)S(1)}, u32[]{:S(2)}, u32[]{:S(2)}) collective-permute-start(bf16[76,768]{1,0:T(8,128)(2,1)S(1)} %fusion.12), channel_id=1, source_target_pairs={{0,16},{16,0},{1,17},{17,1},{2,18},{18,2},{3,19},{19,3},{4,20},{20... | collective-permute-start | bytes 350216 | tf_op jit(solution)/shard_map/ppermute | solution.py:888
  68.8 22.3 %collective-permute-start.5 = (bf16[288,1536]{1,0:T(8,128)(2,1)}, bf16[288,1536]{1,0:T(8,128)(2,1)S(1)}, u32[]{:S(2)}, u32[]{:S(2)}) collective-permute-start(bf16[288,1536]{1,0:T(8,128)(2,1)} %collective-permute-done.2.refs_2_), channel_id=1, source_target_pairs={{0,2},{1,3},{2,0},{3,1},{4,6},{5,7},{6,4},{7,5},{8,10},{9,11},{10,... | collective-permute-start | bytes 2654216 | tf_op jit(solution)/shard_map/ppermute | solution.py:892
  70.3 15.7 %collective-permute-start.6 = (bf16[192,1536]{1,0:T(8,128)(2,1)}, bf16[192,1536]{1,0:T(8,128)(2,1)S(1)}, u32[]{:S(2)}, u32[]{:S(2)}) collective-permute-start(bf16[192,1536]{1,0:T(8,128)(2,1)} %get-tuple-element.279), channel_id=1, source_target_pairs={{0,16},{16,0},{1,17},{17,1},{2,18},{18,2},{3,19},{19,3},{4,20},{20... | collective-permute-start | bytes 1769480 | tf_op jit(solution)/shard_map/ppermute | solution.py:888
  92.7 20.5 %collective-permute-start.7 = (bf16[576,1536]{1,0:T(8,128)(2,1)S(1)}, bf16[576,1536]{1,0:T(8,128)(2,1)S(1)}, u32[]{:S(2)}, u32[]{:S(2)}) collective-permute-start(bf16[576,1536]{1,0:T(8,128)(2,1)S(1)} %pad_maximum_fusion.2), channel_id=1, source_target_pairs={{0,1},{1,0},{2,3},{3,2},{4,5},{5,4},{6,7},{7,6},{8,9},{9,8},{10,11... | collective-permute-start | bytes 5308424 | tf_op jit(solution)/shard_map/ppermute | solution.py:892
  92.8 20.4 %collective-permute-start.8 = (bf16[192,1536]{1,0:T(8,128)(2,1)S(1)}, bf16[192,1536]{1,0:T(8,128)(2,1)S(1)}, u32[]{:S(2)}, u32[]{:S(2)}) collective-permute-start(bf16[192,1536]{1,0:T(8,128)(2,1)S(1)} %collective-permute-done.6.refs_6_), channel_id=1, source_target_pairs={{0,2},{1,3},{2,0},{3,1},{4,6},{5,7},{6,4},{7,5},{8,10},{9,11},{10,... | collective-permute-start | bytes 1769480 | tf_op jit(solution)/shard_map/ppermute | solution.py:892
  236.8 249.9 %reduce-scatter.5.cloned.1.call-start = ((), (), s32[]{:S(2)}) async-start(), calls=%async_computation.3 | async-start | bytes 5013504 | tf_op jit(solution)/shard_map/reduce_scatter | solution.py:897
  257.1 36.5 %collective-permute-start.10 = (bf16[1024,768]{1,0:T(8,128)(2,1)S(1)}, bf16[1024,768]{1,0:T(8,128)(2,1)S(1)}, u32[]{:S(2)}, u32[]{:S(2)}) collective-permute-start(bf16[1024,768]{1,0:T(8,128)(2,1)S(1)} %broadcast_select_fusion.2), channel_id=1, source_target_pairs={{0,16},{16,0},{1,17},{17,1},{2,18},{18,2},{3,19},{19,3},{4,20},{20... | collective-permute-start | bytes 4718600 | tf_op jit(solution)/shard_map/ppermute | solution.py:888
  346.7 14.8 %collective-permute-start.11 = (bf16[768,768]{1,0:T(8,128)(2,1)}, bf16[768,768]{1,0:T(8,128)(2,1)S(1)}, u32[]{:S(2)}, u32[]{:S(2)}) collective-permute-start(bf16[768,768]{1,0:T(8,128)(2,1)} %constant_dynamic-slice_fusion.3), channel_id=1, source_target_pairs={{0,1},{1,0},{2,3},{3,2},{4,5},{5,4},{6,7},{7,6},{8,9},{9,8},{10,11... | collective-permute-start | bytes 3538952 | tf_op jit(solution)/shard_map/ppermute | solution.py:892
  359.8 272.2 %all-gather.2.cloned.1.call-start = ((), (), s32[]{:S(2)}) async-start(), calls=%async_computation.4 | async-start | bytes 5013504 | tf_op jit(solution)/shard_map/all_gather | solution.py:899
  363.1 22.0 %collective-permute-start.12 = (bf16[640,768]{1,0:T(8,128)(2,1)S(1)}, bf16[640,768]{1,0:T(8,128)(2,1)S(1)}, u32[]{:S(2)}, u32[]{:S(2)}) collective-permute-start(bf16[640,768]{1,0:T(8,128)(2,1)S(1)} %constant_dynamic-slice_fusion.2), channel_id=1, source_target_pairs={{0,1},{1,0},{2,3},{3,2},{4,5},{5,4},{6,7},{7,6},{8,9},{9,8},{10,11... | collective-permute-start | bytes 2949128 | tf_op jit(solution)/shard_map/ppermute | solution.py:892
  363.7 30.8 %collective-permute-start.13 = (bf16[768,384]{1,0:T(8,128)(2,1)S(1)}, bf16[768,384]{1,0:T(8,128)(2,1)S(1)}, u32[]{:S(2)}, u32[]{:S(2)}) collective-permute-start(bf16[768,384]{1,0:T(8,128)(2,1)S(1)} %add_convert_fusion.1), channel_id=1, source_target_pairs={{0,16},{16,0},{1,17},{17,1},{2,18},{18,2},{3,19},{19,3},{4,20},{20... | collective-permute-start | bytes 1769480 | tf_op jit(solution)/shard_map/ppermute | solution.py:888
  385.2 21.1 %collective-permute-start.14 = (bf16[320,768]{1,0:T(8,128)(2,1)S(1)}, bf16[320,768]{1,0:T(8,128)(2,1)S(1)}, u32[]{:S(2)}, u32[]{:S(2)}) collective-permute-start(bf16[320,768]{1,0:T(8,128)(2,1)S(1)} %add_convert_fusion.3), channel_id=1, source_target_pairs={{0,2},{1,3},{2,0},{3,1},{4,6},{5,7},{6,4},{7,5},{8,10},{9,11},{10,... | collective-permute-start | bytes 1474568 | tf_op jit(solution)/shard_map/ppermute | solution.py:892
  408.6 33.8 %collective-permute-start.15 = (bf16[768,768]{1,0:T(8,128)(2,1)S(1)}, bf16[768,768]{1,0:T(8,128)(2,1)S(1)}, u32[]{:S(2)}, u32[]{:S(2)}) collective-permute-start(bf16[768,768]{1,0:T(8,128)(2,1)S(1)} %constant_dynamic-slice_fusion.1), channel_id=1, source_target_pairs={{0,1},{1,0},{2,3},{3,2},{4,5},{5,4},{6,7},{7,6},{8,9},{9,8},{10,11... | collective-permute-start | bytes 3538952 | tf_op jit(solution)/shard_map/ppermute | solution.py:892
  408.6 33.7 %collective-permute-start.16 = (bf16[384,384]{1,0:T(8,128)(2,1)S(1)}, bf16[384,384]{1,0:T(8,128)(2,1)S(1)}, u32[]{:S(2)}, u32[]{:S(2)}) collective-permute-start(bf16[384,384]{1,0:T(8,128)(2,1)S(1)} %add_convert_fusion.6), channel_id=1, source_target_pairs={{0,4},{1,5},{2,6},{3,7},{4,0},{5,1},{6,2},{7,3},{8,12},{9,13},{10,... | collective-permute-start | bytes 884744 | tf_op jit(solution)/shard_map/ppermute | solution.py:892
  410.5 31.8 %collective-permute-start.17 = (bf16[160,768]{1,0:T(8,128)(2,1)}, bf16[160,768]{1,0:T(8,128)(2,1)}, u32[]{:S(2)}, u32[]{:S(2)}) collective-permute-start(bf16[160,768]{1,0:T(8,128)(2,1)} %add_convert_fusion.8), channel_id=1, source_target_pairs={{0,4},{1,5},{2,6},{3,7},{4,0},{5,1},{6,2},{7,3},{8,12},{9,13},{10,... | collective-permute-start | bytes 737288 | tf_op jit(solution)/shard_map/ppermute | solution.py:892
  448.3 20.0 %collective-permute-start.18 = (bf16[192,384]{1,0:T(8,128)(2,1)}, bf16[192,384]{1,0:T(8,128)(2,1)}, u32[]{:S(2)}, u32[]{:S(2)}) collective-permute-start(bf16[192,384]{1,0:T(8,128)(2,1)} %add_convert_fusion.10), channel_id=1, source_target_pairs={{0,8},{1,9},{2,10},{3,11},{4,12},{5,13},{6,14},{7,15},{8,0},{9,1},... | collective-permute-start | bytes 442376 | tf_op jit(solution)/shard_map/ppermute | solution.py:892
  451.2 17.1 %collective-permute-start.19 = (bf16[80,768]{1,0:T(8,128)(2,1)}, bf16[80,768]{1,0:T(8,128)(2,1)}, u32[]{:S(2)}, u32[]{:S(2)}) collective-permute-start(bf16[80,768]{1,0:T(8,128)(2,1)} %add_convert_fusion.15), channel_id=1, source_target_pairs={{0,8},{1,9},{2,10},{3,11},{4,12},{5,13},{6,14},{7,15},{8,0},{9,1},... | collective-permute-start | bytes 368648 | tf_op jit(solution)/shard_map/ppermute | solution.py:892
  469.5 17.2 %collective-permute-start.21 = (bf16[640,768]{1,0:T(8,128)(2,1)}, bf16[640,768]{1,0:T(8,128)(2,1)}, u32[]{:S(2)}, u32[]{:S(2)}) collective-permute-start(bf16[640,768]{1,0:T(8,128)(2,1)} %constant_dynamic-slice_fusion), channel_id=1, source_target_pairs={{0,1},{1,0},{2,3},{3,2},{4,5},{5,4},{6,7},{7,6},{8,9},{9,8},{10,11... | collective-permute-start | bytes 2949128 | tf_op jit(solution)/shard_map/ppermute | solution.py:892
  470.6 16.1 %collective-permute-start.20 = (bf16[768,384]{1,0:T(8,128)(2,1)}, bf16[768,384]{1,0:T(8,128)(2,1)}, u32[]{:S(2)}, u32[]{:S(2)}) collective-permute-start(bf16[768,384]{1,0:T(8,128)(2,1)} %add_convert_fusion), channel_id=1, source_target_pairs={{0,16},{16,0},{1,17},{17,1},{2,18},{18,2},{3,19},{19,3},{4,20},{20... | collective-permute-start | bytes 1769480 | tf_op jit(solution)/shard_map/ppermute | solution.py:888
  489.6 12.9 %collective-permute-start.24 = (bf16[320,768]{1,0:T(8,128)(2,1)S(1)}, bf16[320,768]{1,0:T(8,128)(2,1)S(1)}, u32[]{:S(2)}, u32[]{:S(2)}) collective-permute-start(bf16[320,768]{1,0:T(8,128)(2,1)S(1)} %add_convert_fusion.2), channel_id=1, source_target_pairs={{0,2},{1,3},{2,0},{3,1},{4,6},{5,7},{6,4},{7,5},{8,10},{9,11},{10,... | collective-permute-start | bytes 1474568 | tf_op jit(solution)/shard_map/ppermute | solution.py:892
  538.3 12.7 %collective-permute-start.34 = (bf16[96,768]{1,0:T(8,128)(2,1)S(1)}, bf16[96,768]{1,0:T(8,128)(2,1)S(1)}, u32[]{:S(2)}, u32[]{:S(2)}) collective-permute-start(bf16[96,768]{1,0:T(8,128)(2,1)S(1)} %pad_maximum_fusion.11), channel_id=1, source_target_pairs={{0,2},{1,3},{2,0},{3,1},{4,6},{5,7},{6,4},{7,5},{8,10},{9,11},{10,... | collective-permute-start | bytes 442376 | tf_op jit(solution)/shard_map/ppermute | solution.py:892
  551.2 21.7 %collective-permute-start.36 = (bf16[192,768]{1,0:T(8,128)(2,1)S(1)}, bf16[192,768]{1,0:T(8,128)(2,1)S(1)}, u32[]{:S(2)}, u32[]{:S(2)}) collective-permute-start(bf16[192,768]{1,0:T(8,128)(2,1)S(1)} %pad_maximum_fusion.9), channel_id=1, source_target_pairs={{0,8},{1,9},{2,10},{3,11},{4,12},{5,13},{6,14},{7,15},{8,0},{9,1},... | collective-permute-start | bytes 884744 | tf_op jit(solution)/shard_map/ppermute | solution.py:892
  551.3 15.9 %collective-permute-start.35 = (bf16[160,768]{1,0:T(8,128)(2,1)S(1)}, bf16[160,768]{1,0:T(8,128)(2,1)S(1)}, u32[]{:S(2)}, u32[]{:S(2)}) collective-permute-start(bf16[160,768]{1,0:T(8,128)(2,1)S(1)} %pad_maximum_fusion.10), channel_id=1, source_target_pairs={{0,4},{1,5},{2,6},{3,7},{4,0},{5,1},{6,2},{7,3},{8,12},{9,13},{10,... | collective-permute-start | bytes 737288 | tf_op jit(solution)/shard_map/ppermute | solution.py:892
  573.2 22.5 %collective-permute-start.38 = (bf16[384,768]{1,0:T(8,128)(2,1)S(1)}, bf16[384,768]{1,0:T(8,128)(2,1)}, u32[]{:S(2)}, u32[]{:S(2)}) collective-permute-start(bf16[384,768]{1,0:T(8,128)(2,1)S(1)} %pad_maximum_fusion.7), channel_id=1, source_target_pairs={{0,4},{1,5},{2,6},{3,7},{4,0},{5,1},{6,2},{7,3},{8,12},{9,13},{10,... | collective-permute-start | bytes 1769480 | tf_op jit(solution)/shard_map/ppermute | solution.py:892
  573.3 13.3 %collective-permute-start.37 = (bf16[320,768]{1,0:T(8,128)(2,1)S(1)}, bf16[320,768]{1,0:T(8,128)(2,1)S(1)}, u32[]{:S(2)}, u32[]{:S(2)}) collective-permute-start(bf16[320,768]{1,0:T(8,128)(2,1)S(1)} %pad_maximum_fusion.8), channel_id=1, source_target_pairs={{0,2},{1,3},{2,0},{3,1},{4,6},{5,7},{6,4},{7,5},{8,10},{9,11},{10,... | collective-permute-start | bytes 1474568 | tf_op jit(solution)/shard_map/ppermute | solution.py:892
  576.2 35.4 %collective-permute-start.32 = (bf16[1024,768]{1,0:T(8,128)(2,1)}, bf16[1024,768]{1,0:T(8,128)(2,1)}, u32[]{:S(2)}, u32[]{:S(2)}) collective-permute-start(bf16[1024,768]{1,0:T(8,128)(2,1)} %broadcast_select_fusion), channel_id=1, source_target_pairs={{0,16},{16,0},{1,17},{17,1},{2,18},{18,2},{3,19},{19,3},{4,20},{20... | collective-permute-start | bytes 4718600 | tf_op jit(solution)/shard_map/ppermute | solution.py:888
  598.3 16.9 %collective-permute-start.39 = (bf16[640,768]{1,0:T(8,128)(2,1)S(1)}, bf16[640,768]{1,0:T(8,128)(2,1)S(1)}, u32[]{:S(2)}, u32[]{:S(2)}) collective-permute-start(bf16[640,768]{1,0:T(8,128)(2,1)S(1)} %pad_maximum_fusion.6), channel_id=1, source_target_pairs={{0,1},{1,0},{2,3},{3,2},{4,5},{5,4},{6,7},{7,6},{8,9},{9,8},{10,11... | collective-permute-start | bytes 2949128 | tf_op jit(solution)/shard_map/ppermute | solution.py:892
  602.0 21.1 %collective-permute-start.40 = (bf16[768,768]{1,0:T(8,128)(2,1)}, bf16[768,768]{1,0:T(8,128)(2,1)}, u32[]{:S(2)}, u32[]{:S(2)}) collective-permute-start(bf16[768,768]{1,0:T(8,128)(2,1)} %pad_maximum_fusion.5), channel_id=1, source_target_pairs={{0,1},{1,0},{2,3},{3,2},{4,5},{5,4},{6,7},{7,6},{8,9},{9,8},{10,11... | collective-permute-start | bytes 3538952 | tf_op jit(solution)/shard_map/ppermute | solution.py:892
  (50 other events, 710.0 us)
Sparse Core Ops, SparseCore 0:
  236.9 74.9 reduce-scatter.2
  359.9 91.1 reduce-scatter.4
  525.3 62.5 all-gather.1

commit v3 on v2

--- a/solution.py
+++ b/solution.py
@@ -87,9 +87,9 @@
 
     @pl.when(jnp.logical_not(mine))
     def _():
-        a, b, c = pieces
         pairs = []
-        for j, (got, at) in enumerate(((a, 0), (b, 0), (c, 0), (c, a.shape[0]))):
+        for j, got in enumerate(pieces):
+            at = 0
             for n in GROUPS[name]:
                 rows, cols = shapes[n]
                 lines = rows // 4 * cols // got.shape[1]
@@ -127,8 +127,8 @@
             at = 0
             for g, names in layout:
                 own = dict(zip(names, sources[at : at + len(names)]))
-                pieces = sources[at + len(names) : at + len(names) + 3]
-                at += len(names) + 3
+                pieces = sources[at + len(names) : at + len(names) + 4]
+                at += len(names) + 4
                 fetch(place_ref, p["l"], g, shapes, own, pieces, {n: into[n] for n in names}, refs[-1])
 
         kernel(*[into[n] for n in wants], *rest)
@@ -174,12 +174,21 @@
     return jnp.concatenate([part * inv for part in exps], axis=0)
 
 
-def fill_padded(dst, src, rows):
-    width = dst.shape[1]
-    dst[0:PAD, :] = jnp.zeros((PAD, width), F32)
-    dst[rows + PAD : rows + 2 * PAD, :] = jnp.zeros((PAD, width), F32)
-    for b in range(rows // RB):
-        dst[PAD + b * RB : PAD + (b + 1) * RB, :] = src[b * RB : (b + 1) * RB, :].astype(F32)
+def padded(rows, width):
+    return pltpu.VMEM((width // 128, rows + 2 * PAD, 128), F32)
+
+
+def clear_ends(dst):
+    rows = dst.shape[1]
+    dst[:, 0:PAD, :] = jnp.zeros((dst.shape[0], PAD, 128), F32)
+    dst[:, rows - PAD : rows, :] = jnp.zeros((dst.shape[0], PAD, 128), F32)
+
+
+def fill_padded(dst, src):
+    rows = src.shape[0]
+    clear_ends(dst)
+    for c in range(dst.shape[0]):
+        dst[c, PAD : PAD + rows, :] = src[:, c * 128 : (c + 1) * 128].astype(F32)
 
 
 def proj_kernel(
@@ -195,7 +204,7 @@
 
     @pl.when(i == 0)
     def _():
-        fill_padded(hp_ref, h_ref, rows)
+        fill_padded(hp_ref, h_ref)
 
     base = pl.multiple_of(i * RB, RB)
     hb = h_ref[pl.ds(base, RB), :]
@@ -212,10 +221,9 @@
     sp_ref[...] = (dot(hb, wp_ref[:, 3 * att : 4 * att]) + vec_ref[:, 2 * att : 3 * att]).astype(BF)
     for c in range(width // 128):
         cols = slice(c * 128, (c + 1) * 128)
-        win = hp_ref[pl.ds(base, RB + 2 * PAD), cols]
-        acc = dk_ref[0:1, cols] * win[PAD - half : PAD - half + RB]
+        acc = dk_ref[0:1, cols] * hp_ref[c, pl.ds(base + PAD - half, RB), :]
         for j in range(1, taps):
-            acc = acc + dk_ref[j : j + 1, cols] * win[PAD - half + j : PAD - half + j + RB]
+            acc = acc + dk_ref[j : j + 1, cols] * hp_ref[c, pl.ds(base + PAD - half + j, RB), :]
         dep_ref[:, cols] = acc.astype(BF)
     keyconv = dot(dep_ref[...], pw_ref[...]) + vec_ref[:, 3 * att : 4 * att]
     kc_ref[...] = keyconv.astype(BF)
@@ -238,7 +246,7 @@
         + [rows_of(width), rows_of(att), rows_of(att), cols_of(t8)],
         out_shape=[sds((rows, att), BF)] * 4 + [sds((att, rows), BF)] * 3
         + [sds((rows, width), BF), sds((rows, att), BF), sds((rows, att), BF), sds((t8, rows), F32)],
-        scratch_shapes=[pltpu.VMEM((rows + 2 * PAD, width), F32)],
+        scratch_shapes=[padded(rows, width)],
         name="proj_fwd", us=13,
     )
 
@@ -248,20 +256,25 @@
     k = k_ref[...]
     ones = jnp.ones((16, rows), BF)
     zeros = jnp.zeros((head, qb), BF)
-    for b in range(rows // qb):
+    units = [(b, s) for b in range(rows // qb) for s in range(2)]
+
+    def scores(b, s):
+        qt = qt_ref[s * head : (s + 1) * head, b * qb : (b + 1) * qb]
+        return dot(k, jnp.concatenate([qt, zeros] if s == 0 else [zeros, qt], axis=0))
+
+    st = scores(*units[0])
+    for n, (b, s) in enumerate(units):
+        ahead = scores(*units[n + 1]) if n + 1 < len(units) else None
+        lo = s * head
         cols = slice(b * qb, (b + 1) * qb)
-        for s in range(2):
-            lo = s * head
-            qt = qt_ref[lo : lo + head, cols]
-            qz = jnp.concatenate([qt, zeros] if s == 0 else [zeros, qt], axis=0)
-            st = dot(k, qz)
-            top = jnp.max(st, axis=0, keepdims=True)
-            pr = jnp.exp2(st - top).astype(BF)
-            vx = jnp.concatenate([vt_ref[lo : lo + head, :], ones], axis=0)
-            ot = dot(vx, pr)
-            total = ot[head : head + 1]
-            at_ref[lo : lo + head, cols] = ot[0:head] * (1.0 / total)
-            lse_ref[0, s : s + 1, cols] = top + jnp.log2(total)
+        top = jnp.max(st, axis=0, keepdims=True)
+        pr = jnp.exp2(st - top).astype(BF)
+        vx = jnp.concatenate([vt_ref[lo : lo + head, :], ones], axis=0)
+        ot = dot(vx, pr)
+        total = ot[head : head + 1]
+        at_ref[lo : lo + head, cols] = ot[0:head] * (1.0 / total)
+        lse_ref[0, s : s + 1, cols] = top + jnp.log2(total)
+        st = ahead
 
 
 def run_attn(k, q2t, vt, head):
@@ -296,18 +309,17 @@
 
     @pl.when(i == 0)
     def _():
-        fill_padded(spp_ref, sp_ref, rows)
+        fill_padded(spp_ref, sp_ref)
 
     base = pl.multiple_of(i * RB, RB)
     ctx_ref[:, 0:att] = at_ref[...].T.astype(BF)
     kn = kern_ref[...].T.astype(BF)
     for c in range(att // 128):
         cols = slice(c * 128, (c + 1) * 128)
-        win = spp_ref[pl.ds(base, RB + 2 * PAD), cols]
         acc = jnp.zeros((RB, 128), F32)
         for j in range(taps):
             kexp = dot(kn, ex_ref[j, :, cols])
-            acc = acc + kexp * win[PAD - half + j : PAD - half + j + RB]
+            acc = acc + kexp * spp_ref[c, pl.ds(base + PAD - half + j, RB), :]
         ctx_ref[:, att + c * 128 : att + (c + 1) * 128] = acc.astype(BF)
     z = dot(ctx_ref[...], wo_ref[...]) + bo[...] + h_ref[...].astype(F32)
     u1, r1 = norm_rows(z)
@@ -317,22 +329,24 @@
     nl = normed.astype(BF)
     nl_ref[...] = nl
     fb = 512
-    outs = []
-    for g in range(groups):
-        x = nl[:, g * gin : (g + 1) * gin]
-        acc = None
-        for f in range(gout // fb):
-            fs = slice(f * fb, (f + 1) * fb)
-            full = slice(g * gout + f * fb, g * gout + (f + 1) * fb)
-            inner = dot(x, w1_ref[g * gin : (g + 1) * gin, fs]) + b1[:, full]
-            cdf = 0.5 + 0.5 * lax.erf(inner * INV_SQRT2)
-            pdf = jnp.exp(inner * inner * -0.5) * INV_SQRT2PI
-            a = (inner * cdf).astype(BF)
-            act_ref[:, full] = a
-            gp_ref[:, full] = (cdf + inner * pdf).astype(BF)
-            part = dot(a, w2_ref[full, :])
-            acc = part if acc is None else acc + part
-        outs.append(acc)
+    units = [(g, f) for g in range(groups) for f in range(gout // fb)]
+
+    def first_product(g, f):
+        return dot(nl[:, g * gin : (g + 1) * gin], w1_ref[g * gin : (g + 1) * gin, f * fb : (f + 1) * fb])
+
+    outs = [None] * groups
+    ahead = first_product(*units[0])
+    for n, (g, f) in enumerate(units):
+        full = slice(g * gout + f * fb, g * gout + (f + 1) * fb)
+        inner = ahead + b1[:, full]
+        ahead = first_product(*units[n + 1]) if n + 1 < len(units) else None
+        cdf = 0.5 + 0.5 * lax.erf(inner * INV_SQRT2)
+        pdf = jnp.exp(inner * inner * -0.5) * INV_SQRT2PI
+        a = (inner * cdf).astype(BF)
+        act_ref[:, full] = a
+        gp_ref[:, full] = (cdf + inner * pdf).astype(BF)
+        part = dot(a, w2_ref[full, :])
+        outs[g] = part if outs[g] is None else outs[g] + part
     z2 = jnp.concatenate(outs, axis=1) + b2[...] + normed
     u2, r2 = norm_rows(z2)
     u2_ref[...] = u2.astype(BF)
@@ -355,7 +369,7 @@
         out_shape=[sds((rows, width), BF), sds((rows, width), BF), sds((rows, 1), F32), sds((rows, width), BF),
                    sds((rows, ff), BF), sds((rows, ff), BF), sds((rows, width), BF), sds((rows, 1), F32),
                    sds((rows, width), BF)],
-        scratch_shapes=[pltpu.VMEM((rows + 2 * PAD, att), F32)],
+        scratch_shapes=[padded(rows, att)],
         name="ffn_fwd", us=22,
     )
 
@@ -402,20 +416,22 @@
     dlow = dsum.astype(BF)
     ds_ref[...] = dlow
     fb = 512
-    outs = []
-    for g in range(groups):
-        x = dlow[:, g * gin : (g + 1) * gin]
-        acc = None
-        for f in range(gout // fb):
-            fs = slice(f * fb, (f + 1) * fb)
-            full = slice(g * gout + f * fb, g * gout + (f + 1) * fb)
-            dinner = dot_nt(x, w2_ref[full, :]) * gp_ref[:, full].astype(F32)
-            db1_ref[:, full] += jnp.sum(dinner, axis=0, keepdims=True)
-            dil = dinner.astype(BF)
-            di_ref[:, full] = dil
-            part = dot_nt(dil, w1_ref[g * gin : (g + 1) * gin, fs])
-            acc = part if acc is None else acc + part
-        outs.append(acc)
+    units = [(g, f) for g in range(groups) for f in range(gout // fb)]
+
+    def first_product(g, f):
+        return dot_nt(dlow[:, g * gin : (g + 1) * gin], w2_ref[g * gout + f * fb : g * gout + (f + 1) * fb, :])
+
+    outs = [None] * groups
+    ahead = first_product(*units[0])
+    for n, (g, f) in enumerate(units):
+        full = slice(g * gout + f * fb, g * gout + (f + 1) * fb)
+        dinner = ahead * gp_ref[:, full].astype(F32)
+        ahead = first_product(*units[n + 1]) if n + 1 < len(units) else None
+        db1_ref[:, full] += jnp.sum(dinner, axis=0, keepdims=True)
+        dil = dinner.astype(BF)
+        di_ref[:, full] = dil
+        part = dot_nt(dil, w1_ref[g * gin : (g + 1) * gin, f * fb : (f + 1) * fb])
+        outs[g] = part if outs[g] is None else outs[g] + part
     dn = jnp.concatenate(outs, axis=1) + dsum
     u1 = u1_ref[...].astype(F32)
     vec_ref[3:4, :] += jnp.sum(dn * u1, axis=0, keepdims=True)
@@ -462,11 +478,10 @@
 
     @pl.when((phase == 0) & (i == 0))
     def _():
-        fill_padded(ddp_ref, ddn_ref, rows)
-        fill_padded(spp_ref, sp_ref, rows)
-        fill_padded(hp_ref, h_ref, rows)
-        dep_ref[0:PAD, :] = jnp.zeros((PAD, width), F32)
-        dep_ref[rows + PAD : rows + 2 * PAD, :] = jnp.zeros((PAD, width), F32)
+        fill_padded(ddp_ref, ddn_ref)
+        fill_padded(spp_ref, sp_ref)
+        fill_padded(hp_ref, h_ref)
+        clear_ends(dep_ref)
         knp_ref[0:PAD, :] = jnp.zeros((PAD, knp_ref.shape[1]), F32)
         knp_ref[rows + PAD : rows + 2 * PAD, :] = jnp.zeros((PAD, knp_ref.shape[1]), F32)
         dkg_ref[...] = jnp.zeros(dkg_ref.shape, F32)
@@ -484,8 +499,7 @@
             prods = []
             for c in range(att // 128):
                 cols = slice(c * 128, (c + 1) * 128)
-                win = spp_ref[pl.ds(base, RB + 2 * PAD), cols]
-                prods.append((dd[:, cols] * win[PAD - half + j : PAD - half + j + RB]).astype(BF))
+                prods.append((dd[:, cols] * spp_ref[c, pl.ds(base + PAD - half + j, RB), :]).astype(BF))
             part = dot(jnp.concatenate(prods, axis=1), ext_ref[j])
             dkern = part if dkern is None else dkern + part
         dkt = dkern.T
@@ -509,26 +523,26 @@
         dpb_ref[...] += jnp.sum(dkc, axis=0, keepdims=True)
         dkcl = dkc.astype(BF)
         dkc_ref[...] = dkcl
-        dep_ref[pl.ds(base + PAD, RB), :] = dot_nt(dkcl, pw_ref[...])
+        dep = dot_nt(dkcl, pw_ref[...])
+        for c in range(width // 128):
+            dep_ref[c, pl.ds(base + PAD, RB), :] = dep[:, c * 128 : (c + 1) * 128]
 
     @pl.when(phase == 1)
     def _():
         for c in range(width // 128):
             cols = slice(c * 128, (c + 1) * 128)
-            win = dep_ref[pl.ds(base, RB + 2 * PAD), cols]
-            mid = win[PAD : PAD + RB]
-            hw = hp_ref[pl.ds(base, RB + 2 * PAD), cols]
+            mid = dep_ref[c, pl.ds(base + PAD, RB), :]
             acc = dz_ref[:, cols].astype(F32)
             for j in range(taps):
-                acc = acc + dk_ref[j : j + 1, cols] * win[PAD + half - j : PAD + half - j + RB]
+                acc = acc + dk_ref[j : j + 1, cols] * dep_ref[c, pl.ds(base + PAD + half - j, RB), :]
                 dkg_ref[j : j + 1, cols] += jnp.sum(
-                    mid * hw[PAD - half + j : PAD - half + j + RB], axis=0, keepdims=True
+                    mid * hp_ref[c, pl.ds(base + PAD - half + j, RB), :], axis=0, keepdims=True
                 )
             res_ref[:, cols] = acc.astype(BF)
         kn = knp_ref[pl.ds(base, RB + 2 * PAD), :].astype(BF)
         for c in range(att // 128):
             cols = slice(c * 128, (c + 1) * 128)
-            win = ddp_ref[pl.ds(base, RB + 2 * PAD), cols]
+            win = ddp_ref[c, pl.ds(base, RB + 2 * PAD), :]
             acc = jnp.zeros((RB, 128), F32)
             for j in range(taps):
                 prod = dot(kn, ex_ref[j, :, cols]) * win
@@ -566,8 +580,7 @@
                    sds((rows, width), BF), sds(p["dk"].shape, F32), sds((1, att), F32), sds((t8, 1), F32),
                    sds((SUB, att), F32)],
         scratch_shapes=[
-            pltpu.VMEM((rows + 2 * PAD, att), F32), pltpu.VMEM((rows + 2 * PAD, att), F32),
-            pltpu.VMEM((rows + 2 * PAD, width), F32), pltpu.VMEM((rows + 2 * PAD, width), F32),
+            padded(rows, att), padded(rows, att), padded(rows, width), padded(rows, width),
             pltpu.VMEM((rows + 2 * PAD, t8), F32),
         ],
         name="conv_bwd", us=27,
@@ -583,31 +596,42 @@
     v = v_ref[...]
     zeros = jnp.zeros((head, qb), BF)
     lane = lax.broadcasted_iota(jnp.int32, (1, 2 * head), 1)
-    for b in range(rows // qb):
+    units = [(b, s) for b in range(rows // qb) for s in range(2)]
+
+    def products(b, s):
+        lo = s * head
         cols = slice(b * qb, (b + 1) * qb)
-        dqs = []
-        for s in range(2):
-            lo = s * head
-            side = (lane >= lo) & (lane < lo + head)
-            qt = qt_ref[lo : lo + head, cols]
-            qz = jnp.concatenate([qt, zeros] if s == 0 else [zeros, qt], axis=0)
-            dt = dot_ref[lo : lo + head, cols]
-            dz = jnp.concatenate([dt, zeros] if s == 0 else [zeros, dt], axis=0)
-            dd = jnp.sum(dt.astype(F32) * at_ref[lo : lo + head, cols], axis=0, keepdims=True)
-            pr = jnp.exp2(dot(k, qz) - lse_ref[0, s : s + 1, cols])
-            ds = (pr * (dot(v, dz) - dd)).astype(BF)
-            dqs.append(dot(kt_ref[lo : lo + head, :], ds))
-            qn = jnp.where(side, q2_ref[cols, :], jnp.zeros((), BF))
-            dn = jnp.where(side, do_ref[cols, :], jnp.zeros((), BF))
-            gv = dot(pr.astype(BF), dn)
-            gk = dot(ds, qn)
-            if b == 0 and s == 0:
-                av_ref[...] = gv
-                ak_ref[...] = gk
-            else:
-                av_ref[...] += gv
-                ak_ref[...] += gk
-        dq_ref[cols, :] = (jnp.concatenate(dqs, axis=0).T * 0.125).astype(BF)
+        qt = qt_ref[lo : lo + head, cols]
+        dt = dot_ref[lo : lo + head, cols]
+        qz = jnp.concatenate([qt, zeros] if s == 0 else [zeros, qt], axis=0)
+        dz = jnp.concatenate([dt, zeros] if s == 0 else [zeros, dt], axis=0)
+        return dot(k, qz), dot(v, dz)
+
+    ahead = products(*units[0])
+    dqs = []
+    for n, (b, s) in enumerate(units):
+        st, dp = ahead
+        ahead = products(*units[n + 1]) if n + 1 < len(units) else None
+        cols = slice(b * qb, (b + 1) * qb)
+        lo = s * head
+        side = (lane >= lo) & (lane < lo + head)
+        dd = jnp.sum(dot_ref[lo : lo + head, cols].astype(F32) * at_ref[lo : lo + head, cols], axis=0, keepdims=True)
+        pr = jnp.exp2(st - lse_ref[0, s : s + 1, cols])
+        ds = (pr * (dp - dd)).astype(BF)
+        dqs.append(dot(kt_ref[lo : lo + head, :], ds))
+        qn = jnp.where(side, q2_ref[cols, :], jnp.zeros((), BF))
+        dn = jnp.where(side, do_ref[cols, :], jnp.zeros((), BF))
+        gv = dot(pr.astype(BF), dn)
+        gk = dot(ds, qn)
+        if n == 0:
+            av_ref[...] = gv
+            ak_ref[...] = gk
+        else:
+            av_ref[...] += gv
+            ak_ref[...] += gk
+        if s == 1:
+            dq_ref[cols, :] = (jnp.concatenate(dqs, axis=0).T * 0.125).astype(BF)
+            dqs = []
     dk_ref[...] = (ak_ref[...] * (1.0 / LOG2E)).astype(BF)
     dv_ref[...] = av_ref[...].astype(BF)
     dbv_ref[...] = jnp.sum(av_ref[...], axis=0, keepdims=True)
@@ -652,14 +676,13 @@
     )
 
 
-def wide_grad_kernel(nl_ref, di_ref, ds_ref, act_ref, out_ref, nt_ref, dt_ref):
-    @pl.when(pl.program_id(1) == 0)
-    def _():
-        nt_ref[...] = nl_ref[...].T
-        dt_ref[...] = ds_ref[...].T
-
-    out_ref[0] = dot(nt_ref[...], di_ref[...]).astype(BF)
-    out_ref[1] = dot(dt_ref[...], act_ref[...]).astype(BF)
+def dot_tn(a, b):
+    return lax.dot_general(a, b, (((0,), (0,)), ((), ())), preferred_element_type=F32)
+
+
+def wide_grad_kernel(nl_ref, di_ref, ds_ref, act_ref, out_ref):
+    out_ref[0] = dot_tn(nl_ref[...], di_ref[...]).astype(BF)
+    out_ref[1] = dot_tn(ds_ref[...], act_ref[...]).astype(BF)
 
 
 def run_wide_grads(nl, di, ds, act, groups):
@@ -674,7 +697,6 @@
         in_specs=[narrow, wide, narrow, wide],
         out_specs=pl.BlockSpec((2, gin, width), lambda g, q: (0, q * groups + g, 0)),
         out_shape=sds((2, steps * width, width), BF),
-        scratch_shapes=[pltpu.VMEM((gin, rows), BF)] * 2,
         compiler_params=params(),
         cost_estimate=cost(6),
         name="ffn_wgrad",
@@ -787,22 +809,6 @@
     return jnp.pad(rows, ((0, lines - rows.shape[0]), (0, 0))).astype(BF)
 
 
-def small_parts(rows, att, taps, heads, ff):
-    t8 = taps * SUB
-    width = rows.shape[1]
-    at = t8
-    vec = rows[at : at + SUB]
-    b1 = rows[at + SUB : at + SUB + ff // width].reshape(-1)
-    dk = rows[at + 2 * SUB : at + 2 * SUB + taps]
-    four = rows[at + 4 * SUB : at + 4 * SUB + 4, :att]
-    kb = rows[at + 5 * SUB, :t8].reshape(taps, SUB)[:, :heads].T.reshape(-1)
-    kw = rows[:t8, :att].reshape(taps, SUB, att)[:, :heads].transpose(1, 0, 2).reshape(heads * taps, att).T
-    return {
-        "bp": jnp.concatenate([four[0], four[2], four[1]]), "dk": dk, "pb": four[3], "kw": kw, "kb": kb,
-        "bo": vec[5], "g1": vec[3], "s1": vec[4], "b1": b1, "b2": vec[2], "g2": vec[0], "s2": vec[1],
-    }, rows[at + 6 * SUB - 1]
-
-
 def mask_row(taps):
     return taps * SUB + 6 * SUB - 1
 
@@ -811,47 +817,25 @@
     return p["own"]["w1"].shape[0] // p["own"]["w2"].shape[1]
 
 
-def layer_backward(dy, keep, mask, mask_rows, p, ex, ext, head, lines, slot, send, later):
+def layer_backward(dy, keep, mask, mask_rows, p, ex, ext, head, lines, slot, send):
     groups = h_groups(p)
     h = keep["h"]
     dy = slot("ffn", dy)
     ds, di, dz, dat, dan, ddn, vec, db1 = run_ffn_back(dy, keep, p)
     di, dan = slot("wide", (di, dan))
-    wide = run_wide_grads(keep["nl"], di, ds, keep["act"], groups)
-    send(0, wide)
-
-    def mid_chunk(dk, dv):
-        send(1, run_mid_grads(keep["ctx"], dz, h, dk, dv))
-
-    def last_chunk(dq, dk, dv, dsp, dkc, dl, res, sums):
-        last, dkw, mg = run_last_grads(h, dq, dk, dv, dsp, keep["dep"], dkc, keep["mx"], dl, res, mask_rows, p)
-        dkg, dpb, dkb, dbp, dbv = sums
-        small = small_rows(vec, db1, dkg, dbp, dbv, dpb, dkb, dkw, mg[0:1], lines)
-        send(2, jnp.concatenate([last, small]))
-
+    send(0, run_wide_grads(keep["nl"], di, ds, keep["act"], groups))
     dan, dat = slot("attn", (dan, dat))
     dqa, dk, dv, dbv = run_attn_back(dan, dat, keep, head)
-    if not later:
-        dqa, dk, dv = slot("mid", (dqa, dk, dv))
-        mid_chunk(dk, dv)
+    dqa, dk, dv = slot("mid", (dqa, dk, dv))
+    send(1, run_mid_grads(keep["ctx"], dz, h, dk, dv))
     ddn, dqa = slot("conv", (ddn, dqa))
     dl, dq, dsp, dkc, res, dkg, dpb, dkb, dbp = run_conv_back(ddn, dz, dqa, h, keep, ex, ext, p)
-    sums = (dkg, dpb, dkb, dbp, dbv)
-    if not later:
-        dq, dl, res = slot("last", (dq, dl, res))
-        last_chunk(dq, dk, dv, dsp, dkc, dl, res, sums)
+    dq, dl, res = slot("last", (dq, dl, res))
+    last, dkw, mg = run_last_grads(h, dq, dk, dv, dsp, keep["dep"], dkc, keep["mx"], dl, res, mask_rows, p)
+    small = small_rows(vec, db1, dkg, dbp, dbv, dpb, dkb, dkw, mg[0:1], lines)
+    send(2, jnp.concatenate([last, small]))
     dq, res = slot("in", (dq, res))
-    dh = run_in_back(dq, dk, dv, dsp, res, mask, p)
-
-    def rest(name, x):
-        if name == "attn":
-            x, dk_now = lax.optimization_barrier((x, dk))
-            mid_chunk(dk_now, dv)
-            x, dl_now = slot("last", (x, dl))
-            last_chunk(dq, dk, dv, dsp, dkc, dl_now, res, sums)
-        return x
-
-    return slot("end", dh), rest
+    return slot("end", run_in_back(dq, dk, dv, dsp, res, mask, p))
 
 
 def pack_kernel(place_ref, *refs, names):
@@ -893,6 +877,8 @@
 
 
 def move(x, step):
+    if isinstance(step, tuple):
+        return tuple(move(a, b) for a, b in zip(x, step))
     if step == "scatter":
         return lax.psum_scatter(x, "dp", scatter_dimension=0, tiled=True)
     if step == "gather":
@@ -984,15 +970,16 @@
     return total_of([jnp.where(first, share0, share1), got])
 
 
-def collect_flow(share, steps, ordered):
-    for bit in reversed(steps):
+def collect_flow(share, steps):
+    for bit in reversed(steps[1:]):
         got = yield share, bit
-        if bit not in steps[:2] or ordered:
+        if bit == steps[1]:
+            share = jnp.concatenate([share, got])
+        else:
             low = my_bit(bit) == 0
             share = jnp.concatenate([jnp.where(low, share, got), jnp.where(low, got, share)])
-        else:
-            share = jnp.concatenate([share, got])
-    return share
+    got = yield share, steps[0]
+    return share, got
 
 
 def one_move(x, step):
@@ -1001,9 +988,9 @@
 
 def piece_flow(x):
     a = yield x, "section"
-    b = yield a, 1
-    c = yield jnp.concatenate([a, b]), 0
-    return [a, b, c]
+    b, c = yield (a, a), (1, 0)
+    d = yield b, 0
+    return [a, b, c, d]
 
 
 def wide_out_kernel(_, a_ref, b_ref, w1_ref, w2_ref):
@@ -1036,32 +1023,66 @@
     )(place, full, full)
 
 
-def last_out_kernel(at_ref, mid_ref, last_ref, wp_ref, pw_ref, wo_ref):
-    place = at_ref[0]
-    att = pw_ref.shape[1]
-    width = pw_ref.shape[0]
-    n = width // 2
-    for j in range(2):
-        rows = slice(j * n, (j + 1) * n)
-        wo_ref[rows, :] = mid_ref[pl.ds(pl.multiple_of((j ^ place) * n, 16), n), :].astype(F32)
-        wp_ref[rows, att : 3 * att] = mid_ref[pl.ds(pl.multiple_of(((2 + j) ^ place) * n, 16), n), :].astype(F32)
-        wp_ref[rows, 0:att] = last_ref[rows, 0:att].astype(F32)
-        wp_ref[rows, 3 * att :] = last_ref[rows, att:].astype(F32)
-    pw_ref[...] = last_ref[width : width + att, :].astype(F32).T
-
-
-def last_outputs(mid, last, place, att):
-    width = mid.shape[1]
+def last_out_kernel(
+    at_ref, mid_ref, mid_got_ref, last_ref, last_got_ref,
+    wp_ref, pw_ref, wo_ref, bp_ref, dk_ref, pb_ref, kw_ref, kb_ref, bo_ref, g1_ref, s1_ref, b1_ref, b2_ref, g2_ref,
+    s2_ref, mg_ref,
+    all_mid_ref, all_last_ref,
+):
+    width, att = pw_ref.shape
+    taps = dk_ref.shape[0]
+    t8 = taps * SUB
+    for k, (refs, ordered_ref) in enumerate((((mid_ref, mid_got_ref), all_mid_ref),
+                                             ((last_ref, last_got_ref), all_last_ref))):
+        n = ordered_ref.shape[0] // 4
+        for j in range(4):
+            rows = pl.ds(pl.multiple_of((j ^ at_ref[k]) * n, 16), n)
+            ordered_ref[rows, :] = refs[j // 2][j % 2 * n : (j % 2 + 1) * n, :]
+    wo_ref[...] = all_mid_ref[0:width, :].astype(F32)
+    wp_ref[:, att : 3 * att] = all_mid_ref[width:, :].astype(F32)
+    wp_ref[:, 0:att] = all_last_ref[0:width, 0:att].astype(F32)
+    wp_ref[:, 3 * att :] = all_last_ref[0:width, att:].astype(F32)
+    pw_ref[...] = all_last_ref[width : width + att, :].astype(F32).T
+    small = all_last_ref[width + att :, :].astype(F32)
+    source = lax.broadcasted_iota(jnp.int32, (kb_ref.shape[1], t8), 1)
+    target = lax.broadcasted_iota(jnp.int32, (kb_ref.shape[1], t8), 0)
+    pick = lax.div(source, SUB) + lax.rem(source, SUB) * taps == target
+    pick = pick.astype(F32).astype(BF)
+    kw_ref[...] = dot(pick, small[0:t8, 0:att].astype(BF)).T
+    for n, ref in ((0, g2_ref), (1, s2_ref), (2, b2_ref), (3, g1_ref), (4, s1_ref), (5, bo_ref)):
+        ref[...] = small[t8 + n : t8 + n + 1]
+    for n in range(b1_ref.shape[1] // width):
+        b1_ref[:, n * width : (n + 1) * width] = small[t8 + SUB + n : t8 + SUB + n + 1]
+    dk_ref[...] = small[t8 + 2 * SUB : t8 + 2 * SUB + taps]
+    four = t8 + 4 * SUB
+    for n, row in enumerate((0, 2, 1)):
+        bp_ref[:, n * att : (n + 1) * att] = small[four + row : four + row + 1, 0:att]
+    pb_ref[...] = small[four + 3 : four + 4, 0:att]
+    kb_ref[...] = dot_nt(small[t8 + 5 * SUB : t8 + 6 * SUB, 0:t8].astype(BF), pick)[0:1]
+    mg_ref[...] = small[t8 + 6 * SUB - 1 : t8 + 6 * SUB]
+
+
+def last_outputs(mid, last, places, att, taps, heads, ff):
+    width = mid[0].shape[1]
     vm = pl.BlockSpec(memory_space=pltpu.VMEM)
-    return pl.pallas_call(
+    line = sds((1, width), F32)
+    shapes = dict(
+        wp=sds((width, 4 * att), F32), pw=sds((width, att), F32), wo=sds((width, width), F32),
+        bp=sds((1, 3 * att), F32), dk=sds((taps, width), F32), pb=sds((1, att), F32),
+        kw=sds((att, heads * taps), F32), kb=sds((1, heads * taps), F32), bo=line, g1=line, s1=line,
+        b1=sds((1, ff), F32), b2=line, g2=line, s2=line, mask=line,
+    )
+    outs = pl.pallas_call(
         last_out_kernel,
-        in_specs=[pl.BlockSpec(memory_space=pltpu.SMEM), vm, vm],
-        out_specs=[vm] * 3,
-        out_shape=[sds((width, 4 * att), F32), sds((width, att), F32), sds((width, width), F32)],
+        in_specs=[SMEM] + [vm] * 4,
+        out_specs=[vm] * len(shapes),
+        out_shape=list(shapes.values()),
+        scratch_shapes=[pltpu.VMEM((2 * a[0].shape[0], width), BF) for a in (mid, last)],
         compiler_params=params(),
         cost_estimate=cost(6),
         name="last_out",
-    )(place, mid, last)
+    )(places, *mid, *last)
+    return dict(zip(shapes, outs))
 
 
 FORWARD = {
@@ -1071,24 +1092,26 @@
 BACKWARD = {
     "1ffn": ("states",),
     "1attn": ("10",),
-    "1in": ("states",),
-    "0attn": ("10", "00"),
-    "1last": ("11",),
-    "0then": ("11", "12"),
-    "0mid": ("12",),
-    "0conv": ("01", "11", "12"),
-    "0last": ("01", "11", "12"),
-    "0in": ("02", "11", "12"),
-    "0end": ("00", "01", "02", "11", "12"),
+    "1conv": ("11",),
+    "1last": ("11", "states"),
+    "1in": ("12",),
+    "0ffn": ("12",),
+    "0wide": ("11", "12"),
+    "0attn": ("10", "00", "11", "12"),
+    "0mid": ("11", "12"),
+    "0conv": ("01", "11"),
+    "0last": ("01",),
+    "0in": ("01", "02"),
 }
 LAST = (
-    ("wide", "01", "02", "11", "12"),
-    ("wide", "01", "02"),
-    ("01", "02", "mid", "last"),
-    ("mid", "last", "rows"),
+    ("00", "01", "02", "wide", "rows"),
+    ("01", "02", "wide"),
+    ("01", "02", "mid"),
+    ("02", "mid", "last"),
     ("mid", "last"),
     ("mid", "last"),
-    ("mid", "last"),
+    ("mid", "last", "rows"),
+    ("mid", "last", "wide"),
 )
 
 
@@ -1116,23 +1139,23 @@
                      ("w2", second_feed_weight))
     }
     buffers = pack_quarters(own, place, 2 * width)
+    for name, buffer in zip("ABC", buffers):
+        flows.add(name, piece_flow(buffer))
+    biases = flows.step(("A",), (proj_bias, point_bias, out_bias, norm_gain, norm_shift, second_feed_bias, final_gain,
+                                 final_shift, inner_bias))
 
     def lines_of(a):
         return jnp.pad(a, ((0, 0), (0, width - a.shape[1])))
 
-    vec = vector_pack(proj_bias, point_bias, out_bias, norm_gain, norm_shift, second_feed_bias, final_gain, final_shift,
-                      inner_bias)
+    vec = vector_pack(*biases)
     span = heads * taps
     little = jnp.concatenate([lines_of(kernel_weight[0].T), depth_kernel[0], lines_of(kernel_bias),
                               vec.reshape(-1, width)])
     flows.add("little", one_move(little, "section"))
-    for name, buffer in zip("ABC", buffers):
-        flows.add(name, piece_flow(buffer))
 
     def mine(a):
         return lax.dynamic_index_in_dim(a, section, 0, keepdims=False)
 
-    flows.step(("little", "A"), ())
     pos, count = mine(mask_pos), mine(mask_count)
     hits = (pos[:, None] == jnp.arange(seq, dtype=jnp.int32)[None, :]) & (
         jnp.arange(pos.shape[0], dtype=jnp.int32) < count
@@ -1142,9 +1165,10 @@
     mask = masked.astype(F32)
     mask_rows = jnp.broadcast_to(masked.reshape(1, seq), (SUB, seq)).astype(BF)
     ex, ext = spread_matrices(taps, heads, head)
+    early = (hidden, mask, mask_rows, ex, ext, little, mine(cotangent))
+    hidden, mask, mask_rows, ex, ext, little, seed = flows.step(("A", "B", "little"), early)
+    flows.step(("A", "B", "C", "little"), ())
     other = flows.finish("little")
-    flows.step(("A", "B"), ())
-    flows.step(("A", "B", "C"), ())
     pieces = {"A": flows.finish("A")}
 
     def small(rows):
@@ -1184,24 +1208,18 @@
     order = (None, turned[:1] + ["section"] + turned[1:], bits)
     lines = 128
 
-    def backward(layer, dy, mask, mask_rows, before):
+    def backward(layer, dy, mask, mask_rows):
         def slot(name, x):
-            key = str(layer) + name
-            x = flows.step(BACKWARD.get(key, ()), x)
-            if before is not None:
-                x = before(name, x)
-                if name == "attn":
-                    x = flows.step(BACKWARD["0then"], x)
-            return x
+            return flows.step(BACKWARD.get(str(layer) + name, ()), x)
 
         def send(n, packed):
             flow = one_move(packed, "scatter") if n == 0 else sum_flow(packed, order[n])
             flows.add(str(layer) + str(n), flow)
 
-        return layer_backward(dy, keeps[layer], mask, mask_rows, p[layer], ex, ext, head, lines, slot, send, layer == 1)
-
-    d1, rest = backward(1, mine(cotangent), jnp.zeros_like(mask), jnp.zeros_like(mask_rows), None)
-    d0, _ = backward(0, d1, mask, mask_rows, rest)
+        return layer_backward(dy, keeps[layer], mask, mask_rows, p[layer], ex, ext, head, lines, slot, send)
+
+    d1 = backward(1, seed, jnp.zeros_like(mask), jnp.zeros_like(mask_rows))
+    d0 = backward(0, d1, mask, mask_rows)
     states = both_rows(*outs, flows.finish("states"))
 
     start, n = 0, width + att + lines
@@ -1217,29 +1235,33 @@
 
     def mid_flow():
         own = yield from own_halves_flow(flows.finish("01"), flows.finish("11"), first)
-        return (yield from collect_flow(own, turned, False))
+        return (yield from collect_flow(own, turned))
 
     def last_flow():
         a, b = flows.finish("02"), flows.finish("12")
         own = yield from own_total_flow(a, jnp.where(marked, a, b), first)
-        return (yield from collect_flow(own, bits, True))
+        return (yield from collect_flow(own, bits))
 
     flows.add("wide", wide_flow())
     flows.add("mid", mid_flow())
     flows.add("last", last_flow())
     flows.add("rows", other_row(d0, d1))
-    for names in LAST:
+    for names in LAST[:4]:
+        flows.step(names, ())
+    states, = flows.step(LAST[4], (states,))
+    for names in LAST[5:]:
         flows.step(names, ())
     in_grads = both_rows(d0, d1, flows.finish("rows"))
-    wide, mid, last = [flows.finish(n) for n in ("wide", "mid", "last")]
-    w1, w2 = wide_outputs(wide, jnp.zeros((1,), jnp.int32), groups)
-    mid_place = (2 * my_bit(0) + my_bit(turned[1])).reshape(1).astype(jnp.int32)
-    wp, pw, wo = last_outputs(mid, last, mid_place, att)
-    grads, mask_grad = small_parts(last[width + att :].astype(F32), att, taps, heads, inner_bias.shape[1])
-    grads.update(wp=wp, pw=pw, wo=wo, w1=w1.reshape(inner_weight.shape[1:]),
-                 w2=w2.reshape(second_feed_weight.shape[1:]))
+    w1, w2 = wide_outputs(flows.finish("wide"), jnp.zeros((1,), jnp.int32), groups)
+    in_grads, w1, w2 = flows.step(("mid", "last"), (in_grads, w1, w2))
+    mid, last = flows.finish("mid"), flows.finish("last")
+    places = jnp.stack([2 * my_bit(0) + my_bit(turned[1]), quarter]).astype(jnp.int32)
+    grads = last_outputs(mid, last, places, att, taps, heads, inner_bias.shape[1])
+    grads.update(w1=w1.reshape(inner_weight.shape), w2=w2.reshape(second_feed_weight.shape))
+    for n in ("wp", "dk", "pw", "kw", "wo"):
+        grads[n] = grads[n][None]
     names = ("wp", "bp", "dk", "pw", "pb", "kw", "kb", "wo", "bo", "g1", "s1", "w1", "b1", "w2", "b2", "g2", "s2")
-    return (states[None], in_grads[None], mask_grad) + tuple(grads[n][None] for n in names)
+    return (states[None], in_grads[None], grads["mask"].reshape(-1)) + tuple(grads[n] for n in names)
 
 
 def solution(mesh):

time: 657 us -> 604 us (0.919)
  Pallas kernels: 346 us -> 309 us
  other arithmetic: 69.5 us -> 61.8 us
  local copies, waits for them, and re-layouts: 33.9 us -> 26.4 us
    pallas_call x12, Pallas kernels: 213 us -> 195 us  [call(): pl.pallas_call(body, grid=grid, in_specs=[SMEM] + [HBM] * len(operands) +...]
    pallas_call x2, Pallas kernels: 37.7 us -> 24.2 us  [run_attn(): pl.pallas_call(partial(attn_kernel, head=head, qb=256), grid=(pairs,), in...]
    ppermute x30 -> x33, waiting for transfers between devices: 98.7 us -> 93.3 us  [across(): lax.ppermute(x, 'dp', [(i, i ^ 1 << bit) for i in range(lax.axis_size('dp...]
    unnamed x93 -> x122, local copies, waits for them, and re-layouts: 14 us -> 11.3 us
    ppermute x30 -> x33, starting transfers between devices: 28.1 us -> 26.4 us  [across(): lax.ppermute(x, 'dp', [(i, i ^ 1 << bit) for i in range(lax.axis_size('dp...]
  transfers between devices with their start and end apart: 44 -> 47, of which waited for: 20 -> 19; matrix products, arithmetic and copies ran while one was open for 12% -> 10% of each run, Pallas kernels for 33% -> 29%
where the time goes in v3:
time: 604 us; the launch traced here: 592 us
  Pallas kernels  309 us (51%)
  waiting for transfers between devices  136 us (23%)
  other arithmetic  61.8 us (10%)
  starting transfers between devices  43.7 us (7%)
  local copies, waits for them, and re-layouts  26.4 us (4%)
  between operations  15.2 us (3%)
    pallas_call x12, Pallas kernels, call(): pl.pallas_call(body, grid=grid, in_specs=[SMEM] + [HBM] * len(operands) +...  195 us
    ppermute x33, waiting for transfers between devices, across(): lax.ppermute(x, 'dp', [(i, i ^ 1 << bit) for i in range(lax.axis_size('dp...  93.3 us
    ppermute x11, waiting for transfers between devices, swap(): return lax.ppermute(x, 'section', [(0, 1), (1, 0)])  42.4 us
    pallas_call x2, Pallas kernels, run_attn_back(): pl.pallas_call(partial(attn_back_kernel, head=head, qb=256), grid=(pairs,...  36.9 us
    ppermute x33, starting transfers between devices, across(): lax.ppermute(x, 'dp', [(i, i ^ 1 << bit) for i in range(lax.axis_size('dp...  26.4 us
    pallas_call x2, Pallas kernels, run_attn(): pl.pallas_call(partial(attn_kernel, head=head, qb=256), grid=(pairs,), in...  24.2 us
    convert_element_type x16, other arithmetic, total_of(): return total.astype(BF)  23.8 us
    pallas_call x2, Pallas kernels, run_wide_grads(): pl.pallas_call(wide_grad_kernel, grid=(groups, steps), in_specs=[narrow,...  21.8 us
  transfers between devices with their start and end apart: 47, of which 19 were waited for; matrix products, arithmetic and copies ran while one was open for 10% of the time, Pallas kernels for 29%

profile of v3, /device:TPU:0, one launch (start us, length us, event | category | flops | bytes accessed | tf_op | source)
XLA Modules:
  0.0 592.2 jit_solution(13522612711564803805)
XLA Ops:
  8.0 3.8 pack_weights.1
  22.4 9.2 %collective-permute-done.refs_2_.refs_1_ = bf16[240,1536]{1,0:T(8,128)(2,1)} collective-permute-done((bf16[240,1536]{1,0:T(8,128)(2,1)}, bf16[240,1536]{1,0:T(8,128)(2,1)}, u32[]{:S(2)}, u32[]{:S(2)}) %collective-permute-start) | collective-permute-done | bytes 737312 | tf_op jit(solution)/shard_map/ppermute | solution.py:872
  36.0 19.7 %collective-permute-done.4 = bf16[76,768]{1,0:T(8,128)(2,1)S(1)} collective-permute-done((bf16[76,768]{1,0:T(8,128)(2,1)S(1)}, bf16[76,768]{1,0:T(8,128)(2,1)S(1)}, u32[]{:S(2)}, u32[]{:S(2)}) %collective-permute-start.4) | collective-permute-done | bytes 116768 | tf_op jit(solution)/shard_map/ppermute | solution.py:872
  61.9 11.8 %proj_fwd.2 = (bf16[1024,384]{1,0:T(8,128)(2,1)}, bf16[1024,384]{1,0:T(8,128)(2,1)}, bf16[1024,384]{1,0:T(8,128)(2,1)}, bf16[1024,384]{1,0:T(8,128)(2,1)}, bf16[...) custom-call(s32[2]{0:T(128)} %get-tuple-element.722.place_ref, ...), custom_call_target="tpu_custom_call" | custom-call | flops 14300000256 | tf_op jit(solution)/shard_map/proj_fwd/pallas_call | solution.py:136
  74.9 4.6 collective-permute-done.6.refs_3_
  81.3 12.1 %attn_fwd.2 = (f32[384,1024]{1,0:T(8,128)}, f32[3,8,1024]{2,1,0:T(8,128)}) custom-call(bf16[1024,384]{1,0:T(8,128)(2,1)} %get-tuple-element.382.k_ref, bf16[384,1024]{1,0:T(8,128)(2,1)} %get-tuple-element.383.qt_ref, bf16[384,1024]{1,0:T(8,128)(2,1)} %get-tuple-element.384.vt_ref), custom_call_target="tpu_custom_call" | custom-call | flops 20899999744 | tf_op jit(solution)/shard_map/attn_fwd/pallas_call | solution.py:284
  100.0 24.3 %ffn_fwd.2 = (bf16[1024,768]{1,0:T(8,128)(2,1)}, bf16[1024,768]{1,0:T(8,128)(2,1)}, f32[1024,1]{1,0:T(8,128)}, bf16[1024,768]{1,0:T(8,128)(2,1)}, bf16[1024,3072...) custom-call(s32[2]{0:T(128)} %get-tuple-element.722.place_ref, ...), custom_call_target="tpu_custom_call" | custom-call | flops 24199999488 | tf_op jit(solution)/shard_map/ffn_fwd/pallas_call | solution.py:136
  124.3 12.0 %proj_fwd.3 = (bf16[1024,384]{1,0:T(8,128)(2,1)}, bf16[1024,384]{1,0:T(8,128)(2,1)}, bf16[1024,384]{1,0:T(8,128)(2,1)}, bf16[1024,384]{1,0:T(8,128)(2,1)}, bf16[...) custom-call(s32[2]{0:T(128)} %get-tuple-element.722.place_ref, ...), custom_call_target="tpu_custom_call" | custom-call | flops 14300000256 | tf_op jit(solution)/shard_map/proj_fwd/pallas_call | solution.py:136
  136.4 12.1 %attn_fwd.3 = (f32[384,1024]{1,0:T(8,128)}, f32[3,8,1024]{2,1,0:T(8,128)}) custom-call(bf16[1024,384]{1,0:T(8,128)(2,1)} %get-tuple-element.402.k_ref, bf16[384,1024]{1,0:T(8,128)(2,1)} %get-tuple-element.403.qt_ref, bf16[384,1024]{1,0:T(8,128)(2,1)} %get-tuple-element.404.vt_ref), custom_call_target="tpu_custom_call" | custom-call | flops 20899999744 | tf_op jit(solution)/shard_map/attn_fwd/pallas_call | solution.py:284
  148.5 24.4 %ffn_fwd.3 = (bf16[1024,768]{1,0:T(8,128)(2,1)}, bf16[1024,768]{1,0:T(8,128)(2,1)}, f32[1024,1]{1,0:T(8,128)}, bf16[1024,768]{1,0:T(8,128)(2,1)}, bf16[1024,3072...) custom-call(s32[2]{0:T(128)} %get-tuple-element.722.place_ref, ...), custom_call_target="tpu_custom_call" | custom-call | flops 24199999488 | tf_op jit(solution)/shard_map/ffn_fwd/pallas_call | solution.py:136
  174.5 19.7 %ffn_bwd.2 = (bf16[1024,768]{1,0:T(8,128)(2,1)}, bf16[1024,3072]{1,0:T(8,128)(2,1)}, bf16[1024,768]{1,0:T(8,128)(2,1)}, bf16[384,1024]{1,0:T(8,128)(2,1)}, bf16[...) custom-call(s32[2]{0:T(128)} %get-tuple-element.722.place_ref, ...), custom_call_target="tpu_custom_call" | custom-call | flops 19800000512 | tf_op jit(solution)/shard_map/ffn_bwd/pallas_call | solution.py:136
  194.1 10.9 %ffn_wgrad.2 = bf16[2,1536,768]{2,1,0:T(8,128)(2,1)} custom-call(bf16[1024,768]{1,0:T(8,128)(2,1)} %get-tuple-element.425.nl_ref, bf16[1024,3072]{1,0:T(8,128)(2,1)} %get-tuple-element.426.di_ref, bf16[1024,768]{1,0:T(8,128)(2,1)} %get-tuple-element.427.ds_ref, bf16[1024,3072]{1,0:T(8,128)(2,1)} %get-tuple-element.428.act_ref), custom_call_target="tpu_custom_call" | custom-call | flops 6600000000 | tf_op jit(solution)/shard_map/ffn_wgrad/pallas_call | solution.py:694
  205.1 18.2 %attn_bwd.2 = (bf16[1024,384]{1,0:T(8,128)(2,1)}, bf16[1024,384]{1,0:T(8,128)(2,1)}, bf16[1024,384]{1,0:T(8,128)(2,1)}, f32[1,384]{1,0:T(1,128)}) custom-call(bf16[1024,384]{1,0:T(8,128)(2,1)} %get-tuple-element.402.k_ref, bf16[1024,384]{1,0:T(8,128)(2,1)} %get-tuple-element.417.v_ref, bf16[1024,384]{1,0:T(8,128)(2,1)} %get-tuple-element.418.q2_ref.refs_9_, ...), custom_call_target="tpu_custom_call" | custom-call | flops 22000001024 | tf_op jit(solution)/shard_map/attn_bwd/pallas_call | solution.py:645
  223.3 7.2 %mid_wgrad.2 = bf16[1536,768]{1,0:T(8,128)(2,1)} custom-call(bf16[1024,768]{1,0:T(8,128)(2,1)} %get-tuple-element.439.ctx_ref, bf16[1024,768]{1,0:T(8,128)(2,1)} %get-tuple-element.440.dz_ref.refs_11_, bf16[1024,768]{1,0:T(8,128)(2,1)} %get-tuple-element.398.refs_6_.refs_14_.h_ref.refs_10_.refs_5_, ...), custom_call_target="tpu_custom_call" | custom-call | flops 5500000256 | tf_op jit(solution)/shard_map/mid_wgrad/pallas_call | solution.py:717
  233.0 22.4 %conv_bwd.2 = (bf16[1024,72]{1,0:T(8,128)(2,1)}, bf16[1024,384]{1,0:T(8,128)(2,1)}, bf16[1024,384]{1,0:T(8,128)(2,1)}, bf16[1024,384]{1,0:T(8,128)(2,1)}, bf16[1...) custom-call(s32[2]{0:T(128)} %get-tuple-element.722.place_ref, ...), custom_call_target="tpu_custom_call" | custom-call | flops 29699999744 | tf_op jit(solution)/shard_map/conv_bwd/pallas_call | solution.py:136
  258.6 11.1 %collective-permute-done.14 = bf16[1024,768]{1,0:T(8,128)(2,1)S(1)} collective-permute-done((bf16[1024,768]{1,0:T(8,128)(2,1)S(1)}, bf16[1024,768]{1,0:T(8,128)(2,1)S(1)}, u32[]{:S(2)}, u32[]{:S(2)}) %collective-permute-start.14) | collective-permute-done | bytes 1572896 | tf_op jit(solution)/shard_map/ppermute | solution.py:872
  273.3 10.8 %last_wgrad.2 = (bf16[1152,768]{1,0:T(8,128)(2,1)}, f32[72,384]{1,0:T(8,128)}, f32[8,768]{1,0:T(8,128)}) custom-call(s32[2]{0:T(128)} %get-tuple-element.722.place_ref, bf16[768,1536]{1,0:T(8,128)(2,1)} %bitcast.91, bf16[240,1536]{1,0:T(8,128)(2,1)} %collective-permute-done.refs_2_.refs_1_, bf16[240,1536]{1,0:T(8,128)(2,1)} %collective-permute-done.1.refs_3_.refs_2_, ...), custom_call_target="tpu_custom_call" | custom-call | flops 9900000256 | tf_op jit(solution)/shard_map/last_wgrad/pallas_call | solution.py:136
  290.1 8.6 %in_bwd.2.refs_11_ = bf16[1024,768]{1,0:T(8,128)(2,1)} custom-call(s32[2]{0:T(128)} %get-tuple-element.722.place_ref, bf16[768,1536]{1,0:T(8,128)(2,1)} %bitcast.92, bf16[240,1536]{1,0:T(8,128)(2,1)} %collective-permute-done.refs_2_.refs_1_, bf16[240,1536]{1,0:T(8,128)(2,1)} %collective-permute-done.1.refs_3_.refs_2_, ...), custom_call_target="tpu_custom_call" | custom-call | flops 8800000000 | tf_op jit(solution)/shard_map/in_bwd/pallas_call | solution.py:136
  301.9 19.2 %ffn_bwd.3 = (bf16[1024,768]{1,0:T(8,128)(2,1)}, bf16[1024,3072]{1,0:T(8,128)(2,1)}, bf16[1024,768]{1,0:T(8,128)(2,1)}, bf16[384,1024]{1,0:T(8,128)(2,1)}, bf16[...) custom-call(s32[2]{0:T(128)} %get-tuple-element.722.place_ref, ...), custom_call_target="tpu_custom_call" | custom-call | flops 19800000512 | tf_op jit(solution)/shard_map/ffn_bwd/pallas_call | solution.py:136
  327.6 10.9 %ffn_wgrad.3 = bf16[2,1536,768]{2,1,0:T(8,128)(2,1)} custom-call(bf16[1024,768]{1,0:T(8,128)(2,1)} %get-tuple-element.505.nl_ref, bf16[1024,3072]{1,0:T(8,128)(2,1)} %get-tuple-element.506.di_ref, bf16[1024,768]{1,0:T(8,128)(2,1)} %get-tuple-element.507.ds_ref, bf16[1024,3072]{1,0:T(8,128)(2,1)} %get-tuple-element.508.act_ref), custom_call_target="tpu_custom_call" | custom-call | flops 6600000000 | tf_op jit(solution)/shard_map/ffn_wgrad/pallas_call | solution.py:694
  344.8 18.7 %attn_bwd.3 = (bf16[1024,384]{1,0:T(8,128)(2,1)}, bf16[1024,384]{1,0:T(8,128)(2,1)}, bf16[1024,384]{1,0:T(8,128)(2,1)}, f32[1,384]{1,0:T(1,128)}) custom-call(bf16[1024,384]{1,0:T(8,128)(2,1)} %get-tuple-element.382.k_ref, bf16[1024,384]{1,0:T(8,128)(2,1)} %get-tuple-element.488.v_ref, bf16[1024,384]{1,0:T(8,128)(2,1)} %get-tuple-element.489.q2_ref.refs_9_, ...), custom_call_target="tpu_custom_call" | custom-call | flops 22000001024 | tf_op jit(solution)/shard_map/attn_bwd/pallas_call | solution.py:645
  366.1 7.2 %mid_wgrad.3 = bf16[1536,768]{1,0:T(8,128)(2,1)} custom-call(bf16[1024,768]{1,0:T(8,128)(2,1)} %get-tuple-element.528.ctx_ref, bf16[1024,768]{1,0:T(8,128)(2,1)} %get-tuple-element.529.dz_ref.refs_11_, bf16[1024,768]{1,0:T(8,128)(2,1)} %bitcast_select_fusion.refs_6_.refs_14_.h_ref.refs_10_.refs_5_, ...), custom_call_target="tpu_custom_call" | custom-call | flops 5500000256 | tf_op jit(solution)/shard_map/mid_wgrad/pallas_call | solution.py:717
  375.3 22.4 %conv_bwd.3 = (bf16[1024,72]{1,0:T(8,128)(2,1)}, bf16[1024,384]{1,0:T(8,128)(2,1)}, bf16[1024,384]{1,0:T(8,128)(2,1)}, bf16[1024,384]{1,0:T(8,128)(2,1)}, bf16[1...) custom-call(s32[2]{0:T(128)} %get-tuple-element.722.place_ref, ...), custom_call_target="tpu_custom_call" | custom-call | flops 29699999744 | tf_op jit(solution)/shard_map/conv_bwd/pallas_call | solution.py:136
  404.7 11.0 %last_wgrad.3 = (bf16[1152,768]{1,0:T(8,128)(2,1)}, f32[72,384]{1,0:T(8,128)}, f32[8,768]{1,0:T(8,128)}) custom-call(s32[2]{0:T(128)} %get-tuple-element.722.place_ref, bf16[768,1536]{1,0:T(8,128)(2,1)} %bitcast.93, bf16[240,1536]{1,0:T(8,128)(2,1)} %collective-permute-done.refs_2_.refs_1_, bf16[240,1536]{1,0:T(8,128)(2,1)} %collective-permute-done.1.refs_3_.refs_2_, ...), custom_call_target="tpu_custom_call" | custom-call | flops 9900000256 | tf_op jit(solution)/shard_map/last_wgrad/pallas_call | solution.py:136
  422.8 8.5 %in_bwd.3 = bf16[1024,768]{1,0:T(8,128)(2,1)} custom-call(s32[2]{0:T(128)} %get-tuple-element.722.place_ref, bf16[768,1536]{1,0:T(8,128)(2,1)} %bitcast.94, bf16[240,1536]{1,0:T(8,128)(2,1)} %collective-permute-done.refs_2_.refs_1_, bf16[240,1536]{1,0:T(8,128)(2,1)} %collective-permute-done.1.refs_3_.refs_2_, ...), custom_call_target="tpu_custom_call" | custom-call | flops 8800000000 | tf_op jit(solution)/shard_map/in_bwd/pallas_call | solution.py:136
  441.8 6.8 %collective-permute-done.27 = bf16[192,384]{1,0:T(8,128)(2,1)S(1)} collective-permute-done((bf16[192,384]{1,0:T(8,128)(2,1)S(1)}, bf16[192,384]{1,0:T(8,128)(2,1)S(1)}, u32[]{:S(2)}, u32[]{:S(2)}) %collective-permute-start.27) | collective-permute-done | bytes 147488 | tf_op jit(solution)/shard_map/ppermute | solution.py:876
  471.0 8.2 %collective-permute-done.32 = bf16[80,768]{1,0:T(8,128)(2,1)S(1)} collective-permute-done((bf16[80,768]{1,0:T(8,128)(2,1)S(1)}, bf16[80,768]{1,0:T(8,128)(2,1)S(1)}, u32[]{:S(2)}, u32[]{:S(2)}) %collective-permute-start.32) | collective-permute-done | bytes 122912 | tf_op jit(solution)/shard_map/ppermute | solution.py:876
  491.1 31.8 %collective-permute-done.36 = bf16[80,768]{1,0:T(8,128)(2,1)S(1)} collective-permute-done((bf16[80,768]{1,0:T(8,128)(2,1)S(1)}, bf16[80,768]{1,0:T(8,128)(2,1)S(1)}, u32[]{:S(2)}, u32[]{:S(2)}) %collective-permute-start.36) | collective-permute-done | bytes 122912 | tf_op jit(solution)/shard_map/ppermute | solution.py:876
  526.0 18.6 %collective-permute-done.38 = bf16[160,768]{1,0:T(8,128)(2,1)S(1)} collective-permute-done((bf16[160,768]{1,0:T(8,128)(2,1)S(1)}, bf16[160,768]{1,0:T(8,128)(2,1)S(1)}, u32[]{:S(2)}, u32[]{:S(2)}) %collective-permute-start.38) | collective-permute-done | bytes 245792 | tf_op jit(solution)/shard_map/ppermute | solution.py:876
  547.8 13.6 %collective-permute-done.41 = bf16[320,768]{1,0:T(8,128)(2,1)S(1)} collective-permute-done((bf16[320,768]{1,0:T(8,128)(2,1)S(1)}, bf16[320,768]{1,0:T(8,128)(2,1)S(1)}, u32[]{:S(2)}, u32[]{:S(2)}) %collective-permute-start.41) | collective-permute-done | bytes 491552 | tf_op jit(solution)/shard_map/ppermute | solution.py:876
  567.3 6.6 %wide_out.1 = (f32[768,1536]{1,0:T(8,128)}, f32[3072,384]{1,0:T(8,128)}) custom-call(s32[1]{0:T(128)} %constant.674.clone.1._, bf16[3072,768]{1,0:T(8,128)(2,1)} %all-gather.2.cloned.1.call-done.a_ref.b_ref, bf16[3072,768]{1,0:T(8,128)(2,1)} %all-gather.2.cloned.1.call-done.a_ref.b_ref), custom_call_target="tpu_custom_call" | custom-call | flops 6600000000 | tf_op jit(solution)/shard_map/wide_out/pallas_call | solution.py:1005
  574.8 6.2 %last_out.1 = (f32[768,1536]{1,0:T(8,128)}, f32[768,384]{1,0:T(8,128)}, f32[768,768]{1,0:T(8,128)}, f32[1,1152]{1,0:T(1,128)}, f32[9,768]{1,0:T(8,128)}, /*index...) custom-call(s32[2]{0:T(128)} %get-tuple-element.723.at_ref, ...), custom_call_target="tpu_custom_call" | custom-call | flops 6600000000 | tf_op jit(solution)/shard_map/last_out/pallas_call | solution.py:1075
  (329 shorter events, 144.1 us)
Async XLA Ops:
  7.2 332.0 %reduce-scatter.3.cloned.1.call-start = ((), (), s32[]{:S(2)}) async-start(), calls=%async_computation.2 | async-start | bytes 5013504 | tf_op jit(solution)/shard_map/reduce_scatter | solution.py:883
  11.8 19.8 %collective-permute-start = (bf16[240,1536]{1,0:T(8,128)(2,1)}, bf16[240,1536]{1,0:T(8,128)(2,1)}, u32[]{:S(2)}, u32[]{:S(2)}) collective-permute-start(bf16[240,1536]{1,0:T(8,128)(2,1)} %get-tuple-element.348), channel_id=1, source_target_pairs={{0,16},{16,0},{1,17},{17,1},{2,18},{18,2},{3,19},{19,3},{4,20},{20... | collective-permute-start | bytes 2211848 | tf_op jit(solution)/shard_map/ppermute | solution.py:872
  32.2 23.5 %collective-permute-start.3 = (bf16[288,1536]{1,0:T(8,128)(2,1)S(1)}, bf16[288,1536]{1,0:T(8,128)(2,1)S(1)}, u32[]{:S(2)}, u32[]{:S(2)}) collective-permute-start(bf16[288,1536]{1,0:T(8,128)(2,1)S(1)} %copy-done.49), channel_id=1, source_target_pairs={{0,16},{16,0},{1,17},{17,1},{2,18},{18,2},{3,19},{19,3},{4,20},{20... | collective-permute-start | bytes 2654216 | tf_op jit(solution)/shard_map/ppermute | solution.py:872
  33.9 21.7 %collective-permute-start.1 = (bf16[240,1536]{1,0:T(8,128)(2,1)}, bf16[240,1536]{1,0:T(8,128)(2,1)}, u32[]{:S(2)}, u32[]{:S(2)}) collective-permute-start(bf16[240,1536]{1,0:T(8,128)(2,1)} %collective-permute-done.refs_2_.refs_1_), channel_id=1, source_target_pairs={{0,2},{1,3},{2,0},{3,1},{4,6},{5,7},{6,4},{7,5},{8,10},{9,11},{10,... | collective-permute-start | bytes 2211848 | tf_op jit(solution)/shard_map/ppermute | solution.py:876
  35.4 20.2 %collective-permute-start.2 = (bf16[240,1536]{1,0:T(8,128)(2,1)}, bf16[240,1536]{1,0:T(8,128)(2,1)}, u32[]{:S(2)}, u32[]{:S(2)}) collective-permute-start(bf16[240,1536]{1,0:T(8,128)(2,1)} %collective-permute-done.refs_2_.refs_1_), channel_id=1, source_target_pairs={{0,1},{1,0},{2,3},{3,2},{4,5},{5,4},{6,7},{7,6},{8,9},{9,8},{10,11... | collective-permute-start | bytes 2211848 | tf_op jit(solution)/shard_map/ppermute | solution.py:876
  35.4 20.2 %collective-permute-start.4 = (bf16[76,768]{1,0:T(8,128)(2,1)S(1)}, bf16[76,768]{1,0:T(8,128)(2,1)S(1)}, u32[]{:S(2)}, u32[]{:S(2)}) collective-permute-start(bf16[76,768]{1,0:T(8,128)(2,1)S(1)} %fusion.12), channel_id=1, source_target_pairs={{0,16},{16,0},{1,17},{17,1},{2,18},{18,2},{3,19},{19,3},{4,20},{20... | collective-permute-start | bytes 350216 | tf_op jit(solution)/shard_map/ppermute | solution.py:872
  57.5 22.0 %collective-permute-start.6 = (bf16[288,1536]{1,0:T(8,128)(2,1)S(1)}, bf16[288,1536]{1,0:T(8,128)(2,1)S(1)}, u32[]{:S(2)}, u32[]{:S(2)}) collective-permute-start(bf16[288,1536]{1,0:T(8,128)(2,1)S(1)} %collective-permute-done.3.refs_2_), channel_id=1, source_target_pairs={{0,2},{1,3},{2,0},{3,1},{4,6},{5,7},{6,4},{7,5},{8,10},{9,11},{10,... | collective-permute-start | bytes 2654216 | tf_op jit(solution)/shard_map/ppermute | solution.py:876
  59.0 20.5 %collective-permute-start.7 = (bf16[288,1536]{1,0:T(8,128)(2,1)S(1)}, bf16[288,1536]{1,0:T(8,128)(2,1)S(1)}, u32[]{:S(2)}, u32[]{:S(2)}) collective-permute-start(bf16[288,1536]{1,0:T(8,128)(2,1)S(1)} %collective-permute-done.3.refs_2_), channel_id=1, source_target_pairs={{0,1},{1,0},{2,3},{3,2},{4,5},{5,4},{6,7},{7,6},{8,9},{9,8},{10,11... | collective-permute-start | bytes 2654216 | tf_op jit(solution)/shard_map/ppermute | solution.py:876
  59.1 15.8 %collective-permute-start.8 = (bf16[192,1536]{1,0:T(8,128)(2,1)}, bf16[192,1536]{1,0:T(8,128)(2,1)S(1)}, u32[]{:S(2)}, u32[]{:S(2)}) collective-permute-start(bf16[192,1536]{1,0:T(8,128)(2,1)} %get-tuple-element.375), channel_id=1, source_target_pairs={{0,16},{16,0},{1,17},{17,1},{2,18},{18,2},{3,19},{19,3},{4,20},{20... | collective-permute-start | bytes 1769480 | tf_op jit(solution)/shard_map/ppermute | solution.py:872
  79.5 15.9 %collective-permute-start.9 = (bf16[288,1536]{1,0:T(8,128)(2,1)S(1)}, bf16[288,1536]{1,0:T(8,128)(2,1)S(1)}, u32[]{:S(2)}, u32[]{:S(2)}) collective-permute-start(bf16[288,1536]{1,0:T(8,128)(2,1)S(1)} %collective-permute-done.6.refs_3_), channel_id=1, source_target_pairs={{0,1},{1,0},{2,3},{3,2},{4,5},{5,4},{6,7},{7,6},{8,9},{9,8},{10,11... | collective-permute-start | bytes 2654216 | tf_op jit(solution)/shard_map/ppermute | solution.py:876
  79.6 15.8 %collective-permute-start.10 = (bf16[192,1536]{1,0:T(8,128)(2,1)S(1)}, bf16[192,1536]{1,0:T(8,128)(2,1)}, u32[]{:S(2)}, u32[]{:S(2)}) collective-permute-start(bf16[192,1536]{1,0:T(8,128)(2,1)S(1)} %collective-permute-done.8.refs_7_), channel_id=1, source_target_pairs={{0,2},{1,3},{2,0},{3,1},{4,6},{5,7},{6,4},{7,5},{8,10},{9,11},{10,... | collective-permute-start | bytes 1769480 | tf_op jit(solution)/shard_map/ppermute | solution.py:876
  81.1 14.3 %collective-permute-start.11 = (bf16[192,1536]{1,0:T(8,128)(2,1)S(1)}, bf16[192,1536]{1,0:T(8,128)(2,1)S(1)}, u32[]{:S(2)}, u32[]{:S(2)}) collective-permute-start(bf16[192,1536]{1,0:T(8,128)(2,1)S(1)} %collective-permute-done.8.refs_7_), channel_id=1, source_target_pairs={{0,1},{1,0},{2,3},{3,2},{4,5},{5,4},{6,7},{7,6},{8,9},{9,8},{10,11... | collective-permute-start | bytes 1769480 | tf_op jit(solution)/shard_map/ppermute | solution.py:876
  232.9 25.7 %collective-permute-start.13 = (bf16[768,768]{1,0:T(8,128)(2,1)}, bf16[768,768]{1,0:T(8,128)(2,1)}, u32[]{:S(2)}, u32[]{:S(2)}) collective-permute-start(bf16[768,768]{1,0:T(8,128)(2,1)} %constant_dynamic-slice_fusion.3), channel_id=1, source_target_pairs={{0,1},{1,0},{2,3},{3,2},{4,5},{5,4},{6,7},{7,6},{8,9},{9,8},{10,11... | collective-permute-start | bytes 3538952 | tf_op jit(solution)/shard_map/ppermute | solution.py:876
  232.9 36.8 %collective-permute-start.14 = (bf16[1024,768]{1,0:T(8,128)(2,1)S(1)}, bf16[1024,768]{1,0:T(8,128)(2,1)S(1)}, u32[]{:S(2)}, u32[]{:S(2)}) collective-permute-start(bf16[1024,768]{1,0:T(8,128)(2,1)S(1)} %broadcast_select_fusion.2), channel_id=1, source_target_pairs={{0,16},{16,0},{1,17},{17,1},{2,18},{18,2},{3,19},{19,3},{4,20},{20... | collective-permute-start | bytes 4718600 | tf_op jit(solution)/shard_map/ppermute | solution.py:872
  232.9 199.8 %reduce-scatter.5.cloned.1.call-start = ((), (), s32[]{:S(2)}) async-start(), calls=%async_computation.3 | async-start | bytes 5013504 | tf_op jit(solution)/shard_map/reduce_scatter | solution.py:883
  298.7 23.9 %collective-permute-start.16 = (bf16[768,384]{1,0:T(8,128)(2,1)}, bf16[768,384]{1,0:T(8,128)(2,1)}, u32[]{:S(2)}, u32[]{:S(2)}) collective-permute-start(bf16[768,384]{1,0:T(8,128)(2,1)} %add_convert_fusion.1), channel_id=1, source_target_pairs={{0,16},{16,0},{1,17},{17,1},{2,18},{18,2},{3,19},{19,3},{4,20},{20... | collective-permute-start | bytes 1769480 | tf_op jit(solution)/shard_map/ppermute | solution.py:872
  300.3 22.3 %collective-permute-start.17 = (bf16[320,768]{1,0:T(8,128)(2,1)S(1)}, bf16[320,768]{1,0:T(8,128)(2,1)S(1)}, u32[]{:S(2)}, u32[]{:S(2)}) collective-permute-start(bf16[320,768]{1,0:T(8,128)(2,1)S(1)} %add_convert_fusion.3), channel_id=1, source_target_pairs={{0,2},{1,3},{2,0},{3,1},{4,6},{5,7},{6,4},{7,5},{8,10},{9,11},{10,... | collective-permute-start | bytes 1474568 | tf_op jit(solution)/shard_map/ppermute | solution.py:876
  325.5 13.7 %collective-permute-start.18 = (bf16[384,384]{1,0:T(8,128)(2,1)S(1)}, bf16[384,384]{1,0:T(8,128)(2,1)S(1)}, u32[]{:S(2)}, u32[]{:S(2)}) collective-permute-start(bf16[384,384]{1,0:T(8,128)(2,1)S(1)} %add_convert_fusion.6), channel_id=1, source_target_pairs={{0,4},{1,5},{2,6},{3,7},{4,0},{5,1},{6,2},{7,3},{8,12},{9,13},{10,... | collective-permute-start | bytes 884744 | tf_op jit(solution)/shard_map/ppermute | solution.py:876
  341.7 22.5 %collective-permute-start.20 = (bf16[192,384]{1,0:T(8,128)(2,1)S(1)}, bf16[192,384]{1,0:T(8,128)(2,1)S(1)}, u32[]{:S(2)}, u32[]{:S(2)}) collective-permute-start(bf16[192,384]{1,0:T(8,128)(2,1)S(1)} %add_convert_fusion.10), channel_id=1, source_target_pairs={{0,8},{1,9},{2,10},{3,11},{4,12},{5,13},{6,14},{7,15},{8,0},{9,1},... | collective-permute-start | bytes 442376 | tf_op jit(solution)/shard_map/ppermute | solution.py:876
  344.2 19.9 %collective-permute-start.21 = (bf16[80,768]{1,0:T(8,128)(2,1)S(1)}, bf16[80,768]{1,0:T(8,128)(2,1)S(1)}, u32[]{:S(2)}, u32[]{:S(2)}) collective-permute-start(bf16[80,768]{1,0:T(8,128)(2,1)S(1)} %add_convert_fusion.15), channel_id=1, source_target_pairs={{0,8},{1,9},{2,10},{3,11},{4,12},{5,13},{6,14},{7,15},{8,0},{9,1},... | collective-permute-start | bytes 368648 | tf_op jit(solution)/shard_map/ppermute | solution.py:876
  344.7 217.4 %all-gather.2.cloned.1.call-start = ((), (), s32[]{:S(2)}) async-start(), calls=%async_computation.4 | async-start | bytes 5013504 | tf_op jit(solution)/shard_map/all_gather | solution.py:885
  375.3 25.6 %collective-permute-start.23 = (bf16[768,768]{1,0:T(8,128)(2,1)S(1)}, bf16[768,768]{1,0:T(8,128)(2,1)S(1)}, u32[]{:S(2)}, u32[]{:S(2)}) collective-permute-start(bf16[768,768]{1,0:T(8,128)(2,1)S(1)} %constant_dynamic-slice_fusion.1), channel_id=1, source_target_pairs={{0,1},{1,0},{2,3},{3,2},{4,5},{5,4},{6,7},{7,6},{8,9},{9,8},{10,11... | collective-permute-start | bytes 3538952 | tf_op jit(solution)/shard_map/ppermute | solution.py:876
  403.2 16.0 %collective-permute-start.24 = (bf16[768,384]{1,0:T(8,128)(2,1)}, bf16[768,384]{1,0:T(8,128)(2,1)}, u32[]{:S(2)}, u32[]{:S(2)}) collective-permute-start(bf16[768,384]{1,0:T(8,128)(2,1)} %add_convert_fusion), channel_id=1, source_target_pairs={{0,16},{16,0},{1,17},{17,1},{2,18},{18,2},{3,19},{19,3},{4,20},{20... | collective-permute-start | bytes 1769480 | tf_op jit(solution)/shard_map/ppermute | solution.py:872
  435.5 13.4 %collective-permute-start.28 = (bf16[320,768]{1,0:T(8,128)(2,1)S(1)}, bf16[320,768]{1,0:T(8,128)(2,1)}, u32[]{:S(2)}, u32[]{:S(2)}) collective-permute-start(bf16[320,768]{1,0:T(8,128)(2,1)S(1)} %add_convert_fusion.2), channel_id=1, source_target_pairs={{0,2},{1,3},{2,0},{3,1},{4,6},{5,7},{6,4},{7,5},{8,10},{9,11},{10,... | collective-permute-start | bytes 1474568 | tf_op jit(solution)/shard_map/ppermute | solution.py:876
  464.8 14.4 %collective-permute-start.32 = (bf16[80,768]{1,0:T(8,128)(2,1)S(1)}, bf16[80,768]{1,0:T(8,128)(2,1)S(1)}, u32[]{:S(2)}, u32[]{:S(2)}) collective-permute-start(bf16[80,768]{1,0:T(8,128)(2,1)S(1)} %add_convert_fusion.14), channel_id=1, source_target_pairs={{0,8},{1,9},{2,10},{3,11},{4,12},{5,13},{6,14},{7,15},{8,0},{9,1},... | collective-permute-start | bytes 368648 | tf_op jit(solution)/shard_map/ppermute | solution.py:876
  486.3 36.7 %collective-permute-start.37 = (bf16[192,768]{1,0:T(8,128)(2,1)S(1)}, bf16[192,768]{1,0:T(8,128)(2,1)S(1)}, u32[]{:S(2)}, u32[]{:S(2)}) collective-permute-start(bf16[192,768]{1,0:T(8,128)(2,1)S(1)} %pad_maximum_fusion.6), channel_id=1, source_target_pairs={{0,8},{1,9},{2,10},{3,11},{4,12},{5,13},{6,14},{7,15},{8,0},{9,1},... | collective-permute-start | bytes 884744 | tf_op jit(solution)/shard_map/ppermute | solution.py:876
  486.4 58.2 %collective-permute-start.40 = (bf16[1024,768]{1,0:T(8,128)(2,1)S(1)}, bf16[1024,768]{1,0:T(8,128)(2,1)}, u32[]{:S(2)}, u32[]{:S(2)}) collective-permute-start(bf16[1024,768]{1,0:T(8,128)(2,1)S(1)} %copy-done.8), channel_id=1, source_target_pairs={{0,16},{16,0},{1,17},{17,1},{2,18},{18,2},{3,19},{19,3},{4,20},{20... | collective-permute-start | bytes 4718600 | tf_op jit(solution)/shard_map/ppermute | solution.py:872
  488.3 34.6 %collective-permute-start.36 = (bf16[80,768]{1,0:T(8,128)(2,1)S(1)}, bf16[80,768]{1,0:T(8,128)(2,1)S(1)}, u32[]{:S(2)}, u32[]{:S(2)}) collective-permute-start(bf16[80,768]{1,0:T(8,128)(2,1)S(1)} %add_convert_fusion.11), channel_id=1, source_target_pairs={{0,8},{1,9},{2,10},{3,11},{4,12},{5,13},{6,14},{7,15},{8,0},{9,1},... | collective-permute-start | bytes 368648 | tf_op jit(solution)/shard_map/ppermute | solution.py:876
  523.9 20.7 %collective-permute-start.39 = (bf16[384,768]{1,0:T(8,128)(2,1)}, bf16[384,768]{1,0:T(8,128)(2,1)}, u32[]{:S(2)}, u32[]{:S(2)}) collective-permute-start(bf16[384,768]{1,0:T(8,128)(2,1)} %pad_maximum_fusion.4), channel_id=1, source_target_pairs={{0,4},{1,5},{2,6},{3,7},{4,0},{5,1},{6,2},{7,3},{8,12},{9,13},{10,... | collective-permute-start | bytes 1769480 | tf_op jit(solution)/shard_map/ppermute | solution.py:876
  523.9 20.6 %collective-permute-start.38 = (bf16[160,768]{1,0:T(8,128)(2,1)S(1)}, bf16[160,768]{1,0:T(8,128)(2,1)S(1)}, u32[]{:S(2)}, u32[]{:S(2)}) collective-permute-start(bf16[160,768]{1,0:T(8,128)(2,1)S(1)} %pad_maximum_fusion.7), channel_id=1, source_target_pairs={{0,4},{1,5},{2,6},{3,7},{4,0},{5,1},{6,2},{7,3},{8,12},{9,13},{10,... | collective-permute-start | bytes 737288 | tf_op jit(solution)/shard_map/ppermute | solution.py:876
  547.8 14.4 %collective-permute-start.42 = (bf16[768,768]{1,0:T(8,128)(2,1)S(1)}, bf16[768,768]{1,0:T(8,128)(2,1)}, u32[]{:S(2)}, u32[]{:S(2)}) collective-permute-start(bf16[768,768]{1,0:T(8,128)(2,1)S(1)} %pad_maximum_fusion.2.mid_ref), channel_id=1, source_target_pairs={{0,1},{1,0},{2,3},{3,2},{4,5},{5,4},{6,7},{7,6},{8,9},{9,8},{10,11... | collective-permute-start | bytes 3538952 | tf_op jit(solution)/shard_map/ppermute | solution.py:876
  547.8 13.6 %collective-permute-start.41 = (bf16[320,768]{1,0:T(8,128)(2,1)S(1)}, bf16[320,768]{1,0:T(8,128)(2,1)S(1)}, u32[]{:S(2)}, u32[]{:S(2)}) collective-permute-start(bf16[320,768]{1,0:T(8,128)(2,1)S(1)} %pad_maximum_fusion.5), channel_id=1, source_target_pairs={{0,2},{1,3},{2,0},{3,1},{4,6},{5,7},{6,4},{7,5},{8,10},{9,11},{10,... | collective-permute-start | bytes 1474568 | tf_op jit(solution)/shard_map/ppermute | solution.py:876
  (69 other events, 601.1 us)
Sparse Core Ops, SparseCore 0:
  233.0 77.1 reduce-scatter.2
  344.8 75.6 reduce-scatter.4
  454.1 71.0 all-gather.1

commit v4 on v3

--- a/solution.py
+++ b/solution.py
@@ -56,12 +56,14 @@
 SMEM = pl.BlockSpec(memory_space=pltpu.SMEM)
 
 
-def copies(pairs, sems):
+def copies(pairs, sems, start=True, wait=True):
     all_copies = [pltpu.make_async_copy(src, dst, sems.at[n]) for n, (src, dst) in enumerate(pairs)]
-    for c in all_copies:
-        c.start()
-    for c in all_copies:
-        c.wait()
+    if start:
+        for c in all_copies:
+            c.start()
+    if wait:
+        for c in all_copies:
+            c.wait()
 
 
 def tile_pairs(buffer, at, array, start, shape):
@@ -78,12 +80,12 @@
 GROUPS = {"A": ("wp", "pw"), "B": ("w1", "wo"), "C": ("w2",)}
 
 
-def fetch(place_ref, layer, name, shapes, own, pieces, into, sems):
+def fetch(place_ref, layer, name, shapes, own, pieces, into, sems, start, wait):
     mine = place_ref[1] == layer
 
     @pl.when(mine)
     def _():
-        copies([(own[n], into[n]) for n in into], sems)
+        copies([(own[n], into[n]) for n in into], sems, start, wait)
 
     @pl.when(jnp.logical_not(mine))
     def _():
@@ -96,7 +98,7 @@
                 if n in into:
                     pairs += tile_pairs(got, at, into[n], (place_ref[0] ^ j) * (rows // 4), shapes[n])[0]
                 at += lines
-        copies(pairs, sems)
+        copies(pairs, sems, start, wait)
 
 
 def call(kernel, p, wants, inputs, *, grid, in_specs, out_specs, out_shape, scratch_shapes=(), name, us):
@@ -122,16 +124,19 @@
         for axis in range(1, len(grid)):
             first = first & (pl.program_id(axis) == 0)
 
-        @pl.when(first)
-        def _():
-            at = 0
-            for g, names in layout:
-                own = dict(zip(names, sources[at : at + len(names)]))
-                pieces = sources[at + len(names) : at + len(names) + 4]
-                at += len(names) + 4
-                fetch(place_ref, p["l"], g, shapes, own, pieces, {n: into[n] for n in names}, refs[-1])
-
-        kernel(*[into[n] for n in wants], *rest)
+        def weights(start, wait):
+            @pl.when(first)
+            def _():
+                at = 0
+                for n, (g, names) in enumerate(layout):
+                    own = dict(zip(names, sources[at : at + len(names)]))
+                    pieces = sources[at + len(names) : at + len(names) + 4]
+                    at += len(names) + 4
+                    fetch(place_ref, p["l"], g, shapes, own, pieces, {n: into[n] for n in names}, refs[-1].at[n],
+                          start, wait)
+
+        weights(True, False)
+        kernel(lambda: weights(False, True), *[into[n] for n in wants], *rest)
 
     return pl.pallas_call(
         body,
@@ -141,7 +146,7 @@
         out_shape=out_shape,
         scratch_shapes=list(scratch_shapes)
         + [pltpu.VMEM(shapes[n], BF) for n in wants]
-        + [pltpu.SemaphoreType.DMA((tiles,))],
+        + [pltpu.SemaphoreType.DMA((len(layout), tiles))],
         compiler_params=params(),
         cost_estimate=cost(us),
         name=name,
@@ -192,7 +197,7 @@
 
 
 def proj_kernel(
-    wp_ref, pw_ref, h_ref, vec_ref, dk_ref, kwt_ref, kbt_ref,
+    ready, wp_ref, pw_ref, h_ref, vec_ref, dk_ref, kwt_ref, kbt_ref,
     q2_ref, k_ref, v_ref, sp_ref, q2t_ref, kt_ref, vt_ref, dep_ref, kc_ref, mx_ref, kern_ref,
     hp_ref,
 ):
@@ -206,6 +211,7 @@
     def _():
         fill_padded(hp_ref, h_ref)
 
+    ready()
     base = pl.multiple_of(i * RB, RB)
     hb = h_ref[pl.ds(base, RB), :]
     query = dot(hb, wp_ref[:, 0:att]) + vec_ref[:, 0:att]
@@ -282,7 +288,7 @@
     pairs = att // (2 * head)
     blk = pl.BlockSpec((2 * head, rows), lambda g: (g, 0))
     return pl.pallas_call(
-        partial(attn_kernel, head=head, qb=256),
+        partial(attn_kernel, head=head, qb=512),
         grid=(pairs,),
         in_specs=[pl.BlockSpec((rows, 2 * head), lambda g: (0, g)), blk, blk],
         out_specs=[blk, pl.BlockSpec((1, SUB, rows), lambda g: (g, 0, 0))],
@@ -294,7 +300,7 @@
 
 
 def ffn_kernel(
-    w1_ref, wo_ref, w2_ref, at_ref, sp_ref, kern_ref, h_ref, ex_ref, vec_ref,
+    ready, w1_ref, wo_ref, w2_ref, at_ref, sp_ref, kern_ref, h_ref, ex_ref, vec_ref,
     ctx_ref, u1_ref, r1_ref, nl_ref, act_ref, gp_ref, u2_ref, r2_ref, out_ref,
     spp_ref,
 ):
@@ -321,6 +327,7 @@
             kexp = dot(kn, ex_ref[j, :, cols])
             acc = acc + kexp * spp_ref[c, pl.ds(base + PAD - half + j, RB), :]
         ctx_ref[:, att + c * 128 : att + (c + 1) * 128] = acc.astype(BF)
+    ready()
     z = dot(ctx_ref[...], wo_ref[...]) + bo[...] + h_ref[...].astype(F32)
     u1, r1 = norm_rows(z)
     u1_ref[...] = u1.astype(BF)
@@ -392,7 +399,7 @@
 
 
 def ffn_back_kernel(
-    w1_ref, wo_ref, w2_ref, dy_ref, u2_ref, r2_ref, gp_ref, u1_ref, r1_ref, prm_ref,
+    ready, w1_ref, wo_ref, w2_ref, dy_ref, u2_ref, r2_ref, gp_ref, u1_ref, r1_ref, prm_ref,
     ds_ref, di_ref, dz_ref, dat_ref, dan_ref, ddn_ref, vec_ref, db1_ref,
 ):
     i = pl.program_id(0)
@@ -415,6 +422,7 @@
     vec_ref[2:3, :] += jnp.sum(dsum, axis=0, keepdims=True)
     dlow = dsum.astype(BF)
     ds_ref[...] = dlow
+    ready()
     fb = 512
     units = [(g, f) for g in range(groups) for f in range(gout // fb)]
 
@@ -465,7 +473,7 @@
 
 
 def conv_back_kernel(
-    pw_ref, ddn_ref, sp_ref, kern_ref, kc_ref, q2_ref, h_ref, dz_ref, ex_ref, ext_ref, kwt_ref, dk_ref, dqa_ref,
+    ready, pw_ref, ddn_ref, sp_ref, kern_ref, kc_ref, q2_ref, h_ref, dz_ref, ex_ref, ext_ref, kwt_ref, dk_ref, dqa_ref,
     dl_ref, dq_ref, dsp_ref, dkc_ref, res_ref, dkg_ref, dpb_ref, dkb_ref, dbp_ref,
     ddp_ref, spp_ref, hp_ref, dep_ref, knp_ref,
 ):
@@ -489,6 +497,7 @@
         dkb_ref[...] = jnp.zeros(dkb_ref.shape, F32)
         dbp_ref[...] = jnp.zeros(dbp_ref.shape, F32)
 
+    ready()
     base = pl.multiple_of(i * RB, RB)
 
     @pl.when(phase == 0)
@@ -643,7 +652,7 @@
     nat = pl.BlockSpec((rows, 2 * head), lambda g: (0, g))
     tra = pl.BlockSpec((2 * head, rows), lambda g: (g, 0))
     return pl.pallas_call(
-        partial(attn_back_kernel, head=head, qb=256),
+        partial(attn_back_kernel, head=head, qb=128),
         grid=(pairs,),
         in_specs=[nat, nat, nat, nat, tra, tra, tra, tra, pl.BlockSpec((1, SUB, rows), lambda g: (g, 0, 0))],
         out_specs=[nat] * 3 + [pl.BlockSpec((1, 2 * head), lambda g: (0, g))],
@@ -655,8 +664,9 @@
     )(keep["k"], keep["v"], keep["q2"], do, keep["q2t"], keep["kt"], dot_t, keep["at"], keep["lse"])
 
 
-def in_back_kernel(wp_ref, dq_ref, dk_ref, dv_ref, dsp_ref, res_ref, m_ref, dh_ref):
+def in_back_kernel(ready, wp_ref, dq_ref, dk_ref, dv_ref, dsp_ref, res_ref, m_ref, dh_ref):
     att = dq_ref.shape[1]
+    ready()
     dh = res_ref[...].astype(F32)
     for n, ref in enumerate((dq_ref, dk_ref, dv_ref, dsp_ref)):
         dh = dh + dot_nt(ref[...], wp_ref[:, n * att : (n + 1) * att])
@@ -724,7 +734,7 @@
 
 
 def last_grad_kernel(
-    wp_ref, h_ref, dq_ref, dk_ref, dv_ref, dsp_ref, dep_ref, dkc_ref, mx_ref, dl_ref, m_ref, res_ref,
+    ready, wp_ref, h_ref, dq_ref, dk_ref, dv_ref, dsp_ref, dep_ref, dkc_ref, mx_ref, dl_ref, m_ref, res_ref,
     out_ref, kw_ref, mg_ref,
 ):
     width = h_ref.shape[1]
@@ -734,6 +744,7 @@
     out_ref[0:width, att:] = dot(ht, dsp_ref[...]).astype(BF)
     out_ref[width : width + att, :] = dot(dkc_ref[...].T, dep_ref[...]).astype(BF)
     kw_ref[...] = dot(dl_ref[...].T, mx_ref[...])
+    ready()
     m = m_ref[...]
     total = dot(m, res_ref[...])
     for n, ref in enumerate((dq_ref, dk_ref, dv_ref, dsp_ref)):
@@ -1021,6 +1032,46 @@
         cost_estimate=cost(6),
         name="wide_out",
     )(place, full, full)
+
+
+def wide_pair_kernel(at_ref, own_ref, got_ref, w1_ref, w2_ref, rows_ref, *, bits):
+    step = pl.program_id(0) * pl.num_programs(1) + pl.program_id(1)
+    gin = w1_ref.shape[0]
+    half = rows_ref.shape[0] // 2
+
+    @pl.when(step == 0)
+    def _():
+        n = rows_ref.shape[0] >> bits
+        for p in range(1 << bits):
+            owner = sum(((p >> k) & 1) << (bits - 1 - k) for k in range(bits))
+            ref = own_ref if p < 1 << (bits - 1) else got_ref
+            at = p % (1 << (bits - 1)) * n
+            rows_ref[pl.ds(pl.multiple_of((owner ^ at_ref[0]) * n, 16), n), :] = ref[at : at + n, :]
+
+    start = pl.multiple_of(step * gin, 16)
+    w1_ref[...] = rows_ref[pl.ds(start, gin), :].astype(F32)
+    w2_ref[...] = rows_ref[pl.ds(half + start, gin), :].astype(F32).T
+
+
+def wide_pair_outputs(own, got, place, groups):
+    rows, width = 2 * own.shape[0], own.shape[1]
+    gin = width // groups
+    steps = rows // 2 // width
+    bits = len(row_bits())
+    return pl.pallas_call(
+        partial(wide_pair_kernel, bits=bits),
+        grid=(steps, groups),
+        in_specs=[SMEM, whole(own.shape), whole(got.shape)],
+        out_specs=[
+            pl.BlockSpec((gin, width), lambda q, g: (g, q)),
+            pl.BlockSpec((width, gin), lambda q, g: (g * steps + q, 0)),
+        ],
+        out_shape=[sds((width, steps * width), F32), sds((groups * steps * width, gin), F32)],
+        scratch_shapes=[pltpu.VMEM((rows, width), BF)],
+        compiler_params=params(),
+        cost_estimate=cost(7),
+        name="wide_out",
+    )(place, own, got)
 
 
 def last_out_kernel(
@@ -1048,12 +1099,15 @@
     target = lax.broadcasted_iota(jnp.int32, (kb_ref.shape[1], t8), 0)
     pick = lax.div(source, SUB) + lax.rem(source, SUB) * taps == target
     pick = pick.astype(F32).astype(BF)
-    kw_ref[...] = dot(pick, small[0:t8, 0:att].astype(BF)).T
+    kw = dot(pick, small[0:t8, 0:att].astype(BF))
+    for n in range(kw_ref.shape[0]):
+        kw_ref[n] = kw[n : n + 1]
     for n, ref in ((0, g2_ref), (1, s2_ref), (2, b2_ref), (3, g1_ref), (4, s1_ref), (5, bo_ref)):
         ref[...] = small[t8 + n : t8 + n + 1]
     for n in range(b1_ref.shape[1] // width):
         b1_ref[:, n * width : (n + 1) * width] = small[t8 + SUB + n : t8 + SUB + n + 1]
-    dk_ref[...] = small[t8 + 2 * SUB : t8 + 2 * SUB + taps]
+    for n in range(taps):
+        dk_ref[n] = small[t8 + 2 * SUB + n : t8 + 2 * SUB + n + 1]
     four = t8 + 4 * SUB
     for n, row in enumerate((0, 2, 1)):
         bp_ref[:, n * att : (n + 1) * att] = small[four + row : four + row + 1, 0:att]
@@ -1068,8 +1122,8 @@
     line = sds((1, width), F32)
     shapes = dict(
         wp=sds((width, 4 * att), F32), pw=sds((width, att), F32), wo=sds((width, width), F32),
-        bp=sds((1, 3 * att), F32), dk=sds((taps, width), F32), pb=sds((1, att), F32),
-        kw=sds((att, heads * taps), F32), kb=sds((1, heads * taps), F32), bo=line, g1=line, s1=line,
+        bp=sds((1, 3 * att), F32), dk=sds((taps, 1, width), F32), pb=sds((1, att), F32),
+        kw=sds((heads * taps, 1, att), F32), kb=sds((1, heads * taps), F32), bo=line, g1=line, s1=line,
         b1=sds((1, ff), F32), b2=line, g2=line, s2=line, mask=line,
     )
     outs = pl.pallas_call(
@@ -1104,13 +1158,13 @@
     "0in": ("01", "02"),
 }
 LAST = (
-    ("00", "01", "02", "wide", "rows"),
-    ("01", "02", "wide"),
-    ("01", "02", "mid"),
-    ("02", "mid", "last"),
+    ("00", "01", "02", "wide"),
+    ("01", "02", "wide", "rows"),
+    ("01", "02", "mid", "wide"),
+    ("02", "mid", "last", "wide"),
     ("mid", "last"),
     ("mid", "last"),
-    ("mid", "last", "rows"),
+    ("mid", "last", "rows", "wide"),
     ("mid", "last", "wide"),
 )
 
@@ -1230,8 +1284,14 @@
     marked = (line == width + att + mask_row(taps))[:, None]
 
     def wide_flow():
-        own = yield from own_total_flow(flows.finish("00"), flows.finish("10"), first)
-        return (yield own, "gather")
+        share = yield from own_total_flow(flows.finish("00"), flows.finish("10"), first)
+        if share.shape[0] % 16:
+            return (yield share, "gather")
+        for bit in reversed(bits[1:]):
+            got = yield share, bit
+            share = jnp.concatenate([share, got])
+        got = yield share, bits[0]
+        return share, got
 
     def mid_flow():
         own = yield from own_halves_flow(flows.finish("01"), flows.finish("11"), first)
@@ -1245,20 +1305,28 @@
     flows.add("wide", wide_flow())
     flows.add("mid", mid_flow())
     flows.add("last", last_flow())
+    d0, = flows.step(LAST[0], (d0,))
     flows.add("rows", other_row(d0, d1))
-    for names in LAST[:4]:
+    for names in LAST[1:4]:
         flows.step(names, ())
     states, = flows.step(LAST[4], (states,))
-    for names in LAST[5:]:
+    for names in LAST[5:-1]:
         flows.step(names, ())
     in_grads = both_rows(d0, d1, flows.finish("rows"))
-    w1, w2 = wide_outputs(flows.finish("wide"), jnp.zeros((1,), jnp.int32), groups)
-    in_grads, w1, w2 = flows.step(("mid", "last"), (in_grads, w1, w2))
+    in_grads, = flows.step(LAST[-1], (in_grads,))
+    wide = flows.finish("wide")
+    if isinstance(wide, tuple):
+        w1, w2 = wide_pair_outputs(*wide, lax.axis_index("dp").reshape(1).astype(jnp.int32), groups)
+    else:
+        w1, w2 = wide_outputs(wide, jnp.zeros((1,), jnp.int32), groups)
+    w1, w2 = flows.step(("mid", "last"), (w1, w2))
     mid, last = flows.finish("mid"), flows.finish("last")
     places = jnp.stack([2 * my_bit(0) + my_bit(turned[1]), quarter]).astype(jnp.int32)
     grads = last_outputs(mid, last, places, att, taps, heads, inner_bias.shape[1])
     grads.update(w1=w1.reshape(inner_weight.shape), w2=w2.reshape(second_feed_weight.shape))
-    for n in ("wp", "dk", "pw", "kw", "wo"):
+    grads["dk"] = grads["dk"].transpose(1, 0, 2)
+    grads["kw"] = grads["kw"].transpose(1, 2, 0)
+    for n in ("wp", "pw", "wo"):
         grads[n] = grads[n][None]
     names = ("wp", "bp", "dk", "pw", "pb", "kw", "kb", "wo", "bo", "g1", "s1", "w1", "b1", "w2", "b2", "g2", "s2")
     return (states[None], in_grads[None], grads["mask"].reshape(-1)) + tuple(grads[n] for n in names)

time: 604 us -> 592 us (0.980)
  Pallas kernels: 309 us -> 299 us
  waiting for transfers between devices: 136 us -> 126 us
  other arithmetic: 61.8 us -> 71 us
    ppermute x33 -> x37, waiting for transfers between devices: 93.3 us -> 79.9 us  [across(): lax.ppermute(x, 'dp', [(i, i ^ 1 << bit) for i in range(lax.axis_size('dp...]
    pallas_call x12, Pallas kernels: 195 us -> 189 us  [call(): pl.pallas_call(body, grid=grid, in_specs=[SMEM] + [HBM] * len(operands) +...]
    ppermute x11, starting transfers between devices: 17.1 us -> 10.9 us  [swap(): return lax.ppermute(x, 'section', [(0, 1), (1, 0)])]
    ppermute x33 -> x37, starting transfers between devices: 26.4 us -> 32.6 us  [across(): lax.ppermute(x, 'dp', [(i, i ^ 1 << bit) for i in range(lax.axis_size('dp...]
  transfers between devices with their start and end apart: 47 -> 50, of which waited for: 19 -> 18; matrix products, arithmetic and copies ran while one was open for 10% -> 10% of each run, Pallas kernels for 29% -> 28%
where the time goes in v4:
time: 592 us; the launch traced here: 581 us
  Pallas kernels  299 us (51%)
  waiting for transfers between devices  126 us (21%)
  other arithmetic  71 us (12%)
  starting transfers between devices  43.6 us (7%)
  local copies, waits for them, and re-layouts  25.5 us (4%)
  between operations  16 us (3%)
    pallas_call x12, Pallas kernels, call(): pl.pallas_call(body, grid=grid, in_specs=[SMEM] + [HBM] * len(operands) +...  189 us
    ppermute x37, waiting for transfers between devices, across(): lax.ppermute(x, 'dp', [(i, i ^ 1 << bit) for i in range(lax.axis_size('dp...  79.9 us
    ppermute x11, waiting for transfers between devices, swap(): return lax.ppermute(x, 'section', [(0, 1), (1, 0)])  45.8 us
    pallas_call x2, Pallas kernels, run_attn_back(): pl.pallas_call(partial(attn_back_kernel, head=head, qb=128), grid=(pairs,...  36 us
    ppermute x37, starting transfers between devices, across(): lax.ppermute(x, 'dp', [(i, i ^ 1 << bit) for i in range(lax.axis_size('dp...  32.6 us
    convert_element_type x16, other arithmetic, total_of(): return total.astype(BF)  23.8 us
    pallas_call x2, Pallas kernels, run_wide_grads(): pl.pallas_call(wide_grad_kernel, grid=(groups, steps), in_specs=[narrow,...  21.8 us
    pallas_call x2, Pallas kernels, run_attn(): pl.pallas_call(partial(attn_kernel, head=head, qb=512), grid=(pairs,), in...  20.8 us
  transfers between devices with their start and end apart: 50, of which 18 were waited for; matrix products, arithmetic and copies ran while one was open for 10% of the time, Pallas kernels for 28%

profile of v4, /device:TPU:0, one launch (start us, length us, event | category | flops | bytes accessed | tf_op | source)
XLA Modules:
  0.0 581.1 jit_solution(8793770546418607232)
XLA Ops:
  22.5 9.2 %collective-permute-done.refs_2_.refs_1_ = bf16[240,1536]{1,0:T(8,128)(2,1)} collective-permute-done((bf16[240,1536]{1,0:T(8,128)(2,1)}, bf16[240,1536]{1,0:T(8,128)(2,1)}, u32[]{:S(2)}, u32[]{:S(2)}) %collective-permute-start) | collective-permute-done | bytes 737312 | tf_op jit(solution)/shard_map/ppermute | solution.py:883
  36.1 19.7 %collective-permute-done.4 = bf16[76,768]{1,0:T(8,128)(2,1)S(1)} collective-permute-done((bf16[76,768]{1,0:T(8,128)(2,1)S(1)}, bf16[76,768]{1,0:T(8,128)(2,1)S(1)}, u32[]{:S(2)}, u32[]{:S(2)}) %collective-permute-start.4) | collective-permute-done | bytes 116768 | tf_op jit(solution)/shard_map/ppermute | solution.py:883
  62.0 11.6 %proj_fwd.2 = (bf16[1024,384]{1,0:T(8,128)(2,1)}, bf16[1024,384]{1,0:T(8,128)(2,1)}, bf16[1024,384]{1,0:T(8,128)(2,1)}, bf16[1024,384]{1,0:T(8,128)(2,1)}, bf16[...) custom-call(s32[2]{0:T(128)} %get-tuple-element.680.place_ref, ...), custom_call_target="tpu_custom_call" | custom-call | flops 14300000256 | tf_op jit(solution)/shard_map/proj_fwd/pallas_call | solution.py:141
  75.0 4.6 collective-permute-done.6.refs_3_
  81.3 10.4 %attn_fwd.2 = (f32[384,1024]{1,0:T(8,128)}, f32[3,8,1024]{2,1,0:T(8,128)}) custom-call(bf16[1024,384]{1,0:T(8,128)(2,1)} %get-tuple-element.391.k_ref, bf16[384,1024]{1,0:T(8,128)(2,1)} %get-tuple-element.392.qt_ref, bf16[384,1024]{1,0:T(8,128)(2,1)} %get-tuple-element.393.vt_ref), custom_call_target="tpu_custom_call" | custom-call | flops 20899999744 | tf_op jit(solution)/shard_map/attn_fwd/pallas_call | solution.py:290
  100.1 23.7 %ffn_fwd.2 = (bf16[1024,768]{1,0:T(8,128)(2,1)}, bf16[1024,768]{1,0:T(8,128)(2,1)}, f32[1024,1]{1,0:T(8,128)}, bf16[1024,768]{1,0:T(8,128)(2,1)}, bf16[1024,3072...) custom-call(s32[2]{0:T(128)} %get-tuple-element.680.place_ref, ...), custom_call_target="tpu_custom_call" | custom-call | flops 24199999488 | tf_op jit(solution)/shard_map/ffn_fwd/pallas_call | solution.py:141
  123.9 11.8 %proj_fwd.3 = (bf16[1024,384]{1,0:T(8,128)(2,1)}, bf16[1024,384]{1,0:T(8,128)(2,1)}, bf16[1024,384]{1,0:T(8,128)(2,1)}, bf16[1024,384]{1,0:T(8,128)(2,1)}, bf16[...) custom-call(s32[2]{0:T(128)} %get-tuple-element.680.place_ref, ...), custom_call_target="tpu_custom_call" | custom-call | flops 14300000256 | tf_op jit(solution)/shard_map/proj_fwd/pallas_call | solution.py:141
  135.7 10.4 %attn_fwd.3 = (f32[384,1024]{1,0:T(8,128)}, f32[3,8,1024]{2,1,0:T(8,128)}) custom-call(bf16[1024,384]{1,0:T(8,128)(2,1)} %get-tuple-element.411.k_ref, bf16[384,1024]{1,0:T(8,128)(2,1)} %get-tuple-element.412.qt_ref, bf16[384,1024]{1,0:T(8,128)(2,1)} %get-tuple-element.413.vt_ref), custom_call_target="tpu_custom_call" | custom-call | flops 20899999744 | tf_op jit(solution)/shard_map/attn_fwd/pallas_call | solution.py:290
  146.1 23.8 %ffn_fwd.3 = (bf16[1024,768]{1,0:T(8,128)(2,1)}, bf16[1024,768]{1,0:T(8,128)(2,1)}, f32[1024,1]{1,0:T(8,128)}, bf16[1024,768]{1,0:T(8,128)(2,1)}, bf16[1024,3072...) custom-call(s32[2]{0:T(128)} %get-tuple-element.680.place_ref, ...), custom_call_target="tpu_custom_call" | custom-call | flops 24199999488 | tf_op jit(solution)/shard_map/ffn_fwd/pallas_call | solution.py:141
  171.5 18.7 %ffn_bwd.2 = (bf16[1024,768]{1,0:T(8,128)(2,1)}, bf16[1024,3072]{1,0:T(8,128)(2,1)}, bf16[1024,768]{1,0:T(8,128)(2,1)}, bf16[384,1024]{1,0:T(8,128)(2,1)}, bf16[...) custom-call(s32[2]{0:T(128)} %get-tuple-element.680.place_ref, ...), custom_call_target="tpu_custom_call" | custom-call | flops 19800000512 | tf_op jit(solution)/shard_map/ffn_bwd/pallas_call | solution.py:141
  190.2 10.9 %ffn_wgrad.2 = bf16[2,1536,768]{2,1,0:T(8,128)(2,1)} custom-call(bf16[1024,768]{1,0:T(8,128)(2,1)} %get-tuple-element.434.nl_ref, bf16[1024,3072]{1,0:T(8,128)(2,1)} %get-tuple-element.435.di_ref, bf16[1024,768]{1,0:T(8,128)(2,1)} %get-tuple-element.436.ds_ref, bf16[1024,3072]{1,0:T(8,128)(2,1)} %get-tuple-element.437.act_ref), custom_call_target="tpu_custom_call" | custom-call | flops 6600000000 | tf_op jit(solution)/shard_map/ffn_wgrad/pallas_call | solution.py:704
  201.1 17.9 %attn_bwd.2 = (bf16[1024,384]{1,0:T(8,128)(2,1)}, bf16[1024,384]{1,0:T(8,128)(2,1)}, bf16[1024,384]{1,0:T(8,128)(2,1)}, f32[1,384]{1,0:T(1,128)}) custom-call(bf16[1024,384]{1,0:T(8,128)(2,1)} %get-tuple-element.411.k_ref, bf16[1024,384]{1,0:T(8,128)(2,1)} %get-tuple-element.426.v_ref, bf16[1024,384]{1,0:T(8,128)(2,1)} %get-tuple-element.427.q2_ref.refs_9_, ...), custom_call_target="tpu_custom_call" | custom-call | flops 22000001024 | tf_op jit(solution)/shard_map/attn_bwd/pallas_call | solution.py:654
  219.0 7.3 %mid_wgrad.2 = bf16[1536,768]{1,0:T(8,128)(2,1)} custom-call(bf16[1024,768]{1,0:T(8,128)(2,1)} %get-tuple-element.448.ctx_ref, bf16[1024,768]{1,0:T(8,128)(2,1)} %get-tuple-element.449.dz_ref.refs_11_, bf16[1024,768]{1,0:T(8,128)(2,1)} %get-tuple-element.407.refs_6_.refs_14_.h_ref.refs_10_.refs_5_, ...), custom_call_target="tpu_custom_call" | custom-call | flops 5500000256 | tf_op jit(solution)/shard_map/mid_wgrad/pallas_call | solution.py:727
  228.9 22.2 %conv_bwd.2 = (bf16[1024,72]{1,0:T(8,128)(2,1)}, bf16[1024,384]{1,0:T(8,128)(2,1)}, bf16[1024,384]{1,0:T(8,128)(2,1)}, bf16[1024,384]{1,0:T(8,128)(2,1)}, bf16[1...) custom-call(s32[2]{0:T(128)} %get-tuple-element.680.place_ref, ...), custom_call_target="tpu_custom_call" | custom-call | flops 29699999744 | tf_op jit(solution)/shard_map/conv_bwd/pallas_call | solution.py:141
  254.4 11.1 %collective-permute-done.14 = bf16[1024,768]{1,0:T(8,128)(2,1)S(1)} collective-permute-done((bf16[1024,768]{1,0:T(8,128)(2,1)S(1)}, bf16[1024,768]{1,0:T(8,128)(2,1)S(1)}, u32[]{:S(2)}, u32[]{:S(2)}) %collective-permute-start.14) | collective-permute-done | bytes 1572896 | tf_op jit(solution)/shard_map/ppermute | solution.py:883
  269.1 9.3 %last_wgrad.2 = (bf16[1152,768]{1,0:T(8,128)(2,1)}, f32[72,384]{1,0:T(8,128)}, f32[8,768]{1,0:T(8,128)}) custom-call(s32[2]{0:T(128)} %get-tuple-element.680.place_ref, bf16[768,1536]{1,0:T(8,128)(2,1)} %bitcast.90, bf16[240,1536]{1,0:T(8,128)(2,1)} %collective-permute-done.refs_2_.refs_1_, bf16[240,1536]{1,0:T(8,128)(2,1)} %collective-permute-done.1.refs_3_.refs_2_, ...), custom_call_target="tpu_custom_call" | custom-call | flops 9900000256 | tf_op jit(solution)/shard_map/last_wgrad/pallas_call | solution.py:141
  282.9 8.4 %in_bwd.2.refs_11_ = bf16[1024,768]{1,0:T(8,128)(2,1)} custom-call(s32[2]{0:T(128)} %get-tuple-element.680.place_ref, bf16[768,1536]{1,0:T(8,128)(2,1)} %bitcast.91, bf16[240,1536]{1,0:T(8,128)(2,1)} %collective-permute-done.refs_2_.refs_1_, bf16[240,1536]{1,0:T(8,128)(2,1)} %collective-permute-done.1.refs_3_.refs_2_, ...), custom_call_target="tpu_custom_call" | custom-call | flops 8800000000 | tf_op jit(solution)/shard_map/in_bwd/pallas_call | solution.py:141
  294.6 18.8 %ffn_bwd.3 = (bf16[1024,768]{1,0:T(8,128)(2,1)}, bf16[1024,3072]{1,0:T(8,128)(2,1)}, bf16[1024,768]{1,0:T(8,128)(2,1)}, bf16[384,1024]{1,0:T(8,128)(2,1)}, bf16[...) custom-call(s32[2]{0:T(128)} %get-tuple-element.680.place_ref, ...), custom_call_target="tpu_custom_call" | custom-call | flops 19800000512 | tf_op jit(solution)/shard_map/ffn_bwd/pallas_call | solution.py:141
  319.8 10.9 %ffn_wgrad.3 = bf16[2,1536,768]{2,1,0:T(8,128)(2,1)} custom-call(bf16[1024,768]{1,0:T(8,128)(2,1)} %get-tuple-element.514.nl_ref, bf16[1024,3072]{1,0:T(8,128)(2,1)} %get-tuple-element.515.di_ref, bf16[1024,768]{1,0:T(8,128)(2,1)} %get-tuple-element.516.ds_ref, bf16[1024,3072]{1,0:T(8,128)(2,1)} %get-tuple-element.517.act_ref), custom_call_target="tpu_custom_call" | custom-call | flops 6600000000 | tf_op jit(solution)/shard_map/ffn_wgrad/pallas_call | solution.py:704
  337.4 18.1 %attn_bwd.3 = (bf16[1024,384]{1,0:T(8,128)(2,1)}, bf16[1024,384]{1,0:T(8,128)(2,1)}, bf16[1024,384]{1,0:T(8,128)(2,1)}, f32[1,384]{1,0:T(1,128)}) custom-call(bf16[1024,384]{1,0:T(8,128)(2,1)} %get-tuple-element.391.k_ref, bf16[1024,384]{1,0:T(8,128)(2,1)} %get-tuple-element.497.v_ref, bf16[1024,384]{1,0:T(8,128)(2,1)} %get-tuple-element.498.q2_ref.refs_9_, ...), custom_call_target="tpu_custom_call" | custom-call | flops 22000001024 | tf_op jit(solution)/shard_map/attn_bwd/pallas_call | solution.py:654
  358.1 7.3 %mid_wgrad.3 = bf16[1536,768]{1,0:T(8,128)(2,1)} custom-call(bf16[1024,768]{1,0:T(8,128)(2,1)} %get-tuple-element.537.ctx_ref, bf16[1024,768]{1,0:T(8,128)(2,1)} %get-tuple-element.538.dz_ref.refs_11_, bf16[1024,768]{1,0:T(8,128)(2,1)} %bitcast_select_fusion.refs_6_.refs_14_.h_ref.refs_10_.refs_5_, ...), custom_call_target="tpu_custom_call" | custom-call | flops 5500000256 | tf_op jit(solution)/shard_map/mid_wgrad/pallas_call | solution.py:727
  367.4 22.2 %conv_bwd.3 = (bf16[1024,72]{1,0:T(8,128)(2,1)}, bf16[1024,384]{1,0:T(8,128)(2,1)}, bf16[1024,384]{1,0:T(8,128)(2,1)}, bf16[1024,384]{1,0:T(8,128)(2,1)}, bf16[1...) custom-call(s32[2]{0:T(128)} %get-tuple-element.680.place_ref, ...), custom_call_target="tpu_custom_call" | custom-call | flops 29699999744 | tf_op jit(solution)/shard_map/conv_bwd/pallas_call | solution.py:141
  397.1 9.5 %last_wgrad.3 = (bf16[1152,768]{1,0:T(8,128)(2,1)}, f32[72,384]{1,0:T(8,128)}, f32[8,768]{1,0:T(8,128)}) custom-call(s32[2]{0:T(128)} %get-tuple-element.680.place_ref, bf16[768,1536]{1,0:T(8,128)(2,1)} %bitcast.92, bf16[240,1536]{1,0:T(8,128)(2,1)} %collective-permute-done.refs_2_.refs_1_, bf16[240,1536]{1,0:T(8,128)(2,1)} %collective-permute-done.1.refs_3_.refs_2_, ...), custom_call_target="tpu_custom_call" | custom-call | flops 9900000256 | tf_op jit(solution)/shard_map/last_wgrad/pallas_call | solution.py:141
  417.0 8.8 %in_bwd.3 = bf16[1024,768]{1,0:T(8,128)(2,1)} custom-call(s32[2]{0:T(128)} %get-tuple-element.680.place_ref, bf16[768,1536]{1,0:T(8,128)(2,1)} %bitcast.93, bf16[240,1536]{1,0:T(8,128)(2,1)} %collective-permute-done.refs_2_.refs_1_, bf16[240,1536]{1,0:T(8,128)(2,1)} %collective-permute-done.1.refs_3_.refs_2_, ...), custom_call_target="tpu_custom_call" | custom-call | flops 8800000000 | tf_op jit(solution)/shard_map/in_bwd/pallas_call | solution.py:141
  436.2 4.1 collective-permute-done.27
  452.8 8.5 %collective-permute-done.31 = bf16[160,768]{1,0:T(8,128)(2,1)S(1)} collective-permute-done((bf16[160,768]{1,0:T(8,128)(2,1)}, bf16[160,768]{1,0:T(8,128)(2,1)S(1)}, u32[]{:S(2)}, u32[]{:S(2)}) %collective-permute-start.31) | collective-permute-done | bytes 245792 | tf_op jit(solution)/shard_map/ppermute | solution.py:887
  472.9 8.5 %collective-permute-done.33 = bf16[80,768]{1,0:T(8,128)(2,1)S(1)} collective-permute-done((bf16[80,768]{1,0:T(8,128)(2,1)}, bf16[80,768]{1,0:T(8,128)(2,1)S(1)}, u32[]{:S(2)}, u32[]{:S(2)}) %collective-permute-start.33) | collective-permute-done | bytes 122912 | tf_op jit(solution)/shard_map/ppermute | solution.py:887
  496.9 14.5 %collective-permute-done.38 = bf16[80,768]{1,0:T(8,128)(2,1)S(1)} collective-permute-done((bf16[80,768]{1,0:T(8,128)(2,1)S(1)}, bf16[80,768]{1,0:T(8,128)(2,1)S(1)}, u32[]{:S(2)}, u32[]{:S(2)}) %collective-permute-start.38) | collective-permute-done | bytes 122912 | tf_op jit(solution)/shard_map/ppermute | solution.py:887
  518.3 18.7 %collective-permute-done.40 = bf16[160,768]{1,0:T(8,128)(2,1)S(1)} collective-permute-done((bf16[160,768]{1,0:T(8,128)(2,1)}, bf16[160,768]{1,0:T(8,128)(2,1)S(1)}, u32[]{:S(2)}, u32[]{:S(2)}) %collective-permute-start.40) | collective-permute-done | bytes 245792 | tf_op jit(solution)/shard_map/ppermute | solution.py:887
  547.3 9.3 %collective-permute-done.44 = bf16[320,768]{1,0:T(8,128)(2,1)S(1)} collective-permute-done((bf16[320,768]{1,0:T(8,128)(2,1)S(1)}, bf16[320,768]{1,0:T(8,128)(2,1)S(1)}, u32[]{:S(2)}, u32[]{:S(2)}) %collective-permute-start.44) | collective-permute-done | bytes 491552 | tf_op jit(solution)/shard_map/ppermute | solution.py:887
  558.1 7.1 %wide_out.1 = (f32[768,1536]{1,0:T(8,128)}, f32[3072,384]{1,0:T(8,128)}) custom-call(s32[1]{0:T(128)} %bitcast.30.at_ref, bf16[1536,768]{1,0:T(8,128)(2,1)} %copy-done.10, bf16[1536,768]{1,0:T(8,128)(2,1)} %copy-done.55), custom_call_target="tpu_custom_call" | custom-call | flops 7699999744 | tf_op jit(solution)/shard_map/wide_out/pallas_call | solution.py:1061
  566.2 6.2 %last_out.1 = (f32[768,1536]{1,0:T(8,128)}, f32[768,384]{1,0:T(8,128)}, f32[768,768]{1,0:T(8,128)}, f32[1,1152]{1,0:T(1,128)}, f32[9,1,768]{2,1,0:T(1,128)}, /*i...) custom-call(s32[2]{0:T(128)} %get-tuple-element.681.at_ref, ...), custom_call_target="tpu_custom_call" | custom-call | flops 6600000000 | tf_op jit(solution)/shard_map/last_out/pallas_call | solution.py:1129
  (361 shorter events, 161.6 us)
Async XLA Ops:
  7.2 324.6 %reduce-scatter.3.cloned.1.call-start = ((), (), s32[]{:S(2)}) async-start(), calls=%async_computation.2 | async-start | bytes 5013504 | tf_op jit(solution)/shard_map/reduce_scatter | solution.py:894
  11.8 19.8 %collective-permute-start = (bf16[240,1536]{1,0:T(8,128)(2,1)}, bf16[240,1536]{1,0:T(8,128)(2,1)}, u32[]{:S(2)}, u32[]{:S(2)}) collective-permute-start(bf16[240,1536]{1,0:T(8,128)(2,1)} %get-tuple-element.357), channel_id=1, source_target_pairs={{0,16},{16,0},{1,17},{17,1},{2,18},{18,2},{3,19},{19,3},{4,20},{20... | collective-permute-start | bytes 2211848 | tf_op jit(solution)/shard_map/ppermute | solution.py:883
  32.3 23.5 %collective-permute-start.3 = (bf16[288,1536]{1,0:T(8,128)(2,1)S(1)}, bf16[288,1536]{1,0:T(8,128)(2,1)S(1)}, u32[]{:S(2)}, u32[]{:S(2)}) collective-permute-start(bf16[288,1536]{1,0:T(8,128)(2,1)S(1)} %copy-done.62), channel_id=1, source_target_pairs={{0,16},{16,0},{1,17},{17,1},{2,18},{18,2},{3,19},{19,3},{4,20},{20... | collective-permute-start | bytes 2654216 | tf_op jit(solution)/shard_map/ppermute | solution.py:883
  34.0 21.7 %collective-permute-start.1 = (bf16[240,1536]{1,0:T(8,128)(2,1)}, bf16[240,1536]{1,0:T(8,128)(2,1)}, u32[]{:S(2)}, u32[]{:S(2)}) collective-permute-start(bf16[240,1536]{1,0:T(8,128)(2,1)} %collective-permute-done.refs_2_.refs_1_), channel_id=1, source_target_pairs={{0,2},{1,3},{2,0},{3,1},{4,6},{5,7},{6,4},{7,5},{8,10},{9,11},{10,... | collective-permute-start | bytes 2211848 | tf_op jit(solution)/shard_map/ppermute | solution.py:887
  35.5 20.2 %collective-permute-start.2 = (bf16[240,1536]{1,0:T(8,128)(2,1)}, bf16[240,1536]{1,0:T(8,128)(2,1)}, u32[]{:S(2)}, u32[]{:S(2)}) collective-permute-start(bf16[240,1536]{1,0:T(8,128)(2,1)} %collective-permute-done.refs_2_.refs_1_), channel_id=1, source_target_pairs={{0,1},{1,0},{2,3},{3,2},{4,5},{5,4},{6,7},{7,6},{8,9},{9,8},{10,11... | collective-permute-start | bytes 2211848 | tf_op jit(solution)/shard_map/ppermute | solution.py:887
  35.5 20.2 %collective-permute-start.4 = (bf16[76,768]{1,0:T(8,128)(2,1)S(1)}, bf16[76,768]{1,0:T(8,128)(2,1)S(1)}, u32[]{:S(2)}, u32[]{:S(2)}) collective-permute-start(bf16[76,768]{1,0:T(8,128)(2,1)S(1)} %fusion.12), channel_id=1, source_target_pairs={{0,16},{16,0},{1,17},{17,1},{2,18},{18,2},{3,19},{19,3},{4,20},{20... | collective-permute-start | bytes 350216 | tf_op jit(solution)/shard_map/ppermute | solution.py:883
  57.6 22.0 %collective-permute-start.6 = (bf16[288,1536]{1,0:T(8,128)(2,1)S(1)}, bf16[288,1536]{1,0:T(8,128)(2,1)S(1)}, u32[]{:S(2)}, u32[]{:S(2)}) collective-permute-start(bf16[288,1536]{1,0:T(8,128)(2,1)S(1)} %collective-permute-done.3.refs_2_), channel_id=1, source_target_pairs={{0,2},{1,3},{2,0},{3,1},{4,6},{5,7},{6,4},{7,5},{8,10},{9,11},{10,... | collective-permute-start | bytes 2654216 | tf_op jit(solution)/shard_map/ppermute | solution.py:887
  59.0 20.5 %collective-permute-start.7 = (bf16[288,1536]{1,0:T(8,128)(2,1)S(1)}, bf16[288,1536]{1,0:T(8,128)(2,1)S(1)}, u32[]{:S(2)}, u32[]{:S(2)}) collective-permute-start(bf16[288,1536]{1,0:T(8,128)(2,1)S(1)} %collective-permute-done.3.refs_2_), channel_id=1, source_target_pairs={{0,1},{1,0},{2,3},{3,2},{4,5},{5,4},{6,7},{7,6},{8,9},{9,8},{10,11... | collective-permute-start | bytes 2654216 | tf_op jit(solution)/shard_map/ppermute | solution.py:887
  59.2 15.8 %collective-permute-start.8 = (bf16[192,1536]{1,0:T(8,128)(2,1)}, bf16[192,1536]{1,0:T(8,128)(2,1)S(1)}, u32[]{:S(2)}, u32[]{:S(2)}) collective-permute-start(bf16[192,1536]{1,0:T(8,128)(2,1)} %get-tuple-element.384), channel_id=1, source_target_pairs={{0,16},{16,0},{1,17},{17,1},{2,18},{18,2},{3,19},{19,3},{4,20},{20... | collective-permute-start | bytes 1769480 | tf_op jit(solution)/shard_map/ppermute | solution.py:883
  79.6 15.9 %collective-permute-start.9 = (bf16[288,1536]{1,0:T(8,128)(2,1)S(1)}, bf16[288,1536]{1,0:T(8,128)(2,1)S(1)}, u32[]{:S(2)}, u32[]{:S(2)}) collective-permute-start(bf16[288,1536]{1,0:T(8,128)(2,1)S(1)} %collective-permute-done.6.refs_3_), channel_id=1, source_target_pairs={{0,1},{1,0},{2,3},{3,2},{4,5},{5,4},{6,7},{7,6},{8,9},{9,8},{10,11... | collective-permute-start | bytes 2654216 | tf_op jit(solution)/shard_map/ppermute | solution.py:887
  79.7 15.8 %collective-permute-start.10 = (bf16[192,1536]{1,0:T(8,128)(2,1)S(1)}, bf16[192,1536]{1,0:T(8,128)(2,1)}, u32[]{:S(2)}, u32[]{:S(2)}) collective-permute-start(bf16[192,1536]{1,0:T(8,128)(2,1)S(1)} %collective-permute-done.8.refs_7_), channel_id=1, source_target_pairs={{0,2},{1,3},{2,0},{3,1},{4,6},{5,7},{6,4},{7,5},{8,10},{9,11},{10,... | collective-permute-start | bytes 1769480 | tf_op jit(solution)/shard_map/ppermute | solution.py:887
  81.2 14.3 %collective-permute-start.11 = (bf16[192,1536]{1,0:T(8,128)(2,1)S(1)}, bf16[192,1536]{1,0:T(8,128)(2,1)S(1)}, u32[]{:S(2)}, u32[]{:S(2)}) collective-permute-start(bf16[192,1536]{1,0:T(8,128)(2,1)S(1)} %collective-permute-done.8.refs_7_), channel_id=1, source_target_pairs={{0,1},{1,0},{2,3},{3,2},{4,5},{5,4},{6,7},{7,6},{8,9},{9,8},{10,11... | collective-permute-start | bytes 1769480 | tf_op jit(solution)/shard_map/ppermute | solution.py:887
  228.6 25.7 %collective-permute-start.13 = (bf16[768,768]{1,0:T(8,128)(2,1)}, bf16[768,768]{1,0:T(8,128)(2,1)}, u32[]{:S(2)}, u32[]{:S(2)}) collective-permute-start(bf16[768,768]{1,0:T(8,128)(2,1)} %constant_dynamic-slice_fusion.3), channel_id=1, source_target_pairs={{0,1},{1,0},{2,3},{3,2},{4,5},{5,4},{6,7},{7,6},{8,9},{9,8},{10,11... | collective-permute-start | bytes 3538952 | tf_op jit(solution)/shard_map/ppermute | solution.py:887
  228.6 36.8 %collective-permute-start.14 = (bf16[1024,768]{1,0:T(8,128)(2,1)S(1)}, bf16[1024,768]{1,0:T(8,128)(2,1)S(1)}, u32[]{:S(2)}, u32[]{:S(2)}) collective-permute-start(bf16[1024,768]{1,0:T(8,128)(2,1)S(1)} %broadcast_select_fusion.2), channel_id=1, source_target_pairs={{0,16},{16,0},{1,17},{17,1},{2,18},{18,2},{3,19},{19,3},{4,20},{20... | collective-permute-start | bytes 4718600 | tf_op jit(solution)/shard_map/ppermute | solution.py:883
  228.9 197.0 %reduce-scatter.5.cloned.1.call-start = ((), (), s32[]{:S(2)}) async-start(), calls=%async_computation.3 | async-start | bytes 5013504 | tf_op jit(solution)/shard_map/reduce_scatter | solution.py:894
  291.3 23.5 %collective-permute-start.16 = (bf16[768,384]{1,0:T(8,128)(2,1)}, bf16[768,384]{1,0:T(8,128)(2,1)}, u32[]{:S(2)}, u32[]{:S(2)}) collective-permute-start(bf16[768,384]{1,0:T(8,128)(2,1)} %add_convert_fusion.1), channel_id=1, source_target_pairs={{0,16},{16,0},{1,17},{17,1},{2,18},{18,2},{3,19},{19,3},{4,20},{20... | collective-permute-start | bytes 1769480 | tf_op jit(solution)/shard_map/ppermute | solution.py:883
  293.1 21.8 %collective-permute-start.17 = (bf16[320,768]{1,0:T(8,128)(2,1)S(1)}, bf16[320,768]{1,0:T(8,128)(2,1)S(1)}, u32[]{:S(2)}, u32[]{:S(2)}) collective-permute-start(bf16[320,768]{1,0:T(8,128)(2,1)S(1)} %add_convert_fusion.3), channel_id=1, source_target_pairs={{0,2},{1,3},{2,0},{3,1},{4,6},{5,7},{6,4},{7,5},{8,10},{9,11},{10,... | collective-permute-start | bytes 1474568 | tf_op jit(solution)/shard_map/ppermute | solution.py:887
  317.8 14.1 %collective-permute-start.18 = (bf16[384,384]{1,0:T(8,128)(2,1)S(1)}, bf16[384,384]{1,0:T(8,128)(2,1)S(1)}, u32[]{:S(2)}, u32[]{:S(2)}) collective-permute-start(bf16[384,384]{1,0:T(8,128)(2,1)S(1)} %add_convert_fusion.6), channel_id=1, source_target_pairs={{0,4},{1,5},{2,6},{3,7},{4,0},{5,1},{6,2},{7,3},{8,12},{9,13},{10,... | collective-permute-start | bytes 884744 | tf_op jit(solution)/shard_map/ppermute | solution.py:887
  334.4 21.8 %collective-permute-start.20 = (bf16[192,384]{1,0:T(8,128)(2,1)S(1)}, bf16[192,384]{1,0:T(8,128)(2,1)S(1)}, u32[]{:S(2)}, u32[]{:S(2)}) collective-permute-start(bf16[192,384]{1,0:T(8,128)(2,1)S(1)} %add_convert_fusion.10), channel_id=1, source_target_pairs={{0,8},{1,9},{2,10},{3,11},{4,12},{5,13},{6,14},{7,15},{8,0},{9,1},... | collective-permute-start | bytes 442376 | tf_op jit(solution)/shard_map/ppermute | solution.py:887
  337.1 19.1 %collective-permute-start.21 = (bf16[80,768]{1,0:T(8,128)(2,1)S(1)}, bf16[80,768]{1,0:T(8,128)(2,1)S(1)}, u32[]{:S(2)}, u32[]{:S(2)}) collective-permute-start(bf16[80,768]{1,0:T(8,128)(2,1)S(1)} %add_convert_fusion.15), channel_id=1, source_target_pairs={{0,8},{1,9},{2,10},{3,11},{4,12},{5,13},{6,14},{7,15},{8,0},{9,1},... | collective-permute-start | bytes 368648 | tf_op jit(solution)/shard_map/ppermute | solution.py:887
  367.4 25.3 %collective-permute-start.23 = (bf16[768,768]{1,0:T(8,128)(2,1)S(1)}, bf16[768,768]{1,0:T(8,128)(2,1)S(1)}, u32[]{:S(2)}, u32[]{:S(2)}) collective-permute-start(bf16[768,768]{1,0:T(8,128)(2,1)S(1)} %constant_dynamic-slice_fusion.1), channel_id=1, source_target_pairs={{0,1},{1,0},{2,3},{3,2},{4,5},{5,4},{6,7},{7,6},{8,9},{9,8},{10,11... | collective-permute-start | bytes 3538952 | tf_op jit(solution)/shard_map/ppermute | solution.py:887
  395.5 16.8 %collective-permute-start.24 = (bf16[768,384]{1,0:T(8,128)(2,1)}, bf16[768,384]{1,0:T(8,128)(2,1)}, u32[]{:S(2)}, u32[]{:S(2)}) collective-permute-start(bf16[768,384]{1,0:T(8,128)(2,1)} %add_convert_fusion), channel_id=1, source_target_pairs={{0,16},{16,0},{1,17},{17,1},{2,18},{18,2},{3,19},{19,3},{4,20},{20... | collective-permute-start | bytes 1769480 | tf_op jit(solution)/shard_map/ppermute | solution.py:883
  445.5 15.9 %collective-permute-start.32 = (bf16[192,768]{1,0:T(8,128)(2,1)S(1)}, bf16[192,768]{1,0:T(8,128)(2,1)S(1)}, u32[]{:S(2)}, u32[]{:S(2)}) collective-permute-start(bf16[192,768]{1,0:T(8,128)(2,1)S(1)} %add_convert_fusion.4), channel_id=1, source_target_pairs={{0,8},{1,9},{2,10},{3,11},{4,12},{5,13},{6,14},{7,15},{8,0},{9,1},... | collective-permute-start | bytes 884744 | tf_op jit(solution)/shard_map/ppermute | solution.py:887
  466.2 17.4 %collective-permute-start.35 = (bf16[384,768]{1,0:T(8,128)(2,1)}, bf16[384,768]{1,0:T(8,128)(2,1)S(1)}, u32[]{:S(2)}, u32[]{:S(2)}) collective-permute-start(bf16[384,768]{1,0:T(8,128)(2,1)} %pad_maximum_fusion.6), channel_id=1, source_target_pairs={{0,4},{1,5},{2,6},{3,7},{4,0},{5,1},{6,2},{7,3},{8,12},{9,13},{10,... | collective-permute-start | bytes 1769480 | tf_op jit(solution)/shard_map/ppermute | solution.py:887
  466.4 15.0 %collective-permute-start.33 = (bf16[80,768]{1,0:T(8,128)(2,1)}, bf16[80,768]{1,0:T(8,128)(2,1)S(1)}, u32[]{:S(2)}, u32[]{:S(2)}) collective-permute-start(bf16[80,768]{1,0:T(8,128)(2,1)} %add_convert_fusion.14), channel_id=1, source_target_pairs={{0,8},{1,9},{2,10},{3,11},{4,12},{5,13},{6,14},{7,15},{8,0},{9,1},... | collective-permute-start | bytes 368648 | tf_op jit(solution)/shard_map/ppermute | solution.py:887
  493.0 19.0 %collective-permute-start.39 = (bf16[192,768]{1,0:T(8,128)(2,1)S(1)}, bf16[192,768]{1,0:T(8,128)(2,1)}, u32[]{:S(2)}, u32[]{:S(2)}) collective-permute-start(bf16[192,768]{1,0:T(8,128)(2,1)S(1)} %pad_maximum_fusion.9), channel_id=1, source_target_pairs={{0,8},{1,9},{2,10},{3,11},{4,12},{5,13},{6,14},{7,15},{8,0},{9,1},... | collective-permute-start | bytes 884744 | tf_op jit(solution)/shard_map/ppermute | solution.py:887
  494.3 42.8 %collective-permute-start.42 = (bf16[1024,768]{1,0:T(8,128)(2,1)}, bf16[1024,768]{1,0:T(8,128)(2,1)}, u32[]{:S(2)}, u32[]{:S(2)}) collective-permute-start(bf16[1024,768]{1,0:T(8,128)(2,1)} %broadcast_select_fusion.1), channel_id=1, source_target_pairs={{0,16},{16,0},{1,17},{17,1},{2,18},{18,2},{3,19},{19,3},{4,20},{20... | collective-permute-start | bytes 4718600 | tf_op jit(solution)/shard_map/ppermute | solution.py:883
  494.6 16.8 %collective-permute-start.38 = (bf16[80,768]{1,0:T(8,128)(2,1)S(1)}, bf16[80,768]{1,0:T(8,128)(2,1)S(1)}, u32[]{:S(2)}, u32[]{:S(2)}) collective-permute-start(bf16[80,768]{1,0:T(8,128)(2,1)S(1)} %add_convert_fusion.11), channel_id=1, source_target_pairs={{0,8},{1,9},{2,10},{3,11},{4,12},{5,13},{6,14},{7,15},{8,0},{9,1},... | collective-permute-start | bytes 368648 | tf_op jit(solution)/shard_map/ppermute | solution.py:887
  496.3 40.7 %collective-permute-start.43 = (bf16[768,768]{1,0:T(8,128)(2,1)S(1)}, bf16[768,768]{1,0:T(8,128)(2,1)}, u32[]{:S(2)}, u32[]{:S(2)}) collective-permute-start(bf16[768,768]{1,0:T(8,128)(2,1)S(1)} %copy-done.13), channel_id=1, source_target_pairs={{0,2},{1,3},{2,0},{3,1},{4,6},{5,7},{6,4},{7,5},{8,10},{9,11},{10,... | collective-permute-start | bytes 3538952 | tf_op jit(solution)/shard_map/ppermute | solution.py:887
  516.3 20.7 %collective-permute-start.41 = (bf16[384,768]{1,0:T(8,128)(2,1)}, bf16[384,768]{1,0:T(8,128)(2,1)}, u32[]{:S(2)}, u32[]{:S(2)}) collective-permute-start(bf16[384,768]{1,0:T(8,128)(2,1)} %pad_maximum_fusion.7), channel_id=1, source_target_pairs={{0,4},{1,5},{2,6},{3,7},{4,0},{5,1},{6,2},{7,3},{8,12},{9,13},{10,... | collective-permute-start | bytes 1769480 | tf_op jit(solution)/shard_map/ppermute | solution.py:887
  516.3 20.7 %collective-permute-start.40 = (bf16[160,768]{1,0:T(8,128)(2,1)}, bf16[160,768]{1,0:T(8,128)(2,1)S(1)}, u32[]{:S(2)}, u32[]{:S(2)}) collective-permute-start(bf16[160,768]{1,0:T(8,128)(2,1)} %pad_maximum_fusion.10), channel_id=1, source_target_pairs={{0,4},{1,5},{2,6},{3,7},{4,0},{5,1},{6,2},{7,3},{8,12},{9,13},{10,... | collective-permute-start | bytes 737288 | tf_op jit(solution)/shard_map/ppermute | solution.py:887
  542.9 13.8 %collective-permute-start.46 = (bf16[1536,768]{1,0:T(8,128)(2,1)S(1)}, bf16[1536,768]{1,0:T(8,128)(2,1)S(1)}, u32[]{:S(2)}, u32[]{:S(2)}) collective-permute-start(bf16[1536,768]{1,0:T(8,128)(2,1)S(1)} %pad_maximum_fusion.2.own_ref), channel_id=1, source_target_pairs={{0,1},{1,0},{2,3},{3,2},{4,5},{5,4},{6,7},{7,6},{8,9},{9,8},{10,11... | collective-permute-start | bytes 7077896 | tf_op jit(solution)/shard_map/ppermute | solution.py:887
  (85 other events, 821.1 us)
Sparse Core Ops, SparseCore 0:
  229.0 77.0 reduce-scatter.2
  337.5 75.8 reduce-scatter.4

commit v5 on v4

--- a/solution.py
+++ b/solution.py
@@ -735,7 +735,7 @@
 
 def last_grad_kernel(
     ready, wp_ref, h_ref, dq_ref, dk_ref, dv_ref, dsp_ref, dep_ref, dkc_ref, mx_ref, dl_ref, m_ref, res_ref,
-    out_ref, kw_ref, mg_ref,
+    vec_ref, db1_ref, dkg_ref, dbp_ref, dbv_ref, dpb_ref, dkb_ref, out_ref, small_ref,
 ):
     width = h_ref.shape[1]
     att = dq_ref.shape[1]
@@ -743,7 +743,18 @@
     out_ref[0:width, 0:att] = dot(ht, dq_ref[...]).astype(BF)
     out_ref[0:width, att:] = dot(ht, dsp_ref[...]).astype(BF)
     out_ref[width : width + att, :] = dot(dkc_ref[...].T, dep_ref[...]).astype(BF)
-    kw_ref[...] = dot(dl_ref[...].T, mx_ref[...])
+    t8 = dl_ref.shape[1]
+    small_ref[...] = jnp.zeros(small_ref.shape, F32)
+    small_ref[0:t8, 0:att] = dot(dl_ref[...].T, mx_ref[...])
+    small_ref[t8 : t8 + SUB, :] = vec_ref[...]
+    for n in range(db1_ref.shape[1] // width):
+        small_ref[t8 + SUB + n : t8 + SUB + n + 1, :] = db1_ref[:, n * width : (n + 1) * width]
+    small_ref[t8 + 2 * SUB : t8 + 2 * SUB + dkg_ref.shape[0], :] = dkg_ref[...]
+    four = t8 + 4 * SUB
+    small_ref[four : four + 2, 0:att] = dbp_ref[0:2, :]
+    small_ref[four + 2 : four + 3, 0:att] = dbv_ref[...]
+    small_ref[four + 3 : four + 4, 0:att] = dpb_ref[...]
+    small_ref[four + SUB : four + SUB + 1, 0:t8] = jnp.broadcast_to(dkb_ref[...], (t8, 128)).T[0:1]
     ready()
     m = m_ref[...]
     total = dot(m, res_ref[...])
@@ -753,19 +764,21 @@
         low = (part - high.astype(F32)).astype(BF)
         w = wp_ref[:, n * att : (n + 1) * att]
         total = total + dot_nt(high, w) + dot_nt(low, w)
-    mg_ref[...] = total
-
-
-def run_last_grads(h, dq, dk, dv, dsp, dep, dkc, mx, dl, res, mask_rows, p):
+    small_ref[t8 + 6 * SUB - 1 : t8 + 6 * SUB, :] = total[0:1]
+    out_ref[width + att :, :] = small_ref[...].astype(BF)
+
+
+def run_last_grads(h, dq, dk, dv, dsp, dep, dkc, mx, dl, res, mask_rows, sums, lines, p):
     rows, width = h.shape
     att = dq.shape[1]
-    inputs = (h, dq, dk, dv, dsp, dep, dkc, mx, dl, mask_rows, res)
+    inputs = (h, dq, dk, dv, dsp, dep, dkc, mx, dl, mask_rows, res) + sums
     return call(
         last_grad_kernel, p, ("wp",), inputs,
         grid=(1,),
         in_specs=[whole(a.shape) for a in inputs],
-        out_specs=[whole((width + att, width)), whole((dl.shape[1], att)), whole((SUB, width))],
-        out_shape=[sds((width + att, width), BF), sds((dl.shape[1], att), F32), sds((SUB, width), F32)],
+        out_specs=whole((width + att + lines, width)),
+        out_shape=sds((width + att + lines, width), BF),
+        scratch_shapes=[pltpu.VMEM((lines, width), F32)],
         name="last_wgrad", us=9,
     )
 
@@ -803,21 +816,6 @@
     keep = dict(h=h, q2=q2, k=k, v=v, sp=sp, q2t=q2t, kt=kt, dep=dep, kc=kc, mx=mx, kern=kern, at=at, lse=lse,
                 ctx=ctx, u1=u1, r1=r1, nl=nl, act=act, gp=gp, u2=u2, r2=r2)
     return out, keep
-
-
-def small_rows(vec, db1, dkg, dbp, dbv, dpb, dkb, dkw, mg, lines):
-    width = vec.shape[1]
-    att = dpb.shape[1]
-
-    def wide(a, n):
-        return jnp.pad(a, ((0, n - a.shape[0]), (0, width - a.shape[1])))
-
-    rows = [
-        wide(dkw, dkw.shape[0]), vec, wide(db1.reshape(-1, width), SUB), wide(dkg, 2 * SUB),
-        wide(jnp.concatenate([dbp[0:2], dbv, dpb]), SUB), wide(dkb.reshape(1, -1), SUB - 1), mg,
-    ]
-    rows = jnp.concatenate(rows)
-    return jnp.pad(rows, ((0, lines - rows.shape[0]), (0, 0))).astype(BF)
 
 
 def mask_row(taps):
@@ -842,9 +840,8 @@
     ddn, dqa = slot("conv", (ddn, dqa))
     dl, dq, dsp, dkc, res, dkg, dpb, dkb, dbp = run_conv_back(ddn, dz, dqa, h, keep, ex, ext, p)
     dq, dl, res = slot("last", (dq, dl, res))
-    last, dkw, mg = run_last_grads(h, dq, dk, dv, dsp, keep["dep"], dkc, keep["mx"], dl, res, mask_rows, p)
-    small = small_rows(vec, db1, dkg, dbp, dbv, dpb, dkb, dkw, mg[0:1], lines)
-    send(2, jnp.concatenate([last, small]))
+    sums = (vec, db1, dkg, dbp, dbv, dpb, dkb)
+    send(2, run_last_grads(h, dq, dk, dv, dsp, keep["dep"], dkc, keep["mx"], dl, res, mask_rows, sums, lines, p))
     dq, res = slot("in", (dq, res))
     return slot("end", run_in_back(dq, dk, dv, dsp, res, mask, p))
 
@@ -1147,11 +1144,11 @@
     "1ffn": ("states",),
     "1attn": ("10",),
     "1conv": ("11",),
-    "1last": ("11", "states"),
+    "1last": ("11",),
     "1in": ("12",),
     "0ffn": ("12",),
     "0wide": ("11", "12"),
-    "0attn": ("10", "00", "11", "12"),
+    "0attn": ("10", "00", "11", "12", "states"),
     "0mid": ("11", "12"),
     "0conv": ("01", "11"),
     "0last": ("01",),

time: 592 us -> 587 us (level)
  other arithmetic: 71 us -> 55.7 us
  waiting for transfers between devices: 126 us -> 133 us
    another operation x14 -> x0, other arithmetic: 8.77 us -> none
    ppermute x11, waiting for transfers between devices: 45.8 us -> 53.2 us  [swap(): return lax.ppermute(x, 'section', [(0, 1), (1, 0)])]
  transfers between devices with their start and end apart: 50 -> 50, of which waited for: 18 -> 18; matrix products, arithmetic and copies ran while one was open for 10% -> 8% of each run, Pallas kernels for 28% -> 29%
where the time goes in v5:
time: 587 us; the launch traced here: 578 us
  Pallas kernels  300 us (51%)
  waiting for transfers between devices  133 us (23%)
  other arithmetic  55.7 us (9%)
  starting transfers between devices  45.4 us (8%)
  local copies, waits for them, and re-layouts  28.3 us (5%)
  between operations  15.6 us (3%)
    pallas_call x12, Pallas kernels, call(): pl.pallas_call(body, grid=grid, in_specs=[SMEM] + [HBM] * len(operands) +...  190 us
    ppermute x37, waiting for transfers between devices, across(): lax.ppermute(x, 'dp', [(i, i ^ 1 << bit) for i in range(lax.axis_size('dp...  79.4 us
    ppermute x11, waiting for transfers between devices, swap(): return lax.ppermute(x, 'section', [(0, 1), (1, 0)])  53.2 us
    pallas_call x2, Pallas kernels, run_attn_back(): pl.pallas_call(partial(attn_back_kernel, head=head, qb=128), grid=(pairs,...  35.9 us
    ppermute x37, starting transfers between devices, across(): lax.ppermute(x, 'dp', [(i, i ^ 1 << bit) for i in range(lax.axis_size('dp...  33.9 us
    convert_element_type x16, other arithmetic, total_of(): return total.astype(BF)  23.4 us
    pallas_call x2, Pallas kernels, run_wide_grads(): pl.pallas_call(wide_grad_kernel, grid=(groups, steps), in_specs=[narrow,...  21.8 us
    pallas_call x2, Pallas kernels, run_attn(): pl.pallas_call(partial(attn_kernel, head=head, qb=512), grid=(pairs,), in...  20.8 us
  transfers between devices with their start and end apart: 50, of which 18 were waited for; matrix products, arithmetic and copies ran while one was open for 8% of the time, Pallas kernels for 29%

profile of v5, /device:TPU:0, one launch (start us, length us, event | category | flops | bytes accessed | tf_op | source)
XLA Modules:
  0.0 577.6 jit_solution(1173397990237069338)
XLA Ops:
  22.5 9.2 %collective-permute-done.refs_2_.refs_1_ = bf16[240,1536]{1,0:T(8,128)(2,1)} collective-permute-done((bf16[240,1536]{1,0:T(8,128)(2,1)}, bf16[240,1536]{1,0:T(8,128)(2,1)}, u32[]{:S(2)}, u32[]{:S(2)}) %collective-permute-start) | collective-permute-done | bytes 737312 | tf_op jit(solution)/shard_map/ppermute | solution.py:880
  36.1 19.7 %collective-permute-done.4 = bf16[76,768]{1,0:T(8,128)(2,1)S(1)} collective-permute-done((bf16[76,768]{1,0:T(8,128)(2,1)S(1)}, bf16[76,768]{1,0:T(8,128)(2,1)S(1)}, u32[]{:S(2)}, u32[]{:S(2)}) %collective-permute-start.4) | collective-permute-done | bytes 116768 | tf_op jit(solution)/shard_map/ppermute | solution.py:880
  62.0 11.6 %proj_fwd.2 = (bf16[1024,384]{1,0:T(8,128)(2,1)}, bf16[1024,384]{1,0:T(8,128)(2,1)}, bf16[1024,384]{1,0:T(8,128)(2,1)}, bf16[1024,384]{1,0:T(8,128)(2,1)}, bf16[...) custom-call(s32[2]{0:T(128)} %get-tuple-element.668.place_ref, ...), custom_call_target="tpu_custom_call" | custom-call | flops 14300000256 | tf_op jit(solution)/shard_map/proj_fwd/pallas_call | solution.py:141
  75.2 4.4 collective-permute-done.6.refs_3_
  81.3 10.4 %attn_fwd.2 = (f32[384,1024]{1,0:T(8,128)}, f32[3,8,1024]{2,1,0:T(8,128)}) custom-call(bf16[1024,384]{1,0:T(8,128)(2,1)} %get-tuple-element.385.k_ref, bf16[384,1024]{1,0:T(8,128)(2,1)} %get-tuple-element.386.qt_ref, bf16[384,1024]{1,0:T(8,128)(2,1)} %get-tuple-element.387.vt_ref), custom_call_target="tpu_custom_call" | custom-call | flops 20899999744 | tf_op jit(solution)/shard_map/attn_fwd/pallas_call | solution.py:290
  100.1 23.8 %ffn_fwd.2 = (bf16[1024,768]{1,0:T(8,128)(2,1)}, bf16[1024,768]{1,0:T(8,128)(2,1)}, f32[1024,1]{1,0:T(8,128)}, bf16[1024,768]{1,0:T(8,128)(2,1)}, bf16[1024,3072...) custom-call(s32[2]{0:T(128)} %get-tuple-element.668.place_ref, ...), custom_call_target="tpu_custom_call" | custom-call | flops 24199999488 | tf_op jit(solution)/shard_map/ffn_fwd/pallas_call | solution.py:141
  123.9 11.8 %proj_fwd.3 = (bf16[1024,384]{1,0:T(8,128)(2,1)}, bf16[1024,384]{1,0:T(8,128)(2,1)}, bf16[1024,384]{1,0:T(8,128)(2,1)}, bf16[1024,384]{1,0:T(8,128)(2,1)}, bf16[...) custom-call(s32[2]{0:T(128)} %get-tuple-element.668.place_ref, ...), custom_call_target="tpu_custom_call" | custom-call | flops 14300000256 | tf_op jit(solution)/shard_map/proj_fwd/pallas_call | solution.py:141
  135.7 10.4 %attn_fwd.3 = (f32[384,1024]{1,0:T(8,128)}, f32[3,8,1024]{2,1,0:T(8,128)}) custom-call(bf16[1024,384]{1,0:T(8,128)(2,1)} %get-tuple-element.405.k_ref, bf16[384,1024]{1,0:T(8,128)(2,1)} %get-tuple-element.406.qt_ref, bf16[384,1024]{1,0:T(8,128)(2,1)} %get-tuple-element.407.vt_ref), custom_call_target="tpu_custom_call" | custom-call | flops 20899999744 | tf_op jit(solution)/shard_map/attn_fwd/pallas_call | solution.py:290
  146.1 23.8 %ffn_fwd.3 = (bf16[1024,768]{1,0:T(8,128)(2,1)}, bf16[1024,768]{1,0:T(8,128)(2,1)}, f32[1024,1]{1,0:T(8,128)}, bf16[1024,768]{1,0:T(8,128)(2,1)}, bf16[1024,3072...) custom-call(s32[2]{0:T(128)} %get-tuple-element.668.place_ref, ...), custom_call_target="tpu_custom_call" | custom-call | flops 24199999488 | tf_op jit(solution)/shard_map/ffn_fwd/pallas_call | solution.py:141
  171.5 18.7 %ffn_bwd.2 = (bf16[1024,768]{1,0:T(8,128)(2,1)}, bf16[1024,3072]{1,0:T(8,128)(2,1)}, bf16[1024,768]{1,0:T(8,128)(2,1)}, bf16[384,1024]{1,0:T(8,128)(2,1)}, bf16[...) custom-call(s32[2]{0:T(128)} %get-tuple-element.668.place_ref, ...), custom_call_target="tpu_custom_call" | custom-call | flops 19800000512 | tf_op jit(solution)/shard_map/ffn_bwd/pallas_call | solution.py:141
  190.2 10.9 %ffn_wgrad.2 = bf16[2,1536,768]{2,1,0:T(8,128)(2,1)} custom-call(bf16[1024,768]{1,0:T(8,128)(2,1)} %get-tuple-element.428.nl_ref, bf16[1024,3072]{1,0:T(8,128)(2,1)} %get-tuple-element.429.di_ref, bf16[1024,768]{1,0:T(8,128)(2,1)} %get-tuple-element.430.ds_ref, bf16[1024,3072]{1,0:T(8,128)(2,1)} %get-tuple-element.431.act_ref), custom_call_target="tpu_custom_call" | custom-call | flops 6600000000 | tf_op jit(solution)/shard_map/ffn_wgrad/pallas_call | solution.py:704
  201.1 17.9 %attn_bwd.2 = (bf16[1024,384]{1,0:T(8,128)(2,1)}, bf16[1024,384]{1,0:T(8,128)(2,1)}, bf16[1024,384]{1,0:T(8,128)(2,1)}, f32[1,384]{1,0:T(1,128)}) custom-call(bf16[1024,384]{1,0:T(8,128)(2,1)} %get-tuple-element.405.k_ref, bf16[1024,384]{1,0:T(8,128)(2,1)} %get-tuple-element.420.v_ref, bf16[1024,384]{1,0:T(8,128)(2,1)} %get-tuple-element.421.q2_ref.refs_9_, ...), custom_call_target="tpu_custom_call" | custom-call | flops 22000001024 | tf_op jit(solution)/shard_map/attn_bwd/pallas_call | solution.py:654
  219.0 7.3 %mid_wgrad.2 = bf16[1536,768]{1,0:T(8,128)(2,1)} custom-call(bf16[1024,768]{1,0:T(8,128)(2,1)} %get-tuple-element.442.ctx_ref, bf16[1024,768]{1,0:T(8,128)(2,1)} %get-tuple-element.443.dz_ref.refs_11_, bf16[1024,768]{1,0:T(8,128)(2,1)} %get-tuple-element.401.refs_6_.refs_14_.h_ref.refs_10_.refs_5_, ...), custom_call_target="tpu_custom_call" | custom-call | flops 5500000256 | tf_op jit(solution)/shard_map/mid_wgrad/pallas_call | solution.py:727
  228.7 22.2 %conv_bwd.2 = (bf16[1024,72]{1,0:T(8,128)(2,1)}, bf16[1024,384]{1,0:T(8,128)(2,1)}, bf16[1024,384]{1,0:T(8,128)(2,1)}, bf16[1024,384]{1,0:T(8,128)(2,1)}, bf16[1...) custom-call(s32[2]{0:T(128)} %get-tuple-element.668.place_ref, ...), custom_call_target="tpu_custom_call" | custom-call | flops 29699999744 | tf_op jit(solution)/shard_map/conv_bwd/pallas_call | solution.py:141
  254.2 10.1 %last_wgrad.2 = bf16[1280,768]{1,0:T(8,128)(2,1)} custom-call(s32[2]{0:T(128)} %get-tuple-element.668.place_ref, bf16[768,1536]{1,0:T(8,128)(2,1)} %bitcast.86, bf16[240,1536]{1,0:T(8,128)(2,1)} %collective-permute-done.refs_2_.refs_1_, bf16[240,1536]{1,0:T(8,128)(2,1)} %collective-permute-done.1.refs_3_.refs_2_, bf16[240,1536]{1,0:T(8,128)(2,1)} %copy-done.62, ...), custom_call_target="tpu_custom_call" | custom-call | flops 9900000256 | tf_op jit(solution)/shard_map/last_wgrad/pallas_call | solution.py:141
  268.1 8.5 %in_bwd.2.refs_11_ = bf16[1024,768]{1,0:T(8,128)(2,1)} custom-call(s32[2]{0:T(128)} %get-tuple-element.668.place_ref, bf16[768,1536]{1,0:T(8,128)(2,1)} %bitcast.87, bf16[240,1536]{1,0:T(8,128)(2,1)} %collective-permute-done.refs_2_.refs_1_, bf16[240,1536]{1,0:T(8,128)(2,1)} %collective-permute-done.1.refs_3_.refs_2_, bf16[240,1536]{1,0:T(8,128)(2,1)} %copy-done.62, ...), custom_call_target="tpu_custom_call" | custom-call | flops 8800000000 | tf_op jit(solution)/shard_map/in_bwd/pallas_call | solution.py:141
  281.5 18.8 %ffn_bwd.3 = (bf16[1024,768]{1,0:T(8,128)(2,1)}, bf16[1024,3072]{1,0:T(8,128)(2,1)}, bf16[1024,768]{1,0:T(8,128)(2,1)}, bf16[384,1024]{1,0:T(8,128)(2,1)}, bf16[...) custom-call(s32[2]{0:T(128)} %get-tuple-element.668.place_ref, ...), custom_call_target="tpu_custom_call" | custom-call | flops 19800000512 | tf_op jit(solution)/shard_map/ffn_bwd/pallas_call | solution.py:141
  300.3 15.6 %collective-permute-done.15 = bf16[768,384]{1,0:T(8,128)(2,1)S(1)} collective-permute-done((bf16[768,384]{1,0:T(8,128)(2,1)S(1)}, bf16[768,384]{1,0:T(8,128)(2,1)S(1)}, u32[]{:S(2)}, u32[]{:S(2)}) %collective-permute-start.15) | collective-permute-done | bytes 589856 | tf_op jit(solution)/shard_map/ppermute | solution.py:880
  321.1 10.9 %ffn_wgrad.3 = bf16[2,1536,768]{2,1,0:T(8,128)(2,1)} custom-call(bf16[1024,768]{1,0:T(8,128)(2,1)} %get-tuple-element.505.nl_ref, bf16[1024,3072]{1,0:T(8,128)(2,1)} %get-tuple-element.506.di_ref, bf16[1024,768]{1,0:T(8,128)(2,1)} %get-tuple-element.507.ds_ref, bf16[1024,3072]{1,0:T(8,128)(2,1)} %get-tuple-element.508.act_ref), custom_call_target="tpu_custom_call" | custom-call | flops 6600000000 | tf_op jit(solution)/shard_map/ffn_wgrad/pallas_call | solution.py:704
  338.8 18.1 %attn_bwd.3 = (bf16[1024,384]{1,0:T(8,128)(2,1)}, bf16[1024,384]{1,0:T(8,128)(2,1)}, bf16[1024,384]{1,0:T(8,128)(2,1)}, f32[1,384]{1,0:T(1,128)}) custom-call(bf16[1024,384]{1,0:T(8,128)(2,1)} %get-tuple-element.385.k_ref, bf16[1024,384]{1,0:T(8,128)(2,1)} %get-tuple-element.501.v_ref, bf16[1024,384]{1,0:T(8,128)(2,1)} %get-tuple-element.502.q2_ref.refs_9_, ...), custom_call_target="tpu_custom_call" | custom-call | flops 22000001024 | tf_op jit(solution)/shard_map/attn_bwd/pallas_call | solution.py:654
  359.6 7.3 %mid_wgrad.3 = bf16[1536,768]{1,0:T(8,128)(2,1)} custom-call(bf16[1024,768]{1,0:T(8,128)(2,1)} %get-tuple-element.528.ctx_ref, bf16[1024,768]{1,0:T(8,128)(2,1)} %get-tuple-element.529.dz_ref.refs_11_, bf16[1024,768]{1,0:T(8,128)(2,1)} %bitcast_select_fusion.refs_6_.refs_14_.h_ref.refs_10_.refs_5_, ...), custom_call_target="tpu_custom_call" | custom-call | flops 5500000256 | tf_op jit(solution)/shard_map/mid_wgrad/pallas_call | solution.py:727
  368.9 21.9 %conv_bwd.3 = (bf16[1024,72]{1,0:T(8,128)(2,1)}, bf16[1024,384]{1,0:T(8,128)(2,1)}, bf16[1024,384]{1,0:T(8,128)(2,1)}, bf16[1024,384]{1,0:T(8,128)(2,1)}, bf16[1...) custom-call(s32[2]{0:T(128)} %get-tuple-element.668.place_ref, ...), custom_call_target="tpu_custom_call" | custom-call | flops 29699999744 | tf_op jit(solution)/shard_map/conv_bwd/pallas_call | solution.py:141
  393.7 10.1 %last_wgrad.3 = bf16[1280,768]{1,0:T(8,128)(2,1)} custom-call(s32[2]{0:T(128)} %get-tuple-element.668.place_ref, bf16[768,1536]{1,0:T(8,128)(2,1)} %bitcast.88, bf16[240,1536]{1,0:T(8,128)(2,1)} %collective-permute-done.refs_2_.refs_1_, bf16[240,1536]{1,0:T(8,128)(2,1)} %collective-permute-done.1.refs_3_.refs_2_, bf16[240,1536]{1,0:T(8,128)(2,1)} %copy-done.62, ...), custom_call_target="tpu_custom_call" | custom-call | flops 9900000256 | tf_op jit(solution)/shard_map/last_wgrad/pallas_call | solution.py:141
  414.1 8.8 %in_bwd.3 = bf16[1024,768]{1,0:T(8,128)(2,1)} custom-call(s32[2]{0:T(128)} %get-tuple-element.668.place_ref, bf16[768,1536]{1,0:T(8,128)(2,1)} %bitcast.89, bf16[240,1536]{1,0:T(8,128)(2,1)} %collective-permute-done.refs_2_.refs_1_, bf16[240,1536]{1,0:T(8,128)(2,1)} %collective-permute-done.1.refs_3_.refs_2_, bf16[240,1536]{1,0:T(8,128)(2,1)} %copy-done.62, ...), custom_call_target="tpu_custom_call" | custom-call | flops 8800000000 | tf_op jit(solution)/shard_map/in_bwd/pallas_call | solution.py:141
  431.2 5.5 collective-permute-done.27
  451.4 8.6 %collective-permute-done.31 = bf16[160,768]{1,0:T(8,128)(2,1)} collective-permute-done((bf16[160,768]{1,0:T(8,128)(2,1)}, bf16[160,768]{1,0:T(8,128)(2,1)}, u32[]{:S(2)}, u32[]{:S(2)}) %collective-permute-start.31) | collective-permute-done | bytes 245792 | tf_op jit(solution)/shard_map/ppermute | solution.py:884
  472.5 8.3 %collective-permute-done.33 = bf16[80,768]{1,0:T(8,128)(2,1)S(1)} collective-permute-done((bf16[80,768]{1,0:T(8,128)(2,1)}, bf16[80,768]{1,0:T(8,128)(2,1)S(1)}, u32[]{:S(2)}, u32[]{:S(2)}) %collective-permute-start.33) | collective-permute-done | bytes 122912 | tf_op jit(solution)/shard_map/ppermute | solution.py:884
  497.9 13.7 %collective-permute-done.38 = bf16[80,768]{1,0:T(8,128)(2,1)S(1)} collective-permute-done((bf16[80,768]{1,0:T(8,128)(2,1)S(1)}, bf16[80,768]{1,0:T(8,128)(2,1)S(1)}, u32[]{:S(2)}, u32[]{:S(2)}) %collective-permute-start.38) | collective-permute-done | bytes 122912 | tf_op jit(solution)/shard_map/ppermute | solution.py:884
  516.3 18.7 %collective-permute-done.40 = bf16[160,768]{1,0:T(8,128)(2,1)S(1)} collective-permute-done((bf16[160,768]{1,0:T(8,128)(2,1)S(1)}, bf16[160,768]{1,0:T(8,128)(2,1)S(1)}, u32[]{:S(2)}, u32[]{:S(2)}) %collective-permute-start.40) | collective-permute-done | bytes 245792 | tf_op jit(solution)/shard_map/ppermute | solution.py:884
  544.9 8.3 %collective-permute-done.44 = bf16[320,768]{1,0:T(8,128)(2,1)S(1)} collective-permute-done((bf16[320,768]{1,0:T(8,128)(2,1)S(1)}, bf16[320,768]{1,0:T(8,128)(2,1)S(1)}, u32[]{:S(2)}, u32[]{:S(2)}) %collective-permute-start.44) | collective-permute-done | bytes 491552 | tf_op jit(solution)/shard_map/ppermute | solution.py:884
  555.1 6.8 %wide_out.1 = (f32[768,1536]{1,0:T(8,128)}, f32[3072,384]{1,0:T(8,128)}) custom-call(s32[1]{0:T(128)} %bitcast.30.at_ref, bf16[1536,768]{1,0:T(8,128)(2,1)} %copy-done.8, bf16[1536,768]{1,0:T(8,128)(2,1)} %copy-done.54), custom_call_target="tpu_custom_call" | custom-call | flops 7699999744 | tf_op jit(solution)/shard_map/wide_out/pallas_call | solution.py:1058
  562.8 6.2 %last_out.1 = (f32[768,1536]{1,0:T(8,128)}, f32[768,384]{1,0:T(8,128)}, f32[768,768]{1,0:T(8,128)}, f32[1,1152]{1,0:T(1,128)}, f32[9,1,768]{2,1,0:T(1,128)}, /*i...) custom-call(s32[2]{0:T(128)} %get-tuple-element.669.at_ref, ...), custom_call_target="tpu_custom_call" | custom-call | flops 6600000000 | tf_op jit(solution)/shard_map/last_out/pallas_call | solution.py:1126
  (327 shorter events, 153.9 us)
Async XLA Ops:
  7.2 326.0 %reduce-scatter.3.cloned.1.call-start = ((), (), s32[]{:S(2)}) async-start(), calls=%async_computation.2 | async-start | bytes 5013504 | tf_op jit(solution)/shard_map/reduce_scatter | solution.py:891
  11.8 19.8 %collective-permute-start = (bf16[240,1536]{1,0:T(8,128)(2,1)}, bf16[240,1536]{1,0:T(8,128)(2,1)}, u32[]{:S(2)}, u32[]{:S(2)}) collective-permute-start(bf16[240,1536]{1,0:T(8,128)(2,1)} %get-tuple-element.351), channel_id=1, source_target_pairs={{0,16},{16,0},{1,17},{17,1},{2,18},{18,2},{3,19},{19,3},{4,20},{20... | collective-permute-start | bytes 2211848 | tf_op jit(solution)/shard_map/ppermute | solution.py:880
  32.3 23.5 %collective-permute-start.3 = (bf16[288,1536]{1,0:T(8,128)(2,1)S(1)}, bf16[288,1536]{1,0:T(8,128)(2,1)S(1)}, u32[]{:S(2)}, u32[]{:S(2)}) collective-permute-start(bf16[288,1536]{1,0:T(8,128)(2,1)S(1)} %copy-done.61), channel_id=1, source_target_pairs={{0,16},{16,0},{1,17},{17,1},{2,18},{18,2},{3,19},{19,3},{4,20},{20... | collective-permute-start | bytes 2654216 | tf_op jit(solution)/shard_map/ppermute | solution.py:880
  34.0 21.7 %collective-permute-start.1 = (bf16[240,1536]{1,0:T(8,128)(2,1)}, bf16[240,1536]{1,0:T(8,128)(2,1)}, u32[]{:S(2)}, u32[]{:S(2)}) collective-permute-start(bf16[240,1536]{1,0:T(8,128)(2,1)} %collective-permute-done.refs_2_.refs_1_), channel_id=1, source_target_pairs={{0,2},{1,3},{2,0},{3,1},{4,6},{5,7},{6,4},{7,5},{8,10},{9,11},{10,... | collective-permute-start | bytes 2211848 | tf_op jit(solution)/shard_map/ppermute | solution.py:884
  35.5 20.2 %collective-permute-start.2 = (bf16[240,1536]{1,0:T(8,128)(2,1)}, bf16[240,1536]{1,0:T(8,128)(2,1)S(1)}, u32[]{:S(2)}, u32[]{:S(2)}) collective-permute-start(bf16[240,1536]{1,0:T(8,128)(2,1)} %collective-permute-done.refs_2_.refs_1_), channel_id=1, source_target_pairs={{0,1},{1,0},{2,3},{3,2},{4,5},{5,4},{6,7},{7,6},{8,9},{9,8},{10,11... | collective-permute-start | bytes 2211848 | tf_op jit(solution)/shard_map/ppermute | solution.py:884
  35.5 20.2 %collective-permute-start.4 = (bf16[76,768]{1,0:T(8,128)(2,1)S(1)}, bf16[76,768]{1,0:T(8,128)(2,1)S(1)}, u32[]{:S(2)}, u32[]{:S(2)}) collective-permute-start(bf16[76,768]{1,0:T(8,128)(2,1)S(1)} %fusion.8), channel_id=1, source_target_pairs={{0,16},{16,0},{1,17},{17,1},{2,18},{18,2},{3,19},{19,3},{4,20},{20... | collective-permute-start | bytes 350216 | tf_op jit(solution)/shard_map/ppermute | solution.py:880
  57.8 21.8 %collective-permute-start.6 = (bf16[288,1536]{1,0:T(8,128)(2,1)S(1)}, bf16[288,1536]{1,0:T(8,128)(2,1)S(1)}, u32[]{:S(2)}, u32[]{:S(2)}) collective-permute-start(bf16[288,1536]{1,0:T(8,128)(2,1)S(1)} %collective-permute-done.3.refs_2_), channel_id=1, source_target_pairs={{0,2},{1,3},{2,0},{3,1},{4,6},{5,7},{6,4},{7,5},{8,10},{9,11},{10,... | collective-permute-start | bytes 2654216 | tf_op jit(solution)/shard_map/ppermute | solution.py:884
  59.2 20.4 %collective-permute-start.7 = (bf16[288,1536]{1,0:T(8,128)(2,1)S(1)}, bf16[288,1536]{1,0:T(8,128)(2,1)S(1)}, u32[]{:S(2)}, u32[]{:S(2)}) collective-permute-start(bf16[288,1536]{1,0:T(8,128)(2,1)S(1)} %collective-permute-done.3.refs_2_), channel_id=1, source_target_pairs={{0,1},{1,0},{2,3},{3,2},{4,5},{5,4},{6,7},{7,6},{8,9},{9,8},{10,11... | collective-permute-start | bytes 2654216 | tf_op jit(solution)/shard_map/ppermute | solution.py:884
  59.2 16.0 %collective-permute-start.8 = (bf16[192,1536]{1,0:T(8,128)(2,1)}, bf16[192,1536]{1,0:T(8,128)(2,1)S(1)}, u32[]{:S(2)}, u32[]{:S(2)}) collective-permute-start(bf16[192,1536]{1,0:T(8,128)(2,1)} %get-tuple-element.378), channel_id=1, source_target_pairs={{0,16},{16,0},{1,17},{17,1},{2,18},{18,2},{3,19},{19,3},{4,20},{20... | collective-permute-start | bytes 1769480 | tf_op jit(solution)/shard_map/ppermute | solution.py:880
  79.6 15.9 %collective-permute-start.9 = (bf16[288,1536]{1,0:T(8,128)(2,1)S(1)}, bf16[288,1536]{1,0:T(8,128)(2,1)S(1)}, u32[]{:S(2)}, u32[]{:S(2)}) collective-permute-start(bf16[288,1536]{1,0:T(8,128)(2,1)S(1)} %collective-permute-done.6.refs_3_), channel_id=1, source_target_pairs={{0,1},{1,0},{2,3},{3,2},{4,5},{5,4},{6,7},{7,6},{8,9},{9,8},{10,11... | collective-permute-start | bytes 2654216 | tf_op jit(solution)/shard_map/ppermute | solution.py:884
  79.6 15.8 %collective-permute-start.10 = (bf16[192,1536]{1,0:T(8,128)(2,1)S(1)}, bf16[192,1536]{1,0:T(8,128)(2,1)}, u32[]{:S(2)}, u32[]{:S(2)}) collective-permute-start(bf16[192,1536]{1,0:T(8,128)(2,1)S(1)} %collective-permute-done.8.refs_7_), channel_id=1, source_target_pairs={{0,2},{1,3},{2,0},{3,1},{4,6},{5,7},{6,4},{7,5},{8,10},{9,11},{10,... | collective-permute-start | bytes 1769480 | tf_op jit(solution)/shard_map/ppermute | solution.py:884
  81.2 14.3 %collective-permute-start.11 = (bf16[192,1536]{1,0:T(8,128)(2,1)S(1)}, bf16[192,1536]{1,0:T(8,128)(2,1)S(1)}, u32[]{:S(2)}, u32[]{:S(2)}) collective-permute-start(bf16[192,1536]{1,0:T(8,128)(2,1)S(1)} %collective-permute-done.8.refs_7_), channel_id=1, source_target_pairs={{0,1},{1,0},{2,3},{3,2},{4,5},{5,4},{6,7},{7,6},{8,9},{9,8},{10,11... | collective-permute-start | bytes 1769480 | tf_op jit(solution)/shard_map/ppermute | solution.py:884
  228.6 22.3 %collective-permute-start.13 = (bf16[768,768]{1,0:T(8,128)(2,1)}, bf16[768,768]{1,0:T(8,128)(2,1)S(1)}, u32[]{:S(2)}, u32[]{:S(2)}) collective-permute-start(bf16[768,768]{1,0:T(8,128)(2,1)} %constant_dynamic-slice_fusion.3), channel_id=1, source_target_pairs={{0,1},{1,0},{2,3},{3,2},{4,5},{5,4},{6,7},{7,6},{8,9},{9,8},{10,11... | collective-permute-start | bytes 3538952 | tf_op jit(solution)/shard_map/ppermute | solution.py:884
  228.6 194.3 %reduce-scatter.5.cloned.1.call-start = ((), (), s32[]{:S(2)}) async-start(), calls=%async_computation.3 | async-start | bytes 5013504 | tf_op jit(solution)/shard_map/reduce_scatter | solution.py:891
  267.0 65.0 %collective-permute-start.19 = (bf16[1024,768]{1,0:T(8,128)(2,1)S(1)}, bf16[1024,768]{1,0:T(8,128)(2,1)S(1)}, u32[]{:S(2)}, u32[]{:S(2)}) collective-permute-start(bf16[1024,768]{1,0:T(8,128)(2,1)S(1)} %broadcast_select_fusion.2), channel_id=1, source_target_pairs={{0,16},{16,0},{1,17},{17,1},{2,18},{18,2},{3,19},{19,3},{4,20},{20... | collective-permute-start | bytes 4718600 | tf_op jit(solution)/shard_map/ppermute | solution.py:880
  276.7 39.3 %collective-permute-start.15 = (bf16[768,384]{1,0:T(8,128)(2,1)S(1)}, bf16[768,384]{1,0:T(8,128)(2,1)S(1)}, u32[]{:S(2)}, u32[]{:S(2)}) collective-permute-start(bf16[768,384]{1,0:T(8,128)(2,1)S(1)} %copy-done.20), channel_id=1, source_target_pairs={{0,16},{16,0},{1,17},{17,1},{2,18},{18,2},{3,19},{19,3},{4,20},{20... | collective-permute-start | bytes 1769480 | tf_op jit(solution)/shard_map/ppermute | solution.py:880
  280.0 36.0 %collective-permute-start.16 = (bf16[320,768]{1,0:T(8,128)(2,1)S(1)}, bf16[320,768]{1,0:T(8,128)(2,1)S(1)}, u32[]{:S(2)}, u32[]{:S(2)}) collective-permute-start(bf16[320,768]{1,0:T(8,128)(2,1)S(1)} %add_convert_fusion.3), channel_id=1, source_target_pairs={{0,2},{1,3},{2,0},{3,1},{4,6},{5,7},{6,4},{7,5},{8,10},{9,11},{10,... | collective-permute-start | bytes 1474568 | tf_op jit(solution)/shard_map/ppermute | solution.py:884
  319.0 14.2 %collective-permute-start.17 = (bf16[384,384]{1,0:T(8,128)(2,1)S(1)}, bf16[384,384]{1,0:T(8,128)(2,1)S(1)}, u32[]{:S(2)}, u32[]{:S(2)}) collective-permute-start(bf16[384,384]{1,0:T(8,128)(2,1)S(1)} %add_convert_fusion.6), channel_id=1, source_target_pairs={{0,4},{1,5},{2,6},{3,7},{4,0},{5,1},{6,2},{7,3},{8,12},{9,13},{10,... | collective-permute-start | bytes 884744 | tf_op jit(solution)/shard_map/ppermute | solution.py:884
  335.8 21.1 %collective-permute-start.20 = (bf16[192,384]{1,0:T(8,128)(2,1)S(1)}, bf16[192,384]{1,0:T(8,128)(2,1)S(1)}, u32[]{:S(2)}, u32[]{:S(2)}) collective-permute-start(bf16[192,384]{1,0:T(8,128)(2,1)S(1)} %add_convert_fusion.10), channel_id=1, source_target_pairs={{0,8},{1,9},{2,10},{3,11},{4,12},{5,13},{6,14},{7,15},{8,0},{9,1},... | collective-permute-start | bytes 442376 | tf_op jit(solution)/shard_map/ppermute | solution.py:884
  338.4 18.5 %collective-permute-start.21 = (bf16[80,768]{1,0:T(8,128)(2,1)S(1)}, bf16[80,768]{1,0:T(8,128)(2,1)S(1)}, u32[]{:S(2)}, u32[]{:S(2)}) collective-permute-start(bf16[80,768]{1,0:T(8,128)(2,1)S(1)} %add_convert_fusion.15), channel_id=1, source_target_pairs={{0,8},{1,9},{2,10},{3,11},{4,12},{5,13},{6,14},{7,15},{8,0},{9,1},... | collective-permute-start | bytes 368648 | tf_op jit(solution)/shard_map/ppermute | solution.py:884
  368.9 21.9 %collective-permute-start.23 = (bf16[768,768]{1,0:T(8,128)(2,1)S(1)}, bf16[768,768]{1,0:T(8,128)(2,1)S(1)}, u32[]{:S(2)}, u32[]{:S(2)}) collective-permute-start(bf16[768,768]{1,0:T(8,128)(2,1)S(1)} %constant_dynamic-slice_fusion.1), channel_id=1, source_target_pairs={{0,1},{1,0},{2,3},{3,2},{4,5},{5,4},{6,7},{7,6},{8,9},{9,8},{10,11... | collective-permute-start | bytes 3538952 | tf_op jit(solution)/shard_map/ppermute | solution.py:884
  392.7 15.8 %collective-permute-start.24 = (bf16[768,384]{1,0:T(8,128)(2,1)S(1)}, bf16[768,384]{1,0:T(8,128)(2,1)S(1)}, u32[]{:S(2)}, u32[]{:S(2)}) collective-permute-start(bf16[768,384]{1,0:T(8,128)(2,1)S(1)} %add_convert_fusion), channel_id=1, source_target_pairs={{0,16},{16,0},{1,17},{17,1},{2,18},{18,2},{3,19},{19,3},{4,20},{20... | collective-permute-start | bytes 1769480 | tf_op jit(solution)/shard_map/ppermute | solution.py:880
  443.9 16.1 %collective-permute-start.32 = (bf16[192,768]{1,0:T(8,128)(2,1)S(1)}, bf16[192,768]{1,0:T(8,128)(2,1)}, u32[]{:S(2)}, u32[]{:S(2)}) collective-permute-start(bf16[192,768]{1,0:T(8,128)(2,1)S(1)} %add_convert_fusion.4), channel_id=1, source_target_pairs={{0,8},{1,9},{2,10},{3,11},{4,12},{5,13},{6,14},{7,15},{8,0},{9,1},... | collective-permute-start | bytes 884744 | tf_op jit(solution)/shard_map/ppermute | solution.py:884
  465.9 17.1 %collective-permute-start.35 = (bf16[384,768]{1,0:T(8,128)(2,1)}, bf16[384,768]{1,0:T(8,128)(2,1)}, u32[]{:S(2)}, u32[]{:S(2)}) collective-permute-start(bf16[384,768]{1,0:T(8,128)(2,1)} %pad_maximum_fusion.6), channel_id=1, source_target_pairs={{0,4},{1,5},{2,6},{3,7},{4,0},{5,1},{6,2},{7,3},{8,12},{9,13},{10,... | collective-permute-start | bytes 1769480 | tf_op jit(solution)/shard_map/ppermute | solution.py:884
  466.1 14.7 %collective-permute-start.33 = (bf16[80,768]{1,0:T(8,128)(2,1)}, bf16[80,768]{1,0:T(8,128)(2,1)S(1)}, u32[]{:S(2)}, u32[]{:S(2)}) collective-permute-start(bf16[80,768]{1,0:T(8,128)(2,1)} %add_convert_fusion.14), channel_id=1, source_target_pairs={{0,8},{1,9},{2,10},{3,11},{4,12},{5,13},{6,14},{7,15},{8,0},{9,1},... | collective-permute-start | bytes 368648 | tf_op jit(solution)/shard_map/ppermute | solution.py:884
  493.3 18.3 %collective-permute-start.39 = (bf16[192,768]{1,0:T(8,128)(2,1)S(1)}, bf16[192,768]{1,0:T(8,128)(2,1)S(1)}, u32[]{:S(2)}, u32[]{:S(2)}) collective-permute-start(bf16[192,768]{1,0:T(8,128)(2,1)S(1)} %pad_maximum_fusion.9), channel_id=1, source_target_pairs={{0,8},{1,9},{2,10},{3,11},{4,12},{5,13},{6,14},{7,15},{8,0},{9,1},... | collective-permute-start | bytes 884744 | tf_op jit(solution)/shard_map/ppermute | solution.py:884
  494.4 40.5 %collective-permute-start.42 = (bf16[1024,768]{1,0:T(8,128)(2,1)S(1)}, bf16[1024,768]{1,0:T(8,128)(2,1)}, u32[]{:S(2)}, u32[]{:S(2)}) collective-permute-start(bf16[1024,768]{1,0:T(8,128)(2,1)S(1)} %copy-done.9), channel_id=1, source_target_pairs={{0,16},{16,0},{1,17},{17,1},{2,18},{18,2},{3,19},{19,3},{4,20},{20... | collective-permute-start | bytes 4718600 | tf_op jit(solution)/shard_map/ppermute | solution.py:880
  494.6 17.0 %collective-permute-start.38 = (bf16[80,768]{1,0:T(8,128)(2,1)S(1)}, bf16[80,768]{1,0:T(8,128)(2,1)S(1)}, u32[]{:S(2)}, u32[]{:S(2)}) collective-permute-start(bf16[80,768]{1,0:T(8,128)(2,1)S(1)} %add_convert_fusion.11), channel_id=1, source_target_pairs={{0,8},{1,9},{2,10},{3,11},{4,12},{5,13},{6,14},{7,15},{8,0},{9,1},... | collective-permute-start | bytes 368648 | tf_op jit(solution)/shard_map/ppermute | solution.py:884
  496.4 39.2 %collective-permute-start.43 = (bf16[768,768]{1,0:T(8,128)(2,1)}, bf16[768,768]{1,0:T(8,128)(2,1)}, u32[]{:S(2)}, u32[]{:S(2)}) collective-permute-start(bf16[768,768]{1,0:T(8,128)(2,1)} %pad_maximum_fusion.3), channel_id=1, source_target_pairs={{0,2},{1,3},{2,0},{3,1},{4,6},{5,7},{6,4},{7,5},{8,10},{9,11},{10,... | collective-permute-start | bytes 3538952 | tf_op jit(solution)/shard_map/ppermute | solution.py:884
  514.2 20.7 %collective-permute-start.41 = (bf16[384,768]{1,0:T(8,128)(2,1)}, bf16[384,768]{1,0:T(8,128)(2,1)}, u32[]{:S(2)}, u32[]{:S(2)}) collective-permute-start(bf16[384,768]{1,0:T(8,128)(2,1)} %pad_maximum_fusion.7), channel_id=1, source_target_pairs={{0,4},{1,5},{2,6},{3,7},{4,0},{5,1},{6,2},{7,3},{8,12},{9,13},{10,... | collective-permute-start | bytes 1769480 | tf_op jit(solution)/shard_map/ppermute | solution.py:884
  514.2 20.7 %collective-permute-start.40 = (bf16[160,768]{1,0:T(8,128)(2,1)S(1)}, bf16[160,768]{1,0:T(8,128)(2,1)S(1)}, u32[]{:S(2)}, u32[]{:S(2)}) collective-permute-start(bf16[160,768]{1,0:T(8,128)(2,1)S(1)} %pad_maximum_fusion.10), channel_id=1, source_target_pairs={{0,4},{1,5},{2,6},{3,7},{4,0},{5,1},{6,2},{7,3},{8,12},{9,13},{10,... | collective-permute-start | bytes 737288 | tf_op jit(solution)/shard_map/ppermute | solution.py:884
  539.5 13.8 %collective-permute-start.46 = (bf16[1536,768]{1,0:T(8,128)(2,1)S(1)}, bf16[1536,768]{1,0:T(8,128)(2,1)S(1)}, u32[]{:S(2)}, u32[]{:S(2)}) collective-permute-start(bf16[1536,768]{1,0:T(8,128)(2,1)S(1)} %pad_maximum_fusion.2.own_ref), channel_id=1, source_target_pairs={{0,1},{1,0},{2,3},{3,2},{4,5},{5,4},{6,7},{7,6},{8,9},{9,8},{10,11... | collective-permute-start | bytes 7077896 | tf_op jit(solution)/shard_map/ppermute | solution.py:884
  (85 other events, 805.9 us)
Sparse Core Ops, SparseCore 0:
  228.8 76.8 reduce-scatter.2
  338.9 75.8 reduce-scatter.4

commit v6 on v5

--- a/solution.py
+++ b/solution.py
@@ -1147,11 +1147,10 @@
     "1last": ("11",),
     "1in": ("12",),
     "0ffn": ("12",),
-    "0wide": ("11", "12"),
     "0attn": ("10", "00", "11", "12", "states"),
     "0mid": ("11", "12"),
-    "0conv": ("01", "11"),
-    "0last": ("01",),
+    "0conv": ("01", "11", "12"),
+    "0last": ("01", "11"),
     "0in": ("01", "02"),
 }
 LAST = (

time: 587 us -> 586 us (level)
    ppermute x11, waiting for transfers between devices: 53.2 us -> 42.4 us  [swap(): return lax.ppermute(x, 'section', [(0, 1), (1, 0)])]
    ppermute x37, waiting for transfers between devices: 79.4 us -> 86.5 us  [across(): lax.ppermute(x, 'dp', [(i, i ^ 1 << bit) for i in range(lax.axis_size('dp...]
    unnamed x146 -> x144, local copies, waits for them, and re-layouts: 11.8 us -> 12 us
  transfers between devices with their start and end apart: 50 -> 50, of which waited for: 18 -> 19; matrix products, arithmetic and copies ran while one was open for 8% -> 8% of each run, Pallas kernels for 29% -> 29%
where the time goes in v6:
time: 586 us; the launch traced here: 576 us
  Pallas kernels  300 us (51%)
  waiting for transfers between devices  129 us (22%)
  other arithmetic  55.6 us (9%)
  starting transfers between devices  47.9 us (8%)
  local copies, waits for them, and re-layouts  28.4 us (5%)
  between operations  15.4 us (3%)
    pallas_call x12, Pallas kernels, call(): pl.pallas_call(body, grid=grid, in_specs=[SMEM] + [HBM] * len(operands) +...  190 us
    ppermute x37, waiting for transfers between devices, across(): lax.ppermute(x, 'dp', [(i, i ^ 1 << bit) for i in range(lax.axis_size('dp...  86.5 us
    ppermute x11, waiting for transfers between devices, swap(): return lax.ppermute(x, 'section', [(0, 1), (1, 0)])  42.4 us
    ppermute x37, starting transfers between devices, across(): lax.ppermute(x, 'dp', [(i, i ^ 1 << bit) for i in range(lax.axis_size('dp...  38.1 us
    pallas_call x2, Pallas kernels, run_attn_back(): pl.pallas_call(partial(attn_back_kernel, head=head, qb=128), grid=(pairs,...  36.2 us
    convert_element_type x16, other arithmetic, total_of(): return total.astype(BF)  23.3 us
    pallas_call x2, Pallas kernels, run_wide_grads(): pl.pallas_call(wide_grad_kernel, grid=(groups, steps), in_specs=[narrow,...  21.9 us
    pallas_call x2, Pallas kernels, run_attn(): pl.pallas_call(partial(attn_kernel, head=head, qb=512), grid=(pairs,), in...  20.8 us
  transfers between devices with their start and end apart: 50, of which 19 were waited for; matrix products, arithmetic and copies ran while one was open for 8% of the time, Pallas kernels for 29%

profile of v6, /device:TPU:0, one launch (start us, length us, event | category | flops | bytes accessed | tf_op | source)
XLA Modules:
  0.0 576.2 jit_solution(14180759359443544483)
XLA Ops:
  22.4 9.2 %collective-permute-done.refs_2_.refs_1_ = bf16[240,1536]{1,0:T(8,128)(2,1)} collective-permute-done((bf16[240,1536]{1,0:T(8,128)(2,1)}, bf16[240,1536]{1,0:T(8,128)(2,1)}, u32[]{:S(2)}, u32[]{:S(2)}) %collective-permute-start) | collective-permute-done | bytes 737312 | tf_op jit(solution)/shard_map/ppermute | solution.py:880
  36.0 19.7 %collective-permute-done.4 = bf16[76,768]{1,0:T(8,128)(2,1)S(1)} collective-permute-done((bf16[76,768]{1,0:T(8,128)(2,1)S(1)}, bf16[76,768]{1,0:T(8,128)(2,1)S(1)}, u32[]{:S(2)}, u32[]{:S(2)}) %collective-permute-start.4) | collective-permute-done | bytes 116768 | tf_op jit(solution)/shard_map/ppermute | solution.py:880
  61.9 11.6 %proj_fwd.2 = (bf16[1024,384]{1,0:T(8,128)(2,1)}, bf16[1024,384]{1,0:T(8,128)(2,1)}, bf16[1024,384]{1,0:T(8,128)(2,1)}, bf16[1024,384]{1,0:T(8,128)(2,1)}, bf16[...) custom-call(s32[2]{0:T(128)} %get-tuple-element.664.place_ref, ...), custom_call_target="tpu_custom_call" | custom-call | flops 14300000256 | tf_op jit(solution)/shard_map/proj_fwd/pallas_call | solution.py:141
  75.1 4.4 collective-permute-done.6.refs_3_
  81.3 10.4 %attn_fwd.2 = (f32[384,1024]{1,0:T(8,128)}, f32[3,8,1024]{2,1,0:T(8,128)}) custom-call(bf16[1024,384]{1,0:T(8,128)(2,1)} %get-tuple-element.383.k_ref, bf16[384,1024]{1,0:T(8,128)(2,1)} %get-tuple-element.384.qt_ref, bf16[384,1024]{1,0:T(8,128)(2,1)} %get-tuple-element.385.vt_ref), custom_call_target="tpu_custom_call" | custom-call | flops 20899999744 | tf_op jit(solution)/shard_map/attn_fwd/pallas_call | solution.py:290
  100.0 23.8 %ffn_fwd.2 = (bf16[1024,768]{1,0:T(8,128)(2,1)}, bf16[1024,768]{1,0:T(8,128)(2,1)}, f32[1024,1]{1,0:T(8,128)}, bf16[1024,768]{1,0:T(8,128)(2,1)}, bf16[1024,3072...) custom-call(s32[2]{0:T(128)} %get-tuple-element.664.place_ref, ...), custom_call_target="tpu_custom_call" | custom-call | flops 24199999488 | tf_op jit(solution)/shard_map/ffn_fwd/pallas_call | solution.py:141
  123.8 11.8 %proj_fwd.3 = (bf16[1024,384]{1,0:T(8,128)(2,1)}, bf16[1024,384]{1,0:T(8,128)(2,1)}, bf16[1024,384]{1,0:T(8,128)(2,1)}, bf16[1024,384]{1,0:T(8,128)(2,1)}, bf16[...) custom-call(s32[2]{0:T(128)} %get-tuple-element.664.place_ref, ...), custom_call_target="tpu_custom_call" | custom-call | flops 14300000256 | tf_op jit(solution)/shard_map/proj_fwd/pallas_call | solution.py:141
  135.7 10.4 %attn_fwd.3 = (f32[384,1024]{1,0:T(8,128)}, f32[3,8,1024]{2,1,0:T(8,128)}) custom-call(bf16[1024,384]{1,0:T(8,128)(2,1)} %get-tuple-element.403.k_ref, bf16[384,1024]{1,0:T(8,128)(2,1)} %get-tuple-element.404.qt_ref, bf16[384,1024]{1,0:T(8,128)(2,1)} %get-tuple-element.405.vt_ref), custom_call_target="tpu_custom_call" | custom-call | flops 20899999744 | tf_op jit(solution)/shard_map/attn_fwd/pallas_call | solution.py:290
  146.1 23.8 %ffn_fwd.3 = (bf16[1024,768]{1,0:T(8,128)(2,1)}, bf16[1024,768]{1,0:T(8,128)(2,1)}, f32[1024,1]{1,0:T(8,128)}, bf16[1024,768]{1,0:T(8,128)(2,1)}, bf16[1024,3072...) custom-call(s32[2]{0:T(128)} %get-tuple-element.664.place_ref, ...), custom_call_target="tpu_custom_call" | custom-call | flops 24199999488 | tf_op jit(solution)/shard_map/ffn_fwd/pallas_call | solution.py:141
  171.5 18.8 %ffn_bwd.2 = (bf16[1024,768]{1,0:T(8,128)(2,1)}, bf16[1024,3072]{1,0:T(8,128)(2,1)}, bf16[1024,768]{1,0:T(8,128)(2,1)}, bf16[384,1024]{1,0:T(8,128)(2,1)}, bf16[...) custom-call(s32[2]{0:T(128)} %get-tuple-element.664.place_ref, ...), custom_call_target="tpu_custom_call" | custom-call | flops 19800000512 | tf_op jit(solution)/shard_map/ffn_bwd/pallas_call | solution.py:141
  190.4 10.9 %ffn_wgrad.2 = bf16[2,1536,768]{2,1,0:T(8,128)(2,1)} custom-call(bf16[1024,768]{1,0:T(8,128)(2,1)} %get-tuple-element.426.nl_ref, bf16[1024,3072]{1,0:T(8,128)(2,1)} %get-tuple-element.427.di_ref, bf16[1024,768]{1,0:T(8,128)(2,1)} %get-tuple-element.428.ds_ref, bf16[1024,3072]{1,0:T(8,128)(2,1)} %get-tuple-element.429.act_ref), custom_call_target="tpu_custom_call" | custom-call | flops 6600000000 | tf_op jit(solution)/shard_map/ffn_wgrad/pallas_call | solution.py:704
  201.3 17.9 %attn_bwd.2 = (bf16[1024,384]{1,0:T(8,128)(2,1)}, bf16[1024,384]{1,0:T(8,128)(2,1)}, bf16[1024,384]{1,0:T(8,128)(2,1)}, f32[1,384]{1,0:T(1,128)}) custom-call(bf16[1024,384]{1,0:T(8,128)(2,1)} %get-tuple-element.403.k_ref, bf16[1024,384]{1,0:T(8,128)(2,1)} %get-tuple-element.418.v_ref, bf16[1024,384]{1,0:T(8,128)(2,1)} %get-tuple-element.419.q2_ref.refs_9_, ...), custom_call_target="tpu_custom_call" | custom-call | flops 22000001024 | tf_op jit(solution)/shard_map/attn_bwd/pallas_call | solution.py:654
  219.2 7.3 %mid_wgrad.2 = bf16[1536,768]{1,0:T(8,128)(2,1)} custom-call(bf16[1024,768]{1,0:T(8,128)(2,1)} %get-tuple-element.440.ctx_ref, bf16[1024,768]{1,0:T(8,128)(2,1)} %get-tuple-element.441.dz_ref.refs_11_, bf16[1024,768]{1,0:T(8,128)(2,1)} %get-tuple-element.399.refs_6_.refs_14_.h_ref.refs_10_.refs_5_, ...), custom_call_target="tpu_custom_call" | custom-call | flops 5500000256 | tf_op jit(solution)/shard_map/mid_wgrad/pallas_call | solution.py:727
  229.0 22.0 %conv_bwd.2 = (bf16[1024,72]{1,0:T(8,128)(2,1)}, bf16[1024,384]{1,0:T(8,128)(2,1)}, bf16[1024,384]{1,0:T(8,128)(2,1)}, bf16[1024,384]{1,0:T(8,128)(2,1)}, bf16[1...) custom-call(s32[2]{0:T(128)} %get-tuple-element.664.place_ref, ...), custom_call_target="tpu_custom_call" | custom-call | flops 29699999744 | tf_op jit(solution)/shard_map/conv_bwd/pallas_call | solution.py:141
  254.3 10.0 %last_wgrad.2 = bf16[1280,768]{1,0:T(8,128)(2,1)} custom-call(s32[2]{0:T(128)} %get-tuple-element.664.place_ref, bf16[768,1536]{1,0:T(8,128)(2,1)} %bitcast.86, bf16[240,1536]{1,0:T(8,128)(2,1)} %collective-permute-done.refs_2_.refs_1_, bf16[240,1536]{1,0:T(8,128)(2,1)} %collective-permute-done.1.refs_3_.refs_2_, bf16[240,1536]{1,0:T(8,128)(2,1)} %copy-done.61, ...), custom_call_target="tpu_custom_call" | custom-call | flops 9900000256 | tf_op jit(solution)/shard_map/last_wgrad/pallas_call | solution.py:141
  268.2 8.5 %in_bwd.2.refs_11_ = bf16[1024,768]{1,0:T(8,128)(2,1)} custom-call(s32[2]{0:T(128)} %get-tuple-element.664.place_ref, bf16[768,1536]{1,0:T(8,128)(2,1)} %bitcast.87, bf16[240,1536]{1,0:T(8,128)(2,1)} %collective-permute-done.refs_2_.refs_1_, bf16[240,1536]{1,0:T(8,128)(2,1)} %collective-permute-done.1.refs_3_.refs_2_, bf16[240,1536]{1,0:T(8,128)(2,1)} %copy-done.61, ...), custom_call_target="tpu_custom_call" | custom-call | flops 8800000000 | tf_op jit(solution)/shard_map/in_bwd/pallas_call | solution.py:141
  280.0 18.9 %ffn_bwd.3 = (bf16[1024,768]{1,0:T(8,128)(2,1)}, bf16[1024,3072]{1,0:T(8,128)(2,1)}, bf16[1024,768]{1,0:T(8,128)(2,1)}, bf16[384,1024]{1,0:T(8,128)(2,1)}, bf16[...) custom-call(s32[2]{0:T(128)} %get-tuple-element.664.place_ref, ...), custom_call_target="tpu_custom_call" | custom-call | flops 19800000512 | tf_op jit(solution)/shard_map/ffn_bwd/pallas_call | solution.py:141
  300.4 10.9 %ffn_wgrad.3 = bf16[2,1536,768]{2,1,0:T(8,128)(2,1)} custom-call(bf16[1024,768]{1,0:T(8,128)(2,1)} %get-tuple-element.497.nl_ref, bf16[1024,3072]{1,0:T(8,128)(2,1)} %get-tuple-element.498.di_ref, bf16[1024,768]{1,0:T(8,128)(2,1)} %get-tuple-element.499.ds_ref, bf16[1024,3072]{1,0:T(8,128)(2,1)} %get-tuple-element.500.act_ref), custom_call_target="tpu_custom_call" | custom-call | flops 6600000000 | tf_op jit(solution)/shard_map/ffn_wgrad/pallas_call | solution.py:704
  321.8 18.3 %attn_bwd.3 = (bf16[1024,384]{1,0:T(8,128)(2,1)}, bf16[1024,384]{1,0:T(8,128)(2,1)}, bf16[1024,384]{1,0:T(8,128)(2,1)}, f32[1,384]{1,0:T(1,128)}) custom-call(bf16[1024,384]{1,0:T(8,128)(2,1)} %get-tuple-element.383.k_ref, bf16[1024,384]{1,0:T(8,128)(2,1)} %get-tuple-element.493.v_ref, bf16[1024,384]{1,0:T(8,128)(2,1)} %get-tuple-element.494.q2_ref.refs_9_, ...), custom_call_target="tpu_custom_call" | custom-call | flops 22000001024 | tf_op jit(solution)/shard_map/attn_bwd/pallas_call | solution.py:654
  345.7 7.2 %mid_wgrad.3 = bf16[1536,768]{1,0:T(8,128)(2,1)} custom-call(bf16[1024,768]{1,0:T(8,128)(2,1)} %get-tuple-element.522.ctx_ref, bf16[1024,768]{1,0:T(8,128)(2,1)} %get-tuple-element.523.dz_ref.refs_11_, bf16[1024,768]{1,0:T(8,128)(2,1)} %bitcast_select_fusion.refs_6_.refs_14_.h_ref.refs_10_.refs_5_, ...), custom_call_target="tpu_custom_call" | custom-call | flops 5500000256 | tf_op jit(solution)/shard_map/mid_wgrad/pallas_call | solution.py:727
  354.3 7.8 %collective-permute-done.21 = bf16[80,768]{1,0:T(8,128)(2,1)S(1)} collective-permute-done((bf16[80,768]{1,0:T(8,128)(2,1)S(1)}, bf16[80,768]{1,0:T(8,128)(2,1)S(1)}, u32[]{:S(2)}, u32[]{:S(2)}) %collective-permute-start.21) | collective-permute-done | bytes 122912 | tf_op jit(solution)/shard_map/ppermute | solution.py:884
  365.7 22.0 %conv_bwd.3 = (bf16[1024,72]{1,0:T(8,128)(2,1)}, bf16[1024,384]{1,0:T(8,128)(2,1)}, bf16[1024,384]{1,0:T(8,128)(2,1)}, bf16[1024,384]{1,0:T(8,128)(2,1)}, bf16[1...) custom-call(s32[2]{0:T(128)} %get-tuple-element.664.place_ref, ...), custom_call_target="tpu_custom_call" | custom-call | flops 29699999744 | tf_op jit(solution)/shard_map/conv_bwd/pallas_call | solution.py:141
  389.8 10.1 %last_wgrad.3 = bf16[1280,768]{1,0:T(8,128)(2,1)} custom-call(s32[2]{0:T(128)} %get-tuple-element.664.place_ref, bf16[768,1536]{1,0:T(8,128)(2,1)} %bitcast.88, bf16[240,1536]{1,0:T(8,128)(2,1)} %collective-permute-done.refs_2_.refs_1_, bf16[240,1536]{1,0:T(8,128)(2,1)} %collective-permute-done.1.refs_3_.refs_2_, bf16[240,1536]{1,0:T(8,128)(2,1)} %copy-done.61, ...), custom_call_target="tpu_custom_call" | custom-call | flops 9900000256 | tf_op jit(solution)/shard_map/last_wgrad/pallas_call | solution.py:141
  412.6 8.5 %in_bwd.3 = bf16[1024,768]{1,0:T(8,128)(2,1)} custom-call(s32[2]{0:T(128)} %get-tuple-element.664.place_ref, bf16[768,1536]{1,0:T(8,128)(2,1)} %bitcast.89, bf16[240,1536]{1,0:T(8,128)(2,1)} %collective-permute-done.refs_2_.refs_1_, bf16[240,1536]{1,0:T(8,128)(2,1)} %collective-permute-done.1.refs_3_.refs_2_, bf16[240,1536]{1,0:T(8,128)(2,1)} %copy-done.61, ...), custom_call_target="tpu_custom_call" | custom-call | flops 8800000000 | tf_op jit(solution)/shard_map/in_bwd/pallas_call | solution.py:141
  429.7 5.7 collective-permute-done.27
  451.1 8.3 %collective-permute-done.31 = bf16[160,768]{1,0:T(8,128)(2,1)} collective-permute-done((bf16[160,768]{1,0:T(8,128)(2,1)}, bf16[160,768]{1,0:T(8,128)(2,1)}, u32[]{:S(2)}, u32[]{:S(2)}) %collective-permute-start.31) | collective-permute-done | bytes 245792 | tf_op jit(solution)/shard_map/ppermute | solution.py:884
  472.4 8.2 %collective-permute-done.33 = bf16[80,768]{1,0:T(8,128)(2,1)S(1)} collective-permute-done((bf16[80,768]{1,0:T(8,128)(2,1)}, bf16[80,768]{1,0:T(8,128)(2,1)S(1)}, u32[]{:S(2)}, u32[]{:S(2)}) %collective-permute-start.33) | collective-permute-done | bytes 122912 | tf_op jit(solution)/shard_map/ppermute | solution.py:884
  497.1 13.3 %collective-permute-done.38 = bf16[80,768]{1,0:T(8,128)(2,1)S(1)} collective-permute-done((bf16[80,768]{1,0:T(8,128)(2,1)S(1)}, bf16[80,768]{1,0:T(8,128)(2,1)S(1)}, u32[]{:S(2)}, u32[]{:S(2)}) %collective-permute-start.38) | collective-permute-done | bytes 122912 | tf_op jit(solution)/shard_map/ppermute | solution.py:884
  515.1 18.7 %collective-permute-done.40 = bf16[160,768]{1,0:T(8,128)(2,1)S(1)} collective-permute-done((bf16[160,768]{1,0:T(8,128)(2,1)S(1)}, bf16[160,768]{1,0:T(8,128)(2,1)S(1)}, u32[]{:S(2)}, u32[]{:S(2)}) %collective-permute-start.40) | collective-permute-done | bytes 245792 | tf_op jit(solution)/shard_map/ppermute | solution.py:884
  544.3 7.8 %collective-permute-done.44 = bf16[320,768]{1,0:T(8,128)(2,1)S(1)} collective-permute-done((bf16[320,768]{1,0:T(8,128)(2,1)S(1)}, bf16[320,768]{1,0:T(8,128)(2,1)S(1)}, u32[]{:S(2)}, u32[]{:S(2)}) %collective-permute-start.44) | collective-permute-done | bytes 491552 | tf_op jit(solution)/shard_map/ppermute | solution.py:884
  554.0 6.8 %wide_out.1 = (f32[768,1536]{1,0:T(8,128)}, f32[3072,384]{1,0:T(8,128)}) custom-call(s32[1]{0:T(128)} %bitcast.30.at_ref, bf16[1536,768]{1,0:T(8,128)(2,1)} %copy-done.8, bf16[1536,768]{1,0:T(8,128)(2,1)} %copy-done.53), custom_call_target="tpu_custom_call" | custom-call | flops 7699999744 | tf_op jit(solution)/shard_map/wide_out/pallas_call | solution.py:1058
  561.7 6.2 %last_out.1 = (f32[768,1536]{1,0:T(8,128)}, f32[768,384]{1,0:T(8,128)}, f32[768,768]{1,0:T(8,128)}, f32[1,1152]{1,0:T(1,128)}, f32[9,1,768]{2,1,0:T(1,128)}, /*i...) custom-call(s32[2]{0:T(128)} %get-tuple-element.665.at_ref, ...), custom_call_target="tpu_custom_call" | custom-call | flops 6600000000 | tf_op jit(solution)/shard_map/last_out/pallas_call | solution.py:1126
  (325 shorter events, 161.3 us)
Async XLA Ops:
  7.2 309.6 %reduce-scatter.3.cloned.1.call-start = ((), (), s32[]{:S(2)}) async-start(), calls=%async_computation.2 | async-start | bytes 5013504 | tf_op jit(solution)/shard_map/reduce_scatter | solution.py:891
  11.8 19.8 %collective-permute-start = (bf16[240,1536]{1,0:T(8,128)(2,1)}, bf16[240,1536]{1,0:T(8,128)(2,1)}, u32[]{:S(2)}, u32[]{:S(2)}) collective-permute-start(bf16[240,1536]{1,0:T(8,128)(2,1)} %get-tuple-element.349), channel_id=1, source_target_pairs={{0,16},{16,0},{1,17},{17,1},{2,18},{18,2},{3,19},{19,3},{4,20},{20... | collective-permute-start | bytes 2211848 | tf_op jit(solution)/shard_map/ppermute | solution.py:880
  32.2 23.5 %collective-permute-start.3 = (bf16[288,1536]{1,0:T(8,128)(2,1)S(1)}, bf16[288,1536]{1,0:T(8,128)(2,1)S(1)}, u32[]{:S(2)}, u32[]{:S(2)}) collective-permute-start(bf16[288,1536]{1,0:T(8,128)(2,1)S(1)} %copy-done.60), channel_id=1, source_target_pairs={{0,16},{16,0},{1,17},{17,1},{2,18},{18,2},{3,19},{19,3},{4,20},{20... | collective-permute-start | bytes 2654216 | tf_op jit(solution)/shard_map/ppermute | solution.py:880
  33.9 21.7 %collective-permute-start.1 = (bf16[240,1536]{1,0:T(8,128)(2,1)}, bf16[240,1536]{1,0:T(8,128)(2,1)}, u32[]{:S(2)}, u32[]{:S(2)}) collective-permute-start(bf16[240,1536]{1,0:T(8,128)(2,1)} %collective-permute-done.refs_2_.refs_1_), channel_id=1, source_target_pairs={{0,2},{1,3},{2,0},{3,1},{4,6},{5,7},{6,4},{7,5},{8,10},{9,11},{10,... | collective-permute-start | bytes 2211848 | tf_op jit(solution)/shard_map/ppermute | solution.py:884
  35.5 20.2 %collective-permute-start.2 = (bf16[240,1536]{1,0:T(8,128)(2,1)}, bf16[240,1536]{1,0:T(8,128)(2,1)S(1)}, u32[]{:S(2)}, u32[]{:S(2)}) collective-permute-start(bf16[240,1536]{1,0:T(8,128)(2,1)} %collective-permute-done.refs_2_.refs_1_), channel_id=1, source_target_pairs={{0,1},{1,0},{2,3},{3,2},{4,5},{5,4},{6,7},{7,6},{8,9},{9,8},{10,11... | collective-permute-start | bytes 2211848 | tf_op jit(solution)/shard_map/ppermute | solution.py:884
  35.5 20.2 %collective-permute-start.4 = (bf16[76,768]{1,0:T(8,128)(2,1)S(1)}, bf16[76,768]{1,0:T(8,128)(2,1)S(1)}, u32[]{:S(2)}, u32[]{:S(2)}) collective-permute-start(bf16[76,768]{1,0:T(8,128)(2,1)S(1)} %fusion.8), channel_id=1, source_target_pairs={{0,16},{16,0},{1,17},{17,1},{2,18},{18,2},{3,19},{19,3},{4,20},{20... | collective-permute-start | bytes 350216 | tf_op jit(solution)/shard_map/ppermute | solution.py:880
  57.7 21.8 %collective-permute-start.6 = (bf16[288,1536]{1,0:T(8,128)(2,1)S(1)}, bf16[288,1536]{1,0:T(8,128)(2,1)S(1)}, u32[]{:S(2)}, u32[]{:S(2)}) collective-permute-start(bf16[288,1536]{1,0:T(8,128)(2,1)S(1)} %collective-permute-done.3.refs_2_), channel_id=1, source_target_pairs={{0,2},{1,3},{2,0},{3,1},{4,6},{5,7},{6,4},{7,5},{8,10},{9,11},{10,... | collective-permute-start | bytes 2654216 | tf_op jit(solution)/shard_map/ppermute | solution.py:884
  59.2 20.3 %collective-permute-start.7 = (bf16[288,1536]{1,0:T(8,128)(2,1)S(1)}, bf16[288,1536]{1,0:T(8,128)(2,1)S(1)}, u32[]{:S(2)}, u32[]{:S(2)}) collective-permute-start(bf16[288,1536]{1,0:T(8,128)(2,1)S(1)} %collective-permute-done.3.refs_2_), channel_id=1, source_target_pairs={{0,1},{1,0},{2,3},{3,2},{4,5},{5,4},{6,7},{7,6},{8,9},{9,8},{10,11... | collective-permute-start | bytes 2654216 | tf_op jit(solution)/shard_map/ppermute | solution.py:884
  59.2 16.0 %collective-permute-start.8 = (bf16[192,1536]{1,0:T(8,128)(2,1)}, bf16[192,1536]{1,0:T(8,128)(2,1)S(1)}, u32[]{:S(2)}, u32[]{:S(2)}) collective-permute-start(bf16[192,1536]{1,0:T(8,128)(2,1)} %get-tuple-element.376), channel_id=1, source_target_pairs={{0,16},{16,0},{1,17},{17,1},{2,18},{18,2},{3,19},{19,3},{4,20},{20... | collective-permute-start | bytes 1769480 | tf_op jit(solution)/shard_map/ppermute | solution.py:880
  79.5 15.9 %collective-permute-start.9 = (bf16[288,1536]{1,0:T(8,128)(2,1)S(1)}, bf16[288,1536]{1,0:T(8,128)(2,1)S(1)}, u32[]{:S(2)}, u32[]{:S(2)}) collective-permute-start(bf16[288,1536]{1,0:T(8,128)(2,1)S(1)} %collective-permute-done.6.refs_3_), channel_id=1, source_target_pairs={{0,1},{1,0},{2,3},{3,2},{4,5},{5,4},{6,7},{7,6},{8,9},{9,8},{10,11... | collective-permute-start | bytes 2654216 | tf_op jit(solution)/shard_map/ppermute | solution.py:884
  79.6 15.8 %collective-permute-start.10 = (bf16[192,1536]{1,0:T(8,128)(2,1)S(1)}, bf16[192,1536]{1,0:T(8,128)(2,1)}, u32[]{:S(2)}, u32[]{:S(2)}) collective-permute-start(bf16[192,1536]{1,0:T(8,128)(2,1)S(1)} %collective-permute-done.8.refs_7_), channel_id=1, source_target_pairs={{0,2},{1,3},{2,0},{3,1},{4,6},{5,7},{6,4},{7,5},{8,10},{9,11},{10,... | collective-permute-start | bytes 1769480 | tf_op jit(solution)/shard_map/ppermute | solution.py:884
  228.9 22.0 %collective-permute-start.13 = (bf16[768,768]{1,0:T(8,128)(2,1)}, bf16[768,768]{1,0:T(8,128)(2,1)S(1)}, u32[]{:S(2)}, u32[]{:S(2)}) collective-permute-start(bf16[768,768]{1,0:T(8,128)(2,1)} %constant_dynamic-slice_fusion.3), channel_id=1, source_target_pairs={{0,1},{1,0},{2,3},{3,2},{4,5},{5,4},{6,7},{7,6},{8,9},{9,8},{10,11... | collective-permute-start | bytes 3538952 | tf_op jit(solution)/shard_map/ppermute | solution.py:884
  228.9 192.3 %reduce-scatter.5.cloned.1.call-start = ((), (), s32[]{:S(2)}) async-start(), calls=%async_computation.3 | async-start | bytes 5013504 | tf_op jit(solution)/shard_map/reduce_scatter | solution.py:891
  267.0 44.3 %collective-permute-start.17 = (bf16[1024,768]{1,0:T(8,128)(2,1)S(1)}, bf16[1024,768]{1,0:T(8,128)(2,1)S(1)}, u32[]{:S(2)}, u32[]{:S(2)}) collective-permute-start(bf16[1024,768]{1,0:T(8,128)(2,1)S(1)} %broadcast_select_fusion.2), channel_id=1, source_target_pairs={{0,16},{16,0},{1,17},{17,1},{2,18},{18,2},{3,19},{19,3},{4,20},{20... | collective-permute-start | bytes 4718600 | tf_op jit(solution)/shard_map/ppermute | solution.py:880
  276.7 39.3 %collective-permute-start.15 = (bf16[768,384]{1,0:T(8,128)(2,1)S(1)}, bf16[768,384]{1,0:T(8,128)(2,1)S(1)}, u32[]{:S(2)}, u32[]{:S(2)}) collective-permute-start(bf16[768,384]{1,0:T(8,128)(2,1)S(1)} %copy-done.20), channel_id=1, source_target_pairs={{0,16},{16,0},{1,17},{17,1},{2,18},{18,2},{3,19},{19,3},{4,20},{20... | collective-permute-start | bytes 1769480 | tf_op jit(solution)/shard_map/ppermute | solution.py:880
  298.9 17.9 %collective-permute-start.16 = (bf16[320,768]{1,0:T(8,128)(2,1)S(1)}, bf16[320,768]{1,0:T(8,128)(2,1)}, u32[]{:S(2)}, u32[]{:S(2)}) collective-permute-start(bf16[320,768]{1,0:T(8,128)(2,1)S(1)} %add_convert_fusion.3), channel_id=1, source_target_pairs={{0,2},{1,3},{2,0},{3,1},{4,6},{5,7},{6,4},{7,5},{8,10},{9,11},{10,... | collective-permute-start | bytes 1474568 | tf_op jit(solution)/shard_map/ppermute | solution.py:884
  319.6 20.4 %collective-permute-start.18 = (bf16[384,384]{1,0:T(8,128)(2,1)S(1)}, bf16[384,384]{1,0:T(8,128)(2,1)S(1)}, u32[]{:S(2)}, u32[]{:S(2)}) collective-permute-start(bf16[384,384]{1,0:T(8,128)(2,1)S(1)} %add_convert_fusion.6), channel_id=1, source_target_pairs={{0,4},{1,5},{2,6},{3,7},{4,0},{5,1},{6,2},{7,3},{8,12},{9,13},{10,... | collective-permute-start | bytes 884744 | tf_op jit(solution)/shard_map/ppermute | solution.py:884
  321.2 18.8 %collective-permute-start.19 = (bf16[160,768]{1,0:T(8,128)(2,1)S(1)}, bf16[160,768]{1,0:T(8,128)(2,1)S(1)}, u32[]{:S(2)}, u32[]{:S(2)}) collective-permute-start(bf16[160,768]{1,0:T(8,128)(2,1)S(1)} %add_convert_fusion.8), channel_id=1, source_target_pairs={{0,4},{1,5},{2,6},{3,7},{4,0},{5,1},{6,2},{7,3},{8,12},{9,13},{10,... | collective-permute-start | bytes 737288 | tf_op jit(solution)/shard_map/ppermute | solution.py:884
  342.7 19.4 %collective-permute-start.20 = (bf16[192,384]{1,0:T(8,128)(2,1)S(1)}, bf16[192,384]{1,0:T(8,128)(2,1)S(1)}, u32[]{:S(2)}, u32[]{:S(2)}) collective-permute-start(bf16[192,384]{1,0:T(8,128)(2,1)S(1)} %add_convert_fusion.10), channel_id=1, source_target_pairs={{0,8},{1,9},{2,10},{3,11},{4,12},{5,13},{6,14},{7,15},{8,0},{9,1},... | collective-permute-start | bytes 442376 | tf_op jit(solution)/shard_map/ppermute | solution.py:884
  345.4 16.7 %collective-permute-start.21 = (bf16[80,768]{1,0:T(8,128)(2,1)S(1)}, bf16[80,768]{1,0:T(8,128)(2,1)S(1)}, u32[]{:S(2)}, u32[]{:S(2)}) collective-permute-start(bf16[80,768]{1,0:T(8,128)(2,1)S(1)} %add_convert_fusion.15), channel_id=1, source_target_pairs={{0,8},{1,9},{2,10},{3,11},{4,12},{5,13},{6,14},{7,15},{8,0},{9,1},... | collective-permute-start | bytes 368648 | tf_op jit(solution)/shard_map/ppermute | solution.py:884
  363.9 23.9 %collective-permute-start.22 = (bf16[768,768]{1,0:T(8,128)(2,1)S(1)}, bf16[768,768]{1,0:T(8,128)(2,1)S(1)}, u32[]{:S(2)}, u32[]{:S(2)}) collective-permute-start(bf16[768,768]{1,0:T(8,128)(2,1)S(1)} %constant_dynamic-slice_fusion.1), channel_id=1, source_target_pairs={{0,1},{1,0},{2,3},{3,2},{4,5},{5,4},{6,7},{7,6},{8,9},{9,8},{10,11... | collective-permute-start | bytes 3538952 | tf_op jit(solution)/shard_map/ppermute | solution.py:884
  363.9 23.8 %collective-permute-start.23 = (bf16[96,384]{1,0:T(8,128)(2,1)S(1)}, bf16[96,384]{1,0:T(8,128)(2,1)S(1)}, u32[]{:S(2)}, u32[]{:S(2)}) collective-permute-start(bf16[96,384]{1,0:T(8,128)(2,1)S(1)} %add_convert_fusion.19), channel_id=1, source_target_pairs={{0,2},{1,3},{2,0},{3,1},{4,6},{5,7},{6,4},{7,5},{8,10},{9,11},{10,... | collective-permute-start | bytes 221192 | tf_op jit(solution)/shard_map/ppermute | solution.py:884
  389.7 15.5 %collective-permute-start.24 = (bf16[768,384]{1,0:T(8,128)(2,1)S(1)}, bf16[768,384]{1,0:T(8,128)(2,1)S(1)}, u32[]{:S(2)}, u32[]{:S(2)}) collective-permute-start(bf16[768,384]{1,0:T(8,128)(2,1)S(1)} %add_convert_fusion), channel_id=1, source_target_pairs={{0,16},{16,0},{1,17},{17,1},{2,18},{18,2},{3,19},{19,3},{4,20},{20... | collective-permute-start | bytes 1769480 | tf_op jit(solution)/shard_map/ppermute | solution.py:880
  442.1 17.3 %collective-permute-start.32 = (bf16[192,768]{1,0:T(8,128)(2,1)S(1)}, bf16[192,768]{1,0:T(8,128)(2,1)}, u32[]{:S(2)}, u32[]{:S(2)}) collective-permute-start(bf16[192,768]{1,0:T(8,128)(2,1)S(1)} %add_convert_fusion.4), channel_id=1, source_target_pairs={{0,8},{1,9},{2,10},{3,11},{4,12},{5,13},{6,14},{7,15},{8,0},{9,1},... | collective-permute-start | bytes 884744 | tf_op jit(solution)/shard_map/ppermute | solution.py:884
  465.4 17.4 %collective-permute-start.35 = (bf16[384,768]{1,0:T(8,128)(2,1)}, bf16[384,768]{1,0:T(8,128)(2,1)}, u32[]{:S(2)}, u32[]{:S(2)}) collective-permute-start(bf16[384,768]{1,0:T(8,128)(2,1)} %pad_maximum_fusion.6), channel_id=1, source_target_pairs={{0,4},{1,5},{2,6},{3,7},{4,0},{5,1},{6,2},{7,3},{8,12},{9,13},{10,... | collective-permute-start | bytes 1769480 | tf_op jit(solution)/shard_map/ppermute | solution.py:884
  465.7 15.0 %collective-permute-start.33 = (bf16[80,768]{1,0:T(8,128)(2,1)}, bf16[80,768]{1,0:T(8,128)(2,1)S(1)}, u32[]{:S(2)}, u32[]{:S(2)}) collective-permute-start(bf16[80,768]{1,0:T(8,128)(2,1)} %add_convert_fusion.14), channel_id=1, source_target_pairs={{0,8},{1,9},{2,10},{3,11},{4,12},{5,13},{6,14},{7,15},{8,0},{9,1},... | collective-permute-start | bytes 368648 | tf_op jit(solution)/shard_map/ppermute | solution.py:884
  492.3 18.1 %collective-permute-start.39 = (bf16[192,768]{1,0:T(8,128)(2,1)S(1)}, bf16[192,768]{1,0:T(8,128)(2,1)S(1)}, u32[]{:S(2)}, u32[]{:S(2)}) collective-permute-start(bf16[192,768]{1,0:T(8,128)(2,1)S(1)} %pad_maximum_fusion.9), channel_id=1, source_target_pairs={{0,8},{1,9},{2,10},{3,11},{4,12},{5,13},{6,14},{7,15},{8,0},{9,1},... | collective-permute-start | bytes 884744 | tf_op jit(solution)/shard_map/ppermute | solution.py:884
  493.4 40.4 %collective-permute-start.42 = (bf16[1024,768]{1,0:T(8,128)(2,1)S(1)}, bf16[1024,768]{1,0:T(8,128)(2,1)}, u32[]{:S(2)}, u32[]{:S(2)}) collective-permute-start(bf16[1024,768]{1,0:T(8,128)(2,1)S(1)} %copy-done.9), channel_id=1, source_target_pairs={{0,16},{16,0},{1,17},{17,1},{2,18},{18,2},{3,19},{19,3},{4,20},{20... | collective-permute-start | bytes 4718600 | tf_op jit(solution)/shard_map/ppermute | solution.py:880
  493.6 16.8 %collective-permute-start.38 = (bf16[80,768]{1,0:T(8,128)(2,1)S(1)}, bf16[80,768]{1,0:T(8,128)(2,1)S(1)}, u32[]{:S(2)}, u32[]{:S(2)}) collective-permute-start(bf16[80,768]{1,0:T(8,128)(2,1)S(1)} %add_convert_fusion.11), channel_id=1, source_target_pairs={{0,8},{1,9},{2,10},{3,11},{4,12},{5,13},{6,14},{7,15},{8,0},{9,1},... | collective-permute-start | bytes 368648 | tf_op jit(solution)/shard_map/ppermute | solution.py:884
  495.4 39.0 %collective-permute-start.43 = (bf16[768,768]{1,0:T(8,128)(2,1)}, bf16[768,768]{1,0:T(8,128)(2,1)}, u32[]{:S(2)}, u32[]{:S(2)}) collective-permute-start(bf16[768,768]{1,0:T(8,128)(2,1)} %pad_maximum_fusion.3), channel_id=1, source_target_pairs={{0,2},{1,3},{2,0},{3,1},{4,6},{5,7},{6,4},{7,5},{8,10},{9,11},{10,... | collective-permute-start | bytes 3538952 | tf_op jit(solution)/shard_map/ppermute | solution.py:884
  513.1 20.7 %collective-permute-start.41 = (bf16[384,768]{1,0:T(8,128)(2,1)}, bf16[384,768]{1,0:T(8,128)(2,1)}, u32[]{:S(2)}, u32[]{:S(2)}) collective-permute-start(bf16[384,768]{1,0:T(8,128)(2,1)} %pad_maximum_fusion.7), channel_id=1, source_target_pairs={{0,4},{1,5},{2,6},{3,7},{4,0},{5,1},{6,2},{7,3},{8,12},{9,13},{10,... | collective-permute-start | bytes 1769480 | tf_op jit(solution)/shard_map/ppermute | solution.py:884
  513.1 20.7 %collective-permute-start.40 = (bf16[160,768]{1,0:T(8,128)(2,1)S(1)}, bf16[160,768]{1,0:T(8,128)(2,1)S(1)}, u32[]{:S(2)}, u32[]{:S(2)}) collective-permute-start(bf16[160,768]{1,0:T(8,128)(2,1)S(1)} %pad_maximum_fusion.10), channel_id=1, source_target_pairs={{0,4},{1,5},{2,6},{3,7},{4,0},{5,1},{6,2},{7,3},{8,12},{9,13},{10,... | collective-permute-start | bytes 737288 | tf_op jit(solution)/shard_map/ppermute | solution.py:884
  (84 other events, 821.1 us)
Sparse Core Ops, SparseCore 0:
  229.0 76.1 reduce-scatter.2
  321.9 76.6 reduce-scatter.4
